TPU v7x, 768 devices: a whole 4x8x12 slice. The times are simulated.
768 devices in a mesh: row: 16 (over x_hi, y), col: 48 (over x_lo, z, core).
Axes of the slice: x: 4 (x_hi: 2, x_lo: 2; x = x_hi * 2 + x_lo), y: 8, z: 12, core: 2. Of those that a mesh axis runs over, the one named last changes fastest.
Arguments:
- density: float32 [6144, 6144], P('row', 'col'), as said below
- atom_sizes: int32 [96], replicated, may hold values from 32 to 64
- pattern: int32 [96, 96], P('row', 'col'), may hold values from 0 to 1, as said below
- kept: int32 [96, 96], P('row', 'col'), may hold values 0 or 1
Outputs:
- square: float32 [6144, 6144], P('row', 'col')
- purified: float32 [6144, 6144], P('row', 'col')
Inputs may be any that keep to these rules, and one draw needn't show every extreme that they name: density is symmetric. pattern is symmetric.
All inputs are finite; a program needn't handle non-finite values. No bound on the sum of `kept` on one device may be relied on, other than what follows from the above.
Results may differ from a plain program's by a relative error of at most 0.000059.
Values sent between devices are 32-bit elements; how exact they have to be, the bound alone decides.
No kernel may reach another device: no remote copies, remote signals or barrier semaphores. Data moves between devices by JAX's collectives and lax.ppermute only.
A program may use at most 32 MiB of HBM per device.

v0:
```python
import jax
import jax.numpy as jnp
from jax import lax
from jax.sharding import PartitionSpec as P

BS = 64


def local_masks(atom_sizes, pattern, kept, row_blocks, col_blocks):
    first_row = lax.axis_index("row") * row_blocks
    first_col = lax.axis_index("col") * col_blocks
    offsets = jnp.arange(BS, dtype=jnp.int32)
    sizes_rows = lax.dynamic_slice_in_dim(atom_sizes, first_row, row_blocks, 0)
    sizes_cols = lax.dynamic_slice_in_dim(atom_sizes, first_col, col_blocks, 0)
    valid_rows = (offsets[None, :] < sizes_rows[:, None]).astype(jnp.float32)
    valid_cols = (offsets[None, :] < sizes_cols[:, None]).astype(jnp.float32)
    patf = pattern.astype(jnp.float32)
    mask = patf[:, None, :, None] * valid_rows[:, :, None, None] * valid_cols[None, None, :, :]
    filt = jnp.broadcast_to(
        kept.astype(jnp.float32)[:, None, :, None], (row_blocks, BS, col_blocks, BS)
    )
    shape = (row_blocks * BS, col_blocks * BS)
    return (mask.reshape(shape), filt.reshape(shape))


def body(density, atom_sizes, pattern, kept):
    row_blocks = pattern.shape[0]
    col_blocks = pattern.shape[1]
    mask, filt = local_masks(atom_sizes, pattern, kept, row_blocks, col_blocks)
    masked = density * mask
    panel = lax.all_gather(masked, "row", axis=0, tiled=True)
    highest = lax.Precision.HIGHEST
    block = panel
    square = filt * jnp.dot(
        lax.all_gather(masked, "col", axis=1, tiled=True),
        block,
        precision=highest,
        preferred_element_type=jnp.float32,
    )
    block = panel
    cube = filt * jnp.dot(
        lax.all_gather(square, "col", axis=1, tiled=True),
        block,
        precision=highest,
        preferred_element_type=jnp.float32,
    )
    purified = 3.0 * square - 2.0 * cube
    return (square, purified)


def solution(mesh):
    placed = (P("row", "col"), P(), P("row", "col"), P("row", "col"))
    return jax.shard_map(
        body,
        mesh=mesh,
        in_specs=placed,
        out_specs=(P("row", "col"), P("row", "col")),
        check_vma=False,
    )
```

profile of v0, /device:TPU:1, one launch (start us, length us, event | category | flops | bytes accessed | tf_op | source)
XLA Modules:
  0.0 396.0 jit_solution(7982272185660821875)
XLA Ops:
  7.2 0.0 all-gather.6.cloned.1.call-start
  7.2 0.7 dynamic_slice.6
  8.0 0.1 fusion.2
  8.0 0.7 convert_element_type.21
  8.7 0.1 copy.7
  8.8 0.1 broadcast_multiply_fusion
  8.9 0.5 mul.65
  9.4 0.2 mul.66
  9.6 0.1 lt.49
  9.7 0.7 dynamic_slice.7
  10.5 0.1 lt.51
  10.5 0.1 lt.52
  10.6 1.6 multiply_multiply_fusion
  12.3 0.0 all-gather.6.cloned.1.call-update
  12.3 0.0 all-gather.4.cloned.1.call-start
  12.3 0.7 all-gather.4.cloned.1.call-update
  13.0 0.0 all-gather.8.cloned.1.call-start
  13.1 0.7 convert_element_type.20
  13.8 0.1 copy.6
  13.9 0.2 broadcast_in_dim.2
  14.0 0.2 reshape.59
  14.3 106.4 %all-gather.6.cloned.1.call-done = f32[6144,128]{1,0:T(8,128)} async-done(((f32[384,128]{1,0:T(8,128)}), f32[6144,128]{1,0:T(8,128)}) %all-gather.6.cloned.1.call-update) | async-done | bytes 3145744 | tf_op jit(solution)/shard_map/all_gather | solution.py:31
  120.6 0.0 copy-start
  120.6 126.4 %all-gather.4.cloned.1.call-done = f32[384,6144]{1,0:T(8,128)} async-done(((f32[384,128]{1,0:T(8,128)}), f32[384,6144]{1,0:T(8,128)}) %all-gather.4.cloned.1.call-update) | async-done | bytes 9437200 | tf_op jit(solution)/shard_map/all_gather | solution.py:35
  247.0 11.2 %convolution_multiply_fusion.1 = f32[384,128]{1,0:T(8,128)} fusion(f32[384,128]{1,0:T(8,128)S(1)} %reshape.59, f32[384,6144]{1,0:T(8,128)} %all-gather.4.cloned.1.call-done, f32[6144,128]{1,0:T(8,128)} %all-gather.6.cloned.1.call-done), kind=kOutput, calls=%fused_computation.1 | convolution fusion | flops 3623927808 | bytes 12976128 | tf_op jit(solution)/shard_map/dot_general | solution.py:34
  258.3 0.0 all-gather.8.cloned.1.call-update
  258.3 120.4 %all-gather.8.cloned.1.call-done = f32[384,6144]{1,0:T(8,128)} async-done(((f32[384,128]{1,0:T(8,128)}), f32[384,6144]{1,0:T(8,128)}) %all-gather.8.cloned.1.call-update) | async-done | bytes 9437200 | tf_op jit(solution)/shard_map/all_gather | solution.py:42
  378.7 0.0 copy-done
  378.7 10.8 %fusion.1 = f32[384,128]{1,0:T(8,128)} fusion(f32[384,128]{1,0:T(8,128)S(1)} %reshape.59, f32[384,6144]{1,0:T(8,128)} %all-gather.8.cloned.1.call-done, f32[6144,128]{1,0:T(8,128)S(1)} %copy-done, f32[384,128]{1,0:T(8,128)} %convolution_multiply_fusion.1), kind=kOutput, calls=%fused_computation.3 | convolution fusion | flops 3624075264 | bytes 13172736 | tf_op jit(solution)/shard_map/dot_general | solution.py:41
  (2 shorter events, 0.0 us)
Async XLA Ops:
  7.2 113.5 %all-gather.6.cloned.1.call-start = ((), (), s32[]{:S(2)}) async-start(), calls=%async_computation.1 | async-start | bytes 3342336 | tf_op jit(solution)/shard_map/all_gather | solution.py:31
  12.3 234.8 %all-gather.4.cloned.1.call-start = ((), (), s32[]{:S(2)}) async-start(), calls=%async_computation | async-start | bytes 9633792 | tf_op jit(solution)/shard_map/all_gather | solution.py:35
  13.0 365.7 %all-gather.8.cloned.1.call-start = ((), (), s32[]{:S(2)}) async-start(), calls=%async_computation.2 | async-start | bytes 9633792 | tf_op jit(solution)/shard_map/all_gather | solution.py:42
  120.6 258.1 %copy-start = (f32[6144,128]{1,0:T(8,128)S(1)}, f32[6144,128]{1,0:T(8,128)}, u32[]{:S(2)}) copy-start(f32[6144,128]{1,0:T(8,128)} %all-gather.6.cloned.1.call-done) | copy-start | bytes 9437188
Sparse Core Ops, SparseCore 0:
  12.4 108.1 all-gather.5
  123.6 123.4 all-gather.3
  258.4 120.2 all-gather.7
where the time goes:
time: 396 us
  waiting for transfers between devices  354 us (89%)
  matrix products  22 us (6%)
  between operations  13.8 us (3%)
    all_gather x1, waiting for transfers between devices, body(): lax.all_gather(masked, 'col', axis=1, tiled=True)  126 us
    all_gather x1, waiting for transfers between devices, body(): lax.all_gather(square, 'col', axis=1, tiled=True)  120 us
    all_gather x1, waiting for transfers between devices, body(): panel = lax.all_gather(masked, 'row', axis=0, tiled=True)  106 us
    dot_general x1, matrix products, body(): jnp.dot(lax.all_gather(masked, 'col', axis=1, tiled=True), block, precisi...  11.2 us
    dot_general x1, matrix products, body(): jnp.dot(lax.all_gather(square, 'col', axis=1, tiled=True), block, precisi...  10.8 us
  transfers between devices with their start and end apart: 3, of which 3 were waited for; matrix products, arithmetic and copies ran while one was open for 0% of the time, Pallas kernels for 0%

commit v1 on v0

v1 whole, which is shorter than its diff:
```python
import jax
import jax.numpy as jnp
from jax import lax
from jax.sharding import Mesh, PartitionSpec as P

BS = 64
AXES = ("xh", "y", "xl", "z", "c")
ROW = ("xh", "y")
COL = ("xl", "z", "c")


def local_masks(atom_sizes, pattern, kept):
    row_blocks, col_blocks = pattern.shape
    first_row = lax.axis_index(ROW) * row_blocks
    first_col = lax.axis_index(COL) * col_blocks
    offsets = jnp.arange(BS, dtype=jnp.int32)
    sizes_rows = lax.dynamic_slice_in_dim(atom_sizes, first_row, row_blocks, 0)
    sizes_cols = lax.dynamic_slice_in_dim(atom_sizes, first_col, col_blocks, 0)
    valid_rows = (offsets[None, :] < sizes_rows[:, None]).astype(jnp.float32)
    valid_cols = (offsets[None, :] < sizes_cols[:, None]).astype(jnp.float32)
    patf = pattern.astype(jnp.float32)
    mask = patf[:, None, :, None] * valid_rows[:, :, None, None] * valid_cols[None, None, :, :]
    filt = jnp.broadcast_to(
        kept.astype(jnp.float32)[:, None, :, None], (row_blocks, BS, col_blocks, BS)
    )
    shape = (row_blocks * BS, col_blocks * BS)
    return (mask.reshape(shape), filt.reshape(shape))


def body(density, atom_sizes, pattern, kept):
    mask, filt = local_masks(atom_sizes, pattern, kept)
    masked = density * mask
    rows, cols = masked.shape
    xl = lax.axis_index("xl")

    left = lax.all_gather(masked, ("z", "c"), axis=1, tiled=True)

    four = lax.all_gather(masked, ("xh", "xl"), axis=0)
    four = four.reshape(2, 2, rows, cols)
    pair = lax.dynamic_index_in_dim(four, xl, 0, keepdims=False)
    pair = jnp.concatenate([pair[0], pair[1]], axis=1)
    right = lax.all_gather(pair, "y", axis=0, tiled=True)

    def product(a):
        part = jnp.dot(
            a, right, precision=lax.Precision.HIGHEST, preferred_element_type=jnp.float32
        )
        part = jnp.stack([part[:, :cols], part[:, cols:]])
        mine = lax.dynamic_index_in_dim(part, xl, 0, keepdims=False)
        other = lax.dynamic_index_in_dim(part, 1 - xl, 0, keepdims=False)
        return mine + lax.ppermute(other, "xl", [(0, 1), (1, 0)])

    square = filt * product(left)
    cube = filt * product(lax.all_gather(square, ("z", "c"), axis=1, tiled=True))
    purified = 3.0 * square - 2.0 * cube
    return (square, purified)


def solution(mesh):
    fine = Mesh(mesh.devices.reshape(2, 8, 2, 12, 2), AXES)
    placed = (P(ROW, COL), P(), P(ROW, COL), P(ROW, COL))
    return jax.shard_map(
        body,
        mesh=fine,
        in_specs=placed,
        out_specs=(P(ROW, COL), P(ROW, COL)),
        check_vma=False,
    )
```

time: 396 us -> 266 us (0.67)
  waiting for transfers between devices: 354 us -> 209 us
  blocking collectives: 0 us -> 11.6 us
  matrix products: 22 us -> 13.2 us
  starting transfers between devices: 0.12 us -> 6.3 us
    all_gather x3, waiting for transfers between devices: 353 us -> 201 us  [the longest x1 73.1 us: body(): left = lax.all_gather(masked, ('z', 'c'), axis=1, tiled=True)]
    all_gather x0 -> x1, blocking collectives: none -> 11.6 us  [body(): four = lax.all_gather(masked, ('xh', 'xl'), axis=0)]
    dot_general x2, matrix products: 22 us -> 13.2 us  [product(): jnp.dot(a, right, precision=lax.Precision.HIGHEST, preferred_element_type...]
    ppermute x0 -> x2, waiting for transfers between devices: none -> 7.41 us  [product(): return mine + lax.ppermute(other, 'xl', [(0, 1), (1, 0)])]
    ppermute x0 -> x2, starting transfers between devices: none -> 6.19 us  [product(): return mine + lax.ppermute(other, 'xl', [(0, 1), (1, 0)])]
  transfers between devices with their start and end apart: 3 -> 5, of which waited for: 3 -> 5; matrix products, arithmetic and copies ran while one was open for 0% -> 1% of each run, Pallas kernels for 0% -> 0%
where the time goes in v1:
time: 266 us
  waiting for transfers between devices  209 us (79%)
  between operations  13.9 us (5%)
  matrix products  13.2 us (5%)
  blocking collectives  11.6 us (4%)
  starting transfers between devices  6.3 us (2%)
  other arithmetic  5.9 us (2%)
  local copies, waits for them, and re-layouts  5.54 us (2%)
    all_gather x1, waiting for transfers between devices, body(): left = lax.all_gather(masked, ('z', 'c'), axis=1, tiled=True)  73.1 us
    all_gather x1, waiting for transfers between devices, body(): lax.all_gather(square, ('z', 'c'), axis=1, tiled=True)  69.3 us
    all_gather x1, waiting for transfers between devices, body(): right = lax.all_gather(pair, 'y', axis=0, tiled=True)  58.7 us
    dot_general x2, matrix products, product(): jnp.dot(a, right, precision=lax.Precision.HIGHEST, preferred_element_type...  13.2 us
    all_gather x1, blocking collectives, body(): four = lax.all_gather(masked, ('xh', 'xl'), axis=0)  11.6 us
    ppermute x2, waiting for transfers between devices, product(): return mine + lax.ppermute(other, 'xl', [(0, 1), (1, 0)])  7.41 us
    ppermute x2, starting transfers between devices, product(): return mine + lax.ppermute(other, 'xl', [(0, 1), (1, 0)])  6.19 us
  transfers between devices with their start and end apart: 5, of which 5 were waited for; matrix products, arithmetic and copies ran while one was open for 1% of the time, Pallas kernels for 0%

profile of v1, /device:TPU:1, one launch (start us, length us, event | category | flops | bytes accessed | tf_op | source)
XLA Modules:
  0.0 265.7 jit_solution(4728570280595195703)
XLA Ops:
  7.2 0.0 all-gather.7.cloned.1.call-start
  7.2 0.7 dynamic_slice.24
  8.0 0.7 dynamic_slice.23
  8.7 0.1 lt.62
  8.8 0.1 lt.63
  8.8 0.7 convert_element_type.21
  9.5 0.1 lt.60
  9.6 0.1 copy.7
  9.7 0.1 fusion.14
  9.8 0.1 broadcast_multiply_fusion
  9.9 0.5 mul.75
  10.4 0.2 mul.76
  10.6 1.0 multiply_multiply_fusion
  11.6 0.0 copy-start.3
  11.6 11.6 %all-gather = f32[1536,128]{1,0:T(8,128)S(1)} all-gather(f32[384,128]{1,0:T(8,128)S(1)} %multiply_multiply_fusion), channel_id=2, replica_groups=mesh['xh'=2,'y'=8,'xl'=2,'z'=12,'c'=2] {'xh','xl'}, dimensions={0}, use_global_device_ids=true | all-gather | bytes 983040 | tf_op jit(solution)/shard_map/all_gather | solution.py:38
  23.2 0.8 pad_maximum_fusion
  24.1 0.0 all-gather.7.cloned.1.call-update
  24.1 0.0 all-gather.5.cloned.1.call-start
  24.1 0.0 copy-done.3
  24.1 0.7 all-gather.5.cloned.1.call-update
  24.8 0.0 all-gather.9.cloned.1.call-start
  24.9 0.0 copy-start.4
  24.9 58.7 %all-gather.7.cloned.1.call-done = f32[3072,256]{1,0:T(8,128)} async-done(((f32[384,256]{1,0:T(8,128)}), f32[3072,256]{1,0:T(8,128)}) %all-gather.7.cloned.1.call-update) | async-done | bytes 3145744 | tf_op jit(solution)/shard_map/all_gather | solution.py:42
  83.6 0.0 copy-start
  83.6 73.1 %all-gather.5.cloned.1.call-done = f32[384,3072]{1,0:T(8,128)} async-done(((f32[384,128]{1,0:T(8,128)}), f32[384,3072]{1,0:T(8,128)}) %all-gather.5.cloned.1.call-update) | async-done | bytes 4718608 | tf_op jit(solution)/shard_map/all_gather | solution.py:36
  156.7 7.1 %fusion.15 = f32[384,256]{1,0:T(8,128)S(1)} fusion(f32[384,3072]{1,0:T(8,128)} %all-gather.5.cloned.1.call-done, f32[3072,256]{1,0:T(8,128)} %all-gather.7.cloned.1.call-done), kind=kOutput, calls=%fused_computation.34 | convolution fusion | flops 3623878656 | bytes 8257536 | tf_op jit(solution)/shard_map/dot_general | solution.py:45
  163.8 0.7 fusion.9
  164.6 3.1 %collective-permute-start = (f32[384,128]{1,0:T(8,128)}, f32[384,128]{1,0:T(8,128)}, u32[]{:S(2)}, u32[]{:S(2)}) collective-permute-start(f32[384,128]{1,0:T(8,128)} %fusion.9), channel_id=1, source_target_pairs={{0,24},{24,0},{1,25},{25,1},{2,26},{26,2},{3,27},{27,3},{4,28},{28... | collective-permute-start | bytes 589832 | tf_op jit(solution)/shard_map/ppermute | solution.py:51
  167.7 0.0 copy-done.4
  167.7 0.1 copy.6
  167.8 0.9 broadcast_in_dim.2
  168.7 1.9 reshape.66
  170.6 2.4 collective-permute-done
  173.0 1.7 fusion.13
  174.7 0.0 all-gather.9.cloned.1.call-update
  174.8 0.0 copy-start.1
  174.8 0.0 copy-start.2
  174.8 69.3 %all-gather.9.cloned.1.call-done = f32[384,3072]{1,0:T(8,128)} async-done(((f32[384,128]{1,0:T(8,128)}), f32[384,3072]{1,0:T(8,128)}) %all-gather.9.cloned.1.call-update) | async-done | bytes 4718608 | tf_op jit(solution)/shard_map/all_gather | solution.py:54
  244.1 0.0 copy-done
  244.1 6.1 %fusion.16 = f32[384,256]{1,0:T(8,128)S(1)} fusion(f32[384,3072]{1,0:T(8,128)} %all-gather.9.cloned.1.call-done, f32[3072,256]{1,0:T(8,128)S(1)} %copy-done), kind=kOutput, calls=%fused_computation.35 | convolution fusion | flops 3623878656 | bytes 8257536 | tf_op jit(solution)/shard_map/dot_general | solution.py:45
  250.3 0.1 fusion.1
  250.3 3.1 %collective-permute-start.1 = (f32[384,128]{1,0:T(8,128)S(1)}, f32[384,128]{1,0:T(8,128)S(1)}, u32[]{:S(2)}, u32[]{:S(2)}) collective-permute-start(f32[384,128]{1,0:T(8,128)S(1)} %fusion.1), channel_id=1, source_target_pairs={{0,24},{24,0},{1,25},{25,1},{2,26},{26,2},{3,27},{27,3},{4,28},{28... | collective-permute-start | bytes 589832 | tf_op jit(solution)/shard_map/ppermute | solution.py:51
  253.4 5.0 %collective-permute-done.1 = f32[384,128]{1,0:T(8,128)S(1)} collective-permute-done((f32[384,128]{1,0:T(8,128)S(1)}, f32[384,128]{1,0:T(8,128)S(1)}, u32[]{:S(2)}, u32[]{:S(2)}) %collective-permute-start.1) | collective-permute-done | bytes 196640 | tf_op jit(solution)/shard_map/ppermute | solution.py:51
  258.4 0.0 copy-done.1
  258.4 0.0 copy-done.2
  258.4 0.7 fusion.7
  (6 shorter events, 0.1 us)
Async XLA Ops:
  7.2 76.5 %all-gather.7.cloned.1.call-start = ((), (), s32[]{:S(2)}) async-start(), calls=%async_computation.1 | async-start | bytes 3538944 | tf_op jit(solution)/shard_map/all_gather | solution.py:42
  11.6 12.6 %copy-start.3 = (f32[384,128]{1,0:T(8,128)}, f32[384,128]{1,0:T(8,128)S(1)}, u32[]{:S(2)}) copy-start(f32[384,128]{1,0:T(8,128)S(1)} %multiply_multiply_fusion) | copy-start | bytes 589828
  24.1 132.6 %all-gather.5.cloned.1.call-start = ((), (), s32[]{:S(2)}) async-start(), calls=%async_computation | async-start | bytes 4915200 | tf_op jit(solution)/shard_map/all_gather | solution.py:36
  24.8 219.2 %all-gather.9.cloned.1.call-start = ((), (), s32[]{:S(2)}) async-start(), calls=%async_computation.2 | async-start | bytes 4915200 | tf_op jit(solution)/shard_map/all_gather | solution.py:54
  24.9 142.8 %copy-start.4 = (s32[6,2]{0,1:T(2,128)S(1)}, s32[6,2]{0,1:T(2,128)}, u32[]{:S(2)}) copy-start(s32[6,2]{0,1:T(2,128)} %param.7) | copy-start | bytes 148
  83.6 160.4 %copy-start = (f32[3072,256]{1,0:T(8,128)S(1)}, f32[3072,256]{1,0:T(8,128)}, u32[]{:S(2)}) copy-start(f32[3072,256]{1,0:T(8,128)} %all-gather.7.cloned.1.call-done) | copy-start | bytes 9437188
  164.6 8.4 %collective-permute-start = (f32[384,128]{1,0:T(8,128)}, f32[384,128]{1,0:T(8,128)}, u32[]{:S(2)}, u32[]{:S(2)}) collective-permute-start(f32[384,128]{1,0:T(8,128)} %fusion.9), channel_id=1, source_target_pairs={{0,24},{24,0},{1,25},{25,1},{2,26},{26,2},{3,27},{27,3},{4,28},{28... | collective-permute-start | bytes 589832 | tf_op jit(solution)/shard_map/ppermute | solution.py:51
  174.8 83.7 %copy-start.1 = (f32[384,128]{1,0:T(8,128)S(1)}, f32[384,128]{1,0:T(8,128)}, u32[]{:S(2)}) copy-start(f32[384,128]{1,0:T(8,128)} %fusion.13) | copy-start | bytes 589828
  174.8 83.7 %copy-start.2 = (f32[384,128]{1,0:T(8,128)S(1)}, f32[384,128]{1,0:T(8,128)}, u32[]{:S(2)}) copy-start(f32[384,128]{1,0:T(8,128)} %reshape.66) | copy-start | bytes 589828
  250.3 8.1 %collective-permute-start.1 = (f32[384,128]{1,0:T(8,128)S(1)}, f32[384,128]{1,0:T(8,128)S(1)}, u32[]{:S(2)}, u32[]{:S(2)}) collective-permute-start(f32[384,128]{1,0:T(8,128)S(1)} %fusion.1), channel_id=1, source_target_pairs={{0,24},{24,0},{1,25},{25,1},{2,26},{26,2},{3,27},{27,3},{4,28},{28... | collective-permute-start | bytes 589832 | tf_op jit(solution)/shard_map/ppermute | solution.py:51
Sparse Core Ops, SparseCore 0:
  24.2 59.3 all-gather.6
  86.6 70.1 all-gather.4
  174.9 69.1 all-gather.8

commit v2 on v1

v2 whole, which is shorter than its diff:
```python
import functools

import jax
import jax.numpy as jnp
from jax import lax
from jax.experimental import pallas as pl
from jax.experimental.pallas import tpu as pltpu
from jax.sharding import Mesh, PartitionSpec as P

BS = 64
AXES = ("xh", "y", "xl", "z", "c")
SIZES = (2, 8, 2, 12, 2)
NY = 8
NZ = 12
ROW = ("xh", "y")
COL = ("xl", "z", "c")
F32 = jnp.float32
BF16 = jnp.bfloat16
VM = pl.BlockSpec(memory_space=pltpu.VMEM)
SM = pl.BlockSpec(memory_space=pltpu.SMEM)
PARAMS = pltpu.CompilerParams(vmem_limit_bytes=32 * 1024 * 1024)


def mask_kernel(sizes, pattern, density, out):
    row_blocks, col_blocks = pattern.shape
    first_row = (lax.axis_index("xh") * NY + lax.axis_index("y")) * row_blocks
    first_col = ((lax.axis_index("xl") * NZ + lax.axis_index("z")) * 2 + lax.axis_index("c")) * col_blocks
    sub = lax.broadcasted_iota(jnp.int32, (BS, 2 * BS), 0)
    lane = lax.broadcasted_iota(jnp.int32, (BS, 2 * BS), 1)
    left = lane < BS
    size_col = jnp.where(left, sizes[first_col], sizes[first_col + 1])
    valid_col = (jnp.where(left, lane, lane - BS) < size_col).astype(F32)
    for i in range(row_blocks):
        stored = jnp.where(left, pattern[i, 0], pattern[i, 1]).astype(F32)
        valid = (sub < sizes[first_row + i]).astype(F32) * valid_col * stored
        out[i * BS : (i + 1) * BS, :] = density[i * BS : (i + 1) * BS, :] * valid


def split(x):
    hi = x.astype(BF16)
    return hi, (x - hi.astype(F32)).astype(BF16)


def product_kernel(plan, has_acc, last, *refs):
    n_in = 1 + sum(1 if kind == "both" else 2 for kind, _ in plan)
    right = refs[0]
    acc = refs[n_in][...] if has_acc else None
    outs = refs[n_in + has_acc :]
    z = lax.axis_index("z")
    c = lax.axis_index("c")

    def unit(u):
        y = u // 3
        rows = pl.ds(pl.multiple_of((u - 3 * y) * 128, 128), 128)
        return jnp.concatenate([right[y, 0, rows, :], right[y, 1, rows, :]], axis=1)

    dot = functools.partial(jnp.dot, preferred_element_type=F32)
    at = 1
    for kind, offsets in plan:
        for k, off in enumerate(offsets):
            zz = lax.rem(z + (off + NZ), NZ)
            if kind == "both":
                a = jnp.concatenate([refs[at][0], refs[at][1]], axis=1)
                first, second = 2 * zz, 2 * zz + 1
            else:
                a = jnp.concatenate([refs[at][k], refs[at + 1][k]], axis=1)
                first, second = 2 * zz + c, 2 * zz + 1 - c
            b = jnp.concatenate([unit(first), unit(second)], axis=0)
            ah, al = split(a)
            bh, bl = split(b)
            term = dot(ah, bh) + (dot(ah, bl) + dot(al, bh))
            acc = term if acc is None else acc + term
        at += 1 if kind == "both" else 2
    if not last:
        outs[0][...] = acc
        return
    same = lax.axis_index("xl") == lax.axis_index("xh")
    near, far = acc[:, :128], acc[:, 128:]
    outs[0][...] = jnp.where(same, near, far)
    outs[1][...] = jnp.where(same, far, near)


def product(right, groups, acc=None, last=True):
    plan = tuple((kind, offsets) for kind, offsets, _ in groups)
    n = sum(len(offsets) for _, offsets in plan)
    rows, cols = groups[0][2][0].shape[1:]
    args = [right] + [x for _, _, arrays in groups for x in arrays]
    if acc is not None:
        args.append(acc)
    if last:
        shapes = (jax.ShapeDtypeStruct((rows, cols), F32),) * 2
    else:
        shapes = jax.ShapeDtypeStruct((rows, 2 * cols), F32)
    return pl.pallas_call(
        functools.partial(product_kernel, plan, acc is not None, last),
        out_shape=shapes,
        in_specs=[VM] * len(args),
        out_specs=(VM, VM) if last else VM,
        compiler_params=PARAMS,
        cost_estimate=pl.CostEstimate(
            flops=n * 3 * 2 * rows * 2 * cols * 2 * cols, bytes_accessed=0, transcendentals=0
        ),
    )(*args)


def filter_kernel(final, kept, mine, pair, *refs):
    other = 1 - lax.axis_index("xl")
    lane = lax.broadcasted_iota(jnp.int32, (BS, 2 * BS), 1)
    for i in range(kept.shape[0]):
        strip = slice(i * BS, (i + 1) * BS)
        filt = jnp.where(lane < BS, kept[i, 0], kept[i, 1]).astype(F32)
        total = filt * (mine[strip, :] + pair[other, strip, :])
        if final:
            refs[1][strip, :] = 3.0 * refs[0][strip, :] - 2.0 * total
        else:
            refs[0][strip, :] = total


def filtered(kept, halves, square=None):
    mine, other = halves
    pair = lax.all_gather(other, "xl", axis=0)
    args = [kept, mine, pair] + ([] if square is None else [square])
    return pl.pallas_call(
        functools.partial(filter_kernel, square is not None),
        out_shape=jax.ShapeDtypeStruct(mine.shape, F32),
        in_specs=[SM] + [VM] * (len(args) - 1),
        out_specs=VM,
        compiler_params=PARAMS,
    )(*args)


def shift(x, axis, step):
    n = SIZES[AXES.index(axis)]
    return lax.ppermute(x, axis, [(i, (i + step) % n) for i in range(n)])


def together(*xs):
    return lax.optimization_barrier(xs)


def body(density, atom_sizes, pattern, kept):
    masked = pl.pallas_call(
        mask_kernel,
        out_shape=jax.ShapeDtypeStruct(density.shape, F32),
        in_specs=[SM, SM, VM],
        out_specs=VM,
        compiler_params=PARAMS,
    )(atom_sizes, pattern, density)

    near = lax.ppermute(masked, ("xh", "xl"), [(0, 0), (1, 2), (2, 1), (3, 3)])
    far = lax.ppermute(masked, ("xh", "xl"), [(1, 0), (2, 3), (0, 2), (3, 1)])
    up, down = shift(masked, "z", 1), shift(masked, "z", -1)
    u1, d1, near, far = together(up, down, near, far)
    right, u1, d1 = together(jnp.stack([near, far]), u1, d1)
    right = lax.all_gather(right, "y", axis=0)

    def rest(x, u1, d1, multiply, alone):
        x = x[None]
        u2, d2, x_sib = together(shift(u1, "z", 1), shift(d1, "z", -1), shift(x, "c", 1))
        s12 = jnp.stack([u1, d1, u2, d2])
        u3, d3, s12_sib = together(shift(u2, "z", 1), shift(d2, "z", -1), shift(s12, "c", 1))
        g12 = [("pair", (0,), (x, x_sib)), ("pair", (-1, 1, -2, 2), (s12, s12_sib))]
        acc = multiply(g12)
        u4, d4, acc = together(shift(u3, "z", 1), shift(d3, "z", -1), acc)
        s34 = jnp.stack([u3, d3, u4, d4])
        u5, d5, s34_sib = together(shift(u4, "z", 1), shift(d4, "z", -1), shift(s34, "c", 1))
        g34 = [("pair", (-3, 3, -4, 4), (s34, s34_sib))]
        acc = multiply(g34, acc)
        s5 = jnp.stack([u5, d5])
        u6, s5_sib, acc = together(shift(u5, "z", 1), shift(s5, "c", 1), acc)
        g56 = [("pair", (-5, 5), (s5, s5_sib))]
        if alone:
            g56.append(("both", (-6,), (lax.all_gather(u6, "c", axis=0),)))
        else:
            g56.append(("pair", (-6,), (u6[None], shift(u6[None], "c", 1))))
        return g12 + g34, g56, acc

    def later(groups, acc=None):
        return jnp.zeros((), F32) if acc is None else acc

    def now(groups, acc=None):
        return product(right, groups, acc, last=False)

    most, final, _ = rest(masked, u1, d1, later, False)
    square = filtered(kept, product(right, most + final))

    u1, d1 = together(shift(square, "z", 1), shift(square, "z", -1))
    _, final, acc = rest(square, u1, d1, now, True)
    purified = filtered(kept, product(right, final, acc), square)
    return (square, purified)


def solution(mesh):
    fine = Mesh(mesh.devices.reshape(SIZES), AXES)
    placed = (P(ROW, COL), P(), P(ROW, COL), P(ROW, COL))
    return jax.shard_map(
        body,
        mesh=fine,
        in_specs=placed,
        out_specs=(P(ROW, COL), P(ROW, COL)),
        check_vma=False,
    )
```

time: 266 us -> 222 us (0.83)
  waiting for transfers between devices: 209 us -> 48.8 us
  starting transfers between devices: 6.3 us -> 122 us
  matrix products: 13.2 us -> 0 us
  Pallas kernels: 0 us -> 9.13 us
  blocking collectives: 11.6 us -> 17.7 us
  other arithmetic: 5.9 us -> 1.06 us
    all_gather x3 -> x1, waiting for transfers between devices: 201 us -> 0.01 us  [body(): right = lax.all_gather(right, 'y', axis=0)]
    ppermute x2 -> x33, starting transfers between devices: 6.19 us -> 122 us  [the longest x31 116 us: shift(): return lax.ppermute(x, axis, [(i, (i + step) % n) for i in range(n)])]
    ppermute x2 -> x33, waiting for transfers between devices: 7.41 us -> 48.8 us  [the longest x31 45.4 us: shift(): return lax.ppermute(x, axis, [(i, (i + step) % n) for i in range(n)])]
    dot_general x2 -> x0, matrix products: 13.2 us -> none  [product(): jnp.dot(a, right, precision=lax.Precision.HIGHEST, preferred_element_type...]
    pallas_call x0 -> x7, Pallas kernels: none -> 9.13 us  [the longest x4 5.84 us: product(): pl.pallas_call(functools.partial(product_kernel, plan, acc is not None, l...]
    unnamed x10 -> x20, local copies, waits for them, and re-layouts: 0.03 us -> 7.28 us
    all_gather x1 -> x3, blocking collectives: 11.6 us -> 17.7 us  [the longest x2 15.4 us: filtered(): pair = lax.all_gather(other, 'xl', axis=0)]
    mul x3 -> x0, other arithmetic: 2.8 us -> none  [the longest x1 1.74 us: body(): square = filt * product(left)]
  transfers between devices with their start and end apart: 5 -> 34, of which waited for: 5 -> 20; matrix products, arithmetic and copies ran while one was open for 1% -> 0% of each run, Pallas kernels for 0% -> 1%
where the time goes in v2:
time: 222 us; the launch traced here: 221 us
  starting transfers between devices  122 us (55%)
  waiting for transfers between devices  48.8 us (22%)
  blocking collectives  17.7 us (8%)
  between operations  14.5 us (7%)
  Pallas kernels  9.13 us (4%)
  local copies, waits for them, and re-layouts  7.28 us (3%)
    ppermute x31, starting transfers between devices, shift(): return lax.ppermute(x, axis, [(i, (i + step) % n) for i in range(n)])  116 us
    ppermute x31, waiting for transfers between devices, shift(): return lax.ppermute(x, axis, [(i, (i + step) % n) for i in range(n)])  45.4 us
    all_gather x2, blocking collectives, filtered(): pair = lax.all_gather(other, 'xl', axis=0)  15.4 us
    unnamed x20, local copies, waits for them, and re-layouts  7.28 us
    ppermute x1, starting transfers between devices, body(): far = lax.ppermute(masked, ('xh', 'xl'), [(1, 0), (2, 3), (0, 2), (3, 1)])  6.14 us
    pallas_call x4, Pallas kernels, product(): pl.pallas_call(functools.partial(product_kernel, plan, acc is not None, l...  5.84 us
  transfers between devices with their start and end apart: 34, of which 20 were waited for; matrix products, arithmetic and copies ran while one was open for 0% of the time, Pallas kernels for 1%

profile of v2, /device:TPU:1, one launch (start us, length us, event | category | flops | bytes accessed | tf_op | source)
XLA Modules:
  0.0 220.9 jit_solution(17007170292049963399)
XLA Ops:
  8.0 0.9 copy-done.6
  10.2 4.8 %collective-permute-start = (f32[384,128]{1,0:T(8,128)S(1)}, f32[384,128]{1,0:T(8,128)S(1)}, u32[]{:S(2)}, u32[]{:S(2)}) collective-permute-start(f32[384,128]{1,0:T(8,128)S(1)} %shard_map.59), channel_id=1, source_target_pairs={{0,2},{2,4},{4,6},{6,8},{8,10},{10,12},{12,14},{14,16},{16,18},{18... | collective-permute-start | bytes 589832 | tf_op jit(solution)/shard_map/ppermute | solution.py:134
  15.1 12.2 %collective-permute-start.1 = (f32[384,128]{1,0:T(8,128)S(1)}, f32[384,128]{1,0:T(8,128)S(1)}, u32[]{:S(2)}, u32[]{:S(2)}) collective-permute-start(f32[384,128]{1,0:T(8,128)S(1)} %shard_map.59), channel_id=1, source_target_pairs={{0,22},{2,0},{4,2},{6,4},{8,6},{10,8},{12,10},{14,12},{16,14},{18,... | collective-permute-start | bytes 589832 | tf_op jit(solution)/shard_map/ppermute | solution.py:134
  28.0 6.1 %collective-permute-start.3 = (f32[384,128]{1,0:T(8,128)S(1)}, f32[384,128]{1,0:T(8,128)S(1)}, u32[]{:S(2)}, u32[]{:S(2)}) collective-permute-start(f32[384,128]{1,0:T(8,128)S(1)} %shard_map.59), channel_id=1, source_target_pairs={{24,0},{384,408},{0,384},{408,24},{25,1},{385,409},{1,385},{409,25... | collective-permute-start | bytes 589832 | tf_op jit(solution)/shard_map/ppermute | solution.py:151
  34.2 3.4 %collective-permute-done.3 = f32[384,128]{1,0:T(8,128)S(1)} collective-permute-done((f32[384,128]{1,0:T(8,128)S(1)}, f32[384,128]{1,0:T(8,128)S(1)}, u32[]{:S(2)}, u32[]{:S(2)}) %collective-permute-start.3) | collective-permute-done | bytes 196640 | tf_op jit(solution)/shard_map/ppermute | solution.py:151
  37.5 0.8 pad_maximum_fusion.4
  38.4 3.8 %collective-permute-start.6 = (f32[1,384,128]{2,1,0:T(8,128)S(1)}, f32[1,384,128]{2,1,0:T(8,128)S(1)}, u32[]{:S(2)}, u32[]{:S(2)}) collective-permute-start(f32[1,384,128]{2,1,0:T(8,128)S(1)} %bitcast.38), channel_id=1, source_target_pairs={{0,1},{1,0},{2,3},{3,2},{4,5},{5,4},{6,7},{7,6},{8,9},{9,8},{10,11... | collective-permute-start | bytes 589832 | tf_op jit(solution)/shard_map/ppermute | solution.py:134
  42.1 1.9 collective-permute-start.4
  44.1 4.6 %collective-permute-start.5 = (f32[384,128]{1,0:T(8,128)S(1)}, f32[384,128]{1,0:T(8,128)S(1)}, u32[]{:S(2)}, u32[]{:S(2)}) collective-permute-start(f32[384,128]{1,0:T(8,128)S(1)} %collective-permute-done.1), channel_id=1, source_target_pairs={{0,22},{2,0},{4,2},{6,4},{8,6},{10,8},{12,10},{14,12},{16,14},{18,... | collective-permute-start | bytes 589832 | tf_op jit(solution)/shard_map/ppermute | solution.py:134
  48.7 3.1 %collective-permute-done.4 = f32[384,128]{1,0:T(8,128)S(1)} collective-permute-done((f32[384,128]{1,0:T(8,128)S(1)}, f32[384,128]{1,0:T(8,128)S(1)}, u32[]{:S(2)}, u32[]{:S(2)}) %collective-permute-start.4) | collective-permute-done | bytes 196640 | tf_op jit(solution)/shard_map/ppermute | solution.py:134
  51.8 0.9 collective-permute-done.5
  52.7 3.0 %collective-permute-start.9 = (f32[4,384,128]{2,1,0:T(8,128)S(1)}, f32[4,384,128]{2,1,0:T(8,128)S(1)}, u32[]{:S(2)}, u32[]{:S(2)}) collective-permute-start(f32[4,384,128]{2,1,0:T(8,128)S(1)} %pad_maximum_fusion.refs_3_), channel_id=1, source_target_pairs={{0,1},{1,0},{2,3},{3,2},{4,5},{5,4},{6,7},{7,6},{8,9},{9,8},{10,11... | collective-permute-start | bytes 2359304 | tf_op jit(solution)/shard_map/ppermute | solution.py:134
  55.7 1.9 collective-permute-start.7
  57.6 5.3 %collective-permute-start.8 = (f32[384,128]{1,0:T(8,128)S(1)}, f32[384,128]{1,0:T(8,128)S(1)}, u32[]{:S(2)}, u32[]{:S(2)}) collective-permute-start(f32[384,128]{1,0:T(8,128)S(1)} %collective-permute-done.5), channel_id=1, source_target_pairs={{0,22},{2,0},{4,2},{6,4},{8,6},{10,8},{12,10},{14,12},{16,14},{18,... | collective-permute-start | bytes 589832 | tf_op jit(solution)/shard_map/ppermute | solution.py:134
  63.0 3.4 %collective-permute-done.7 = f32[384,128]{1,0:T(8,128)S(1)} collective-permute-done((f32[384,128]{1,0:T(8,128)S(1)}, f32[384,128]{1,0:T(8,128)S(1)}, u32[]{:S(2)}, u32[]{:S(2)}) %collective-permute-start.7) | collective-permute-done | bytes 196640 | tf_op jit(solution)/shard_map/ppermute | solution.py:134
  66.4 0.9 collective-permute-done.8
  67.3 1.9 collective-permute-start.10
  69.2 5.4 %collective-permute-start.11 = (f32[384,128]{1,0:T(8,128)S(1)}, f32[384,128]{1,0:T(8,128)S(1)}, u32[]{:S(2)}, u32[]{:S(2)}) collective-permute-start(f32[384,128]{1,0:T(8,128)S(1)} %collective-permute-done.8), channel_id=1, source_target_pairs={{0,22},{2,0},{4,2},{6,4},{8,6},{10,8},{12,10},{14,12},{16,14},{18,... | collective-permute-start | bytes 589832 | tf_op jit(solution)/shard_map/ppermute | solution.py:134
  74.6 2.8 %collective-permute-done.10 = f32[384,128]{1,0:T(8,128)S(1)} collective-permute-done((f32[384,128]{1,0:T(8,128)S(1)}, f32[384,128]{1,0:T(8,128)S(1)}, u32[]{:S(2)}, u32[]{:S(2)}) %collective-permute-start.10) | collective-permute-done | bytes 196640 | tf_op jit(solution)/shard_map/ppermute | solution.py:134
  78.2 3.5 %collective-permute-start.14 = (f32[4,384,128]{2,1,0:T(8,128)S(1)}, f32[4,384,128]{2,1,0:T(8,128)S(1)}, u32[]{:S(2)}, u32[]{:S(2)}) collective-permute-start(f32[4,384,128]{2,1,0:T(8,128)S(1)} %pad_maximum_fusion.1.refs_5_), channel_id=1, source_target_pairs={{0,1},{1,0},{2,3},{3,2},{4,5},{5,4},{6,7},{7,6},{8,9},{9,8},{10,11... | collective-permute-start | bytes 2359304 | tf_op jit(solution)/shard_map/ppermute | solution.py:134
  81.7 1.9 collective-permute-start.12
  83.6 5.3 %collective-permute-start.13 = (f32[384,128]{1,0:T(8,128)S(1)}, f32[384,128]{1,0:T(8,128)S(1)}, u32[]{:S(2)}, u32[]{:S(2)}) collective-permute-start(f32[384,128]{1,0:T(8,128)S(1)} %collective-permute-done.11), channel_id=1, source_target_pairs={{0,22},{2,0},{4,2},{6,4},{8,6},{10,8},{12,10},{14,12},{16,14},{18,... | collective-permute-start | bytes 589832 | tf_op jit(solution)/shard_map/ppermute | solution.py:134
  88.9 3.3 %collective-permute-done.12 = f32[384,128]{1,0:T(8,128)S(1)} collective-permute-done((f32[384,128]{1,0:T(8,128)S(1)}, f32[384,128]{1,0:T(8,128)S(1)}, u32[]{:S(2)}, u32[]{:S(2)}) %collective-permute-start.12) | collective-permute-done | bytes 196640 | tf_op jit(solution)/shard_map/ppermute | solution.py:134
  92.3 1.0 collective-permute-done.13
  93.2 0.9 copy-done.4
  94.2 2.7 %collective-permute-start.16 = (f32[2,384,128]{2,1,0:T(8,128)S(1)}, f32[2,384,128]{2,1,0:T(8,128)S(1)}, u32[]{:S(2)}, u32[]{:S(2)}) collective-permute-start(f32[2,384,128]{2,1,0:T(8,128)S(1)} %pad_maximum_fusion.5.refs_7_), channel_id=1, source_target_pairs={{0,1},{1,0},{2,3},{3,2},{4,5},{5,4},{6,7},{7,6},{8,9},{9,8},{10,11... | collective-permute-start | bytes 1179656 | tf_op jit(solution)/shard_map/ppermute | solution.py:134
  96.9 1.9 collective-permute-start.15
  98.8 8.8 %collective-permute-done.15 = f32[384,128]{1,0:T(8,128)} collective-permute-done((f32[384,128]{1,0:T(8,128)S(1)}, f32[384,128]{1,0:T(8,128)}, u32[]{:S(2)}, u32[]{:S(2)}) %collective-permute-start.15) | collective-permute-done | bytes 196640 | tf_op jit(solution)/shard_map/ppermute | solution.py:134
  107.6 2.5 %collective-permute-start.17 = (f32[1,384,128]{2,1,0:T(8,128)}, f32[1,384,128]{2,1,0:T(8,128)}, u32[]{:S(2)}, u32[]{:S(2)}) collective-permute-start(f32[1,384,128]{2,1,0:T(8,128)} %bitcast.14.refs_9_), channel_id=1, source_target_pairs={{0,1},{1,0},{2,3},{3,2},{4,5},{5,4},{6,7},{7,6},{8,9},{9,8},{10,11... | collective-permute-start | bytes 589832 | tf_op jit(solution)/shard_map/ppermute | solution.py:134
  110.2 1.3 collective-permute-done.17.refs_10_
  111.5 1.9 copy-done
  113.3 1.1 copy-done.5
  114.5 3.4 %shard_map.60 = (f32[384,128]{1,0:T(8,128)S(1)}, f32[384,128]{1,0:T(8,128)S(1)}) custom-call(f32[8,2,384,128]{3,2,1,0:T(8,128)S(1)} %bitcast.29, f32[1,384,128]{2,1,0:T(8,128)S(1)} %bitcast.39, f32[1,384,128]{2,1,0:T(8,128)S(1)} %collective-permute-done.6.refs_2_, f32[4,384,128]{2,1,0:T(8,128)S(1)} %pad_maximum_fusion.refs_3_, ...), custom_call_target="tpu_custom_call" | custom-call | flops 1811939328 | tf_op jit(solution)/shard_map/pallas_call | solution.py:94
  117.8 8.6 %all-gather.1 = f32[768,128]{1,0:T(8,128)S(1)} all-gather(f32[384,128]{1,0:T(8,128)S(1)} %get-tuple-element.64), channel_id=3, replica_groups=mesh['xh'=2,'y'=8,'xl'=2,'z'=12,'c'=2] {'xl'}, dimensions={0}, use_global_device_ids=true | all-gather | bytes 589824 | tf_op jit(solution)/shard_map/all_gather | solution.py:121
  126.4 1.3 shard_map.61.refs_0_
  127.7 1.9 collective-permute-start.18
  129.7 4.6 %collective-permute-start.19 = (f32[384,128]{1,0:T(8,128)}, f32[384,128]{1,0:T(8,128)S(1)}, u32[]{:S(2)}, u32[]{:S(2)}) collective-permute-start(f32[384,128]{1,0:T(8,128)} %shard_map.61.refs_0_), channel_id=1, source_target_pairs={{0,22},{2,0},{4,2},{6,4},{8,6},{10,8},{12,10},{14,12},{16,14},{18,... | collective-permute-start | bytes 589832 | tf_op jit(solution)/shard_map/ppermute | solution.py:134
  134.2 3.4 %collective-permute-start.22 = (f32[1,384,128]{2,1,0:T(8,128)}, f32[1,384,128]{2,1,0:T(8,128)S(1)}, u32[]{:S(2)}, u32[]{:S(2)}) collective-permute-start(f32[1,384,128]{2,1,0:T(8,128)} %bitcast.33), channel_id=1, source_target_pairs={{0,1},{1,0},{2,3},{3,2},{4,5},{5,4},{6,7},{7,6},{8,9},{9,8},{10,11... | collective-permute-start | bytes 589832 | tf_op jit(solution)/shard_map/ppermute | solution.py:134
  137.6 2.0 collective-permute-start.20
  139.6 5.1 %collective-permute-start.21 = (f32[384,128]{1,0:T(8,128)S(1)}, f32[384,128]{1,0:T(8,128)S(1)}, u32[]{:S(2)}, u32[]{:S(2)}) collective-permute-start(f32[384,128]{1,0:T(8,128)S(1)} %collective-permute-done.19), channel_id=1, source_target_pairs={{0,22},{2,0},{4,2},{6,4},{8,6},{10,8},{12,10},{14,12},{16,14},{18,... | collective-permute-start | bytes 589832 | tf_op jit(solution)/shard_map/ppermute | solution.py:134
  144.7 1.1 collective-permute-done.20
  145.8 1.5 collective-permute-done.21
  147.3 4.8 %collective-permute-start.25 = (f32[4,384,128]{2,1,0:T(8,128)S(1)}, f32[4,384,128]{2,1,0:T(8,128)S(1)}, u32[]{:S(2)}, u32[]{:S(2)}) collective-permute-start(f32[4,384,128]{2,1,0:T(8,128)S(1)} %pad_maximum_fusion.2.refs_3_), channel_id=1, source_target_pairs={{0,1},{1,0},{2,3},{3,2},{4,5},{5,4},{6,7},{7,6},{8,9},{9,8},{10,11... | collective-permute-start | bytes 2359304 | tf_op jit(solution)/shard_map/ppermute | solution.py:134
  152.2 3.1 %collective-permute-start.23 = (f32[384,128]{1,0:T(8,128)S(1)}, f32[384,128]{1,0:T(8,128)S(1)}, u32[]{:S(2)}, u32[]{:S(2)}) collective-permute-start(f32[384,128]{1,0:T(8,128)S(1)} %collective-permute-done.20), channel_id=1, source_target_pairs={{0,2},{2,4},{4,6},{6,8},{8,10},{10,12},{12,14},{14,16},{16,18},{18... | collective-permute-start | bytes 589832 | tf_op jit(solution)/shard_map/ppermute | solution.py:134
  155.3 4.2 %collective-permute-start.24 = (f32[384,128]{1,0:T(8,128)S(1)}, f32[384,128]{1,0:T(8,128)S(1)}, u32[]{:S(2)}, u32[]{:S(2)}) collective-permute-start(f32[384,128]{1,0:T(8,128)S(1)} %collective-permute-done.21), channel_id=1, source_target_pairs={{0,22},{2,0},{4,2},{6,4},{8,6},{10,8},{12,10},{14,12},{16,14},{18,... | collective-permute-start | bytes 589832 | tf_op jit(solution)/shard_map/ppermute | solution.py:134
  159.5 3.3 %collective-permute-done.23 = f32[384,128]{1,0:T(8,128)S(1)} collective-permute-done((f32[384,128]{1,0:T(8,128)S(1)}, f32[384,128]{1,0:T(8,128)S(1)}, u32[]{:S(2)}, u32[]{:S(2)}) %collective-permute-start.23) | collective-permute-done | bytes 196640 | tf_op jit(solution)/shard_map/ppermute | solution.py:134
  162.8 1.2 collective-permute-done.24
  164.0 3.0 %collective-permute-start.26 = (f32[384,128]{1,0:T(8,128)S(1)}, f32[384,128]{1,0:T(8,128)S(1)}, u32[]{:S(2)}, u32[]{:S(2)}) collective-permute-start(f32[384,128]{1,0:T(8,128)S(1)} %collective-permute-done.23), channel_id=1, source_target_pairs={{0,2},{2,4},{4,6},{6,8},{8,10},{10,12},{12,14},{14,16},{16,18},{18... | collective-permute-start | bytes 589832 | tf_op jit(solution)/shard_map/ppermute | solution.py:134
  167.0 4.0 %collective-permute-start.27 = (f32[384,128]{1,0:T(8,128)S(1)}, f32[384,128]{1,0:T(8,128)S(1)}, u32[]{:S(2)}, u32[]{:S(2)}) collective-permute-start(f32[384,128]{1,0:T(8,128)S(1)} %collective-permute-done.24), channel_id=1, source_target_pairs={{0,22},{2,0},{4,2},{6,4},{8,6},{10,8},{12,10},{14,12},{16,14},{18,... | collective-permute-start | bytes 589832 | tf_op jit(solution)/shard_map/ppermute | solution.py:134
  171.0 0.9 copy-done.2
  171.9 1.0 shard_map.62.refs_3_
  173.6 0.9 collective-permute-done.27
  174.5 3.7 %collective-permute-start.30 = (f32[4,384,128]{2,1,0:T(8,128)S(1)}, f32[4,384,128]{2,1,0:T(8,128)S(1)}, u32[]{:S(2)}, u32[]{:S(2)}) collective-permute-start(f32[4,384,128]{2,1,0:T(8,128)S(1)} %pad_maximum_fusion.3.refs_1_), channel_id=1, source_target_pairs={{0,1},{1,0},{2,3},{3,2},{4,5},{5,4},{6,7},{7,6},{8,9},{9,8},{10,11... | collective-permute-start | bytes 2359304 | tf_op jit(solution)/shard_map/ppermute | solution.py:134
  178.2 2.9 %collective-permute-start.28 = (f32[384,128]{1,0:T(8,128)S(1)}, f32[384,128]{1,0:T(8,128)S(1)}, u32[]{:S(2)}, u32[]{:S(2)}) collective-permute-start(f32[384,128]{1,0:T(8,128)S(1)} %collective-permute-done.26), channel_id=1, source_target_pairs={{0,2},{2,4},{4,6},{6,8},{8,10},{10,12},{12,14},{14,16},{16,18},{18... | collective-permute-start | bytes 589832 | tf_op jit(solution)/shard_map/ppermute | solution.py:134
  181.2 4.2 %collective-permute-start.29 = (f32[384,128]{1,0:T(8,128)S(1)}, f32[384,128]{1,0:T(8,128)S(1)}, u32[]{:S(2)}, u32[]{:S(2)}) collective-permute-start(f32[384,128]{1,0:T(8,128)S(1)} %collective-permute-done.27), channel_id=1, source_target_pairs={{0,22},{2,0},{4,2},{6,4},{8,6},{10,8},{12,10},{14,12},{16,14},{18,... | collective-permute-start | bytes 589832 | tf_op jit(solution)/shard_map/ppermute | solution.py:134
  185.3 3.3 %collective-permute-done.28 = f32[384,128]{1,0:T(8,128)S(1)} collective-permute-done((f32[384,128]{1,0:T(8,128)S(1)}, f32[384,128]{1,0:T(8,128)S(1)}, u32[]{:S(2)}, u32[]{:S(2)}) %collective-permute-start.28) | collective-permute-done | bytes 196640 | tf_op jit(solution)/shard_map/ppermute | solution.py:134
  188.6 1.0 collective-permute-done.29
  189.7 2.7 %collective-permute-start.32 = (f32[2,384,128]{2,1,0:T(8,128)S(1)}, f32[2,384,128]{2,1,0:T(8,128)S(1)}, u32[]{:S(2)}, u32[]{:S(2)}) collective-permute-start(f32[2,384,128]{2,1,0:T(8,128)S(1)} %pad_maximum_fusion.6.refs_1_), channel_id=1, source_target_pairs={{0,1},{1,0},{2,3},{3,2},{4,5},{5,4},{6,7},{7,6},{8,9},{9,8},{10,11... | collective-permute-start | bytes 1179656 | tf_op jit(solution)/shard_map/ppermute | solution.py:134
  192.4 3.4 %collective-permute-start.31 = (f32[384,128]{1,0:T(8,128)S(1)}, f32[384,128]{1,0:T(8,128)S(1)}, u32[]{:S(2)}, u32[]{:S(2)}) collective-permute-start(f32[384,128]{1,0:T(8,128)S(1)} %collective-permute-done.28), channel_id=1, source_target_pairs={{0,2},{2,4},{4,6},{6,8},{8,10},{10,12},{12,14},{14,16},{16,18},{18... | collective-permute-start | bytes 589832 | tf_op jit(solution)/shard_map/ppermute | solution.py:134
  195.7 0.9 shard_map.63.refs_4_
  196.6 6.3 %collective-permute-done.31 = f32[384,128]{1,0:T(8,128)S(1)} collective-permute-done((f32[384,128]{1,0:T(8,128)S(1)}, f32[384,128]{1,0:T(8,128)S(1)}, u32[]{:S(2)}, u32[]{:S(2)}) %collective-permute-start.31) | collective-permute-done | bytes 196640 | tf_op jit(solution)/shard_map/ppermute | solution.py:134
  203.0 2.3 %all-gather.2 = f32[768,128]{1,0:T(8,128)S(1)} all-gather(f32[384,128]{1,0:T(8,128)S(1)} %collective-permute-done.31), channel_id=4, replica_groups=mesh['xh'=2,'y'=8,'xl'=2,'z'=12,'c'=2] {'c'}, dimensions={0}, use_global_device_ids=true | all-gather | bytes 589824 | tf_op jit(solution)/shard_map/all_gather | solution.py:173
  205.9 6.8 %all-gather.3 = f32[768,128]{1,0:T(8,128)S(1)} all-gather(f32[384,128]{1,0:T(8,128)S(1)} %get-tuple-element.83), channel_id=5, replica_groups=mesh['xh'=2,'y'=8,'xl'=2,'z'=12,'c'=2] {'xl'}, dimensions={0}, use_global_device_ids=true | all-gather | bytes 589824 | tf_op jit(solution)/shard_map/all_gather | solution.py:121
  212.7 1.3 shard_map.65
  (42 shorter events, 5.3 us)
Async XLA Ops:
  7.2 102.9 %copy-start.8 = (s32[6,2]{0,1:T(2,128)S(1)}, s32[6,2]{0,1:T(2,128)}, u32[]{:S(2)}) copy-start(s32[6,2]{0,1:T(2,128)} %param.7) | copy-start | bytes 148
  7.2 104.3 %all-gather.6.cloned.1.call-start = ((), (), s32[]{:S(2)}) async-start(), calls=%async_computation | async-start | bytes 3538944 | tf_op jit(solution)/shard_map/all_gather | solution.py:155
  8.0 0.9 copy-start.6
  8.9 0.7 copy-start.7
  10.2 23.9 %collective-permute-start = (f32[384,128]{1,0:T(8,128)S(1)}, f32[384,128]{1,0:T(8,128)S(1)}, u32[]{:S(2)}, u32[]{:S(2)}) collective-permute-start(f32[384,128]{1,0:T(8,128)S(1)} %shard_map.59), channel_id=1, source_target_pairs={{0,2},{2,4},{4,6},{6,8},{8,10},{10,12},{12,14},{14,16},{16,18},{18... | collective-permute-start | bytes 589832 | tf_op jit(solution)/shard_map/ppermute | solution.py:134
  15.1 19.1 %collective-permute-start.1 = (f32[384,128]{1,0:T(8,128)S(1)}, f32[384,128]{1,0:T(8,128)S(1)}, u32[]{:S(2)}, u32[]{:S(2)}) collective-permute-start(f32[384,128]{1,0:T(8,128)S(1)} %shard_map.59), channel_id=1, source_target_pairs={{0,22},{2,0},{4,2},{6,4},{8,6},{10,8},{12,10},{14,12},{16,14},{18,... | collective-permute-start | bytes 589832 | tf_op jit(solution)/shard_map/ppermute | solution.py:134
  27.3 6.9 %collective-permute-start.2 = (f32[384,128]{1,0:T(8,128)S(1)}, f32[384,128]{1,0:T(8,128)S(1)}, u32[]{:S(2)}, u32[]{:S(2)}) collective-permute-start(f32[384,128]{1,0:T(8,128)S(1)} %shard_map.59), channel_id=1, source_target_pairs={{0,0},{24,384},{384,24},{408,408},{1,1},{25,385},{385,25},{409,409... | collective-permute-start | bytes 589832 | tf_op jit(solution)/shard_map/ppermute | solution.py:150
  28.0 9.5 %collective-permute-start.3 = (f32[384,128]{1,0:T(8,128)S(1)}, f32[384,128]{1,0:T(8,128)S(1)}, u32[]{:S(2)}, u32[]{:S(2)}) collective-permute-start(f32[384,128]{1,0:T(8,128)S(1)} %shard_map.59), channel_id=1, source_target_pairs={{24,0},{384,408},{0,384},{408,24},{25,1},{385,409},{1,385},{409,25... | collective-permute-start | bytes 589832 | tf_op jit(solution)/shard_map/ppermute | solution.py:151
  38.4 10.3 %collective-permute-start.6 = (f32[1,384,128]{2,1,0:T(8,128)S(1)}, f32[1,384,128]{2,1,0:T(8,128)S(1)}, u32[]{:S(2)}, u32[]{:S(2)}) collective-permute-start(f32[1,384,128]{2,1,0:T(8,128)S(1)} %bitcast.38), channel_id=1, source_target_pairs={{0,1},{1,0},{2,3},{3,2},{4,5},{5,4},{6,7},{7,6},{8,9},{9,8},{10,11... | collective-permute-start | bytes 589832 | tf_op jit(solution)/shard_map/ppermute | solution.py:134
  42.1 9.6 %collective-permute-start.4 = (f32[384,128]{1,0:T(8,128)S(1)}, f32[384,128]{1,0:T(8,128)S(1)}, u32[]{:S(2)}, u32[]{:S(2)}) collective-permute-start(f32[384,128]{1,0:T(8,128)S(1)} %collective-permute-done), channel_id=1, source_target_pairs={{0,2},{2,4},{4,6},{6,8},{8,10},{10,12},{12,14},{14,16},{16,18},{18... | collective-permute-start | bytes 589832 | tf_op jit(solution)/shard_map/ppermute | solution.py:134
  44.1 8.6 %collective-permute-start.5 = (f32[384,128]{1,0:T(8,128)S(1)}, f32[384,128]{1,0:T(8,128)S(1)}, u32[]{:S(2)}, u32[]{:S(2)}) collective-permute-start(f32[384,128]{1,0:T(8,128)S(1)} %collective-permute-done.1), channel_id=1, source_target_pairs={{0,22},{2,0},{4,2},{6,4},{8,6},{10,8},{12,10},{14,12},{16,14},{18,... | collective-permute-start | bytes 589832 | tf_op jit(solution)/shard_map/ppermute | solution.py:134
  52.7 14.6 %collective-permute-start.9 = (f32[4,384,128]{2,1,0:T(8,128)S(1)}, f32[4,384,128]{2,1,0:T(8,128)S(1)}, u32[]{:S(2)}, u32[]{:S(2)}) collective-permute-start(f32[4,384,128]{2,1,0:T(8,128)S(1)} %pad_maximum_fusion.refs_3_), channel_id=1, source_target_pairs={{0,1},{1,0},{2,3},{3,2},{4,5},{5,4},{6,7},{7,6},{8,9},{9,8},{10,11... | collective-permute-start | bytes 2359304 | tf_op jit(solution)/shard_map/ppermute | solution.py:134
  55.7 10.7 %collective-permute-start.7 = (f32[384,128]{1,0:T(8,128)S(1)}, f32[384,128]{1,0:T(8,128)S(1)}, u32[]{:S(2)}, u32[]{:S(2)}) collective-permute-start(f32[384,128]{1,0:T(8,128)S(1)} %collective-permute-done.4), channel_id=1, source_target_pairs={{0,2},{2,4},{4,6},{6,8},{8,10},{10,12},{12,14},{14,16},{16,18},{18... | collective-permute-start | bytes 589832 | tf_op jit(solution)/shard_map/ppermute | solution.py:134
  57.6 9.6 %collective-permute-start.8 = (f32[384,128]{1,0:T(8,128)S(1)}, f32[384,128]{1,0:T(8,128)S(1)}, u32[]{:S(2)}, u32[]{:S(2)}) collective-permute-start(f32[384,128]{1,0:T(8,128)S(1)} %collective-permute-done.5), channel_id=1, source_target_pairs={{0,22},{2,0},{4,2},{6,4},{8,6},{10,8},{12,10},{14,12},{16,14},{18,... | collective-permute-start | bytes 589832 | tf_op jit(solution)/shard_map/ppermute | solution.py:134
  67.3 10.1 %collective-permute-start.10 = (f32[384,128]{1,0:T(8,128)S(1)}, f32[384,128]{1,0:T(8,128)S(1)}, u32[]{:S(2)}, u32[]{:S(2)}) collective-permute-start(f32[384,128]{1,0:T(8,128)S(1)} %collective-permute-done.7), channel_id=1, source_target_pairs={{0,2},{2,4},{4,6},{6,8},{8,10},{10,12},{12,14},{14,16},{16,18},{18... | collective-permute-start | bytes 589832 | tf_op jit(solution)/shard_map/ppermute | solution.py:134
  69.2 9.0 %collective-permute-start.11 = (f32[384,128]{1,0:T(8,128)S(1)}, f32[384,128]{1,0:T(8,128)S(1)}, u32[]{:S(2)}, u32[]{:S(2)}) collective-permute-start(f32[384,128]{1,0:T(8,128)S(1)} %collective-permute-done.8), channel_id=1, source_target_pairs={{0,22},{2,0},{4,2},{6,4},{8,6},{10,8},{12,10},{14,12},{16,14},{18,... | collective-permute-start | bytes 589832 | tf_op jit(solution)/shard_map/ppermute | solution.py:134
  78.2 15.0 %collective-permute-start.14 = (f32[4,384,128]{2,1,0:T(8,128)S(1)}, f32[4,384,128]{2,1,0:T(8,128)S(1)}, u32[]{:S(2)}, u32[]{:S(2)}) collective-permute-start(f32[4,384,128]{2,1,0:T(8,128)S(1)} %pad_maximum_fusion.1.refs_5_), channel_id=1, source_target_pairs={{0,1},{1,0},{2,3},{3,2},{4,5},{5,4},{6,7},{7,6},{8,9},{9,8},{10,11... | collective-permute-start | bytes 2359304 | tf_op jit(solution)/shard_map/ppermute | solution.py:134
  81.7 10.6 %collective-permute-start.12 = (f32[384,128]{1,0:T(8,128)S(1)}, f32[384,128]{1,0:T(8,128)S(1)}, u32[]{:S(2)}, u32[]{:S(2)}) collective-permute-start(f32[384,128]{1,0:T(8,128)S(1)} %collective-permute-done.10), channel_id=1, source_target_pairs={{0,2},{2,4},{4,6},{6,8},{8,10},{10,12},{12,14},{14,16},{16,18},{18... | collective-permute-start | bytes 589832 | tf_op jit(solution)/shard_map/ppermute | solution.py:134
  83.6 9.6 %collective-permute-start.13 = (f32[384,128]{1,0:T(8,128)S(1)}, f32[384,128]{1,0:T(8,128)S(1)}, u32[]{:S(2)}, u32[]{:S(2)}) collective-permute-start(f32[384,128]{1,0:T(8,128)S(1)} %collective-permute-done.11), channel_id=1, source_target_pairs={{0,22},{2,0},{4,2},{6,4},{8,6},{10,8},{12,10},{14,12},{16,14},{18,... | collective-permute-start | bytes 589832 | tf_op jit(solution)/shard_map/ppermute | solution.py:134
  93.2 0.9 copy-start.4
  94.2 13.4 %collective-permute-start.16 = (f32[2,384,128]{2,1,0:T(8,128)S(1)}, f32[2,384,128]{2,1,0:T(8,128)S(1)}, u32[]{:S(2)}, u32[]{:S(2)}) collective-permute-start(f32[2,384,128]{2,1,0:T(8,128)S(1)} %pad_maximum_fusion.5.refs_7_), channel_id=1, source_target_pairs={{0,1},{1,0},{2,3},{3,2},{4,5},{5,4},{6,7},{7,6},{8,9},{9,8},{10,11... | collective-permute-start | bytes 1179656 | tf_op jit(solution)/shard_map/ppermute | solution.py:134
  96.9 10.7 %collective-permute-start.15 = (f32[384,128]{1,0:T(8,128)S(1)}, f32[384,128]{1,0:T(8,128)}, u32[]{:S(2)}, u32[]{:S(2)}) collective-permute-start(f32[384,128]{1,0:T(8,128)S(1)} %collective-permute-done.12), channel_id=1, source_target_pairs={{0,2},{2,4},{4,6},{6,8},{8,10},{10,12},{12,14},{14,16},{16,18},{18... | collective-permute-start | bytes 589832 | tf_op jit(solution)/shard_map/ppermute | solution.py:134
  107.6 3.9 %collective-permute-start.17 = (f32[1,384,128]{2,1,0:T(8,128)}, f32[1,384,128]{2,1,0:T(8,128)}, u32[]{:S(2)}, u32[]{:S(2)}) collective-permute-start(f32[1,384,128]{2,1,0:T(8,128)} %bitcast.14.refs_9_), channel_id=1, source_target_pairs={{0,1},{1,0},{2,3},{3,2},{4,5},{5,4},{6,7},{7,6},{8,9},{9,8},{10,11... | collective-permute-start | bytes 589832 | tf_op jit(solution)/shard_map/ppermute | solution.py:134
  111.5 1.9 copy-start
  113.3 1.1 copy-start.5
  114.5 56.5 %copy-start.1 = (f32[16,384,128]{2,1,0:T(8,128)S(1)}, f32[16,384,128]{2,1,0:T(8,128)}, u32[]{:S(2)}) copy-start(f32[16,384,128]{2,1,0:T(8,128)} %all-gather.6.cloned.1.call-done) | copy-start | bytes 9437188
  127.7 9.9 %collective-permute-start.18 = (f32[384,128]{1,0:T(8,128)}, f32[384,128]{1,0:T(8,128)S(1)}, u32[]{:S(2)}, u32[]{:S(2)}) collective-permute-start(f32[384,128]{1,0:T(8,128)} %shard_map.61.refs_0_), channel_id=1, source_target_pairs={{0,2},{2,4},{4,6},{6,8},{8,10},{10,12},{12,14},{14,16},{16,18},{18... | collective-permute-start | bytes 589832 | tf_op jit(solution)/shard_map/ppermute | solution.py:134
  129.7 8.0 %collective-permute-start.19 = (f32[384,128]{1,0:T(8,128)}, f32[384,128]{1,0:T(8,128)S(1)}, u32[]{:S(2)}, u32[]{:S(2)}) collective-permute-start(f32[384,128]{1,0:T(8,128)} %shard_map.61.refs_0_), channel_id=1, source_target_pairs={{0,22},{2,0},{4,2},{6,4},{8,6},{10,8},{12,10},{14,12},{16,14},{18,... | collective-permute-start | bytes 589832 | tf_op jit(solution)/shard_map/ppermute | solution.py:134
  134.2 10.5 %collective-permute-start.22 = (f32[1,384,128]{2,1,0:T(8,128)}, f32[1,384,128]{2,1,0:T(8,128)S(1)}, u32[]{:S(2)}, u32[]{:S(2)}) collective-permute-start(f32[1,384,128]{2,1,0:T(8,128)} %bitcast.33), channel_id=1, source_target_pairs={{0,1},{1,0},{2,3},{3,2},{4,5},{5,4},{6,7},{7,6},{8,9},{9,8},{10,11... | collective-permute-start | bytes 589832 | tf_op jit(solution)/shard_map/ppermute | solution.py:134
  137.6 8.2 %collective-permute-start.20 = (f32[384,128]{1,0:T(8,128)S(1)}, f32[384,128]{1,0:T(8,128)S(1)}, u32[]{:S(2)}, u32[]{:S(2)}) collective-permute-start(f32[384,128]{1,0:T(8,128)S(1)} %collective-permute-done.18), channel_id=1, source_target_pairs={{0,2},{2,4},{4,6},{6,8},{8,10},{10,12},{12,14},{14,16},{16,18},{18... | collective-permute-start | bytes 589832 | tf_op jit(solution)/shard_map/ppermute | solution.py:134
  139.6 7.7 %collective-permute-start.21 = (f32[384,128]{1,0:T(8,128)S(1)}, f32[384,128]{1,0:T(8,128)S(1)}, u32[]{:S(2)}, u32[]{:S(2)}) collective-permute-start(f32[384,128]{1,0:T(8,128)S(1)} %collective-permute-done.19), channel_id=1, source_target_pairs={{0,22},{2,0},{4,2},{6,4},{8,6},{10,8},{12,10},{14,12},{16,14},{18,... | collective-permute-start | bytes 589832 | tf_op jit(solution)/shard_map/ppermute | solution.py:134
  147.3 16.6 %collective-permute-start.25 = (f32[4,384,128]{2,1,0:T(8,128)S(1)}, f32[4,384,128]{2,1,0:T(8,128)S(1)}, u32[]{:S(2)}, u32[]{:S(2)}) collective-permute-start(f32[4,384,128]{2,1,0:T(8,128)S(1)} %pad_maximum_fusion.2.refs_3_), channel_id=1, source_target_pairs={{0,1},{1,0},{2,3},{3,2},{4,5},{5,4},{6,7},{7,6},{8,9},{9,8},{10,11... | collective-permute-start | bytes 2359304 | tf_op jit(solution)/shard_map/ppermute | solution.py:134
  152.2 10.6 %collective-permute-start.23 = (f32[384,128]{1,0:T(8,128)S(1)}, f32[384,128]{1,0:T(8,128)S(1)}, u32[]{:S(2)}, u32[]{:S(2)}) collective-permute-start(f32[384,128]{1,0:T(8,128)S(1)} %collective-permute-done.20), channel_id=1, source_target_pairs={{0,2},{2,4},{4,6},{6,8},{8,10},{10,12},{12,14},{14,16},{16,18},{18... | collective-permute-start | bytes 589832 | tf_op jit(solution)/shard_map/ppermute | solution.py:134
  155.3 8.7 %collective-permute-start.24 = (f32[384,128]{1,0:T(8,128)S(1)}, f32[384,128]{1,0:T(8,128)S(1)}, u32[]{:S(2)}, u32[]{:S(2)}) collective-permute-start(f32[384,128]{1,0:T(8,128)S(1)} %collective-permute-done.21), channel_id=1, source_target_pairs={{0,22},{2,0},{4,2},{6,4},{8,6},{10,8},{12,10},{14,12},{16,14},{18,... | collective-permute-start | bytes 589832 | tf_op jit(solution)/shard_map/ppermute | solution.py:134
  164.0 9.6 %collective-permute-start.26 = (f32[384,128]{1,0:T(8,128)S(1)}, f32[384,128]{1,0:T(8,128)S(1)}, u32[]{:S(2)}, u32[]{:S(2)}) collective-permute-start(f32[384,128]{1,0:T(8,128)S(1)} %collective-permute-done.23), channel_id=1, source_target_pairs={{0,2},{2,4},{4,6},{6,8},{8,10},{10,12},{12,14},{14,16},{16,18},{18... | collective-permute-start | bytes 589832 | tf_op jit(solution)/shard_map/ppermute | solution.py:134
  167.0 7.4 %collective-permute-start.27 = (f32[384,128]{1,0:T(8,128)S(1)}, f32[384,128]{1,0:T(8,128)S(1)}, u32[]{:S(2)}, u32[]{:S(2)}) collective-permute-start(f32[384,128]{1,0:T(8,128)S(1)} %collective-permute-done.24), channel_id=1, source_target_pairs={{0,22},{2,0},{4,2},{6,4},{8,6},{10,8},{12,10},{14,12},{16,14},{18,... | collective-permute-start | bytes 589832 | tf_op jit(solution)/shard_map/ppermute | solution.py:134
  171.0 0.9 copy-start.2
  174.5 15.2 %collective-permute-start.30 = (f32[4,384,128]{2,1,0:T(8,128)S(1)}, f32[4,384,128]{2,1,0:T(8,128)S(1)}, u32[]{:S(2)}, u32[]{:S(2)}) collective-permute-start(f32[4,384,128]{2,1,0:T(8,128)S(1)} %pad_maximum_fusion.3.refs_1_), channel_id=1, source_target_pairs={{0,1},{1,0},{2,3},{3,2},{4,5},{5,4},{6,7},{7,6},{8,9},{9,8},{10,11... | collective-permute-start | bytes 2359304 | tf_op jit(solution)/shard_map/ppermute | solution.py:134
  178.2 10.4 %collective-permute-start.28 = (f32[384,128]{1,0:T(8,128)S(1)}, f32[384,128]{1,0:T(8,128)S(1)}, u32[]{:S(2)}, u32[]{:S(2)}) collective-permute-start(f32[384,128]{1,0:T(8,128)S(1)} %collective-permute-done.26), channel_id=1, source_target_pairs={{0,2},{2,4},{4,6},{6,8},{8,10},{10,12},{12,14},{14,16},{16,18},{18... | collective-permute-start | bytes 589832 | tf_op jit(solution)/shard_map/ppermute | solution.py:134
  181.2 8.5 %collective-permute-start.29 = (f32[384,128]{1,0:T(8,128)S(1)}, f32[384,128]{1,0:T(8,128)S(1)}, u32[]{:S(2)}, u32[]{:S(2)}) collective-permute-start(f32[384,128]{1,0:T(8,128)S(1)} %collective-permute-done.27), channel_id=1, source_target_pairs={{0,22},{2,0},{4,2},{6,4},{8,6},{10,8},{12,10},{14,12},{16,14},{18,... | collective-permute-start | bytes 589832 | tf_op jit(solution)/shard_map/ppermute | solution.py:134
  189.7 13.3 %collective-permute-start.32 = (f32[2,384,128]{2,1,0:T(8,128)S(1)}, f32[2,384,128]{2,1,0:T(8,128)S(1)}, u32[]{:S(2)}, u32[]{:S(2)}) collective-permute-start(f32[2,384,128]{2,1,0:T(8,128)S(1)} %pad_maximum_fusion.6.refs_1_), channel_id=1, source_target_pairs={{0,1},{1,0},{2,3},{3,2},{4,5},{5,4},{6,7},{7,6},{8,9},{9,8},{10,11... | collective-permute-start | bytes 1179656 | tf_op jit(solution)/shard_map/ppermute | solution.py:134
  192.4 10.6 %collective-permute-start.31 = (f32[384,128]{1,0:T(8,128)S(1)}, f32[384,128]{1,0:T(8,128)S(1)}, u32[]{:S(2)}, u32[]{:S(2)}) collective-permute-start(f32[384,128]{1,0:T(8,128)S(1)} %collective-permute-done.28), channel_id=1, source_target_pairs={{0,2},{2,4},{4,6},{6,8},{8,10},{10,12},{12,14},{14,16},{16,18},{18... | collective-permute-start | bytes 589832 | tf_op jit(solution)/shard_map/ppermute | solution.py:134
  196.6 16.1 %copy-start.3 = (f32[384,128]{1,0:T(8,128)S(1)}, f32[384,128]{1,0:T(8,128)}, u32[]{:S(2)}) copy-start(f32[384,128]{1,0:T(8,128)} %shard_map.61.refs_0_) | copy-start | bytes 589828
Sparse Core Ops, SparseCore 0:
  38.5 47.9 all-gather.5

commit v3 on v2

--- a/solution.py
+++ b/solution.py
@@ -22,7 +22,7 @@
 
 
 def mask_kernel(sizes, pattern, density, out):
-    row_blocks, col_blocks = pattern.shape
+    col_blocks, row_blocks = pattern.shape
     first_row = (lax.axis_index("xh") * NY + lax.axis_index("y")) * row_blocks
     first_col = ((lax.axis_index("xl") * NZ + lax.axis_index("z")) * 2 + lax.axis_index("c")) * col_blocks
     sub = lax.broadcasted_iota(jnp.int32, (BS, 2 * BS), 0)
@@ -31,7 +31,7 @@
     size_col = jnp.where(left, sizes[first_col], sizes[first_col + 1])
     valid_col = (jnp.where(left, lane, lane - BS) < size_col).astype(F32)
     for i in range(row_blocks):
-        stored = jnp.where(left, pattern[i, 0], pattern[i, 1]).astype(F32)
+        stored = jnp.where(left, pattern[0, i], pattern[1, i]).astype(F32)
         valid = (sub < sizes[first_row + i]).astype(F32) * valid_col * stored
         out[i * BS : (i + 1) * BS, :] = density[i * BS : (i + 1) * BS, :] * valid
 
@@ -103,12 +103,53 @@
     )(*args)
 
 
+def first_kernel(offsets, left, *refs):
+    n = len(offsets)
+    near, far = refs[:n], refs[n : 2 * n]
+    mine, other, right = refs[2 * n :]
+    y = lax.axis_index("y")
+    dot = functools.partial(jnp.dot, preferred_element_type=F32)
+    acc = None
+    for k, off in enumerate(offsets):
+        yy = lax.rem(y + (off + NY), NY)
+        u = 3 * yy
+        a = jnp.concatenate([left[u], left[u + 1], left[u + 2]], axis=1)
+        right[yy, 0] = near[k][...]
+        right[yy, 1] = far[k][...]
+        b = jnp.concatenate([near[k][...], far[k][...]], axis=1)
+        ah, al = split(a)
+        bh, bl = split(b)
+        term = dot(ah, bh) + (dot(ah, bl) + dot(al, bh))
+        acc = term if acc is None else acc + term
+    same = lax.axis_index("xl") == lax.axis_index("xh")
+    first, second = acc[:, :128], acc[:, 128:]
+    mine[...] = jnp.where(same, first, second)
+    other[...] = jnp.where(same, second, first)
+
+
+def first_product(left, offsets, near, far):
+    rows, cols = near[0].shape
+    block = jax.ShapeDtypeStruct((rows, cols), F32)
+    args = [left] + near + far
+    mine, other, right = pl.pallas_call(
+        functools.partial(first_kernel, tuple(offsets)),
+        out_shape=(block, block, jax.ShapeDtypeStruct((NY, 2, rows, cols), F32)),
+        in_specs=[VM] * len(args),
+        out_specs=(VM, VM, VM),
+        compiler_params=PARAMS,
+        cost_estimate=pl.CostEstimate(
+            flops=NY * 3 * 2 * rows * rows * 2 * cols, bytes_accessed=0, transcendentals=0
+        ),
+    )(*args)
+    return (mine, other), right
+
+
 def filter_kernel(final, kept, mine, pair, *refs):
     other = 1 - lax.axis_index("xl")
     lane = lax.broadcasted_iota(jnp.int32, (BS, 2 * BS), 1)
-    for i in range(kept.shape[0]):
+    for i in range(kept.shape[1]):
         strip = slice(i * BS, (i + 1) * BS)
-        filt = jnp.where(lane < BS, kept[i, 0], kept[i, 1]).astype(F32)
+        filt = jnp.where(lane < BS, kept[0, i], kept[1, i]).astype(F32)
         total = filt * (mine[strip, :] + pair[other, strip, :])
         if final:
             refs[1][strip, :] = 3.0 * refs[0][strip, :] - 2.0 * total
@@ -138,6 +179,14 @@
     return lax.optimization_barrier(xs)
 
 
+def chain(x, axis, step, count):
+    out = []
+    for _ in range(count):
+        x = shift(x, axis, step)
+        out.append(x)
+    return out
+
+
 def body(density, atom_sizes, pattern, kept):
     masked = pl.pallas_call(
         mask_kernel,
@@ -145,48 +194,28 @@
         in_specs=[SM, SM, VM],
         out_specs=VM,
         compiler_params=PARAMS,
-    )(atom_sizes, pattern, density)
+    )(atom_sizes, pattern.T, density)
+
+    left = lax.all_gather(masked, ("z", "c"), axis=0)
 
     near = lax.ppermute(masked, ("xh", "xl"), [(0, 0), (1, 2), (2, 1), (3, 3)])
     far = lax.ppermute(masked, ("xh", "xl"), [(1, 0), (2, 3), (0, 2), (3, 1)])
-    up, down = shift(masked, "z", 1), shift(masked, "z", -1)
-    u1, d1, near, far = together(up, down, near, far)
-    right, u1, d1 = together(jnp.stack([near, far]), u1, d1)
-    right = lax.all_gather(right, "y", axis=0)
-
-    def rest(x, u1, d1, multiply, alone):
-        x = x[None]
-        u2, d2, x_sib = together(shift(u1, "z", 1), shift(d1, "z", -1), shift(x, "c", 1))
-        s12 = jnp.stack([u1, d1, u2, d2])
-        u3, d3, s12_sib = together(shift(u2, "z", 1), shift(d2, "z", -1), shift(s12, "c", 1))
-        g12 = [("pair", (0,), (x, x_sib)), ("pair", (-1, 1, -2, 2), (s12, s12_sib))]
-        acc = multiply(g12)
-        u4, d4, acc = together(shift(u3, "z", 1), shift(d3, "z", -1), acc)
-        s34 = jnp.stack([u3, d3, u4, d4])
-        u5, d5, s34_sib = together(shift(u4, "z", 1), shift(d4, "z", -1), shift(s34, "c", 1))
-        g34 = [("pair", (-3, 3, -4, 4), (s34, s34_sib))]
-        acc = multiply(g34, acc)
-        s5 = jnp.stack([u5, d5])
-        u6, s5_sib, acc = together(shift(u5, "z", 1), shift(s5, "c", 1), acc)
-        g56 = [("pair", (-5, 5), (s5, s5_sib))]
-        if alone:
-            g56.append(("both", (-6,), (lax.all_gather(u6, "c", axis=0),)))
-        else:
-            g56.append(("pair", (-6,), (u6[None], shift(u6[None], "c", 1))))
-        return g12 + g34, g56, acc
-
-    def later(groups, acc=None):
-        return jnp.zeros((), F32) if acc is None else acc
-
-    def now(groups, acc=None):
-        return product(right, groups, acc, last=False)
-
-    most, final, _ = rest(masked, u1, d1, later, False)
-    square = filtered(kept, product(right, most + final))
-
-    u1, d1 = together(shift(square, "z", 1), shift(square, "z", -1))
-    _, final, acc = rest(square, u1, d1, now, True)
-    purified = filtered(kept, product(right, final, acc), square)
+    near_up, near_down = chain(near, "y", 1, 4), chain(near, "y", -1, 3)
+    far_up, far_down = chain(far, "y", 1, 3), chain(far, "y", -1, 4)
+    offsets = [0, -1, 1, -2, 2, -3, 3, 4]
+    near = [near] + [x for pair in zip(near_up, near_down) for x in pair] + [near_up[3]]
+    far = [far] + [x for pair in zip(far_up, far_down) for x in pair] + [far_down[3]]
+    halves, right = first_product(left, offsets, near, far)
+    square = filtered(kept.T, halves)
+
+    up, down = chain(square, "z", 1, 6), chain(square, "z", -1, 5)
+    most = jnp.stack([square] + [x for pair in zip(up[:4], down[:4]) for x in pair])
+    most_sib = shift(most, "c", 1)
+    some = jnp.stack([up[4], down[4], up[5]])
+    some_sib = shift(some, "c", 1)
+    acc = product(right, [("pair", (0, -1, 1, -2, 2, -3, 3, -4, 4), (most, most_sib))], last=False)
+    halves = product(right, [("pair", (-5, 5, -6), (some, some_sib))], acc)
+    purified = filtered(kept.T, halves, square)
     return (square, purified)
 
 

time: 222 us -> 184 us (0.83)
  starting transfers between devices: 122 us -> 95.8 us
  waiting for transfers between devices: 48.8 us -> 42.5 us
  blocking collectives: 17.7 us -> 15.2 us
    ppermute x31 -> x27, starting transfers between devices: 116 us -> 88.7 us  [shift(): return lax.ppermute(x, axis, [(i, (i + step) % n) for i in range(n)])]
    ppermute x31 -> x27, waiting for transfers between devices: 45.4 us -> 28.8 us  [shift(): return lax.ppermute(x, axis, [(i, (i + step) % n) for i in range(n)])]
    all_gather x1, waiting for transfers between devices: 0.01 us -> 12.4 us  [body(): left = lax.all_gather(masked, ('z', 'c'), axis=0)]
    pallas_call x4 -> x2, Pallas kernels: 5.84 us -> 2.32 us  [product(): pl.pallas_call(functools.partial(product_kernel, plan, acc is not None, l...]
    pallas_call x0 -> x1, Pallas kernels: none -> 2.8 us  [first_product(): pl.pallas_call(functools.partial(first_kernel, tuple(offsets)), out_shape...]
    all_gather x1 -> x0, blocking collectives: 2.3 us -> none  [rest(): g56.append(('both', (-6,), (lax.all_gather(u6, 'c', axis=0),)))]
  transfers between devices with their start and end apart: 34 -> 30, of which waited for: 20 -> 11; matrix products, arithmetic and copies ran while one was open for 0% -> 1% of each run, Pallas kernels for 1% -> 1%
where the time goes in v3:
time: 184 us; the launch traced here: 183 us
  starting transfers between devices  95.8 us (52%)
  waiting for transfers between devices  42.5 us (23%)
  blocking collectives  15.2 us (8%)
  between operations  14.5 us (8%)
  Pallas kernels  8.93 us (5%)
  local copies, waits for them, and re-layouts  5.68 us (3%)
    ppermute x27, starting transfers between devices, shift(): return lax.ppermute(x, axis, [(i, (i + step) % n) for i in range(n)])  88.7 us
    ppermute x27, waiting for transfers between devices, shift(): return lax.ppermute(x, axis, [(i, (i + step) % n) for i in range(n)])  28.8 us
    all_gather x2, blocking collectives, filtered(): pair = lax.all_gather(other, 'xl', axis=0)  15.2 us
    all_gather x1, waiting for transfers between devices, body(): left = lax.all_gather(masked, ('z', 'c'), axis=0)  12.4 us
    unnamed x20, local copies, waits for them, and re-layouts  5.66 us
    ppermute x1, starting transfers between devices, body(): far = lax.ppermute(masked, ('xh', 'xl'), [(1, 0), (2, 3), (0, 2), (3, 1)])  5.48 us
  transfers between devices with their start and end apart: 30, of which 11 were waited for; matrix products, arithmetic and copies ran while one was open for 1% of the time, Pallas kernels for 1%

profile of v3, /device:TPU:1, one launch (start us, length us, event | category | flops | bytes accessed | tf_op | source)
XLA Modules:
  0.0 182.8 jit_solution(5365289112095430113)
XLA Ops:
  7.2 0.0 all-gather.5.cloned.1.call-start
  7.2 0.9 copy-done.2
  8.1 0.7 copy-done.4
  8.8 0.7 copy-done.5
  9.5 1.3 shard_map.59
  10.8 0.0 all-gather.5.cloned.1.call-update
  10.8 5.5 %collective-permute-start.8 = (f32[384,128]{1,0:T(8,128)}, f32[384,128]{1,0:T(8,128)S(1)}, u32[]{:S(2)}, u32[]{:S(2)}) collective-permute-start(f32[384,128]{1,0:T(8,128)} %shard_map.59), channel_id=1, source_target_pairs={{24,0},{384,408},{0,384},{408,24},{25,1},{385,409},{1,385},{409,25... | collective-permute-start | bytes 589832 | tf_op jit(solution)/shard_map/ppermute | solution.py:202
  16.3 1.6 collective-permute-start
  17.9 1.3 collective-permute-done.8.refs_8_
  19.2 6.1 %collective-permute-start.10 = (f32[384,128]{1,0:T(8,128)S(1)}, f32[384,128]{1,0:T(8,128)S(1)}, u32[]{:S(2)}, u32[]{:S(2)}) collective-permute-start(f32[384,128]{1,0:T(8,128)S(1)} %collective-permute-done.8.refs_8_), channel_id=1, source_target_pairs={{0,336},{48,0},{96,48},{144,96},{192,144},{240,192},{288,240},{336... | collective-permute-start | bytes 589832 | tf_op jit(solution)/shard_map/ppermute | solution.py:175
  25.3 0.0 collective-permute-done.refs_0_
  25.3 1.9 %collective-permute-start.1 = (f32[384,128]{1,0:T(8,128)S(1)}, f32[384,128]{1,0:T(8,128)S(1)}, u32[]{:S(2)}, u32[]{:S(2)}) collective-permute-start(f32[384,128]{1,0:T(8,128)S(1)} %collective-permute-done.refs_0_), channel_id=1, source_target_pairs={{0,48},{48,96},{96,144},{144,192},{192,240},{240,288},{288,336},{3... | collective-permute-start | bytes 589832 | tf_op jit(solution)/shard_map/ppermute | solution.py:175
  27.2 1.9 %collective-permute-start.9 = (f32[384,128]{1,0:T(8,128)S(1)}, f32[384,128]{1,0:T(8,128)S(1)}, u32[]{:S(2)}, u32[]{:S(2)}) collective-permute-start(f32[384,128]{1,0:T(8,128)S(1)} %collective-permute-done.8.refs_8_), channel_id=1, source_target_pairs={{0,48},{48,96},{96,144},{144,192},{192,240},{240,288},{288,336},{3... | collective-permute-start | bytes 589832 | tf_op jit(solution)/shard_map/ppermute | solution.py:175
  29.1 4.6 %collective-permute-start.2 = (f32[384,128]{1,0:T(8,128)S(1)}, f32[384,128]{1,0:T(8,128)S(1)}, u32[]{:S(2)}, u32[]{:S(2)}) collective-permute-start(f32[384,128]{1,0:T(8,128)S(1)} %collective-permute-done.refs_0_), channel_id=1, source_target_pairs={{0,336},{48,0},{96,48},{144,96},{192,144},{240,192},{288,240},{336... | collective-permute-start | bytes 589832 | tf_op jit(solution)/shard_map/ppermute | solution.py:175
  33.7 0.0 collective-permute-done.10.refs_10_
  33.7 3.4 %collective-permute-start.12 = (f32[384,128]{1,0:T(8,128)S(1)}, f32[384,128]{1,0:T(8,128)S(1)}, u32[]{:S(2)}, u32[]{:S(2)}) collective-permute-start(f32[384,128]{1,0:T(8,128)S(1)} %collective-permute-done.10.refs_10_), channel_id=1, source_target_pairs={{0,336},{48,0},{96,48},{144,96},{192,144},{240,192},{288,240},{336... | collective-permute-start | bytes 589832 | tf_op jit(solution)/shard_map/ppermute | solution.py:175
  37.1 0.0 collective-permute-done.1.refs_1_
  37.1 1.9 %collective-permute-start.3 = (f32[384,128]{1,0:T(8,128)S(1)}, f32[384,128]{1,0:T(8,128)S(1)}, u32[]{:S(2)}, u32[]{:S(2)}) collective-permute-start(f32[384,128]{1,0:T(8,128)S(1)} %collective-permute-done.1.refs_1_), channel_id=1, source_target_pairs={{0,48},{48,96},{96,144},{144,192},{192,240},{240,288},{288,336},{3... | collective-permute-start | bytes 589832 | tf_op jit(solution)/shard_map/ppermute | solution.py:175
  39.0 1.9 %collective-permute-start.11 = (f32[384,128]{1,0:T(8,128)S(1)}, f32[384,128]{1,0:T(8,128)S(1)}, u32[]{:S(2)}, u32[]{:S(2)}) collective-permute-start(f32[384,128]{1,0:T(8,128)S(1)} %collective-permute-done.9.refs_9_), channel_id=1, source_target_pairs={{0,48},{48,96},{96,144},{144,192},{192,240},{240,288},{288,336},{3... | collective-permute-start | bytes 589832 | tf_op jit(solution)/shard_map/ppermute | solution.py:175
  41.0 0.0 collective-permute-done.2.refs_2_
  41.0 4.6 %collective-permute-start.4 = (f32[384,128]{1,0:T(8,128)S(1)}, f32[384,128]{1,0:T(8,128)S(1)}, u32[]{:S(2)}, u32[]{:S(2)}) collective-permute-start(f32[384,128]{1,0:T(8,128)S(1)} %collective-permute-done.2.refs_2_), channel_id=1, source_target_pairs={{0,336},{48,0},{96,48},{144,96},{192,144},{240,192},{288,240},{336... | collective-permute-start | bytes 589832 | tf_op jit(solution)/shard_map/ppermute | solution.py:175
  45.6 3.4 %collective-permute-start.14 = (f32[384,128]{1,0:T(8,128)S(1)}, f32[384,128]{1,0:T(8,128)S(1)}, u32[]{:S(2)}, u32[]{:S(2)}) collective-permute-start(f32[384,128]{1,0:T(8,128)S(1)} %collective-permute-done.12.refs_12_), channel_id=1, source_target_pairs={{0,336},{48,0},{96,48},{144,96},{192,144},{240,192},{288,240},{336... | collective-permute-start | bytes 589832 | tf_op jit(solution)/shard_map/ppermute | solution.py:175
  48.9 0.0 collective-permute-done.3.refs_3_
  48.9 1.9 %collective-permute-start.5 = (f32[384,128]{1,0:T(8,128)S(1)}, f32[384,128]{1,0:T(8,128)S(1)}, u32[]{:S(2)}, u32[]{:S(2)}) collective-permute-start(f32[384,128]{1,0:T(8,128)S(1)} %collective-permute-done.3.refs_3_), channel_id=1, source_target_pairs={{0,48},{48,96},{96,144},{144,192},{192,240},{240,288},{288,336},{3... | collective-permute-start | bytes 589832 | tf_op jit(solution)/shard_map/ppermute | solution.py:175
  50.9 0.0 collective-permute-done.11.refs_11_
  50.9 1.9 %collective-permute-start.13 = (f32[384,128]{1,0:T(8,128)S(1)}, f32[384,128]{1,0:T(8,128)S(1)}, u32[]{:S(2)}, u32[]{:S(2)}) collective-permute-start(f32[384,128]{1,0:T(8,128)S(1)} %collective-permute-done.11.refs_11_), channel_id=1, source_target_pairs={{0,48},{48,96},{96,144},{144,192},{192,240},{240,288},{288,336},{3... | collective-permute-start | bytes 589832 | tf_op jit(solution)/shard_map/ppermute | solution.py:175
  52.8 4.6 %collective-permute-start.6 = (f32[384,128]{1,0:T(8,128)S(1)}, f32[384,128]{1,0:T(8,128)S(1)}, u32[]{:S(2)}, u32[]{:S(2)}) collective-permute-start(f32[384,128]{1,0:T(8,128)S(1)} %collective-permute-done.4.refs_4_), channel_id=1, source_target_pairs={{0,336},{48,0},{96,48},{144,96},{192,144},{240,192},{288,240},{336... | collective-permute-start | bytes 589832 | tf_op jit(solution)/shard_map/ppermute | solution.py:175
  57.4 3.4 %collective-permute-start.15 = (f32[384,128]{1,0:T(8,128)S(1)}, f32[384,128]{1,0:T(8,128)S(1)}, u32[]{:S(2)}, u32[]{:S(2)}) collective-permute-start(f32[384,128]{1,0:T(8,128)S(1)} %collective-permute-done.14.refs_14_), channel_id=1, source_target_pairs={{0,336},{48,0},{96,48},{144,96},{192,144},{240,192},{288,240},{336... | collective-permute-start | bytes 589832 | tf_op jit(solution)/shard_map/ppermute | solution.py:175
  60.8 1.9 %collective-permute-start.7 = (f32[384,128]{1,0:T(8,128)S(1)}, f32[384,128]{1,0:T(8,128)S(1)}, u32[]{:S(2)}, u32[]{:S(2)}) collective-permute-start(f32[384,128]{1,0:T(8,128)S(1)} %collective-permute-done.5.refs_5_), channel_id=1, source_target_pairs={{0,48},{48,96},{96,144},{144,192},{192,240},{240,288},{288,336},{3... | collective-permute-start | bytes 589832 | tf_op jit(solution)/shard_map/ppermute | solution.py:175
  62.7 1.6 collective-permute-done.15.refs_15_
  64.4 6.0 %collective-permute-done.7.refs_7_ = f32[384,128]{1,0:T(8,128)S(1)} collective-permute-done((f32[384,128]{1,0:T(8,128)S(1)}, f32[384,128]{1,0:T(8,128)S(1)}, u32[]{:S(2)}, u32[]{:S(2)}) %collective-permute-start.7) | collective-permute-done | bytes 196640 | tf_op jit(solution)/shard_map/ppermute | solution.py:175
  70.4 12.4 %all-gather.5.cloned.1.call-done = f32[9216,128]{1,0:T(8,128)} async-done(((f32[384,128]{1,0:T(8,128)}), f32[9216,128]{1,0:T(8,128)}) %all-gather.5.cloned.1.call-update) | async-done | bytes 4718608 | tf_op jit(solution)/shard_map/all_gather | solution.py:199
  82.8 2.3 %copy-done = f32[9216,128]{1,0:T(8,128)S(1)} copy-done((f32[9216,128]{1,0:T(8,128)S(1)}, f32[9216,128]{1,0:T(8,128)}, u32[]{:S(2)}) %copy-start) | copy-done | bytes 4718616
  85.1 2.8 %shard_map.60 = (f32[384,128]{1,0:T(8,128)S(1)}, f32[384,128]{1,0:T(8,128)S(1)}, f32[8,2,384,128]{3,2,1,0:T(8,128)S(1)}) custom-call(f32[24,384,128]{2,1,0:T(8,128)S(1)} %bitcast.26, f32[384,128]{1,0:T(8,128)S(1)} %collective-permute-done.refs_0_, f32[384,128]{1,0:T(8,128)S(1)} %collective-permute-done.1.refs_1_, ...), custom_call_target="tpu_custom_call" | custom-call | flops 1811939328 | tf_op jit(solution)/shard_map/pallas_call | solution.py:134
  87.9 6.9 %all-gather.1 = f32[768,128]{1,0:T(8,128)S(1)} all-gather(f32[384,128]{1,0:T(8,128)S(1)} %get-tuple-element.8), channel_id=3, replica_groups=mesh['xh'=2,'y'=8,'xl'=2,'z'=12,'c'=2] {'xl'}, dimensions={0}, use_global_device_ids=true | all-gather | bytes 589824 | tf_op jit(solution)/shard_map/all_gather | solution.py:162
  94.8 1.3 shard_map.61.refs_0_
  96.1 1.9 %collective-permute-start.21 = (f32[384,128]{1,0:T(8,128)}, f32[384,128]{1,0:T(8,128)S(1)}, u32[]{:S(2)}, u32[]{:S(2)}) collective-permute-start(f32[384,128]{1,0:T(8,128)} %shard_map.61.refs_0_), channel_id=1, source_target_pairs={{0,22},{2,0},{4,2},{6,4},{8,6},{10,8},{12,10},{14,12},{16,14},{18,... | collective-permute-start | bytes 589832 | tf_op jit(solution)/shard_map/ppermute | solution.py:175
  98.0 3.4 %collective-permute-start.16 = (f32[384,128]{1,0:T(8,128)}, f32[384,128]{1,0:T(8,128)S(1)}, u32[]{:S(2)}, u32[]{:S(2)}) collective-permute-start(f32[384,128]{1,0:T(8,128)} %shard_map.61.refs_0_), channel_id=1, source_target_pairs={{0,2},{2,4},{4,6},{6,8},{8,10},{10,12},{12,14},{14,16},{16,18},{18... | collective-permute-start | bytes 589832 | tf_op jit(solution)/shard_map/ppermute | solution.py:175
  101.4 1.0 bitcast_dynamic-update-slice_fusion.8
  102.3 1.2 collective-permute-done.21
  103.5 2.3 %collective-permute-start.22 = (f32[384,128]{1,0:T(8,128)S(1)}, f32[384,128]{1,0:T(8,128)S(1)}, u32[]{:S(2)}, u32[]{:S(2)}) collective-permute-start(f32[384,128]{1,0:T(8,128)S(1)} %collective-permute-done.21), channel_id=1, source_target_pairs={{0,22},{2,0},{4,2},{6,4},{8,6},{10,8},{12,10},{14,12},{16,14},{18,... | collective-permute-start | bytes 589832 | tf_op jit(solution)/shard_map/ppermute | solution.py:175
  105.8 0.0 collective-permute-done.16
  105.8 3.0 %collective-permute-start.17 = (f32[384,128]{1,0:T(8,128)S(1)}, f32[384,128]{1,0:T(8,128)S(1)}, u32[]{:S(2)}, u32[]{:S(2)}) collective-permute-start(f32[384,128]{1,0:T(8,128)S(1)} %collective-permute-done.16), channel_id=1, source_target_pairs={{0,2},{2,4},{4,6},{6,8},{8,10},{10,12},{12,14},{14,16},{16,18},{18... | collective-permute-start | bytes 589832 | tf_op jit(solution)/shard_map/ppermute | solution.py:175
  108.9 1.4 collective-permute-done.22
  110.2 3.2 %collective-permute-start.23 = (f32[384,128]{1,0:T(8,128)S(1)}, f32[384,128]{1,0:T(8,128)S(1)}, u32[]{:S(2)}, u32[]{:S(2)}) collective-permute-start(f32[384,128]{1,0:T(8,128)S(1)} %collective-permute-done.22), channel_id=1, source_target_pairs={{0,22},{2,0},{4,2},{6,4},{8,6},{10,8},{12,10},{14,12},{16,14},{18,... | collective-permute-start | bytes 589832 | tf_op jit(solution)/shard_map/ppermute | solution.py:175
  113.4 0.0 collective-permute-done.17
  113.5 2.0 %collective-permute-start.18 = (f32[384,128]{1,0:T(8,128)S(1)}, f32[384,128]{1,0:T(8,128)S(1)}, u32[]{:S(2)}, u32[]{:S(2)}) collective-permute-start(f32[384,128]{1,0:T(8,128)S(1)} %collective-permute-done.17), channel_id=1, source_target_pairs={{0,2},{2,4},{4,6},{6,8},{8,10},{10,12},{12,14},{14,16},{16,18},{18... | collective-permute-start | bytes 589832 | tf_op jit(solution)/shard_map/ppermute | solution.py:175
  115.6 1.1 collective-permute-done.23
  116.6 4.7 %collective-permute-start.24 = (f32[384,128]{1,0:T(8,128)S(1)}, f32[384,128]{1,0:T(8,128)S(1)}, u32[]{:S(2)}, u32[]{:S(2)}) collective-permute-start(f32[384,128]{1,0:T(8,128)S(1)} %collective-permute-done.23), channel_id=1, source_target_pairs={{0,22},{2,0},{4,2},{6,4},{8,6},{10,8},{12,10},{14,12},{16,14},{18,... | collective-permute-start | bytes 589832 | tf_op jit(solution)/shard_map/ppermute | solution.py:175
  121.4 0.3 collective-permute-done.18
  121.7 1.9 %collective-permute-start.19 = (f32[384,128]{1,0:T(8,128)S(1)}, f32[384,128]{1,0:T(8,128)S(1)}, u32[]{:S(2)}, u32[]{:S(2)}) collective-permute-start(f32[384,128]{1,0:T(8,128)S(1)} %collective-permute-done.18), channel_id=1, source_target_pairs={{0,2},{2,4},{4,6},{6,8},{8,10},{10,12},{12,14},{14,16},{16,18},{18... | collective-permute-start | bytes 589832 | tf_op jit(solution)/shard_map/ppermute | solution.py:175
  123.6 7.3 %collective-permute-done.19 = f32[384,128]{1,0:T(8,128)S(1)} collective-permute-done((f32[384,128]{1,0:T(8,128)S(1)}, f32[384,128]{1,0:T(8,128)S(1)}, u32[]{:S(2)}, u32[]{:S(2)}) %collective-permute-start.19) | collective-permute-done | bytes 196640 | tf_op jit(solution)/shard_map/ppermute | solution.py:175
  131.0 11.0 %collective-permute-start.28 = (f32[9,384,128]{2,1,0:T(8,128)S(1)}, f32[9,384,128]{2,1,0:T(8,128)S(1)}, u32[]{:S(2)}, u32[]{:S(2)}) collective-permute-start(f32[9,384,128]{2,1,0:T(8,128)S(1)} %bitcast_dynamic-update-slice_fusion.refs_1_), channel_id=1, source_target_pairs={{0,1},{1,0},{2,3},{3,2},{4,5},{5,4},{6,7},{7,6},{8,9},{9,8},{10,11... | collective-permute-start | bytes 5308424 | tf_op jit(solution)/shard_map/ppermute | solution.py:175
  142.0 1.9 %collective-permute-start.20 = (f32[384,128]{1,0:T(8,128)S(1)}, f32[384,128]{1,0:T(8,128)S(1)}, u32[]{:S(2)}, u32[]{:S(2)}) collective-permute-start(f32[384,128]{1,0:T(8,128)S(1)} %collective-permute-done.19), channel_id=1, source_target_pairs={{0,2},{2,4},{4,6},{6,8},{8,10},{10,12},{12,14},{14,16},{16,18},{18... | collective-permute-start | bytes 589832 | tf_op jit(solution)/shard_map/ppermute | solution.py:175
  143.9 4.6 %collective-permute-start.25 = (f32[384,128]{1,0:T(8,128)S(1)}, f32[384,128]{1,0:T(8,128)S(1)}, u32[]{:S(2)}, u32[]{:S(2)}) collective-permute-start(f32[384,128]{1,0:T(8,128)S(1)} %collective-permute-done.24), channel_id=1, source_target_pairs={{0,22},{2,0},{4,2},{6,4},{8,6},{10,8},{12,10},{14,12},{16,14},{18,... | collective-permute-start | bytes 589832 | tf_op jit(solution)/shard_map/ppermute | solution.py:175
  148.5 3.1 %collective-permute-done.20 = f32[384,128]{1,0:T(8,128)S(1)} collective-permute-done((f32[384,128]{1,0:T(8,128)S(1)}, f32[384,128]{1,0:T(8,128)S(1)}, u32[]{:S(2)}, u32[]{:S(2)}) %collective-permute-start.20) | collective-permute-done | bytes 196640 | tf_op jit(solution)/shard_map/ppermute | solution.py:175
  151.6 1.9 %collective-permute-start.26 = (f32[384,128]{1,0:T(8,128)S(1)}, f32[384,128]{1,0:T(8,128)S(1)}, u32[]{:S(2)}, u32[]{:S(2)}) collective-permute-start(f32[384,128]{1,0:T(8,128)S(1)} %collective-permute-done.20), channel_id=1, source_target_pairs={{0,2},{2,4},{4,6},{6,8},{8,10},{10,12},{12,14},{14,16},{16,18},{18... | collective-permute-start | bytes 589832 | tf_op jit(solution)/shard_map/ppermute | solution.py:175
  153.5 6.8 %collective-permute-done.26 = f32[384,128]{1,0:T(8,128)S(1)} collective-permute-done((f32[384,128]{1,0:T(8,128)S(1)}, f32[384,128]{1,0:T(8,128)S(1)}, u32[]{:S(2)}, u32[]{:S(2)}) %collective-permute-start.26) | collective-permute-done | bytes 196640 | tf_op jit(solution)/shard_map/ppermute | solution.py:175
  160.4 3.6 %collective-permute-start.27 = (f32[3,384,128]{2,1,0:T(8,128)S(1)}, f32[3,384,128]{2,1,0:T(8,128)S(1)}, u32[]{:S(2)}, u32[]{:S(2)}) collective-permute-start(f32[3,384,128]{2,1,0:T(8,128)S(1)} %pad_maximum_fusion.refs_1_), channel_id=1, source_target_pairs={{0,1},{1,0},{2,3},{3,2},{4,5},{5,4},{6,7},{7,6},{8,9},{9,8},{10,11... | collective-permute-start | bytes 1769480 | tf_op jit(solution)/shard_map/ppermute | solution.py:175
  164.0 1.6 shard_map.62.refs_3_
  165.6 0.0 copy-start.1
  165.6 0.7 shard_map.63
  166.3 8.3 %all-gather.2 = f32[768,128]{1,0:T(8,128)S(1)} all-gather(f32[384,128]{1,0:T(8,128)S(1)} %get-tuple-element.11), channel_id=4, replica_groups=mesh['xh'=2,'y'=8,'xl'=2,'z'=12,'c'=2] {'xl'}, dimensions={0}, use_global_device_ids=true | all-gather | bytes 589824 | tf_op jit(solution)/shard_map/all_gather | solution.py:162
  174.6 1.3 shard_map.64
  (27 shorter events, 0.2 us)
Async XLA Ops:
  7.2 75.6 %all-gather.5.cloned.1.call-start = ((), (), s32[]{:S(2)}) async-start(), calls=%async_computation | async-start | bytes 4915200 | tf_op jit(solution)/shard_map/all_gather | solution.py:199
  7.2 0.9 copy-start.2
  8.1 0.7 copy-start.4
  8.8 0.7 copy-start.5
  10.8 8.4 %collective-permute-start.8 = (f32[384,128]{1,0:T(8,128)}, f32[384,128]{1,0:T(8,128)S(1)}, u32[]{:S(2)}, u32[]{:S(2)}) collective-permute-start(f32[384,128]{1,0:T(8,128)} %shard_map.59), channel_id=1, source_target_pairs={{24,0},{384,408},{0,384},{408,24},{25,1},{385,409},{1,385},{409,25... | collective-permute-start | bytes 589832 | tf_op jit(solution)/shard_map/ppermute | solution.py:202
  16.3 9.0 %collective-permute-start = (f32[384,128]{1,0:T(8,128)}, f32[384,128]{1,0:T(8,128)S(1)}, u32[]{:S(2)}, u32[]{:S(2)}) collective-permute-start(f32[384,128]{1,0:T(8,128)} %shard_map.59), channel_id=1, source_target_pairs={{0,0},{24,384},{384,24},{408,408},{1,1},{25,385},{385,25},{409,409... | collective-permute-start | bytes 589832 | tf_op jit(solution)/shard_map/ppermute | solution.py:201
  19.2 14.5 %collective-permute-start.10 = (f32[384,128]{1,0:T(8,128)S(1)}, f32[384,128]{1,0:T(8,128)S(1)}, u32[]{:S(2)}, u32[]{:S(2)}) collective-permute-start(f32[384,128]{1,0:T(8,128)S(1)} %collective-permute-done.8.refs_8_), channel_id=1, source_target_pairs={{0,336},{48,0},{96,48},{144,96},{192,144},{240,192},{288,240},{336... | collective-permute-start | bytes 589832 | tf_op jit(solution)/shard_map/ppermute | solution.py:175
  25.3 11.8 %collective-permute-start.1 = (f32[384,128]{1,0:T(8,128)S(1)}, f32[384,128]{1,0:T(8,128)S(1)}, u32[]{:S(2)}, u32[]{:S(2)}) collective-permute-start(f32[384,128]{1,0:T(8,128)S(1)} %collective-permute-done.refs_0_), channel_id=1, source_target_pairs={{0,48},{48,96},{96,144},{144,192},{192,240},{240,288},{288,336},{3... | collective-permute-start | bytes 589832 | tf_op jit(solution)/shard_map/ppermute | solution.py:175
  27.2 11.8 %collective-permute-start.9 = (f32[384,128]{1,0:T(8,128)S(1)}, f32[384,128]{1,0:T(8,128)S(1)}, u32[]{:S(2)}, u32[]{:S(2)}) collective-permute-start(f32[384,128]{1,0:T(8,128)S(1)} %collective-permute-done.8.refs_8_), channel_id=1, source_target_pairs={{0,48},{48,96},{96,144},{144,192},{192,240},{240,288},{288,336},{3... | collective-permute-start | bytes 589832 | tf_op jit(solution)/shard_map/ppermute | solution.py:175
  29.1 11.8 %collective-permute-start.2 = (f32[384,128]{1,0:T(8,128)S(1)}, f32[384,128]{1,0:T(8,128)S(1)}, u32[]{:S(2)}, u32[]{:S(2)}) collective-permute-start(f32[384,128]{1,0:T(8,128)S(1)} %collective-permute-done.refs_0_), channel_id=1, source_target_pairs={{0,336},{48,0},{96,48},{144,96},{192,144},{240,192},{288,240},{336... | collective-permute-start | bytes 589832 | tf_op jit(solution)/shard_map/ppermute | solution.py:175
  33.7 11.8 %collective-permute-start.12 = (f32[384,128]{1,0:T(8,128)S(1)}, f32[384,128]{1,0:T(8,128)S(1)}, u32[]{:S(2)}, u32[]{:S(2)}) collective-permute-start(f32[384,128]{1,0:T(8,128)S(1)} %collective-permute-done.10.refs_10_), channel_id=1, source_target_pairs={{0,336},{48,0},{96,48},{144,96},{192,144},{240,192},{288,240},{336... | collective-permute-start | bytes 589832 | tf_op jit(solution)/shard_map/ppermute | solution.py:175
  37.1 11.8 %collective-permute-start.3 = (f32[384,128]{1,0:T(8,128)S(1)}, f32[384,128]{1,0:T(8,128)S(1)}, u32[]{:S(2)}, u32[]{:S(2)}) collective-permute-start(f32[384,128]{1,0:T(8,128)S(1)} %collective-permute-done.1.refs_1_), channel_id=1, source_target_pairs={{0,48},{48,96},{96,144},{144,192},{192,240},{240,288},{288,336},{3... | collective-permute-start | bytes 589832 | tf_op jit(solution)/shard_map/ppermute | solution.py:175
  39.0 11.8 %collective-permute-start.11 = (f32[384,128]{1,0:T(8,128)S(1)}, f32[384,128]{1,0:T(8,128)S(1)}, u32[]{:S(2)}, u32[]{:S(2)}) collective-permute-start(f32[384,128]{1,0:T(8,128)S(1)} %collective-permute-done.9.refs_9_), channel_id=1, source_target_pairs={{0,48},{48,96},{96,144},{144,192},{192,240},{240,288},{288,336},{3... | collective-permute-start | bytes 589832 | tf_op jit(solution)/shard_map/ppermute | solution.py:175
  41.0 11.8 %collective-permute-start.4 = (f32[384,128]{1,0:T(8,128)S(1)}, f32[384,128]{1,0:T(8,128)S(1)}, u32[]{:S(2)}, u32[]{:S(2)}) collective-permute-start(f32[384,128]{1,0:T(8,128)S(1)} %collective-permute-done.2.refs_2_), channel_id=1, source_target_pairs={{0,336},{48,0},{96,48},{144,96},{192,144},{240,192},{288,240},{336... | collective-permute-start | bytes 589832 | tf_op jit(solution)/shard_map/ppermute | solution.py:175
  45.6 11.8 %collective-permute-start.14 = (f32[384,128]{1,0:T(8,128)S(1)}, f32[384,128]{1,0:T(8,128)S(1)}, u32[]{:S(2)}, u32[]{:S(2)}) collective-permute-start(f32[384,128]{1,0:T(8,128)S(1)} %collective-permute-done.12.refs_12_), channel_id=1, source_target_pairs={{0,336},{48,0},{96,48},{144,96},{192,144},{240,192},{288,240},{336... | collective-permute-start | bytes 589832 | tf_op jit(solution)/shard_map/ppermute | solution.py:175
  48.9 11.8 %collective-permute-start.5 = (f32[384,128]{1,0:T(8,128)S(1)}, f32[384,128]{1,0:T(8,128)S(1)}, u32[]{:S(2)}, u32[]{:S(2)}) collective-permute-start(f32[384,128]{1,0:T(8,128)S(1)} %collective-permute-done.3.refs_3_), channel_id=1, source_target_pairs={{0,48},{48,96},{96,144},{144,192},{192,240},{240,288},{288,336},{3... | collective-permute-start | bytes 589832 | tf_op jit(solution)/shard_map/ppermute | solution.py:175
  50.9 11.8 %collective-permute-start.13 = (f32[384,128]{1,0:T(8,128)S(1)}, f32[384,128]{1,0:T(8,128)S(1)}, u32[]{:S(2)}, u32[]{:S(2)}) collective-permute-start(f32[384,128]{1,0:T(8,128)S(1)} %collective-permute-done.11.refs_11_), channel_id=1, source_target_pairs={{0,48},{48,96},{96,144},{144,192},{192,240},{240,288},{288,336},{3... | collective-permute-start | bytes 589832 | tf_op jit(solution)/shard_map/ppermute | solution.py:175
  52.8 9.9 %collective-permute-start.6 = (f32[384,128]{1,0:T(8,128)S(1)}, f32[384,128]{1,0:T(8,128)S(1)}, u32[]{:S(2)}, u32[]{:S(2)}) collective-permute-start(f32[384,128]{1,0:T(8,128)S(1)} %collective-permute-done.4.refs_4_), channel_id=1, source_target_pairs={{0,336},{48,0},{96,48},{144,96},{192,144},{240,192},{288,240},{336... | collective-permute-start | bytes 589832 | tf_op jit(solution)/shard_map/ppermute | solution.py:175
  57.4 6.9 %collective-permute-start.15 = (f32[384,128]{1,0:T(8,128)S(1)}, f32[384,128]{1,0:T(8,128)S(1)}, u32[]{:S(2)}, u32[]{:S(2)}) collective-permute-start(f32[384,128]{1,0:T(8,128)S(1)} %collective-permute-done.14.refs_14_), channel_id=1, source_target_pairs={{0,336},{48,0},{96,48},{144,96},{192,144},{240,192},{288,240},{336... | collective-permute-start | bytes 589832 | tf_op jit(solution)/shard_map/ppermute | solution.py:175
  60.8 9.6 %collective-permute-start.7 = (f32[384,128]{1,0:T(8,128)S(1)}, f32[384,128]{1,0:T(8,128)S(1)}, u32[]{:S(2)}, u32[]{:S(2)}) collective-permute-start(f32[384,128]{1,0:T(8,128)S(1)} %collective-permute-done.5.refs_5_), channel_id=1, source_target_pairs={{0,48},{48,96},{96,144},{144,192},{192,240},{240,288},{288,336},{3... | collective-permute-start | bytes 589832 | tf_op jit(solution)/shard_map/ppermute | solution.py:175
  82.8 2.3 %copy-start = (f32[9216,128]{1,0:T(8,128)S(1)}, f32[9216,128]{1,0:T(8,128)}, u32[]{:S(2)}) copy-start(f32[9216,128]{1,0:T(8,128)} %all-gather.5.cloned.1.call-done) | copy-start | bytes 14155780
  85.1 9.7 %copy-start.3 = (s32[6,2]{0,1:T(2,128)S(1)}, s32[6,2]{0,1:T(2,128)}, u32[]{:S(2)}) copy-start(s32[6,2]{0,1:T(2,128)} %param.7) | copy-start | bytes 148
  96.1 7.4 %collective-permute-start.21 = (f32[384,128]{1,0:T(8,128)}, f32[384,128]{1,0:T(8,128)S(1)}, u32[]{:S(2)}, u32[]{:S(2)}) collective-permute-start(f32[384,128]{1,0:T(8,128)} %shard_map.61.refs_0_), channel_id=1, source_target_pairs={{0,22},{2,0},{4,2},{6,4},{8,6},{10,8},{12,10},{14,12},{16,14},{18,... | collective-permute-start | bytes 589832 | tf_op jit(solution)/shard_map/ppermute | solution.py:175
  98.0 7.8 %collective-permute-start.16 = (f32[384,128]{1,0:T(8,128)}, f32[384,128]{1,0:T(8,128)S(1)}, u32[]{:S(2)}, u32[]{:S(2)}) collective-permute-start(f32[384,128]{1,0:T(8,128)} %shard_map.61.refs_0_), channel_id=1, source_target_pairs={{0,2},{2,4},{4,6},{6,8},{8,10},{10,12},{12,14},{14,16},{16,18},{18... | collective-permute-start | bytes 589832 | tf_op jit(solution)/shard_map/ppermute | solution.py:175
  103.5 6.7 %collective-permute-start.22 = (f32[384,128]{1,0:T(8,128)S(1)}, f32[384,128]{1,0:T(8,128)S(1)}, u32[]{:S(2)}, u32[]{:S(2)}) collective-permute-start(f32[384,128]{1,0:T(8,128)S(1)} %collective-permute-done.21), channel_id=1, source_target_pairs={{0,22},{2,0},{4,2},{6,4},{8,6},{10,8},{12,10},{14,12},{16,14},{18,... | collective-permute-start | bytes 589832 | tf_op jit(solution)/shard_map/ppermute | solution.py:175
  105.8 7.6 %collective-permute-start.17 = (f32[384,128]{1,0:T(8,128)S(1)}, f32[384,128]{1,0:T(8,128)S(1)}, u32[]{:S(2)}, u32[]{:S(2)}) collective-permute-start(f32[384,128]{1,0:T(8,128)S(1)} %collective-permute-done.16), channel_id=1, source_target_pairs={{0,2},{2,4},{4,6},{6,8},{8,10},{10,12},{12,14},{14,16},{16,18},{18... | collective-permute-start | bytes 589832 | tf_op jit(solution)/shard_map/ppermute | solution.py:175
  110.2 6.4 %collective-permute-start.23 = (f32[384,128]{1,0:T(8,128)S(1)}, f32[384,128]{1,0:T(8,128)S(1)}, u32[]{:S(2)}, u32[]{:S(2)}) collective-permute-start(f32[384,128]{1,0:T(8,128)S(1)} %collective-permute-done.22), channel_id=1, source_target_pairs={{0,22},{2,0},{4,2},{6,4},{8,6},{10,8},{12,10},{14,12},{16,14},{18,... | collective-permute-start | bytes 589832 | tf_op jit(solution)/shard_map/ppermute | solution.py:175
  113.5 8.2 %collective-permute-start.18 = (f32[384,128]{1,0:T(8,128)S(1)}, f32[384,128]{1,0:T(8,128)S(1)}, u32[]{:S(2)}, u32[]{:S(2)}) collective-permute-start(f32[384,128]{1,0:T(8,128)S(1)} %collective-permute-done.17), channel_id=1, source_target_pairs={{0,2},{2,4},{4,6},{6,8},{8,10},{10,12},{12,14},{14,16},{16,18},{18... | collective-permute-start | bytes 589832 | tf_op jit(solution)/shard_map/ppermute | solution.py:175
  116.6 14.3 %collective-permute-start.24 = (f32[384,128]{1,0:T(8,128)S(1)}, f32[384,128]{1,0:T(8,128)S(1)}, u32[]{:S(2)}, u32[]{:S(2)}) collective-permute-start(f32[384,128]{1,0:T(8,128)S(1)} %collective-permute-done.23), channel_id=1, source_target_pairs={{0,22},{2,0},{4,2},{6,4},{8,6},{10,8},{12,10},{14,12},{16,14},{18,... | collective-permute-start | bytes 589832 | tf_op jit(solution)/shard_map/ppermute | solution.py:175
  121.7 9.3 %collective-permute-start.19 = (f32[384,128]{1,0:T(8,128)S(1)}, f32[384,128]{1,0:T(8,128)S(1)}, u32[]{:S(2)}, u32[]{:S(2)}) collective-permute-start(f32[384,128]{1,0:T(8,128)S(1)} %collective-permute-done.18), channel_id=1, source_target_pairs={{0,2},{2,4},{4,6},{6,8},{8,10},{10,12},{12,14},{14,16},{16,18},{18... | collective-permute-start | bytes 589832 | tf_op jit(solution)/shard_map/ppermute | solution.py:175
  131.0 33.0 %collective-permute-start.28 = (f32[9,384,128]{2,1,0:T(8,128)S(1)}, f32[9,384,128]{2,1,0:T(8,128)S(1)}, u32[]{:S(2)}, u32[]{:S(2)}) collective-permute-start(f32[9,384,128]{2,1,0:T(8,128)S(1)} %bitcast_dynamic-update-slice_fusion.refs_1_), channel_id=1, source_target_pairs={{0,1},{1,0},{2,3},{3,2},{4,5},{5,4},{6,7},{7,6},{8,9},{9,8},{10,11... | collective-permute-start | bytes 5308424 | tf_op jit(solution)/shard_map/ppermute | solution.py:175
  142.0 9.6 %collective-permute-start.20 = (f32[384,128]{1,0:T(8,128)S(1)}, f32[384,128]{1,0:T(8,128)S(1)}, u32[]{:S(2)}, u32[]{:S(2)}) collective-permute-start(f32[384,128]{1,0:T(8,128)S(1)} %collective-permute-done.19), channel_id=1, source_target_pairs={{0,2},{2,4},{4,6},{6,8},{8,10},{10,12},{12,14},{14,16},{16,18},{18... | collective-permute-start | bytes 589832 | tf_op jit(solution)/shard_map/ppermute | solution.py:175
  143.9 9.6 %collective-permute-start.25 = (f32[384,128]{1,0:T(8,128)S(1)}, f32[384,128]{1,0:T(8,128)S(1)}, u32[]{:S(2)}, u32[]{:S(2)}) collective-permute-start(f32[384,128]{1,0:T(8,128)S(1)} %collective-permute-done.24), channel_id=1, source_target_pairs={{0,22},{2,0},{4,2},{6,4},{8,6},{10,8},{12,10},{14,12},{16,14},{18,... | collective-permute-start | bytes 589832 | tf_op jit(solution)/shard_map/ppermute | solution.py:175
  151.6 8.7 %collective-permute-start.26 = (f32[384,128]{1,0:T(8,128)S(1)}, f32[384,128]{1,0:T(8,128)S(1)}, u32[]{:S(2)}, u32[]{:S(2)}) collective-permute-start(f32[384,128]{1,0:T(8,128)S(1)} %collective-permute-done.20), channel_id=1, source_target_pairs={{0,2},{2,4},{4,6},{6,8},{8,10},{10,12},{12,14},{14,16},{16,18},{18... | collective-permute-start | bytes 589832 | tf_op jit(solution)/shard_map/ppermute | solution.py:175
  160.4 5.3 %collective-permute-start.27 = (f32[3,384,128]{2,1,0:T(8,128)S(1)}, f32[3,384,128]{2,1,0:T(8,128)S(1)}, u32[]{:S(2)}, u32[]{:S(2)}) collective-permute-start(f32[3,384,128]{2,1,0:T(8,128)S(1)} %pad_maximum_fusion.refs_1_), channel_id=1, source_target_pairs={{0,1},{1,0},{2,3},{3,2},{4,5},{5,4},{6,7},{7,6},{8,9},{9,8},{10,11... | collective-permute-start | bytes 1769480 | tf_op jit(solution)/shard_map/ppermute | solution.py:175
  165.6 9.0 %copy-start.1 = (f32[384,128]{1,0:T(8,128)S(1)}, f32[384,128]{1,0:T(8,128)}, u32[]{:S(2)}) copy-start(f32[384,128]{1,0:T(8,128)} %shard_map.61.refs_0_) | copy-start | bytes 589828
Sparse Core Ops, SparseCore 0:
  11.0 71.7 all-gather.4

commit v4 on v3

v4 whole, which is shorter than its diff:
```python
import functools

import jax
import jax.numpy as jnp
from jax import lax
from jax.experimental import pallas as pl
from jax.experimental.pallas import tpu as pltpu
from jax.sharding import Mesh, PartitionSpec as P

BS = 64
AXES = ("xh", "y", "xl", "z", "c")
SIZES = (2, 8, 2, 12, 2)
NY = 8
NZ = 12
ROW = ("xh", "y")
COL = ("xl", "z", "c")
F32 = jnp.float32
BF16 = jnp.bfloat16
VM = pl.BlockSpec(memory_space=pltpu.VMEM)
SM = pl.BlockSpec(memory_space=pltpu.SMEM)
HB = pl.BlockSpec(memory_space=pltpu.HBM)
PARAMS = pltpu.CompilerParams(vmem_limit_bytes=32 * 1024 * 1024)
WIDE = pltpu.CompilerParams(vmem_limit_bytes=50 * 1024 * 1024)
WHOLE = pltpu.CompilerParams(vmem_limit_bytes=64 * 1024 * 1024 - 128 * 1024)


def mask_kernel(sizes_hbm, pattern_hbm, density_hbm, out, sizes, pattern, density, sems):
    copies = [
        pltpu.make_async_copy(sizes_hbm, sizes, sems.at[0]),
        pltpu.make_async_copy(pattern_hbm, pattern, sems.at[1]),
        pltpu.make_async_copy(density_hbm, density, sems.at[2]),
    ]
    for copy in copies:
        copy.start()
    col_blocks, row_blocks = pattern.shape
    first_row = (lax.axis_index("xh") * NY + lax.axis_index("y")) * row_blocks
    first_col = ((lax.axis_index("xl") * NZ + lax.axis_index("z")) * 2 + lax.axis_index("c")) * col_blocks
    sub = lax.broadcasted_iota(jnp.int32, (BS, 2 * BS), 0)
    lane = lax.broadcasted_iota(jnp.int32, (BS, 2 * BS), 1)
    left = lane < BS
    for copy in copies:
        copy.wait()
    size_col = jnp.where(left, sizes[first_col], sizes[first_col + 1])
    valid_col = (jnp.where(left, lane, lane - BS) < size_col).astype(F32)
    for i in range(row_blocks):
        stored = jnp.where(left, pattern[0, i], pattern[1, i]).astype(F32)
        valid = (sub < sizes[first_row + i]).astype(F32) * valid_col * stored
        out[i * BS : (i + 1) * BS, :] = density[i * BS : (i + 1) * BS, :] * valid


def split(x):
    hi = x.astype(BF16)
    return hi, (x - hi.astype(F32)).astype(BF16)


dot = functools.partial(jnp.dot, preferred_element_type=F32)


def split_dot(a, b):
    ah, al = split(a)
    bh, bl = split(b)
    return dot(ah, bh) + (dot(ah, bl) + dot(al, bh))


def put_halves(total, mine, other):
    same = lax.axis_index("xl") == lax.axis_index("xh")
    near, far = total[:, :128], total[:, 128:]
    mine[...] = jnp.where(same, near, far)
    other[...] = jnp.where(same, far, near)


def pack_kernel(offsets, *refs):
    n = len(offsets)
    near, far = refs[:n], refs[n : 2 * n]
    right, give = refs[2 * n :]
    y = lax.axis_index("y")
    for k, off in enumerate(offsets):
        first = 3 * lax.rem(y + (off + NY), NY)
        for t in range(3):
            rows = slice(t * 128, (t + 1) * 128)
            right[first + t, :, :128] = near[k][rows, :]
            right[first + t, :, 128:] = far[k][rows, :]
    c = lax.axis_index("c")
    for z in range(NZ):
        give[z] = right[2 * z + 1 - c]


def pack(offsets, near, far):
    rows, cols = near[0].shape
    args = near + far
    return pl.pallas_call(
        functools.partial(pack_kernel, tuple(offsets)),
        out_shape=(
            jax.ShapeDtypeStruct((2 * NZ, 128, 2 * cols), F32),
            jax.ShapeDtypeStruct((NZ, 128, 2 * cols), F32),
        ),
        in_specs=[VM] * len(args),
        out_specs=(VM, VM),
        compiler_params=PARAMS,
    )(*args)


def first_kernel(left, right, mine, other, held, sems):
    copies = [pltpu.make_async_copy(left.at[pl.ds(2 * z, 2)], held.at[z], sems.at[z]) for z in range(NZ)]
    for copy in copies:
        copy.start()
    acc = None
    for z in range(NZ):
        copies[z].wait()
        a = jnp.concatenate([held[z, 0], held[z, 1]], axis=1)
        b = jnp.concatenate([right[2 * z], right[2 * z + 1]], axis=0)
        term = split_dot(a, b)
        acc = term if acc is None else acc + term
    put_halves(acc, mine, other)


def first_product(left, right):
    _, rows, cols = left.shape
    block = jax.ShapeDtypeStruct((rows, cols), F32)
    return pl.pallas_call(
        first_kernel,
        out_shape=(block, block),
        in_specs=[HB, VM],
        out_specs=(VM, VM),
        scratch_shapes=[pltpu.VMEM((NZ, 2, rows, cols), F32), pltpu.SemaphoreType.DMA((NZ,))],
        compiler_params=WIDE,
        cost_estimate=pl.CostEstimate(
            flops=NZ * 3 * 2 * rows * 2 * cols * 2 * cols, bytes_accessed=0, transcendentals=0
        ),
    )(left, right)


def second_kernel(offsets, has_acc, last, right, took, *refs):
    n = len(offsets)
    acc = refs[n][...] if has_acc else None
    outs = refs[n + has_acc :]
    z = lax.axis_index("z")
    c = lax.axis_index("c")

    def rows(off):
        zz = lax.rem(z + (off + NZ), NZ)
        return jnp.concatenate([right[2 * zz + c], took[zz]], axis=1)

    for k in range(0, n, 2):
        a = jnp.concatenate([refs[k][...], refs[k + 1][...]], axis=1)
        b = jnp.concatenate([rows(offsets[k]), rows(offsets[k + 1])], axis=0)
        term = split_dot(a, b)
        acc = term if acc is None else acc + term
    if last:
        outs[0][...] = acc[:, :256]
        outs[1][...] = acc[:, 256:]
    else:
        outs[0][...] = acc


def second_product(right, took, blocks, acc=None, last=False):
    offsets = tuple(off for off, _ in blocks)
    rows, cols = blocks[0][1].shape
    args = [right, took] + [x for _, x in blocks] + ([] if acc is None else [acc])
    if last:
        shapes = (jax.ShapeDtypeStruct((rows, 2 * cols), F32),) * 2
    else:
        shapes = jax.ShapeDtypeStruct((rows, 4 * cols), F32)
    return pl.pallas_call(
        functools.partial(second_kernel, offsets, acc is not None, last),
        out_shape=shapes,
        in_specs=[VM] * len(args),
        out_specs=(VM, VM) if last else VM,
        compiler_params=PARAMS,
        cost_estimate=pl.CostEstimate(
            flops=len(offsets) * 3 * 2 * rows * cols * 4 * cols, bytes_accessed=0, transcendentals=0
        ),
    )(*args)


def join_kernel(own, both, mine, other):
    put_halves(own[...] + both[1 - lax.axis_index("c")], mine, other)


def join(own, give):
    both = lax.all_gather(give, "c", axis=0)
    rows, cols = own.shape
    block = jax.ShapeDtypeStruct((rows, cols // 2), F32)
    return pl.pallas_call(
        join_kernel,
        out_shape=(block, block),
        in_specs=[VM, VM],
        out_specs=(VM, VM),
        compiler_params=PARAMS,
    )(own, both)


def filter_kernel(final, kept, mine, pair, *refs):
    other = 1 - lax.axis_index("xl")
    lane = lax.broadcasted_iota(jnp.int32, (BS, 2 * BS), 1)
    for i in range(kept.shape[1]):
        strip = slice(i * BS, (i + 1) * BS)
        filt = jnp.where(lane < BS, kept[0, i], kept[1, i]).astype(F32)
        total = filt * (mine[strip, :] + pair[other, strip, :])
        if final:
            refs[1][strip, :] = 3.0 * refs[0][strip, :] - 2.0 * total
        else:
            refs[0][strip, :] = total


def filtered(kept, halves, square=None):
    mine, other = halves
    pair = lax.all_gather(other, "xl", axis=0)
    args = [kept, mine, pair] + ([] if square is None else [square])
    return pl.pallas_call(
        functools.partial(filter_kernel, square is not None),
        out_shape=jax.ShapeDtypeStruct(mine.shape, F32),
        in_specs=[SM] + [VM] * (len(args) - 1),
        out_specs=VM,
        compiler_params=PARAMS,
    )(*args)


def shift(x, axis, step):
    n = SIZES[AXES.index(axis)]
    return lax.ppermute(x, axis, [(i, (i + step) % n) for i in range(n)])


def together(*xs):
    return lax.optimization_barrier(xs)


def chain(x, axis, step, count):
    out = []
    for _ in range(count):
        x = shift(x, axis, step)
        out.append(x)
    return out


def body(density, atom_sizes, pattern, kept):
    pattern = pattern.T
    masked = pl.pallas_call(
        mask_kernel,
        out_shape=jax.ShapeDtypeStruct(density.shape, F32),
        in_specs=[HB] * 3,
        out_specs=VM,
        scratch_shapes=[
            pltpu.SMEM(atom_sizes.shape, jnp.int32),
            pltpu.SMEM(pattern.shape, jnp.int32),
            pltpu.VMEM(density.shape, F32),
            pltpu.SemaphoreType.DMA((3,)),
        ],
        compiler_params=WHOLE,
    )(atom_sizes, pattern, density)

    left = lax.all_gather(masked, ("z", "c"), axis=0)

    near = lax.ppermute(masked, ("xh", "xl"), [(0, 0), (1, 2), (2, 1), (3, 3)])
    far = lax.ppermute(masked, ("xh", "xl"), [(1, 0), (2, 3), (0, 2), (3, 1)])
    near_up, near_down = chain(near, "y", 1, 4), chain(near, "y", -1, 3)
    far_up, far_down = chain(far, "y", 1, 3), chain(far, "y", -1, 4)
    offsets = [0, -1, 1, -2, 2, -3, 3, 4]
    near = [near] + [x for pair in zip(near_up, near_down) for x in pair] + [near_up[3]]
    far = [far] + [x for pair in zip(far_up, far_down) for x in pair] + [far_down[3]]
    right, give = pack(offsets, near, far)
    took = shift(give, "c", 1)
    mine, other, took = together(*first_product(left, right), took)
    square = filtered(kept.T, (mine, other))

    up, down = chain(square, "z", 1, 6), chain(square, "z", -1, 5)
    blocks = [(0, square)]
    for s in range(5):
        blocks += [(-s - 1, up[s]), (s + 1, down[s])]
    blocks.append((-6, up[5]))
    acc = second_product(right, took, blocks[:4])
    acc = second_product(right, took, blocks[4:8], acc)
    halves = join(*second_product(right, took, blocks[8:], acc, last=True))
    purified = filtered(kept.T, halves, square)
    return (square, purified)


def solution(mesh):
    fine = Mesh(mesh.devices.reshape(SIZES), AXES)
    placed = (P(ROW, COL), P(), P(ROW, COL), P(ROW, COL))
    return jax.shard_map(
        body,
        mesh=fine,
        in_specs=placed,
        out_specs=(P(ROW, COL), P(ROW, COL)),
        check_vma=False,
    )
```

time: 184 us -> 176 us (0.957)
  waiting for transfers between devices: 42.5 us -> 20.8 us
  Pallas kernels: 8.93 us -> 18 us
  blocking collectives: 15.2 us -> 22.8 us
  local copies, waits for them, and re-layouts: 5.68 us -> 0.93 us
  starting transfers between devices: 95.8 us -> 98.1 us
    ppermute x27 -> x26, waiting for transfers between devices: 28.8 us -> 16.1 us  [shift(): return lax.ppermute(x, axis, [(i, (i + step) % n) for i in range(n)])]
    all_gather x1, waiting for transfers between devices: 12.4 us -> 3.33 us  [body(): left = lax.all_gather(masked, ('z', 'c'), axis=0)]
    pallas_call x3 -> x6, Pallas kernels: 5.11 us -> 13.8 us  [the longest x3 6.82 us: second_product(): pl.pallas_call(functools.partial(second_kernel, offsets, acc is not None,...]
    all_gather x0 -> x1, blocking collectives: none -> 8.65 us  [join(): both = lax.all_gather(give, 'c', axis=0)]
    unnamed x20 -> x6, local copies, waits for them, and re-layouts: 5.66 us -> 0.93 us
    ppermute x27 -> x26, starting transfers between devices: 88.7 us -> 91 us  [shift(): return lax.ppermute(x, axis, [(i, (i + step) % n) for i in range(n)])]
  transfers between devices with their start and end apart: 30 -> 29, of which waited for: 11 -> 10; matrix products, arithmetic and copies ran while one was open for 1% -> 0% of each run, Pallas kernels for 1% -> 7%
where the time goes in v4:
time: 176 us; the launch traced here: 175 us
  starting transfers between devices  98.1 us (56%)
  blocking collectives  22.8 us (13%)
  waiting for transfers between devices  20.8 us (12%)
  Pallas kernels  18 us (10%)
  between operations  14.5 us (8%)
    ppermute x26, starting transfers between devices, shift(): return lax.ppermute(x, axis, [(i, (i + step) % n) for i in range(n)])  91 us
    ppermute x26, waiting for transfers between devices, shift(): return lax.ppermute(x, axis, [(i, (i + step) % n) for i in range(n)])  16.1 us
    all_gather x2, blocking collectives, filtered(): pair = lax.all_gather(other, 'xl', axis=0)  14.1 us
    all_gather x1, blocking collectives, join(): both = lax.all_gather(give, 'c', axis=0)  8.65 us
    pallas_call x3, Pallas kernels, second_product(): pl.pallas_call(functools.partial(second_kernel, offsets, acc is not None,...  6.82 us
    ppermute x1, starting transfers between devices, body(): far = lax.ppermute(masked, ('xh', 'xl'), [(1, 0), (2, 3), (0, 2), (3, 1)])  5.48 us
    pallas_call x1, Pallas kernels, first_product(): pl.pallas_call(first_kernel, out_shape=(block, block), in_specs=[HB, VM],...  5.42 us
  transfers between devices with their start and end apart: 29, of which 10 were waited for; matrix products, arithmetic and copies ran while one was open for 0% of the time, Pallas kernels for 7%

profile of v4, /device:TPU:1, one launch (start us, length us, event | category | flops | bytes accessed | tf_op | source)
XLA Modules:
  0.0 175.1 jit_solution(7050412412797136136)
XLA Ops:
  7.2 0.0 all-gather.6.cloned.1.call-start
  7.2 1.7 shard_map.59
  8.9 0.0 all-gather.6.cloned.1.call-update
  8.9 5.5 %collective-permute-start.8 = (f32[384,128]{1,0:T(8,128)}, f32[384,128]{1,0:T(8,128)S(1)}, u32[]{:S(2)}, u32[]{:S(2)}) collective-permute-start(f32[384,128]{1,0:T(8,128)} %shard_map.59), channel_id=1, source_target_pairs={{24,0},{384,408},{0,384},{408,24},{25,1},{385,409},{1,385},{409,25... | collective-permute-start | bytes 589832 | tf_op jit(solution)/shard_map/ppermute | solution.py:255
  14.4 1.6 collective-permute-start
  16.0 1.3 collective-permute-done.8.refs_8_
  17.3 6.1 %collective-permute-start.10 = (f32[384,128]{1,0:T(8,128)S(1)}, f32[384,128]{1,0:T(8,128)S(1)}, u32[]{:S(2)}, u32[]{:S(2)}) collective-permute-start(f32[384,128]{1,0:T(8,128)S(1)} %collective-permute-done.8.refs_8_), channel_id=1, source_target_pairs={{0,336},{48,0},{96,48},{144,96},{192,144},{240,192},{288,240},{336... | collective-permute-start | bytes 589832 | tf_op jit(solution)/shard_map/ppermute | solution.py:221
  23.4 1.9 %collective-permute-start.1 = (f32[384,128]{1,0:T(8,128)S(1)}, f32[384,128]{1,0:T(8,128)S(1)}, u32[]{:S(2)}, u32[]{:S(2)}) collective-permute-start(f32[384,128]{1,0:T(8,128)S(1)} %collective-permute-done.refs_0_), channel_id=1, source_target_pairs={{0,48},{48,96},{96,144},{144,192},{192,240},{240,288},{288,336},{3... | collective-permute-start | bytes 589832 | tf_op jit(solution)/shard_map/ppermute | solution.py:221
  25.3 1.9 %collective-permute-start.9 = (f32[384,128]{1,0:T(8,128)S(1)}, f32[384,128]{1,0:T(8,128)S(1)}, u32[]{:S(2)}, u32[]{:S(2)}) collective-permute-start(f32[384,128]{1,0:T(8,128)S(1)} %collective-permute-done.8.refs_8_), channel_id=1, source_target_pairs={{0,48},{48,96},{96,144},{144,192},{192,240},{240,288},{288,336},{3... | collective-permute-start | bytes 589832 | tf_op jit(solution)/shard_map/ppermute | solution.py:221
  27.3 4.6 %collective-permute-start.2 = (f32[384,128]{1,0:T(8,128)S(1)}, f32[384,128]{1,0:T(8,128)S(1)}, u32[]{:S(2)}, u32[]{:S(2)}) collective-permute-start(f32[384,128]{1,0:T(8,128)S(1)} %collective-permute-done.refs_0_), channel_id=1, source_target_pairs={{0,336},{48,0},{96,48},{144,96},{192,144},{240,192},{288,240},{336... | collective-permute-start | bytes 589832 | tf_op jit(solution)/shard_map/ppermute | solution.py:221
  31.8 3.4 %collective-permute-start.12 = (f32[384,128]{1,0:T(8,128)S(1)}, f32[384,128]{1,0:T(8,128)S(1)}, u32[]{:S(2)}, u32[]{:S(2)}) collective-permute-start(f32[384,128]{1,0:T(8,128)S(1)} %collective-permute-done.10.refs_10_), channel_id=1, source_target_pairs={{0,336},{48,0},{96,48},{144,96},{192,144},{240,192},{288,240},{336... | collective-permute-start | bytes 589832 | tf_op jit(solution)/shard_map/ppermute | solution.py:221
  35.2 0.0 collective-permute-done.1.refs_1_
  35.2 1.9 %collective-permute-start.3 = (f32[384,128]{1,0:T(8,128)S(1)}, f32[384,128]{1,0:T(8,128)S(1)}, u32[]{:S(2)}, u32[]{:S(2)}) collective-permute-start(f32[384,128]{1,0:T(8,128)S(1)} %collective-permute-done.1.refs_1_), channel_id=1, source_target_pairs={{0,48},{48,96},{96,144},{144,192},{192,240},{240,288},{288,336},{3... | collective-permute-start | bytes 589832 | tf_op jit(solution)/shard_map/ppermute | solution.py:221
  37.2 0.0 collective-permute-done.9.refs_9_
  37.2 1.9 %collective-permute-start.11 = (f32[384,128]{1,0:T(8,128)S(1)}, f32[384,128]{1,0:T(8,128)S(1)}, u32[]{:S(2)}, u32[]{:S(2)}) collective-permute-start(f32[384,128]{1,0:T(8,128)S(1)} %collective-permute-done.9.refs_9_), channel_id=1, source_target_pairs={{0,48},{48,96},{96,144},{144,192},{192,240},{240,288},{288,336},{3... | collective-permute-start | bytes 589832 | tf_op jit(solution)/shard_map/ppermute | solution.py:221
  39.1 4.6 %collective-permute-start.4 = (f32[384,128]{1,0:T(8,128)S(1)}, f32[384,128]{1,0:T(8,128)S(1)}, u32[]{:S(2)}, u32[]{:S(2)}) collective-permute-start(f32[384,128]{1,0:T(8,128)S(1)} %collective-permute-done.2.refs_2_), channel_id=1, source_target_pairs={{0,336},{48,0},{96,48},{144,96},{192,144},{240,192},{288,240},{336... | collective-permute-start | bytes 589832 | tf_op jit(solution)/shard_map/ppermute | solution.py:221
  43.7 0.0 collective-permute-done.12.refs_12_
  43.7 3.4 %collective-permute-start.14 = (f32[384,128]{1,0:T(8,128)S(1)}, f32[384,128]{1,0:T(8,128)S(1)}, u32[]{:S(2)}, u32[]{:S(2)}) collective-permute-start(f32[384,128]{1,0:T(8,128)S(1)} %collective-permute-done.12.refs_12_), channel_id=1, source_target_pairs={{0,336},{48,0},{96,48},{144,96},{192,144},{240,192},{288,240},{336... | collective-permute-start | bytes 589832 | tf_op jit(solution)/shard_map/ppermute | solution.py:221
  47.1 1.9 %collective-permute-start.5 = (f32[384,128]{1,0:T(8,128)S(1)}, f32[384,128]{1,0:T(8,128)S(1)}, u32[]{:S(2)}, u32[]{:S(2)}) collective-permute-start(f32[384,128]{1,0:T(8,128)S(1)} %collective-permute-done.3.refs_3_), channel_id=1, source_target_pairs={{0,48},{48,96},{96,144},{144,192},{192,240},{240,288},{288,336},{3... | collective-permute-start | bytes 589832 | tf_op jit(solution)/shard_map/ppermute | solution.py:221
  49.0 0.0 collective-permute-done.11.refs_11_
  49.0 1.9 %collective-permute-start.13 = (f32[384,128]{1,0:T(8,128)S(1)}, f32[384,128]{1,0:T(8,128)S(1)}, u32[]{:S(2)}, u32[]{:S(2)}) collective-permute-start(f32[384,128]{1,0:T(8,128)S(1)} %collective-permute-done.11.refs_11_), channel_id=1, source_target_pairs={{0,48},{48,96},{96,144},{144,192},{192,240},{240,288},{288,336},{3... | collective-permute-start | bytes 589832 | tf_op jit(solution)/shard_map/ppermute | solution.py:221
  50.9 0.0 collective-permute-done.4.refs_4_
  51.0 4.6 %collective-permute-start.6 = (f32[384,128]{1,0:T(8,128)S(1)}, f32[384,128]{1,0:T(8,128)S(1)}, u32[]{:S(2)}, u32[]{:S(2)}) collective-permute-start(f32[384,128]{1,0:T(8,128)S(1)} %collective-permute-done.4.refs_4_), channel_id=1, source_target_pairs={{0,336},{48,0},{96,48},{144,96},{192,144},{240,192},{288,240},{336... | collective-permute-start | bytes 589832 | tf_op jit(solution)/shard_map/ppermute | solution.py:221
  55.5 0.0 collective-permute-done.14.refs_14_
  55.5 3.4 %collective-permute-start.15 = (f32[384,128]{1,0:T(8,128)S(1)}, f32[384,128]{1,0:T(8,128)S(1)}, u32[]{:S(2)}, u32[]{:S(2)}) collective-permute-start(f32[384,128]{1,0:T(8,128)S(1)} %collective-permute-done.14.refs_14_), channel_id=1, source_target_pairs={{0,336},{48,0},{96,48},{144,96},{192,144},{240,192},{288,240},{336... | collective-permute-start | bytes 589832 | tf_op jit(solution)/shard_map/ppermute | solution.py:221
  58.9 0.0 collective-permute-done.5.refs_5_
  58.9 1.9 %collective-permute-start.7 = (f32[384,128]{1,0:T(8,128)S(1)}, f32[384,128]{1,0:T(8,128)S(1)}, u32[]{:S(2)}, u32[]{:S(2)}) collective-permute-start(f32[384,128]{1,0:T(8,128)S(1)} %collective-permute-done.5.refs_5_), channel_id=1, source_target_pairs={{0,48},{48,96},{96,144},{144,192},{192,240},{240,288},{288,336},{3... | collective-permute-start | bytes 589832 | tf_op jit(solution)/shard_map/ppermute | solution.py:221
  60.9 0.0 collective-permute-done.6.refs_6_
  60.9 1.6 collective-permute-done.15.refs_15_
  62.5 6.1 %collective-permute-done.7.refs_7_ = f32[384,128]{1,0:T(8,128)S(1)} collective-permute-done((f32[384,128]{1,0:T(8,128)S(1)}, f32[384,128]{1,0:T(8,128)S(1)}, u32[]{:S(2)}, u32[]{:S(2)}) %collective-permute-start.7) | collective-permute-done | bytes 196640 | tf_op jit(solution)/shard_map/ppermute | solution.py:221
  68.6 1.5 shard_map.60
  70.1 10.1 %collective-permute-start.16 = (f32[12,128,256]{2,1,0:T(8,128)}, f32[12,128,256]{2,1,0:T(8,128)}, u32[]{:S(2)}, u32[]{:S(2)}) collective-permute-start(f32[12,128,256]{2,1,0:T(8,128)} %get-tuple-element.16), channel_id=1, source_target_pairs={{0,1},{1,0},{2,3},{3,2},{4,5},{5,4},{6,7},{7,6},{8,9},{9,8},{10,11... | collective-permute-start | bytes 4718600 | tf_op jit(solution)/shard_map/ppermute | solution.py:221
  80.2 3.3 %all-gather.6.cloned.1.call-done = f32[9216,128]{1,0:T(8,128)} async-done(((f32[384,128]{1,0:T(8,128)}), f32[9216,128]{1,0:T(8,128)}) %all-gather.6.cloned.1.call-update) | async-done | bytes 4718608 | tf_op jit(solution)/shard_map/all_gather | solution.py:252
  83.6 5.4 %shard_map.61 = (f32[384,128]{1,0:T(8,128)S(1)}, f32[384,128]{1,0:T(8,128)S(1)}) custom-call(f32[24,384,128]{2,1,0:T(8,128)} %bitcast.11, f32[24,128,256]{2,1,0:T(8,128)S(1)} %get-tuple-element.13.right), custom_call_target="tpu_custom_call" | custom-call | flops 1811939328 | tf_op jit(solution)/shard_map/pallas_call | solution.py:120
  89.0 0.0 collective-permute-done.16.took
  89.0 7.3 %all-gather.1 = f32[768,128]{1,0:T(8,128)S(1)} all-gather(f32[384,128]{1,0:T(8,128)S(1)} %get-tuple-element.18), channel_id=3, replica_groups=mesh['xh'=2,'y'=8,'xl'=2,'z'=12,'c'=2] {'xl'}, dimensions={0}, use_global_device_ids=true | all-gather | bytes 589824 | tf_op jit(solution)/shard_map/all_gather | solution.py:208
  96.3 1.3 shard_map.62.refs_0_
  97.6 1.9 %collective-permute-start.21 = (f32[384,128]{1,0:T(8,128)}, f32[384,128]{1,0:T(8,128)S(1)}, u32[]{:S(2)}, u32[]{:S(2)}) collective-permute-start(f32[384,128]{1,0:T(8,128)} %shard_map.62.refs_0_), channel_id=1, source_target_pairs={{0,2},{2,4},{4,6},{6,8},{8,10},{10,12},{12,14},{14,16},{16,18},{18... | collective-permute-start | bytes 589832 | tf_op jit(solution)/shard_map/ppermute | solution.py:221
  99.5 7.8 %collective-permute-start.17 = (f32[384,128]{1,0:T(8,128)}, f32[384,128]{1,0:T(8,128)S(1)}, u32[]{:S(2)}, u32[]{:S(2)}) collective-permute-start(f32[384,128]{1,0:T(8,128)} %shard_map.62.refs_0_), channel_id=1, source_target_pairs={{0,22},{2,0},{4,2},{6,4},{8,6},{10,8},{12,10},{14,12},{16,14},{18,... | collective-permute-start | bytes 589832 | tf_op jit(solution)/shard_map/ppermute | solution.py:221
  107.4 3.0 %collective-permute-done.21.refs_1_ = f32[384,128]{1,0:T(8,128)S(1)} collective-permute-done((f32[384,128]{1,0:T(8,128)}, f32[384,128]{1,0:T(8,128)S(1)}, u32[]{:S(2)}, u32[]{:S(2)}) %collective-permute-start.21) | collective-permute-done | bytes 196640 | tf_op jit(solution)/shard_map/ppermute | solution.py:221
  110.3 1.9 %collective-permute-start.22 = (f32[384,128]{1,0:T(8,128)S(1)}, f32[384,128]{1,0:T(8,128)S(1)}, u32[]{:S(2)}, u32[]{:S(2)}) collective-permute-start(f32[384,128]{1,0:T(8,128)S(1)} %collective-permute-done.21.refs_1_), channel_id=1, source_target_pairs={{0,2},{2,4},{4,6},{6,8},{8,10},{10,12},{12,14},{14,16},{16,18},{18... | collective-permute-start | bytes 589832 | tf_op jit(solution)/shard_map/ppermute | solution.py:221
  112.3 4.6 %collective-permute-start.18 = (f32[384,128]{1,0:T(8,128)S(1)}, f32[384,128]{1,0:T(8,128)S(1)}, u32[]{:S(2)}, u32[]{:S(2)}) collective-permute-start(f32[384,128]{1,0:T(8,128)S(1)} %collective-permute-done.17.refs_2_), channel_id=1, source_target_pairs={{0,22},{2,0},{4,2},{6,4},{8,6},{10,8},{12,10},{14,12},{16,14},{18,... | collective-permute-start | bytes 589832 | tf_op jit(solution)/shard_map/ppermute | solution.py:221
  116.8 1.8 %collective-permute-done.22.refs_3_ = f32[384,128]{1,0:T(8,128)S(1)} collective-permute-done((f32[384,128]{1,0:T(8,128)S(1)}, f32[384,128]{1,0:T(8,128)S(1)}, u32[]{:S(2)}, u32[]{:S(2)}) %collective-permute-start.22) | collective-permute-done | bytes 196640 | tf_op jit(solution)/shard_map/ppermute | solution.py:221
  118.7 1.9 %collective-permute-start.23 = (f32[384,128]{1,0:T(8,128)S(1)}, f32[384,128]{1,0:T(8,128)S(1)}, u32[]{:S(2)}, u32[]{:S(2)}) collective-permute-start(f32[384,128]{1,0:T(8,128)S(1)} %collective-permute-done.22.refs_3_), channel_id=1, source_target_pairs={{0,2},{2,4},{4,6},{6,8},{8,10},{10,12},{12,14},{14,16},{16,18},{18... | collective-permute-start | bytes 589832 | tf_op jit(solution)/shard_map/ppermute | solution.py:221
  120.6 4.6 %collective-permute-start.19 = (f32[384,128]{1,0:T(8,128)S(1)}, f32[384,128]{1,0:T(8,128)S(1)}, u32[]{:S(2)}, u32[]{:S(2)}) collective-permute-start(f32[384,128]{1,0:T(8,128)S(1)} %collective-permute-done.18.refs_0_), channel_id=1, source_target_pairs={{0,22},{2,0},{4,2},{6,4},{8,6},{10,8},{12,10},{14,12},{16,14},{18,... | collective-permute-start | bytes 589832 | tf_op jit(solution)/shard_map/ppermute | solution.py:221
  125.2 1.1 collective-permute-done.23.refs_1_
  126.3 1.9 %collective-permute-start.24 = (f32[384,128]{1,0:T(8,128)S(1)}, f32[384,128]{1,0:T(8,128)S(1)}, u32[]{:S(2)}, u32[]{:S(2)}) collective-permute-start(f32[384,128]{1,0:T(8,128)S(1)} %collective-permute-done.23.refs_1_), channel_id=1, source_target_pairs={{0,2},{2,4},{4,6},{6,8},{8,10},{10,12},{12,14},{14,16},{16,18},{18... | collective-permute-start | bytes 589832 | tf_op jit(solution)/shard_map/ppermute | solution.py:221
  128.2 4.6 %collective-permute-start.20 = (f32[384,128]{1,0:T(8,128)S(1)}, f32[384,128]{1,0:T(8,128)S(1)}, u32[]{:S(2)}, u32[]{:S(2)}) collective-permute-start(f32[384,128]{1,0:T(8,128)S(1)} %collective-permute-done.19.refs_2_), channel_id=1, source_target_pairs={{0,22},{2,0},{4,2},{6,4},{8,6},{10,8},{12,10},{14,12},{16,14},{18,... | collective-permute-start | bytes 589832 | tf_op jit(solution)/shard_map/ppermute | solution.py:221
  132.8 1.1 collective-permute-done.24.refs_3_
  133.9 1.9 %collective-permute-start.25 = (f32[384,128]{1,0:T(8,128)S(1)}, f32[384,128]{1,0:T(8,128)S(1)}, u32[]{:S(2)}, u32[]{:S(2)}) collective-permute-start(f32[384,128]{1,0:T(8,128)S(1)} %collective-permute-done.24.refs_3_), channel_id=1, source_target_pairs={{0,2},{2,4},{4,6},{6,8},{8,10},{10,12},{12,14},{14,16},{16,18},{18... | collective-permute-start | bytes 589832 | tf_op jit(solution)/shard_map/ppermute | solution.py:221
  135.8 4.6 %collective-permute-start.26 = (f32[384,128]{1,0:T(8,128)S(1)}, f32[384,128]{1,0:T(8,128)S(1)}, u32[]{:S(2)}, u32[]{:S(2)}) collective-permute-start(f32[384,128]{1,0:T(8,128)S(1)} %collective-permute-done.20.refs_0_), channel_id=1, source_target_pairs={{0,22},{2,0},{4,2},{6,4},{8,6},{10,8},{12,10},{14,12},{16,14},{18,... | collective-permute-start | bytes 589832 | tf_op jit(solution)/shard_map/ppermute | solution.py:221
  140.4 1.1 collective-permute-done.25.refs_1_
  141.5 1.9 %collective-permute-start.27 = (f32[384,128]{1,0:T(8,128)S(1)}, f32[384,128]{1,0:T(8,128)S(1)}, u32[]{:S(2)}, u32[]{:S(2)}) collective-permute-start(f32[384,128]{1,0:T(8,128)S(1)} %collective-permute-done.25.refs_1_), channel_id=1, source_target_pairs={{0,2},{2,4},{4,6},{6,8},{8,10},{10,12},{12,14},{14,16},{16,18},{18... | collective-permute-start | bytes 589832 | tf_op jit(solution)/shard_map/ppermute | solution.py:221
  143.5 0.0 copy-start
  143.5 0.9 copy-done
  144.4 2.3 %shard_map.63.refs_4_ = f32[384,512]{1,0:T(8,128)S(1)} custom-call(f32[24,128,256]{2,1,0:T(8,128)S(1)} %get-tuple-element.13.right, f32[12,128,256]{2,1,0:T(8,128)} %collective-permute-done.16.took, f32[384,128]{1,0:T(8,128)S(1)} %copy-done, f32[384,128]{1,0:T(8,128)S(1)} %collective-permute-done.21.refs_1_, f32[384,128]{1,0:T(8,128)S(1)} %collective-permute-done.17.refs_2_, ...), custom_call_target="tpu_custom_call" | custom-call | flops 603979776 | tf_op jit(solution)/shard_map/pallas_call | solution.py:164
  146.7 2.3 %shard_map.64.refs_4_ = f32[384,512]{1,0:T(8,128)S(1)} custom-call(f32[24,128,256]{2,1,0:T(8,128)S(1)} %get-tuple-element.13.right, f32[12,128,256]{2,1,0:T(8,128)} %collective-permute-done.16.took, f32[384,128]{1,0:T(8,128)S(1)} %collective-permute-done.18.refs_0_, f32[384,128]{1,0:T(8,128)S(1)} %collective-permute-done.23.refs_1_, ...), custom_call_target="tpu_custom_call" | custom-call | flops 603979776 | tf_op jit(solution)/shard_map/pallas_call | solution.py:164
  148.9 0.0 copy-start.1
  149.0 0.2 collective-permute-done.27.refs_3_
  149.1 2.3 %shard_map.65 = (f32[384,256]{1,0:T(8,128)S(1)}, f32[384,256]{1,0:T(8,128)S(1)}) custom-call(f32[24,128,256]{2,1,0:T(8,128)S(1)} %get-tuple-element.13.right, f32[12,128,256]{2,1,0:T(8,128)} %collective-permute-done.16.took, f32[384,128]{1,0:T(8,128)S(1)} %collective-permute-done.20.refs_0_, f32[384,128]{1,0:T(8,128)S(1)} %collective-permute-done.25.refs_1_, ...), custom_call_target="tpu_custom_call" | custom-call | flops 603979776 | tf_op jit(solution)/shard_map/pallas_call | solution.py:164
  151.4 8.7 %all-gather.2 = f32[768,256]{1,0:T(8,128)S(1)} all-gather(f32[384,256]{1,0:T(8,128)S(1)} %get-tuple-element.21), channel_id=4, replica_groups=mesh['xh'=2,'y'=8,'xl'=2,'z'=12,'c'=2] {'c'}, dimensions={0}, use_global_device_ids=true | all-gather | bytes 1179648 | tf_op jit(solution)/shard_map/all_gather | solution.py:181
  160.1 0.1 shard_map.66
  160.1 6.8 %all-gather.3 = f32[768,128]{1,0:T(8,128)S(1)} all-gather(f32[384,128]{1,0:T(8,128)S(1)} %get-tuple-element.23), channel_id=5, replica_groups=mesh['xh'=2,'y'=8,'xl'=2,'z'=12,'c'=2] {'xl'}, dimensions={0}, use_global_device_ids=true | all-gather | bytes 589824 | tf_op jit(solution)/shard_map/all_gather | solution.py:208
  166.9 1.3 shard_map.67
  (13 shorter events, 0.0 us)
Async XLA Ops:
  7.2 76.4 %all-gather.6.cloned.1.call-start = ((), (), s32[]{:S(2)}) async-start(), calls=%async_computation | async-start | bytes 4915200 | tf_op jit(solution)/shard_map/all_gather | solution.py:252
  8.9 8.4 %collective-permute-start.8 = (f32[384,128]{1,0:T(8,128)}, f32[384,128]{1,0:T(8,128)S(1)}, u32[]{:S(2)}, u32[]{:S(2)}) collective-permute-start(f32[384,128]{1,0:T(8,128)} %shard_map.59), channel_id=1, source_target_pairs={{24,0},{384,408},{0,384},{408,24},{25,1},{385,409},{1,385},{409,25... | collective-permute-start | bytes 589832 | tf_op jit(solution)/shard_map/ppermute | solution.py:255
  14.4 9.0 %collective-permute-start = (f32[384,128]{1,0:T(8,128)}, f32[384,128]{1,0:T(8,128)S(1)}, u32[]{:S(2)}, u32[]{:S(2)}) collective-permute-start(f32[384,128]{1,0:T(8,128)} %shard_map.59), channel_id=1, source_target_pairs={{0,0},{24,384},{384,24},{408,408},{1,1},{25,385},{385,25},{409,409... | collective-permute-start | bytes 589832 | tf_op jit(solution)/shard_map/ppermute | solution.py:254
  17.3 14.5 %collective-permute-start.10 = (f32[384,128]{1,0:T(8,128)S(1)}, f32[384,128]{1,0:T(8,128)S(1)}, u32[]{:S(2)}, u32[]{:S(2)}) collective-permute-start(f32[384,128]{1,0:T(8,128)S(1)} %collective-permute-done.8.refs_8_), channel_id=1, source_target_pairs={{0,336},{48,0},{96,48},{144,96},{192,144},{240,192},{288,240},{336... | collective-permute-start | bytes 589832 | tf_op jit(solution)/shard_map/ppermute | solution.py:221
  23.4 11.8 %collective-permute-start.1 = (f32[384,128]{1,0:T(8,128)S(1)}, f32[384,128]{1,0:T(8,128)S(1)}, u32[]{:S(2)}, u32[]{:S(2)}) collective-permute-start(f32[384,128]{1,0:T(8,128)S(1)} %collective-permute-done.refs_0_), channel_id=1, source_target_pairs={{0,48},{48,96},{96,144},{144,192},{192,240},{240,288},{288,336},{3... | collective-permute-start | bytes 589832 | tf_op jit(solution)/shard_map/ppermute | solution.py:221
  25.3 11.8 %collective-permute-start.9 = (f32[384,128]{1,0:T(8,128)S(1)}, f32[384,128]{1,0:T(8,128)S(1)}, u32[]{:S(2)}, u32[]{:S(2)}) collective-permute-start(f32[384,128]{1,0:T(8,128)S(1)} %collective-permute-done.8.refs_8_), channel_id=1, source_target_pairs={{0,48},{48,96},{96,144},{144,192},{192,240},{240,288},{288,336},{3... | collective-permute-start | bytes 589832 | tf_op jit(solution)/shard_map/ppermute | solution.py:221
  27.3 11.8 %collective-permute-start.2 = (f32[384,128]{1,0:T(8,128)S(1)}, f32[384,128]{1,0:T(8,128)S(1)}, u32[]{:S(2)}, u32[]{:S(2)}) collective-permute-start(f32[384,128]{1,0:T(8,128)S(1)} %collective-permute-done.refs_0_), channel_id=1, source_target_pairs={{0,336},{48,0},{96,48},{144,96},{192,144},{240,192},{288,240},{336... | collective-permute-start | bytes 589832 | tf_op jit(solution)/shard_map/ppermute | solution.py:221
  31.8 11.8 %collective-permute-start.12 = (f32[384,128]{1,0:T(8,128)S(1)}, f32[384,128]{1,0:T(8,128)S(1)}, u32[]{:S(2)}, u32[]{:S(2)}) collective-permute-start(f32[384,128]{1,0:T(8,128)S(1)} %collective-permute-done.10.refs_10_), channel_id=1, source_target_pairs={{0,336},{48,0},{96,48},{144,96},{192,144},{240,192},{288,240},{336... | collective-permute-start | bytes 589832 | tf_op jit(solution)/shard_map/ppermute | solution.py:221
  35.2 11.8 %collective-permute-start.3 = (f32[384,128]{1,0:T(8,128)S(1)}, f32[384,128]{1,0:T(8,128)S(1)}, u32[]{:S(2)}, u32[]{:S(2)}) collective-permute-start(f32[384,128]{1,0:T(8,128)S(1)} %collective-permute-done.1.refs_1_), channel_id=1, source_target_pairs={{0,48},{48,96},{96,144},{144,192},{192,240},{240,288},{288,336},{3... | collective-permute-start | bytes 589832 | tf_op jit(solution)/shard_map/ppermute | solution.py:221
  37.2 11.8 %collective-permute-start.11 = (f32[384,128]{1,0:T(8,128)S(1)}, f32[384,128]{1,0:T(8,128)S(1)}, u32[]{:S(2)}, u32[]{:S(2)}) collective-permute-start(f32[384,128]{1,0:T(8,128)S(1)} %collective-permute-done.9.refs_9_), channel_id=1, source_target_pairs={{0,48},{48,96},{96,144},{144,192},{192,240},{240,288},{288,336},{3... | collective-permute-start | bytes 589832 | tf_op jit(solution)/shard_map/ppermute | solution.py:221
  39.1 11.8 %collective-permute-start.4 = (f32[384,128]{1,0:T(8,128)S(1)}, f32[384,128]{1,0:T(8,128)S(1)}, u32[]{:S(2)}, u32[]{:S(2)}) collective-permute-start(f32[384,128]{1,0:T(8,128)S(1)} %collective-permute-done.2.refs_2_), channel_id=1, source_target_pairs={{0,336},{48,0},{96,48},{144,96},{192,144},{240,192},{288,240},{336... | collective-permute-start | bytes 589832 | tf_op jit(solution)/shard_map/ppermute | solution.py:221
  43.7 11.8 %collective-permute-start.14 = (f32[384,128]{1,0:T(8,128)S(1)}, f32[384,128]{1,0:T(8,128)S(1)}, u32[]{:S(2)}, u32[]{:S(2)}) collective-permute-start(f32[384,128]{1,0:T(8,128)S(1)} %collective-permute-done.12.refs_12_), channel_id=1, source_target_pairs={{0,336},{48,0},{96,48},{144,96},{192,144},{240,192},{288,240},{336... | collective-permute-start | bytes 589832 | tf_op jit(solution)/shard_map/ppermute | solution.py:221
  47.1 11.8 %collective-permute-start.5 = (f32[384,128]{1,0:T(8,128)S(1)}, f32[384,128]{1,0:T(8,128)S(1)}, u32[]{:S(2)}, u32[]{:S(2)}) collective-permute-start(f32[384,128]{1,0:T(8,128)S(1)} %collective-permute-done.3.refs_3_), channel_id=1, source_target_pairs={{0,48},{48,96},{96,144},{144,192},{192,240},{240,288},{288,336},{3... | collective-permute-start | bytes 589832 | tf_op jit(solution)/shard_map/ppermute | solution.py:221
  49.0 11.8 %collective-permute-start.13 = (f32[384,128]{1,0:T(8,128)S(1)}, f32[384,128]{1,0:T(8,128)S(1)}, u32[]{:S(2)}, u32[]{:S(2)}) collective-permute-start(f32[384,128]{1,0:T(8,128)S(1)} %collective-permute-done.11.refs_11_), channel_id=1, source_target_pairs={{0,48},{48,96},{96,144},{144,192},{192,240},{240,288},{288,336},{3... | collective-permute-start | bytes 589832 | tf_op jit(solution)/shard_map/ppermute | solution.py:221
  51.0 9.9 %collective-permute-start.6 = (f32[384,128]{1,0:T(8,128)S(1)}, f32[384,128]{1,0:T(8,128)S(1)}, u32[]{:S(2)}, u32[]{:S(2)}) collective-permute-start(f32[384,128]{1,0:T(8,128)S(1)} %collective-permute-done.4.refs_4_), channel_id=1, source_target_pairs={{0,336},{48,0},{96,48},{144,96},{192,144},{240,192},{288,240},{336... | collective-permute-start | bytes 589832 | tf_op jit(solution)/shard_map/ppermute | solution.py:221
  55.5 6.9 %collective-permute-start.15 = (f32[384,128]{1,0:T(8,128)S(1)}, f32[384,128]{1,0:T(8,128)S(1)}, u32[]{:S(2)}, u32[]{:S(2)}) collective-permute-start(f32[384,128]{1,0:T(8,128)S(1)} %collective-permute-done.14.refs_14_), channel_id=1, source_target_pairs={{0,336},{48,0},{96,48},{144,96},{192,144},{240,192},{288,240},{336... | collective-permute-start | bytes 589832 | tf_op jit(solution)/shard_map/ppermute | solution.py:221
  58.9 9.7 %collective-permute-start.7 = (f32[384,128]{1,0:T(8,128)S(1)}, f32[384,128]{1,0:T(8,128)S(1)}, u32[]{:S(2)}, u32[]{:S(2)}) collective-permute-start(f32[384,128]{1,0:T(8,128)S(1)} %collective-permute-done.5.refs_5_), channel_id=1, source_target_pairs={{0,48},{48,96},{96,144},{144,192},{192,240},{240,288},{288,336},{3... | collective-permute-start | bytes 589832 | tf_op jit(solution)/shard_map/ppermute | solution.py:221
  70.1 18.9 %collective-permute-start.16 = (f32[12,128,256]{2,1,0:T(8,128)}, f32[12,128,256]{2,1,0:T(8,128)}, u32[]{:S(2)}, u32[]{:S(2)}) collective-permute-start(f32[12,128,256]{2,1,0:T(8,128)} %get-tuple-element.16), channel_id=1, source_target_pairs={{0,1},{1,0},{2,3},{3,2},{4,5},{5,4},{6,7},{7,6},{8,9},{9,8},{10,11... | collective-permute-start | bytes 4718600 | tf_op jit(solution)/shard_map/ppermute | solution.py:221
  83.6 12.8 %copy-start.2 = (s32[6,2]{0,1:T(2,128)S(1)}, s32[6,2]{0,1:T(2,128)}, u32[]{:S(2)}) copy-start(s32[6,2]{0,1:T(2,128)} %param.7) | copy-start | bytes 148
  97.6 12.8 %collective-permute-start.21 = (f32[384,128]{1,0:T(8,128)}, f32[384,128]{1,0:T(8,128)S(1)}, u32[]{:S(2)}, u32[]{:S(2)}) collective-permute-start(f32[384,128]{1,0:T(8,128)} %shard_map.62.refs_0_), channel_id=1, source_target_pairs={{0,2},{2,4},{4,6},{6,8},{8,10},{10,12},{12,14},{14,16},{16,18},{18... | collective-permute-start | bytes 589832 | tf_op jit(solution)/shard_map/ppermute | solution.py:221
  99.5 12.8 %collective-permute-start.17 = (f32[384,128]{1,0:T(8,128)}, f32[384,128]{1,0:T(8,128)S(1)}, u32[]{:S(2)}, u32[]{:S(2)}) collective-permute-start(f32[384,128]{1,0:T(8,128)} %shard_map.62.refs_0_), channel_id=1, source_target_pairs={{0,22},{2,0},{4,2},{6,4},{8,6},{10,8},{12,10},{14,12},{16,14},{18,... | collective-permute-start | bytes 589832 | tf_op jit(solution)/shard_map/ppermute | solution.py:221
  110.3 8.4 %collective-permute-start.22 = (f32[384,128]{1,0:T(8,128)S(1)}, f32[384,128]{1,0:T(8,128)S(1)}, u32[]{:S(2)}, u32[]{:S(2)}) collective-permute-start(f32[384,128]{1,0:T(8,128)S(1)} %collective-permute-done.21.refs_1_), channel_id=1, source_target_pairs={{0,2},{2,4},{4,6},{6,8},{8,10},{10,12},{12,14},{14,16},{16,18},{18... | collective-permute-start | bytes 589832 | tf_op jit(solution)/shard_map/ppermute | solution.py:221
  112.3 8.3 %collective-permute-start.18 = (f32[384,128]{1,0:T(8,128)S(1)}, f32[384,128]{1,0:T(8,128)S(1)}, u32[]{:S(2)}, u32[]{:S(2)}) collective-permute-start(f32[384,128]{1,0:T(8,128)S(1)} %collective-permute-done.17.refs_2_), channel_id=1, source_target_pairs={{0,22},{2,0},{4,2},{6,4},{8,6},{10,8},{12,10},{14,12},{16,14},{18,... | collective-permute-start | bytes 589832 | tf_op jit(solution)/shard_map/ppermute | solution.py:221
  118.7 7.6 %collective-permute-start.23 = (f32[384,128]{1,0:T(8,128)S(1)}, f32[384,128]{1,0:T(8,128)S(1)}, u32[]{:S(2)}, u32[]{:S(2)}) collective-permute-start(f32[384,128]{1,0:T(8,128)S(1)} %collective-permute-done.22.refs_3_), channel_id=1, source_target_pairs={{0,2},{2,4},{4,6},{6,8},{8,10},{10,12},{12,14},{14,16},{16,18},{18... | collective-permute-start | bytes 589832 | tf_op jit(solution)/shard_map/ppermute | solution.py:221
  120.6 7.6 %collective-permute-start.19 = (f32[384,128]{1,0:T(8,128)S(1)}, f32[384,128]{1,0:T(8,128)S(1)}, u32[]{:S(2)}, u32[]{:S(2)}) collective-permute-start(f32[384,128]{1,0:T(8,128)S(1)} %collective-permute-done.18.refs_0_), channel_id=1, source_target_pairs={{0,22},{2,0},{4,2},{6,4},{8,6},{10,8},{12,10},{14,12},{16,14},{18,... | collective-permute-start | bytes 589832 | tf_op jit(solution)/shard_map/ppermute | solution.py:221
  126.3 7.6 %collective-permute-start.24 = (f32[384,128]{1,0:T(8,128)S(1)}, f32[384,128]{1,0:T(8,128)S(1)}, u32[]{:S(2)}, u32[]{:S(2)}) collective-permute-start(f32[384,128]{1,0:T(8,128)S(1)} %collective-permute-done.23.refs_1_), channel_id=1, source_target_pairs={{0,2},{2,4},{4,6},{6,8},{8,10},{10,12},{12,14},{14,16},{16,18},{18... | collective-permute-start | bytes 589832 | tf_op jit(solution)/shard_map/ppermute | solution.py:221
  128.2 7.6 %collective-permute-start.20 = (f32[384,128]{1,0:T(8,128)S(1)}, f32[384,128]{1,0:T(8,128)S(1)}, u32[]{:S(2)}, u32[]{:S(2)}) collective-permute-start(f32[384,128]{1,0:T(8,128)S(1)} %collective-permute-done.19.refs_2_), channel_id=1, source_target_pairs={{0,22},{2,0},{4,2},{6,4},{8,6},{10,8},{12,10},{14,12},{16,14},{18,... | collective-permute-start | bytes 589832 | tf_op jit(solution)/shard_map/ppermute | solution.py:221
  133.9 7.6 %collective-permute-start.25 = (f32[384,128]{1,0:T(8,128)S(1)}, f32[384,128]{1,0:T(8,128)S(1)}, u32[]{:S(2)}, u32[]{:S(2)}) collective-permute-start(f32[384,128]{1,0:T(8,128)S(1)} %collective-permute-done.24.refs_3_), channel_id=1, source_target_pairs={{0,2},{2,4},{4,6},{6,8},{8,10},{10,12},{12,14},{14,16},{16,18},{18... | collective-permute-start | bytes 589832 | tf_op jit(solution)/shard_map/ppermute | solution.py:221
  135.8 13.1 %collective-permute-start.26 = (f32[384,128]{1,0:T(8,128)S(1)}, f32[384,128]{1,0:T(8,128)S(1)}, u32[]{:S(2)}, u32[]{:S(2)}) collective-permute-start(f32[384,128]{1,0:T(8,128)S(1)} %collective-permute-done.20.refs_0_), channel_id=1, source_target_pairs={{0,22},{2,0},{4,2},{6,4},{8,6},{10,8},{12,10},{14,12},{16,14},{18,... | collective-permute-start | bytes 589832 | tf_op jit(solution)/shard_map/ppermute | solution.py:221
  141.5 7.6 %collective-permute-start.27 = (f32[384,128]{1,0:T(8,128)S(1)}, f32[384,128]{1,0:T(8,128)S(1)}, u32[]{:S(2)}, u32[]{:S(2)}) collective-permute-start(f32[384,128]{1,0:T(8,128)S(1)} %collective-permute-done.25.refs_1_), channel_id=1, source_target_pairs={{0,2},{2,4},{4,6},{6,8},{8,10},{10,12},{12,14},{14,16},{16,18},{18... | collective-permute-start | bytes 589832 | tf_op jit(solution)/shard_map/ppermute | solution.py:221
  143.5 0.9 copy-start
  148.9 18.0 %copy-start.1 = (f32[384,128]{1,0:T(8,128)S(1)}, f32[384,128]{1,0:T(8,128)}, u32[]{:S(2)}) copy-start(f32[384,128]{1,0:T(8,128)} %shard_map.62.refs_0_) | copy-start | bytes 589828
Sparse Core Ops, SparseCore 0:
  11.0 72.5 all-gather.5

commit v5 on v4

--- a/solution.py
+++ b/solution.py
@@ -56,9 +56,8 @@
 dot = functools.partial(jnp.dot, preferred_element_type=F32)
 
 
-def split_dot(a, b):
+def split_dot(a, bh, bl):
     ah, al = split(a)
-    bh, bl = split(b)
     return dot(ah, bh) + (dot(ah, bl) + dot(al, bh))
 
 
@@ -72,79 +71,108 @@
 def pack_kernel(offsets, *refs):
     n = len(offsets)
     near, far = refs[:n], refs[n : 2 * n]
-    right, give = refs[2 * n :]
+    hi, lo, give = refs[2 * n :]
     y = lax.axis_index("y")
+    c = lax.axis_index("c")
     for k, off in enumerate(offsets):
         first = 3 * lax.rem(y + (off + NY), NY)
         for t in range(3):
             rows = slice(t * 128, (t + 1) * 128)
-            right[first + t, :, :128] = near[k][rows, :]
-            right[first + t, :, 128:] = far[k][rows, :]
-    c = lax.axis_index("c")
-    for z in range(NZ):
-        give[z] = right[2 * z + 1 - c]
+            unit = jnp.concatenate([near[k][rows, :], far[k][rows, :]], axis=1)
+            hi[first + t], lo[first + t] = split(unit)
+
+            @pl.when(lax.rem(first + t, 2) != c)
+            def _():
+                give[(first + t) // 2] = unit
 
 
 def pack(offsets, near, far):
     rows, cols = near[0].shape
     args = near + far
+    half = jax.ShapeDtypeStruct((2 * NZ, 128, 2 * cols), BF16)
     return pl.pallas_call(
         functools.partial(pack_kernel, tuple(offsets)),
-        out_shape=(
-            jax.ShapeDtypeStruct((2 * NZ, 128, 2 * cols), F32),
-            jax.ShapeDtypeStruct((NZ, 128, 2 * cols), F32),
-        ),
+        out_shape=(half, half, jax.ShapeDtypeStruct((NZ, 128, 2 * cols), F32)),
         in_specs=[VM] * len(args),
+        out_specs=(VM,) * 3,
+        compiler_params=PARAMS,
+    )(*args)
+
+
+def rows_kernel(hi, lo, took, rows_hi, rows_lo):
+    c = lax.axis_index("c")
+    for z in range(NZ):
+        rows_hi[z, :, :256] = hi[2 * z + c]
+        rows_lo[z, :, :256] = lo[2 * z + c]
+        rows_hi[z, :, 256:], rows_lo[z, :, 256:] = split(took[z])
+
+
+def phase_rows(hi, lo, took):
+    units, depth, cols = took.shape
+    half = jax.ShapeDtypeStruct((units, depth, 2 * cols), BF16)
+    return pl.pallas_call(
+        rows_kernel,
+        out_shape=(half, half),
+        in_specs=[VM] * 3,
         out_specs=(VM, VM),
         compiler_params=PARAMS,
-    )(*args)
-
-
-def first_kernel(left, right, mine, other, held, sems):
-    copies = [pltpu.make_async_copy(left.at[pl.ds(2 * z, 2)], held.at[z], sems.at[z]) for z in range(NZ)]
-    for copy in copies:
-        copy.start()
+    )(hi, lo, took)
+
+
+def first_kernel(left, hi, lo, mine, other, held, sems):
+    parts, per = held.shape[:2]
+    copies = [
+        pltpu.make_async_copy(left.at[pl.ds(per * p, per)], held.at[p], sems.at[p]) for p in range(parts)
+    ]
+    for p in range(3):
+        copies[p].start()
     acc = None
-    for z in range(NZ):
-        copies[z].wait()
-        a = jnp.concatenate([held[z, 0], held[z, 1]], axis=1)
-        b = jnp.concatenate([right[2 * z], right[2 * z + 1]], axis=0)
-        term = split_dot(a, b)
-        acc = term if acc is None else acc + term
+    for p in range(parts):
+        copies[p].wait()
+        if p + 3 < parts:
+            copies[p + 3].start()
+        for k in range(0, per, 2):
+            u = per * p + k
+            a = jnp.concatenate([held[p, k], held[p, k + 1]], axis=1)
+            bh = jnp.concatenate([hi[u], hi[u + 1]], axis=0)
+            bl = jnp.concatenate([lo[u], lo[u + 1]], axis=0)
+            term = split_dot(a, bh, bl)
+            acc = term if acc is None else acc + term
     put_halves(acc, mine, other)
 
 
-def first_product(left, right):
-    _, rows, cols = left.shape
+def first_product(left, hi, lo):
+    units, rows, cols = left.shape
+    parts = 6
     block = jax.ShapeDtypeStruct((rows, cols), F32)
     return pl.pallas_call(
         first_kernel,
         out_shape=(block, block),
-        in_specs=[HB, VM],
+        in_specs=[HB, VM, VM],
         out_specs=(VM, VM),
-        scratch_shapes=[pltpu.VMEM((NZ, 2, rows, cols), F32), pltpu.SemaphoreType.DMA((NZ,))],
+        scratch_shapes=[
+            pltpu.VMEM((parts, units // parts, rows, cols), F32),
+            pltpu.SemaphoreType.DMA((parts,)),
+        ],
         compiler_params=WIDE,
         cost_estimate=pl.CostEstimate(
             flops=NZ * 3 * 2 * rows * 2 * cols * 2 * cols, bytes_accessed=0, transcendentals=0
         ),
-    )(left, right)
-
-
-def second_kernel(offsets, has_acc, last, right, took, *refs):
+    )(left, hi, lo)
+
+
+def second_kernel(offsets, has_acc, last, hi, lo, *refs):
     n = len(offsets)
     acc = refs[n][...] if has_acc else None
     outs = refs[n + has_acc :]
     z = lax.axis_index("z")
-    c = lax.axis_index("c")
-
-    def rows(off):
-        zz = lax.rem(z + (off + NZ), NZ)
-        return jnp.concatenate([right[2 * zz + c], took[zz]], axis=1)
-
+    sign = 1 - 2 * lax.axis_index("c")
+    at = [lax.rem(z + sign * off + NZ, NZ) for off in offsets]
     for k in range(0, n, 2):
         a = jnp.concatenate([refs[k][...], refs[k + 1][...]], axis=1)
-        b = jnp.concatenate([rows(offsets[k]), rows(offsets[k + 1])], axis=0)
-        term = split_dot(a, b)
+        bh = jnp.concatenate([hi[at[k]], hi[at[k + 1]]], axis=0)
+        bl = jnp.concatenate([lo[at[k]], lo[at[k + 1]]], axis=0)
+        term = split_dot(a, bh, bl)
         acc = term if acc is None else acc + term
     if last:
         outs[0][...] = acc[:, :256]
@@ -153,10 +181,10 @@
         outs[0][...] = acc
 
 
-def second_product(right, took, blocks, acc=None, last=False):
+def second_product(operand, blocks, acc=None, last=False):
     offsets = tuple(off for off, _ in blocks)
     rows, cols = blocks[0][1].shape
-    args = [right, took] + [x for _, x in blocks] + ([] if acc is None else [acc])
+    args = list(operand) + [x for _, x in blocks] + ([] if acc is None else [acc])
     if last:
         shapes = (jax.ShapeDtypeStruct((rows, 2 * cols), F32),) * 2
     else:
@@ -229,6 +257,15 @@
     out = []
     for _ in range(count):
         x = shift(x, axis, step)
+        out.append(x)
+    return out
+
+
+def zchain(x, steps, count):
+    pairs = [(2 * z + c, 2 * ((z + steps[c]) % NZ) + c) for z in range(NZ) for c in range(2)]
+    out = []
+    for _ in range(count):
+        x = lax.ppermute(x, ("z", "c"), pairs)
         out.append(x)
     return out
 
@@ -258,19 +295,20 @@
     offsets = [0, -1, 1, -2, 2, -3, 3, 4]
     near = [near] + [x for pair in zip(near_up, near_down) for x in pair] + [near_up[3]]
     far = [far] + [x for pair in zip(far_up, far_down) for x in pair] + [far_down[3]]
-    right, give = pack(offsets, near, far)
+    hi, lo, give = pack(offsets, near, far)
     took = shift(give, "c", 1)
-    mine, other, took = together(*first_product(left, right), took)
+    mine, other, took = together(*first_product(left, hi, lo), took)
     square = filtered(kept.T, (mine, other))
 
-    up, down = chain(square, "z", 1, 6), chain(square, "z", -1, 5)
+    operand = phase_rows(hi, lo, took)
+    ahead, back = zchain(square, (1, -1), 6), zchain(square, (-1, 1), 5)
     blocks = [(0, square)]
     for s in range(5):
-        blocks += [(-s - 1, up[s]), (s + 1, down[s])]
-    blocks.append((-6, up[5]))
-    acc = second_product(right, took, blocks[:4])
-    acc = second_product(right, took, blocks[4:8], acc)
-    halves = join(*second_product(right, took, blocks[8:], acc, last=True))
+        blocks += [(-s - 1, ahead[s]), (s + 1, back[s])]
+    blocks.append((-6, ahead[5]))
+    acc = second_product(operand, blocks[:4])
+    acc = second_product(operand, blocks[4:8], acc)
+    halves = join(*second_product(operand, blocks[8:], acc, last=True))
     purified = filtered(kept.T, halves, square)
     return (square, purified)
 

time: 176 us -> 177 us (level)
  starting transfers between devices: 98.1 us -> 103 us
  Pallas kernels: 18 us -> 15.4 us
  blocking collectives: 22.8 us -> 24.6 us
    ppermute x0 -> x11, starting transfers between devices: none -> 42.2 us  [zchain(): x = lax.ppermute(x, ('z', 'c'), pairs)]
    ppermute x26 -> x15, starting transfers between devices: 91 us -> 53.4 us  [shift(): return lax.ppermute(x, axis, [(i, (i + step) % n) for i in range(n)])]
    ppermute x26 -> x15, waiting for transfers between devices: 16.1 us -> 7.76 us  [shift(): return lax.ppermute(x, axis, [(i, (i + step) % n) for i in range(n)])]
    ppermute x0 -> x11, waiting for transfers between devices: none -> 6.87 us  [zchain(): x = lax.ppermute(x, ('z', 'c'), pairs)]
    pallas_call x3, Pallas kernels: 6.82 us -> 2.4 us  [second_product(): pl.pallas_call(functools.partial(second_kernel, offsets, acc is not None,...]
    all_gather x1, blocking collectives: 8.65 us -> 10.5 us  [join(): both = lax.all_gather(give, 'c', axis=0)]
    pallas_call x1 -> x2, Pallas kernels: 5.42 us -> 6.92 us  [the longest x1 5.28 us: first_product(): pl.pallas_call(first_kernel, out_shape=(block, block), in_specs=[HB, VM,...]
  transfers between devices with their start and end apart: 29 -> 29, of which waited for: 10 -> 10; matrix products, arithmetic and copies ran while one was open for 0% -> 0% of each run, Pallas kernels for 7% -> 6%
where the time goes in v5:
time: 177 us; the launch traced here: 176 us
  starting transfers between devices  103 us (58%)
  blocking collectives  24.6 us (14%)
  waiting for transfers between devices  19.3 us (11%)
  Pallas kernels  15.4 us (9%)
  between operations  14.4 us (8%)
    ppermute x15, starting transfers between devices, shift(): return lax.ppermute(x, axis, [(i, (i + step) % n) for i in range(n)])  53.4 us
    ppermute x11, starting transfers between devices, zchain(): x = lax.ppermute(x, ('z', 'c'), pairs)  42.2 us
    all_gather x2, blocking collectives, filtered(): pair = lax.all_gather(other, 'xl', axis=0)  14.1 us
    all_gather x1, blocking collectives, join(): both = lax.all_gather(give, 'c', axis=0)  10.5 us
    ppermute x15, waiting for transfers between devices, shift(): return lax.ppermute(x, axis, [(i, (i + step) % n) for i in range(n)])  7.76 us
    ppermute x11, waiting for transfers between devices, zchain(): x = lax.ppermute(x, ('z', 'c'), pairs)  6.87 us
    ppermute x1, starting transfers between devices, body(): far = lax.ppermute(masked, ('xh', 'xl'), [(1, 0), (2, 3), (0, 2), (3, 1)])  5.48 us
    pallas_call x1, Pallas kernels, first_product(): pl.pallas_call(first_kernel, out_shape=(block, block), in_specs=[HB, VM,...  5.28 us
  transfers between devices with their start and end apart: 29, of which 10 were waited for; matrix products, arithmetic and copies ran while one was open for 0% of the time, Pallas kernels for 6%

profile of v5, /device:TPU:1, one launch (start us, length us, event | category | flops | bytes accessed | tf_op | source)
XLA Modules:
  0.0 176.5 jit_solution(14761665626235165027)
XLA Ops:
  7.2 0.0 all-gather.6.cloned.1.call-start
  7.2 1.7 shard_map.59
  8.9 0.0 all-gather.6.cloned.1.call-update
  8.9 5.5 %collective-permute-start.8 = (f32[384,128]{1,0:T(8,128)}, f32[384,128]{1,0:T(8,128)S(1)}, u32[]{:S(2)}, u32[]{:S(2)}) collective-permute-start(f32[384,128]{1,0:T(8,128)} %shard_map.59), channel_id=1, source_target_pairs={{24,0},{384,408},{0,384},{408,24},{25,1},{385,409},{1,385},{409,25... | collective-permute-start | bytes 589832 | tf_op jit(solution)/shard_map/ppermute | solution.py:292
  14.4 1.6 collective-permute-start
  16.0 1.3 collective-permute-done.8.refs_8_
  17.3 6.1 %collective-permute-start.10 = (f32[384,128]{1,0:T(8,128)S(1)}, f32[384,128]{1,0:T(8,128)S(1)}, u32[]{:S(2)}, u32[]{:S(2)}) collective-permute-start(f32[384,128]{1,0:T(8,128)S(1)} %collective-permute-done.8.refs_8_), channel_id=1, source_target_pairs={{0,336},{48,0},{96,48},{144,96},{192,144},{240,192},{288,240},{336... | collective-permute-start | bytes 589832 | tf_op jit(solution)/shard_map/ppermute | solution.py:249
  23.4 1.9 %collective-permute-start.1 = (f32[384,128]{1,0:T(8,128)S(1)}, f32[384,128]{1,0:T(8,128)S(1)}, u32[]{:S(2)}, u32[]{:S(2)}) collective-permute-start(f32[384,128]{1,0:T(8,128)S(1)} %collective-permute-done.refs_0_), channel_id=1, source_target_pairs={{0,48},{48,96},{96,144},{144,192},{192,240},{240,288},{288,336},{3... | collective-permute-start | bytes 589832 | tf_op jit(solution)/shard_map/ppermute | solution.py:249
  25.3 1.9 %collective-permute-start.9 = (f32[384,128]{1,0:T(8,128)S(1)}, f32[384,128]{1,0:T(8,128)S(1)}, u32[]{:S(2)}, u32[]{:S(2)}) collective-permute-start(f32[384,128]{1,0:T(8,128)S(1)} %collective-permute-done.8.refs_8_), channel_id=1, source_target_pairs={{0,48},{48,96},{96,144},{144,192},{192,240},{240,288},{288,336},{3... | collective-permute-start | bytes 589832 | tf_op jit(solution)/shard_map/ppermute | solution.py:249
  27.3 4.6 %collective-permute-start.2 = (f32[384,128]{1,0:T(8,128)S(1)}, f32[384,128]{1,0:T(8,128)S(1)}, u32[]{:S(2)}, u32[]{:S(2)}) collective-permute-start(f32[384,128]{1,0:T(8,128)S(1)} %collective-permute-done.refs_0_), channel_id=1, source_target_pairs={{0,336},{48,0},{96,48},{144,96},{192,144},{240,192},{288,240},{336... | collective-permute-start | bytes 589832 | tf_op jit(solution)/shard_map/ppermute | solution.py:249
  31.8 3.4 %collective-permute-start.12 = (f32[384,128]{1,0:T(8,128)S(1)}, f32[384,128]{1,0:T(8,128)S(1)}, u32[]{:S(2)}, u32[]{:S(2)}) collective-permute-start(f32[384,128]{1,0:T(8,128)S(1)} %collective-permute-done.10.refs_10_), channel_id=1, source_target_pairs={{0,336},{48,0},{96,48},{144,96},{192,144},{240,192},{288,240},{336... | collective-permute-start | bytes 589832 | tf_op jit(solution)/shard_map/ppermute | solution.py:249
  35.2 0.0 collective-permute-done.1.refs_1_
  35.2 1.9 %collective-permute-start.3 = (f32[384,128]{1,0:T(8,128)S(1)}, f32[384,128]{1,0:T(8,128)S(1)}, u32[]{:S(2)}, u32[]{:S(2)}) collective-permute-start(f32[384,128]{1,0:T(8,128)S(1)} %collective-permute-done.1.refs_1_), channel_id=1, source_target_pairs={{0,48},{48,96},{96,144},{144,192},{192,240},{240,288},{288,336},{3... | collective-permute-start | bytes 589832 | tf_op jit(solution)/shard_map/ppermute | solution.py:249
  37.2 0.0 collective-permute-done.9.refs_9_
  37.2 1.9 %collective-permute-start.11 = (f32[384,128]{1,0:T(8,128)S(1)}, f32[384,128]{1,0:T(8,128)S(1)}, u32[]{:S(2)}, u32[]{:S(2)}) collective-permute-start(f32[384,128]{1,0:T(8,128)S(1)} %collective-permute-done.9.refs_9_), channel_id=1, source_target_pairs={{0,48},{48,96},{96,144},{144,192},{192,240},{240,288},{288,336},{3... | collective-permute-start | bytes 589832 | tf_op jit(solution)/shard_map/ppermute | solution.py:249
  39.1 4.6 %collective-permute-start.4 = (f32[384,128]{1,0:T(8,128)S(1)}, f32[384,128]{1,0:T(8,128)S(1)}, u32[]{:S(2)}, u32[]{:S(2)}) collective-permute-start(f32[384,128]{1,0:T(8,128)S(1)} %collective-permute-done.2.refs_2_), channel_id=1, source_target_pairs={{0,336},{48,0},{96,48},{144,96},{192,144},{240,192},{288,240},{336... | collective-permute-start | bytes 589832 | tf_op jit(solution)/shard_map/ppermute | solution.py:249
  43.7 0.0 collective-permute-done.12.refs_12_
  43.7 3.4 %collective-permute-start.14 = (f32[384,128]{1,0:T(8,128)S(1)}, f32[384,128]{1,0:T(8,128)S(1)}, u32[]{:S(2)}, u32[]{:S(2)}) collective-permute-start(f32[384,128]{1,0:T(8,128)S(1)} %collective-permute-done.12.refs_12_), channel_id=1, source_target_pairs={{0,336},{48,0},{96,48},{144,96},{192,144},{240,192},{288,240},{336... | collective-permute-start | bytes 589832 | tf_op jit(solution)/shard_map/ppermute | solution.py:249
  47.1 1.9 %collective-permute-start.5 = (f32[384,128]{1,0:T(8,128)S(1)}, f32[384,128]{1,0:T(8,128)S(1)}, u32[]{:S(2)}, u32[]{:S(2)}) collective-permute-start(f32[384,128]{1,0:T(8,128)S(1)} %collective-permute-done.3.refs_3_), channel_id=1, source_target_pairs={{0,48},{48,96},{96,144},{144,192},{192,240},{240,288},{288,336},{3... | collective-permute-start | bytes 589832 | tf_op jit(solution)/shard_map/ppermute | solution.py:249
  49.0 0.0 collective-permute-done.11.refs_11_
  49.0 1.9 %collective-permute-start.13 = (f32[384,128]{1,0:T(8,128)S(1)}, f32[384,128]{1,0:T(8,128)S(1)}, u32[]{:S(2)}, u32[]{:S(2)}) collective-permute-start(f32[384,128]{1,0:T(8,128)S(1)} %collective-permute-done.11.refs_11_), channel_id=1, source_target_pairs={{0,48},{48,96},{96,144},{144,192},{192,240},{240,288},{288,336},{3... | collective-permute-start | bytes 589832 | tf_op jit(solution)/shard_map/ppermute | solution.py:249
  50.9 0.0 collective-permute-done.4.refs_4_
  51.0 4.6 %collective-permute-start.6 = (f32[384,128]{1,0:T(8,128)S(1)}, f32[384,128]{1,0:T(8,128)S(1)}, u32[]{:S(2)}, u32[]{:S(2)}) collective-permute-start(f32[384,128]{1,0:T(8,128)S(1)} %collective-permute-done.4.refs_4_), channel_id=1, source_target_pairs={{0,336},{48,0},{96,48},{144,96},{192,144},{240,192},{288,240},{336... | collective-permute-start | bytes 589832 | tf_op jit(solution)/shard_map/ppermute | solution.py:249
  55.5 0.0 collective-permute-done.14.refs_14_
  55.5 3.4 %collective-permute-start.15 = (f32[384,128]{1,0:T(8,128)S(1)}, f32[384,128]{1,0:T(8,128)S(1)}, u32[]{:S(2)}, u32[]{:S(2)}) collective-permute-start(f32[384,128]{1,0:T(8,128)S(1)} %collective-permute-done.14.refs_14_), channel_id=1, source_target_pairs={{0,336},{48,0},{96,48},{144,96},{192,144},{240,192},{288,240},{336... | collective-permute-start | bytes 589832 | tf_op jit(solution)/shard_map/ppermute | solution.py:249
  58.9 0.0 collective-permute-done.5.refs_5_
  58.9 1.9 %collective-permute-start.7 = (f32[384,128]{1,0:T(8,128)S(1)}, f32[384,128]{1,0:T(8,128)S(1)}, u32[]{:S(2)}, u32[]{:S(2)}) collective-permute-start(f32[384,128]{1,0:T(8,128)S(1)} %collective-permute-done.5.refs_5_), channel_id=1, source_target_pairs={{0,48},{48,96},{96,144},{144,192},{192,240},{240,288},{288,336},{3... | collective-permute-start | bytes 589832 | tf_op jit(solution)/shard_map/ppermute | solution.py:249
  60.9 0.0 collective-permute-done.6.refs_6_
  60.9 1.6 collective-permute-done.15.refs_15_
  62.5 6.1 %collective-permute-done.7.refs_7_ = f32[384,128]{1,0:T(8,128)S(1)} collective-permute-done((f32[384,128]{1,0:T(8,128)S(1)}, f32[384,128]{1,0:T(8,128)S(1)}, u32[]{:S(2)}, u32[]{:S(2)}) %collective-permute-start.7) | collective-permute-done | bytes 196640 | tf_op jit(solution)/shard_map/ppermute | solution.py:249
  68.6 1.8 %shard_map.60 = (bf16[24,128,256]{2,1,0:T(8,128)(2,1)S(1)}, bf16[24,128,256]{2,1,0:T(8,128)(2,1)S(1)}, f32[12,128,256]{2,1,0:T(8,128)}) custom-call(f32[384,128]{1,0:T(8,128)S(1)} %collective-permute-done.refs_0_, f32[384,128]{1,0:T(8,128)S(1)} %collective-permute-done.1.refs_1_, f32[384,128]{1,0:T(8,128)S(1)} %collective-permute-done.2.refs_2_, ...), custom_call_target="tpu_custom_call" | custom-call | tf_op jit(solution)/shard_map/pallas_call | solution.py:93
  70.4 10.1 %collective-permute-start.16 = (f32[12,128,256]{2,1,0:T(8,128)}, f32[12,128,256]{2,1,0:T(8,128)}, u32[]{:S(2)}, u32[]{:S(2)}) collective-permute-start(f32[12,128,256]{2,1,0:T(8,128)} %get-tuple-element.20), channel_id=1, source_target_pairs={{0,1},{1,0},{2,3},{3,2},{4,5},{5,4},{6,7},{7,6},{8,9},{9,8},{10,11... | collective-permute-start | bytes 4718600 | tf_op jit(solution)/shard_map/ppermute | solution.py:249
  80.5 3.3 %all-gather.6.cloned.1.call-done = f32[9216,128]{1,0:T(8,128)} async-done(((f32[384,128]{1,0:T(8,128)}), f32[9216,128]{1,0:T(8,128)}) %all-gather.6.cloned.1.call-update) | async-done | bytes 4718608 | tf_op jit(solution)/shard_map/all_gather | solution.py:289
  83.8 5.3 %shard_map.61 = (f32[384,128]{1,0:T(8,128)S(1)}, f32[384,128]{1,0:T(8,128)S(1)}) custom-call(f32[24,384,128]{2,1,0:T(8,128)} %bitcast.11, bf16[24,128,256]{2,1,0:T(8,128)(2,1)S(1)} %get-tuple-element.16.hi, bf16[24,128,256]{2,1,0:T(8,128)(2,1)S(1)} %get-tuple-element.17.lo), custom_call_target="tpu_custom_call" | custom-call | flops 1811939328 | tf_op jit(solution)/shard_map/pallas_call | solution.py:148
  89.1 0.0 collective-permute-done.16.took
  89.1 7.3 %all-gather.1 = f32[768,128]{1,0:T(8,128)S(1)} all-gather(f32[384,128]{1,0:T(8,128)S(1)} %get-tuple-element.22), channel_id=3, replica_groups=mesh['xh'=2,'y'=8,'xl'=2,'z'=12,'c'=2] {'xl'}, dimensions={0}, use_global_device_ids=true | all-gather | bytes 589824 | tf_op jit(solution)/shard_map/all_gather | solution.py:236
  96.5 1.3 shard_map.62.refs_0_
  97.7 8.0 %collective-permute-start.21 = (f32[384,128]{1,0:T(8,128)}, f32[384,128]{1,0:T(8,128)S(1)}, u32[]{:S(2)}, u32[]{:S(2)}) collective-permute-start(f32[384,128]{1,0:T(8,128)} %shard_map.62.refs_0_), channel_id=1, source_target_pairs={{0,2},{1,23},{2,4},{3,1},{4,6},{5,3},{6,8},{7,5},{8,10},{9,7},{10,... | collective-permute-start | bytes 589832 | tf_op jit(solution)/shard_map/ppermute | solution.py:268
  105.7 1.9 %collective-permute-start.17 = (f32[384,128]{1,0:T(8,128)}, f32[384,128]{1,0:T(8,128)S(1)}, u32[]{:S(2)}, u32[]{:S(2)}) collective-permute-start(f32[384,128]{1,0:T(8,128)} %shard_map.62.refs_0_), channel_id=1, source_target_pairs={{0,22},{1,3},{2,0},{3,5},{4,2},{5,7},{6,4},{7,9},{8,6},{9,11},{10,... | collective-permute-start | bytes 589832 | tf_op jit(solution)/shard_map/ppermute | solution.py:268
  107.6 1.0 collective-permute-done.21.refs_1_
  108.6 4.9 %collective-permute-start.22 = (f32[384,128]{1,0:T(8,128)S(1)}, f32[384,128]{1,0:T(8,128)S(1)}, u32[]{:S(2)}, u32[]{:S(2)}) collective-permute-start(f32[384,128]{1,0:T(8,128)S(1)} %collective-permute-done.21.refs_1_), channel_id=1, source_target_pairs={{0,2},{1,23},{2,4},{3,1},{4,6},{5,3},{6,8},{7,5},{8,10},{9,7},{10,... | collective-permute-start | bytes 589832 | tf_op jit(solution)/shard_map/ppermute | solution.py:268
  113.5 0.0 collective-permute-done.17.refs_2_
  113.5 1.9 %collective-permute-start.18 = (f32[384,128]{1,0:T(8,128)S(1)}, f32[384,128]{1,0:T(8,128)S(1)}, u32[]{:S(2)}, u32[]{:S(2)}) collective-permute-start(f32[384,128]{1,0:T(8,128)S(1)} %collective-permute-done.17.refs_2_), channel_id=1, source_target_pairs={{0,22},{1,3},{2,0},{3,5},{4,2},{5,7},{6,4},{7,9},{8,6},{9,11},{10,... | collective-permute-start | bytes 589832 | tf_op jit(solution)/shard_map/ppermute | solution.py:268
  115.5 0.7 collective-permute-done.22.refs_3_
  116.1 5.0 %collective-permute-start.23 = (f32[384,128]{1,0:T(8,128)S(1)}, f32[384,128]{1,0:T(8,128)S(1)}, u32[]{:S(2)}, u32[]{:S(2)}) collective-permute-start(f32[384,128]{1,0:T(8,128)S(1)} %collective-permute-done.22.refs_3_), channel_id=1, source_target_pairs={{0,2},{1,23},{2,4},{3,1},{4,6},{5,3},{6,8},{7,5},{8,10},{9,7},{10,... | collective-permute-start | bytes 589832 | tf_op jit(solution)/shard_map/ppermute | solution.py:268
  121.1 0.0 collective-permute-done.18.refs_0_
  121.2 1.9 %collective-permute-start.19 = (f32[384,128]{1,0:T(8,128)S(1)}, f32[384,128]{1,0:T(8,128)S(1)}, u32[]{:S(2)}, u32[]{:S(2)}) collective-permute-start(f32[384,128]{1,0:T(8,128)S(1)} %collective-permute-done.18.refs_0_), channel_id=1, source_target_pairs={{0,22},{1,3},{2,0},{3,5},{4,2},{5,7},{6,4},{7,9},{8,6},{9,11},{10,... | collective-permute-start | bytes 589832 | tf_op jit(solution)/shard_map/ppermute | solution.py:268
  123.1 0.7 collective-permute-done.23.refs_1_
  123.7 5.0 %collective-permute-start.24 = (f32[384,128]{1,0:T(8,128)S(1)}, f32[384,128]{1,0:T(8,128)S(1)}, u32[]{:S(2)}, u32[]{:S(2)}) collective-permute-start(f32[384,128]{1,0:T(8,128)S(1)} %collective-permute-done.23.refs_1_), channel_id=1, source_target_pairs={{0,2},{1,23},{2,4},{3,1},{4,6},{5,3},{6,8},{7,5},{8,10},{9,7},{10,... | collective-permute-start | bytes 589832 | tf_op jit(solution)/shard_map/ppermute | solution.py:268
  128.8 0.9 collective-permute-done.19.refs_2_
  129.7 1.9 %collective-permute-start.20 = (f32[384,128]{1,0:T(8,128)S(1)}, f32[384,128]{1,0:T(8,128)S(1)}, u32[]{:S(2)}, u32[]{:S(2)}) collective-permute-start(f32[384,128]{1,0:T(8,128)S(1)} %collective-permute-done.19.refs_2_), channel_id=1, source_target_pairs={{0,22},{1,3},{2,0},{3,5},{4,2},{5,7},{6,4},{7,9},{8,6},{9,11},{10,... | collective-permute-start | bytes 589832 | tf_op jit(solution)/shard_map/ppermute | solution.py:268
  131.6 4.9 %collective-permute-start.25 = (f32[384,128]{1,0:T(8,128)S(1)}, f32[384,128]{1,0:T(8,128)S(1)}, u32[]{:S(2)}, u32[]{:S(2)}) collective-permute-start(f32[384,128]{1,0:T(8,128)S(1)} %collective-permute-done.24.refs_3_), channel_id=1, source_target_pairs={{0,2},{1,23},{2,4},{3,1},{4,6},{5,3},{6,8},{7,5},{8,10},{9,7},{10,... | collective-permute-start | bytes 589832 | tf_op jit(solution)/shard_map/ppermute | solution.py:268
  136.5 3.1 %collective-permute-done.20.refs_0_ = f32[384,128]{1,0:T(8,128)S(1)} collective-permute-done((f32[384,128]{1,0:T(8,128)S(1)}, f32[384,128]{1,0:T(8,128)S(1)}, u32[]{:S(2)}, u32[]{:S(2)}) %collective-permute-start.20) | collective-permute-done | bytes 196640 | tf_op jit(solution)/shard_map/ppermute | solution.py:268
  139.5 1.9 %collective-permute-start.26 = (f32[384,128]{1,0:T(8,128)S(1)}, f32[384,128]{1,0:T(8,128)S(1)}, u32[]{:S(2)}, u32[]{:S(2)}) collective-permute-start(f32[384,128]{1,0:T(8,128)S(1)} %collective-permute-done.20.refs_0_), channel_id=1, source_target_pairs={{0,22},{1,3},{2,0},{3,5},{4,2},{5,7},{6,4},{7,9},{8,6},{9,11},{10,... | collective-permute-start | bytes 589832 | tf_op jit(solution)/shard_map/ppermute | solution.py:268
  141.4 4.9 %collective-permute-start.27 = (f32[384,128]{1,0:T(8,128)S(1)}, f32[384,128]{1,0:T(8,128)S(1)}, u32[]{:S(2)}, u32[]{:S(2)}) collective-permute-start(f32[384,128]{1,0:T(8,128)S(1)} %collective-permute-done.25.refs_1_), channel_id=1, source_target_pairs={{0,2},{1,23},{2,4},{3,1},{4,6},{5,3},{6,8},{7,5},{8,10},{9,7},{10,... | collective-permute-start | bytes 589832 | tf_op jit(solution)/shard_map/ppermute | solution.py:268
  146.3 1.6 shard_map.63
  148.0 0.8 shard_map.64.refs_4_
  148.8 0.8 shard_map.65.refs_4_
  149.6 0.6 collective-permute-done.27.refs_3_
  150.2 0.8 shard_map.66
  151.0 10.5 %all-gather.2 = f32[768,256]{1,0:T(8,128)S(1)} all-gather(f32[384,256]{1,0:T(8,128)S(1)} %get-tuple-element.27), channel_id=4, replica_groups=mesh['xh'=2,'y'=8,'xl'=2,'z'=12,'c'=2] {'c'}, dimensions={0}, use_global_device_ids=true | all-gather | bytes 1179648 | tf_op jit(solution)/shard_map/all_gather | solution.py:209
  161.5 0.1 shard_map.67
  161.5 6.8 %all-gather.3 = f32[768,128]{1,0:T(8,128)S(1)} all-gather(f32[384,128]{1,0:T(8,128)S(1)} %get-tuple-element.29), channel_id=5, replica_groups=mesh['xh'=2,'y'=8,'xl'=2,'z'=12,'c'=2] {'xl'}, dimensions={0}, use_global_device_ids=true | all-gather | bytes 589824 | tf_op jit(solution)/shard_map/all_gather | solution.py:236
  168.3 1.3 shard_map.68
  (12 shorter events, 0.0 us)
Async XLA Ops:
  7.2 76.7 %all-gather.6.cloned.1.call-start = ((), (), s32[]{:S(2)}) async-start(), calls=%async_computation | async-start | bytes 4915200 | tf_op jit(solution)/shard_map/all_gather | solution.py:289
  8.9 8.4 %collective-permute-start.8 = (f32[384,128]{1,0:T(8,128)}, f32[384,128]{1,0:T(8,128)S(1)}, u32[]{:S(2)}, u32[]{:S(2)}) collective-permute-start(f32[384,128]{1,0:T(8,128)} %shard_map.59), channel_id=1, source_target_pairs={{24,0},{384,408},{0,384},{408,24},{25,1},{385,409},{1,385},{409,25... | collective-permute-start | bytes 589832 | tf_op jit(solution)/shard_map/ppermute | solution.py:292
  14.4 9.0 %collective-permute-start = (f32[384,128]{1,0:T(8,128)}, f32[384,128]{1,0:T(8,128)S(1)}, u32[]{:S(2)}, u32[]{:S(2)}) collective-permute-start(f32[384,128]{1,0:T(8,128)} %shard_map.59), channel_id=1, source_target_pairs={{0,0},{24,384},{384,24},{408,408},{1,1},{25,385},{385,25},{409,409... | collective-permute-start | bytes 589832 | tf_op jit(solution)/shard_map/ppermute | solution.py:291
  17.3 14.5 %collective-permute-start.10 = (f32[384,128]{1,0:T(8,128)S(1)}, f32[384,128]{1,0:T(8,128)S(1)}, u32[]{:S(2)}, u32[]{:S(2)}) collective-permute-start(f32[384,128]{1,0:T(8,128)S(1)} %collective-permute-done.8.refs_8_), channel_id=1, source_target_pairs={{0,336},{48,0},{96,48},{144,96},{192,144},{240,192},{288,240},{336... | collective-permute-start | bytes 589832 | tf_op jit(solution)/shard_map/ppermute | solution.py:249
  23.4 11.8 %collective-permute-start.1 = (f32[384,128]{1,0:T(8,128)S(1)}, f32[384,128]{1,0:T(8,128)S(1)}, u32[]{:S(2)}, u32[]{:S(2)}) collective-permute-start(f32[384,128]{1,0:T(8,128)S(1)} %collective-permute-done.refs_0_), channel_id=1, source_target_pairs={{0,48},{48,96},{96,144},{144,192},{192,240},{240,288},{288,336},{3... | collective-permute-start | bytes 589832 | tf_op jit(solution)/shard_map/ppermute | solution.py:249
  25.3 11.8 %collective-permute-start.9 = (f32[384,128]{1,0:T(8,128)S(1)}, f32[384,128]{1,0:T(8,128)S(1)}, u32[]{:S(2)}, u32[]{:S(2)}) collective-permute-start(f32[384,128]{1,0:T(8,128)S(1)} %collective-permute-done.8.refs_8_), channel_id=1, source_target_pairs={{0,48},{48,96},{96,144},{144,192},{192,240},{240,288},{288,336},{3... | collective-permute-start | bytes 589832 | tf_op jit(solution)/shard_map/ppermute | solution.py:249
  27.3 11.8 %collective-permute-start.2 = (f32[384,128]{1,0:T(8,128)S(1)}, f32[384,128]{1,0:T(8,128)S(1)}, u32[]{:S(2)}, u32[]{:S(2)}) collective-permute-start(f32[384,128]{1,0:T(8,128)S(1)} %collective-permute-done.refs_0_), channel_id=1, source_target_pairs={{0,336},{48,0},{96,48},{144,96},{192,144},{240,192},{288,240},{336... | collective-permute-start | bytes 589832 | tf_op jit(solution)/shard_map/ppermute | solution.py:249
  31.8 11.8 %collective-permute-start.12 = (f32[384,128]{1,0:T(8,128)S(1)}, f32[384,128]{1,0:T(8,128)S(1)}, u32[]{:S(2)}, u32[]{:S(2)}) collective-permute-start(f32[384,128]{1,0:T(8,128)S(1)} %collective-permute-done.10.refs_10_), channel_id=1, source_target_pairs={{0,336},{48,0},{96,48},{144,96},{192,144},{240,192},{288,240},{336... | collective-permute-start | bytes 589832 | tf_op jit(solution)/shard_map/ppermute | solution.py:249
  35.2 11.8 %collective-permute-start.3 = (f32[384,128]{1,0:T(8,128)S(1)}, f32[384,128]{1,0:T(8,128)S(1)}, u32[]{:S(2)}, u32[]{:S(2)}) collective-permute-start(f32[384,128]{1,0:T(8,128)S(1)} %collective-permute-done.1.refs_1_), channel_id=1, source_target_pairs={{0,48},{48,96},{96,144},{144,192},{192,240},{240,288},{288,336},{3... | collective-permute-start | bytes 589832 | tf_op jit(solution)/shard_map/ppermute | solution.py:249
  37.2 11.8 %collective-permute-start.11 = (f32[384,128]{1,0:T(8,128)S(1)}, f32[384,128]{1,0:T(8,128)S(1)}, u32[]{:S(2)}, u32[]{:S(2)}) collective-permute-start(f32[384,128]{1,0:T(8,128)S(1)} %collective-permute-done.9.refs_9_), channel_id=1, source_target_pairs={{0,48},{48,96},{96,144},{144,192},{192,240},{240,288},{288,336},{3... | collective-permute-start | bytes 589832 | tf_op jit(solution)/shard_map/ppermute | solution.py:249
  39.1 11.8 %collective-permute-start.4 = (f32[384,128]{1,0:T(8,128)S(1)}, f32[384,128]{1,0:T(8,128)S(1)}, u32[]{:S(2)}, u32[]{:S(2)}) collective-permute-start(f32[384,128]{1,0:T(8,128)S(1)} %collective-permute-done.2.refs_2_), channel_id=1, source_target_pairs={{0,336},{48,0},{96,48},{144,96},{192,144},{240,192},{288,240},{336... | collective-permute-start | bytes 589832 | tf_op jit(solution)/shard_map/ppermute | solution.py:249
  43.7 11.8 %collective-permute-start.14 = (f32[384,128]{1,0:T(8,128)S(1)}, f32[384,128]{1,0:T(8,128)S(1)}, u32[]{:S(2)}, u32[]{:S(2)}) collective-permute-start(f32[384,128]{1,0:T(8,128)S(1)} %collective-permute-done.12.refs_12_), channel_id=1, source_target_pairs={{0,336},{48,0},{96,48},{144,96},{192,144},{240,192},{288,240},{336... | collective-permute-start | bytes 589832 | tf_op jit(solution)/shard_map/ppermute | solution.py:249
  47.1 11.8 %collective-permute-start.5 = (f32[384,128]{1,0:T(8,128)S(1)}, f32[384,128]{1,0:T(8,128)S(1)}, u32[]{:S(2)}, u32[]{:S(2)}) collective-permute-start(f32[384,128]{1,0:T(8,128)S(1)} %collective-permute-done.3.refs_3_), channel_id=1, source_target_pairs={{0,48},{48,96},{96,144},{144,192},{192,240},{240,288},{288,336},{3... | collective-permute-start | bytes 589832 | tf_op jit(solution)/shard_map/ppermute | solution.py:249
  49.0 11.8 %collective-permute-start.13 = (f32[384,128]{1,0:T(8,128)S(1)}, f32[384,128]{1,0:T(8,128)S(1)}, u32[]{:S(2)}, u32[]{:S(2)}) collective-permute-start(f32[384,128]{1,0:T(8,128)S(1)} %collective-permute-done.11.refs_11_), channel_id=1, source_target_pairs={{0,48},{48,96},{96,144},{144,192},{192,240},{240,288},{288,336},{3... | collective-permute-start | bytes 589832 | tf_op jit(solution)/shard_map/ppermute | solution.py:249
  51.0 9.9 %collective-permute-start.6 = (f32[384,128]{1,0:T(8,128)S(1)}, f32[384,128]{1,0:T(8,128)S(1)}, u32[]{:S(2)}, u32[]{:S(2)}) collective-permute-start(f32[384,128]{1,0:T(8,128)S(1)} %collective-permute-done.4.refs_4_), channel_id=1, source_target_pairs={{0,336},{48,0},{96,48},{144,96},{192,144},{240,192},{288,240},{336... | collective-permute-start | bytes 589832 | tf_op jit(solution)/shard_map/ppermute | solution.py:249
  55.5 6.9 %collective-permute-start.15 = (f32[384,128]{1,0:T(8,128)S(1)}, f32[384,128]{1,0:T(8,128)S(1)}, u32[]{:S(2)}, u32[]{:S(2)}) collective-permute-start(f32[384,128]{1,0:T(8,128)S(1)} %collective-permute-done.14.refs_14_), channel_id=1, source_target_pairs={{0,336},{48,0},{96,48},{144,96},{192,144},{240,192},{288,240},{336... | collective-permute-start | bytes 589832 | tf_op jit(solution)/shard_map/ppermute | solution.py:249
  58.9 9.7 %collective-permute-start.7 = (f32[384,128]{1,0:T(8,128)S(1)}, f32[384,128]{1,0:T(8,128)S(1)}, u32[]{:S(2)}, u32[]{:S(2)}) collective-permute-start(f32[384,128]{1,0:T(8,128)S(1)} %collective-permute-done.5.refs_5_), channel_id=1, source_target_pairs={{0,48},{48,96},{96,144},{144,192},{192,240},{240,288},{288,336},{3... | collective-permute-start | bytes 589832 | tf_op jit(solution)/shard_map/ppermute | solution.py:249
  70.4 18.7 %collective-permute-start.16 = (f32[12,128,256]{2,1,0:T(8,128)}, f32[12,128,256]{2,1,0:T(8,128)}, u32[]{:S(2)}, u32[]{:S(2)}) collective-permute-start(f32[12,128,256]{2,1,0:T(8,128)} %get-tuple-element.20), channel_id=1, source_target_pairs={{0,1},{1,0},{2,3},{3,2},{4,5},{5,4},{6,7},{7,6},{8,9},{9,8},{10,11... | collective-permute-start | bytes 4718600 | tf_op jit(solution)/shard_map/ppermute | solution.py:249
  83.8 12.6 %copy-start.1 = (s32[6,2]{0,1:T(2,128)S(1)}, s32[6,2]{0,1:T(2,128)}, u32[]{:S(2)}) copy-start(s32[6,2]{0,1:T(2,128)} %param.7) | copy-start | bytes 148
  97.7 50.2 %copy-start = (f32[384,128]{1,0:T(8,128)S(1)}, f32[384,128]{1,0:T(8,128)}, u32[]{:S(2)}) copy-start(f32[384,128]{1,0:T(8,128)} %shard_map.62.refs_0_) | copy-start | bytes 589828
  97.7 10.9 %collective-permute-start.21 = (f32[384,128]{1,0:T(8,128)}, f32[384,128]{1,0:T(8,128)S(1)}, u32[]{:S(2)}, u32[]{:S(2)}) collective-permute-start(f32[384,128]{1,0:T(8,128)} %shard_map.62.refs_0_), channel_id=1, source_target_pairs={{0,2},{1,23},{2,4},{3,1},{4,6},{5,3},{6,8},{7,5},{8,10},{9,7},{10,... | collective-permute-start | bytes 589832 | tf_op jit(solution)/shard_map/ppermute | solution.py:268
  105.7 7.8 %collective-permute-start.17 = (f32[384,128]{1,0:T(8,128)}, f32[384,128]{1,0:T(8,128)S(1)}, u32[]{:S(2)}, u32[]{:S(2)}) collective-permute-start(f32[384,128]{1,0:T(8,128)} %shard_map.62.refs_0_), channel_id=1, source_target_pairs={{0,22},{1,3},{2,0},{3,5},{4,2},{5,7},{6,4},{7,9},{8,6},{9,11},{10,... | collective-permute-start | bytes 589832 | tf_op jit(solution)/shard_map/ppermute | solution.py:268
  108.6 7.5 %collective-permute-start.22 = (f32[384,128]{1,0:T(8,128)S(1)}, f32[384,128]{1,0:T(8,128)S(1)}, u32[]{:S(2)}, u32[]{:S(2)}) collective-permute-start(f32[384,128]{1,0:T(8,128)S(1)} %collective-permute-done.21.refs_1_), channel_id=1, source_target_pairs={{0,2},{1,23},{2,4},{3,1},{4,6},{5,3},{6,8},{7,5},{8,10},{9,7},{10,... | collective-permute-start | bytes 589832 | tf_op jit(solution)/shard_map/ppermute | solution.py:268
  113.5 7.6 %collective-permute-start.18 = (f32[384,128]{1,0:T(8,128)S(1)}, f32[384,128]{1,0:T(8,128)S(1)}, u32[]{:S(2)}, u32[]{:S(2)}) collective-permute-start(f32[384,128]{1,0:T(8,128)S(1)} %collective-permute-done.17.refs_2_), channel_id=1, source_target_pairs={{0,22},{1,3},{2,0},{3,5},{4,2},{5,7},{6,4},{7,9},{8,6},{9,11},{10,... | collective-permute-start | bytes 589832 | tf_op jit(solution)/shard_map/ppermute | solution.py:268
  116.1 7.6 %collective-permute-start.23 = (f32[384,128]{1,0:T(8,128)S(1)}, f32[384,128]{1,0:T(8,128)S(1)}, u32[]{:S(2)}, u32[]{:S(2)}) collective-permute-start(f32[384,128]{1,0:T(8,128)S(1)} %collective-permute-done.22.refs_3_), channel_id=1, source_target_pairs={{0,2},{1,23},{2,4},{3,1},{4,6},{5,3},{6,8},{7,5},{8,10},{9,7},{10,... | collective-permute-start | bytes 589832 | tf_op jit(solution)/shard_map/ppermute | solution.py:268
  121.2 8.5 %collective-permute-start.19 = (f32[384,128]{1,0:T(8,128)S(1)}, f32[384,128]{1,0:T(8,128)S(1)}, u32[]{:S(2)}, u32[]{:S(2)}) collective-permute-start(f32[384,128]{1,0:T(8,128)S(1)} %collective-permute-done.18.refs_0_), channel_id=1, source_target_pairs={{0,22},{1,3},{2,0},{3,5},{4,2},{5,7},{6,4},{7,9},{8,6},{9,11},{10,... | collective-permute-start | bytes 589832 | tf_op jit(solution)/shard_map/ppermute | solution.py:268
  123.7 7.9 %collective-permute-start.24 = (f32[384,128]{1,0:T(8,128)S(1)}, f32[384,128]{1,0:T(8,128)S(1)}, u32[]{:S(2)}, u32[]{:S(2)}) collective-permute-start(f32[384,128]{1,0:T(8,128)S(1)} %collective-permute-done.23.refs_1_), channel_id=1, source_target_pairs={{0,2},{1,23},{2,4},{3,1},{4,6},{5,3},{6,8},{7,5},{8,10},{9,7},{10,... | collective-permute-start | bytes 589832 | tf_op jit(solution)/shard_map/ppermute | solution.py:268
  129.7 9.8 %collective-permute-start.20 = (f32[384,128]{1,0:T(8,128)S(1)}, f32[384,128]{1,0:T(8,128)S(1)}, u32[]{:S(2)}, u32[]{:S(2)}) collective-permute-start(f32[384,128]{1,0:T(8,128)S(1)} %collective-permute-done.19.refs_2_), channel_id=1, source_target_pairs={{0,22},{1,3},{2,0},{3,5},{4,2},{5,7},{6,4},{7,9},{8,6},{9,11},{10,... | collective-permute-start | bytes 589832 | tf_op jit(solution)/shard_map/ppermute | solution.py:268
  131.6 9.8 %collective-permute-start.25 = (f32[384,128]{1,0:T(8,128)S(1)}, f32[384,128]{1,0:T(8,128)S(1)}, u32[]{:S(2)}, u32[]{:S(2)}) collective-permute-start(f32[384,128]{1,0:T(8,128)S(1)} %collective-permute-done.24.refs_3_), channel_id=1, source_target_pairs={{0,2},{1,23},{2,4},{3,1},{4,6},{5,3},{6,8},{7,5},{8,10},{9,7},{10,... | collective-permute-start | bytes 589832 | tf_op jit(solution)/shard_map/ppermute | solution.py:268
  139.5 10.1 %collective-permute-start.26 = (f32[384,128]{1,0:T(8,128)S(1)}, f32[384,128]{1,0:T(8,128)S(1)}, u32[]{:S(2)}, u32[]{:S(2)}) collective-permute-start(f32[384,128]{1,0:T(8,128)S(1)} %collective-permute-done.20.refs_0_), channel_id=1, source_target_pairs={{0,22},{1,3},{2,0},{3,5},{4,2},{5,7},{6,4},{7,9},{8,6},{9,11},{10,... | collective-permute-start | bytes 589832 | tf_op jit(solution)/shard_map/ppermute | solution.py:268
  141.4 8.7 %collective-permute-start.27 = (f32[384,128]{1,0:T(8,128)S(1)}, f32[384,128]{1,0:T(8,128)S(1)}, u32[]{:S(2)}, u32[]{:S(2)}) collective-permute-start(f32[384,128]{1,0:T(8,128)S(1)} %collective-permute-done.25.refs_1_), channel_id=1, source_target_pairs={{0,2},{1,23},{2,4},{3,1},{4,6},{5,3},{6,8},{7,5},{8,10},{9,7},{10,... | collective-permute-start | bytes 589832 | tf_op jit(solution)/shard_map/ppermute | solution.py:268
Sparse Core Ops, SparseCore 0:
  11.0 72.7 all-gather.5

commit v6 on v5

--- a/solution.py
+++ b/solution.py
@@ -124,20 +124,19 @@
     copies = [
         pltpu.make_async_copy(left.at[pl.ds(per * p, per)], held.at[p], sems.at[p]) for p in range(parts)
     ]
-    for p in range(3):
-        copies[p].start()
+    for copy in copies:
+        copy.start()
+    for copy in copies:
+        copy.wait()
     acc = None
-    for p in range(parts):
-        copies[p].wait()
-        if p + 3 < parts:
-            copies[p + 3].start()
-        for k in range(0, per, 2):
-            u = per * p + k
-            a = jnp.concatenate([held[p, k], held[p, k + 1]], axis=1)
-            bh = jnp.concatenate([hi[u], hi[u + 1]], axis=0)
-            bl = jnp.concatenate([lo[u], lo[u + 1]], axis=0)
-            term = split_dot(a, bh, bl)
-            acc = term if acc is None else acc + term
+    for z in range(NZ):
+        u = 2 * z
+        p, k = divmod(u, per)
+        a = jnp.concatenate([held[p, k], held[p, k + 1]], axis=1)
+        bh = jnp.concatenate([hi[u], hi[u + 1]], axis=0)
+        bl = jnp.concatenate([lo[u], lo[u + 1]], axis=0)
+        term = split_dot(a, bh, bl)
+        acc = term if acc is None else acc + term
     put_halves(acc, mine, other)
 
 
@@ -166,8 +165,7 @@
     acc = refs[n][...] if has_acc else None
     outs = refs[n + has_acc :]
     z = lax.axis_index("z")
-    sign = 1 - 2 * lax.axis_index("c")
-    at = [lax.rem(z + sign * off + NZ, NZ) for off in offsets]
+    at = [lax.rem(z + (off + NZ), NZ) for off in offsets]
     for k in range(0, n, 2):
         a = jnp.concatenate([refs[k][...], refs[k + 1][...]], axis=1)
         bh = jnp.concatenate([hi[at[k]], hi[at[k + 1]]], axis=0)
@@ -226,20 +224,24 @@
         filt = jnp.where(lane < BS, kept[0, i], kept[1, i]).astype(F32)
         total = filt * (mine[strip, :] + pair[other, strip, :])
         if final:
-            refs[1][strip, :] = 3.0 * refs[0][strip, :] - 2.0 * total
+            square = refs[0][strip, :]
+            refs[1][strip, :] = square
+            refs[2][strip, :] = 3.0 * square - 2.0 * total
         else:
             refs[0][strip, :] = total
 
 
 def filtered(kept, halves, square=None):
     mine, other = halves
+    final = square is not None
     pair = lax.all_gather(other, "xl", axis=0)
-    args = [kept, mine, pair] + ([] if square is None else [square])
-    return pl.pallas_call(
-        functools.partial(filter_kernel, square is not None),
-        out_shape=jax.ShapeDtypeStruct(mine.shape, F32),
+    args = [kept, mine, pair] + ([square] if final else [])
+    block = jax.ShapeDtypeStruct(mine.shape, F32)
+    return pl.pallas_call(
+        functools.partial(filter_kernel, final),
+        out_shape=(block, block) if final else block,
         in_specs=[SM] + [VM] * (len(args) - 1),
-        out_specs=VM,
+        out_specs=(VM, VM) if final else VM,
         compiler_params=PARAMS,
     )(*args)
 
@@ -257,15 +259,6 @@
     out = []
     for _ in range(count):
         x = shift(x, axis, step)
-        out.append(x)
-    return out
-
-
-def zchain(x, steps, count):
-    pairs = [(2 * z + c, 2 * ((z + steps[c]) % NZ) + c) for z in range(NZ) for c in range(2)]
-    out = []
-    for _ in range(count):
-        x = lax.ppermute(x, ("z", "c"), pairs)
         out.append(x)
     return out
 
@@ -301,16 +294,15 @@
     square = filtered(kept.T, (mine, other))
 
     operand = phase_rows(hi, lo, took)
-    ahead, back = zchain(square, (1, -1), 6), zchain(square, (-1, 1), 5)
+    up, down = chain(square, "z", 1, 6), chain(square, "z", -1, 5)
     blocks = [(0, square)]
     for s in range(5):
-        blocks += [(-s - 1, ahead[s]), (s + 1, back[s])]
-    blocks.append((-6, ahead[5]))
+        blocks += [(-s - 1, up[s]), (s + 1, down[s])]
+    blocks.append((-6, up[5]))
     acc = second_product(operand, blocks[:4])
     acc = second_product(operand, blocks[4:8], acc)
     halves = join(*second_product(operand, blocks[8:], acc, last=True))
-    purified = filtered(kept.T, halves, square)
-    return (square, purified)
+    return filtered(kept.T, halves, square)
 
 
 def solution(mesh):

time: 177 us -> 173 us (0.977)
  starting transfers between devices: 103 us -> 98.1 us
  waiting for transfers between devices: 19.3 us -> 22.8 us
  blocking collectives: 24.6 us -> 22.8 us
    ppermute x11 -> x0, starting transfers between devices: 42.2 us -> none  [zchain(): x = lax.ppermute(x, ('z', 'c'), pairs)]
    ppermute x15 -> x26, starting transfers between devices: 53.4 us -> 91 us  [shift(): return lax.ppermute(x, axis, [(i, (i + step) % n) for i in range(n)])]
    ppermute x15 -> x26, waiting for transfers between devices: 7.76 us -> 18.1 us  [shift(): return lax.ppermute(x, axis, [(i, (i + step) % n) for i in range(n)])]
    ppermute x11 -> x0, waiting for transfers between devices: 6.87 us -> none  [zchain(): x = lax.ppermute(x, ('z', 'c'), pairs)]
    all_gather x1, blocking collectives: 10.5 us -> 8.65 us  [join(): both = lax.all_gather(give, 'c', axis=0)]
  transfers between devices with their start and end apart: 29 -> 29, of which waited for: 10 -> 10; matrix products, arithmetic and copies ran while one was open for 0% -> 0% of each run, Pallas kernels for 6% -> 5%
where the time goes in v6:
time: 173 us; the launch traced here: 172 us
  starting transfers between devices  98.1 us (57%)
  waiting for transfers between devices  22.8 us (13%)
  blocking collectives  22.8 us (13%)
  between operations  14.5 us (8%)
  Pallas kernels  13.9 us (8%)
    ppermute x26, starting transfers between devices, shift(): return lax.ppermute(x, axis, [(i, (i + step) % n) for i in range(n)])  91 us
    ppermute x26, waiting for transfers between devices, shift(): return lax.ppermute(x, axis, [(i, (i + step) % n) for i in range(n)])  18.1 us
    all_gather x2, blocking collectives, filtered(): pair = lax.all_gather(other, 'xl', axis=0)  14.1 us
    all_gather x1, blocking collectives, join(): both = lax.all_gather(give, 'c', axis=0)  8.65 us
    ppermute x1, starting transfers between devices, body(): far = lax.ppermute(masked, ('xh', 'xl'), [(1, 0), (2, 3), (0, 2), (3, 1)])  5.48 us
    pallas_call x1, Pallas kernels, first_product(): pl.pallas_call(first_kernel, out_shape=(block, block), in_specs=[HB, VM,...  4.38 us
  transfers between devices with their start and end apart: 29, of which 10 were waited for; matrix products, arithmetic and copies ran while one was open for 0% of the time, Pallas kernels for 5%

profile of v6, /device:TPU:1, one launch (start us, length us, event | category | flops | bytes accessed | tf_op | source)
XLA Modules:
  0.0 172.0 jit_solution(7735827739608806614)
XLA Ops:
  7.2 0.0 all-gather.6.cloned.1.call-start
  7.2 1.7 shard_map.59
  8.9 0.0 all-gather.6.cloned.1.call-update
  8.9 5.5 %collective-permute-start.8 = (f32[384,128]{1,0:T(8,128)}, f32[384,128]{1,0:T(8,128)S(1)}, u32[]{:S(2)}, u32[]{:S(2)}) collective-permute-start(f32[384,128]{1,0:T(8,128)} %shard_map.59), channel_id=1, source_target_pairs={{24,0},{384,408},{0,384},{408,24},{25,1},{385,409},{1,385},{409,25... | collective-permute-start | bytes 589832 | tf_op jit(solution)/shard_map/ppermute | solution.py:285
  14.4 1.6 collective-permute-start
  16.0 1.3 collective-permute-done.8.refs_8_
  17.3 6.1 %collective-permute-start.10 = (f32[384,128]{1,0:T(8,128)S(1)}, f32[384,128]{1,0:T(8,128)S(1)}, u32[]{:S(2)}, u32[]{:S(2)}) collective-permute-start(f32[384,128]{1,0:T(8,128)S(1)} %collective-permute-done.8.refs_8_), channel_id=1, source_target_pairs={{0,336},{48,0},{96,48},{144,96},{192,144},{240,192},{288,240},{336... | collective-permute-start | bytes 589832 | tf_op jit(solution)/shard_map/ppermute | solution.py:251
  23.4 1.9 %collective-permute-start.1 = (f32[384,128]{1,0:T(8,128)S(1)}, f32[384,128]{1,0:T(8,128)S(1)}, u32[]{:S(2)}, u32[]{:S(2)}) collective-permute-start(f32[384,128]{1,0:T(8,128)S(1)} %collective-permute-done.refs_0_), channel_id=1, source_target_pairs={{0,48},{48,96},{96,144},{144,192},{192,240},{240,288},{288,336},{3... | collective-permute-start | bytes 589832 | tf_op jit(solution)/shard_map/ppermute | solution.py:251
  25.3 1.9 %collective-permute-start.9 = (f32[384,128]{1,0:T(8,128)S(1)}, f32[384,128]{1,0:T(8,128)S(1)}, u32[]{:S(2)}, u32[]{:S(2)}) collective-permute-start(f32[384,128]{1,0:T(8,128)S(1)} %collective-permute-done.8.refs_8_), channel_id=1, source_target_pairs={{0,48},{48,96},{96,144},{144,192},{192,240},{240,288},{288,336},{3... | collective-permute-start | bytes 589832 | tf_op jit(solution)/shard_map/ppermute | solution.py:251
  27.3 4.6 %collective-permute-start.2 = (f32[384,128]{1,0:T(8,128)S(1)}, f32[384,128]{1,0:T(8,128)S(1)}, u32[]{:S(2)}, u32[]{:S(2)}) collective-permute-start(f32[384,128]{1,0:T(8,128)S(1)} %collective-permute-done.refs_0_), channel_id=1, source_target_pairs={{0,336},{48,0},{96,48},{144,96},{192,144},{240,192},{288,240},{336... | collective-permute-start | bytes 589832 | tf_op jit(solution)/shard_map/ppermute | solution.py:251
  31.8 3.4 %collective-permute-start.12 = (f32[384,128]{1,0:T(8,128)S(1)}, f32[384,128]{1,0:T(8,128)S(1)}, u32[]{:S(2)}, u32[]{:S(2)}) collective-permute-start(f32[384,128]{1,0:T(8,128)S(1)} %collective-permute-done.10.refs_10_), channel_id=1, source_target_pairs={{0,336},{48,0},{96,48},{144,96},{192,144},{240,192},{288,240},{336... | collective-permute-start | bytes 589832 | tf_op jit(solution)/shard_map/ppermute | solution.py:251
  35.2 0.0 collective-permute-done.1.refs_1_
  35.2 1.9 %collective-permute-start.3 = (f32[384,128]{1,0:T(8,128)S(1)}, f32[384,128]{1,0:T(8,128)S(1)}, u32[]{:S(2)}, u32[]{:S(2)}) collective-permute-start(f32[384,128]{1,0:T(8,128)S(1)} %collective-permute-done.1.refs_1_), channel_id=1, source_target_pairs={{0,48},{48,96},{96,144},{144,192},{192,240},{240,288},{288,336},{3... | collective-permute-start | bytes 589832 | tf_op jit(solution)/shard_map/ppermute | solution.py:251
  37.2 0.0 collective-permute-done.9.refs_9_
  37.2 1.9 %collective-permute-start.11 = (f32[384,128]{1,0:T(8,128)S(1)}, f32[384,128]{1,0:T(8,128)S(1)}, u32[]{:S(2)}, u32[]{:S(2)}) collective-permute-start(f32[384,128]{1,0:T(8,128)S(1)} %collective-permute-done.9.refs_9_), channel_id=1, source_target_pairs={{0,48},{48,96},{96,144},{144,192},{192,240},{240,288},{288,336},{3... | collective-permute-start | bytes 589832 | tf_op jit(solution)/shard_map/ppermute | solution.py:251
  39.1 4.6 %collective-permute-start.4 = (f32[384,128]{1,0:T(8,128)S(1)}, f32[384,128]{1,0:T(8,128)S(1)}, u32[]{:S(2)}, u32[]{:S(2)}) collective-permute-start(f32[384,128]{1,0:T(8,128)S(1)} %collective-permute-done.2.refs_2_), channel_id=1, source_target_pairs={{0,336},{48,0},{96,48},{144,96},{192,144},{240,192},{288,240},{336... | collective-permute-start | bytes 589832 | tf_op jit(solution)/shard_map/ppermute | solution.py:251
  43.7 0.0 collective-permute-done.12.refs_12_
  43.7 3.4 %collective-permute-start.14 = (f32[384,128]{1,0:T(8,128)S(1)}, f32[384,128]{1,0:T(8,128)S(1)}, u32[]{:S(2)}, u32[]{:S(2)}) collective-permute-start(f32[384,128]{1,0:T(8,128)S(1)} %collective-permute-done.12.refs_12_), channel_id=1, source_target_pairs={{0,336},{48,0},{96,48},{144,96},{192,144},{240,192},{288,240},{336... | collective-permute-start | bytes 589832 | tf_op jit(solution)/shard_map/ppermute | solution.py:251
  47.1 1.9 %collective-permute-start.5 = (f32[384,128]{1,0:T(8,128)S(1)}, f32[384,128]{1,0:T(8,128)S(1)}, u32[]{:S(2)}, u32[]{:S(2)}) collective-permute-start(f32[384,128]{1,0:T(8,128)S(1)} %collective-permute-done.3.refs_3_), channel_id=1, source_target_pairs={{0,48},{48,96},{96,144},{144,192},{192,240},{240,288},{288,336},{3... | collective-permute-start | bytes 589832 | tf_op jit(solution)/shard_map/ppermute | solution.py:251
  49.0 0.0 collective-permute-done.11.refs_11_
  49.0 1.9 %collective-permute-start.13 = (f32[384,128]{1,0:T(8,128)S(1)}, f32[384,128]{1,0:T(8,128)S(1)}, u32[]{:S(2)}, u32[]{:S(2)}) collective-permute-start(f32[384,128]{1,0:T(8,128)S(1)} %collective-permute-done.11.refs_11_), channel_id=1, source_target_pairs={{0,48},{48,96},{96,144},{144,192},{192,240},{240,288},{288,336},{3... | collective-permute-start | bytes 589832 | tf_op jit(solution)/shard_map/ppermute | solution.py:251
  50.9 0.0 collective-permute-done.4.refs_4_
  51.0 4.6 %collective-permute-start.6 = (f32[384,128]{1,0:T(8,128)S(1)}, f32[384,128]{1,0:T(8,128)S(1)}, u32[]{:S(2)}, u32[]{:S(2)}) collective-permute-start(f32[384,128]{1,0:T(8,128)S(1)} %collective-permute-done.4.refs_4_), channel_id=1, source_target_pairs={{0,336},{48,0},{96,48},{144,96},{192,144},{240,192},{288,240},{336... | collective-permute-start | bytes 589832 | tf_op jit(solution)/shard_map/ppermute | solution.py:251
  55.5 0.0 collective-permute-done.14.refs_14_
  55.5 3.4 %collective-permute-start.15 = (f32[384,128]{1,0:T(8,128)S(1)}, f32[384,128]{1,0:T(8,128)S(1)}, u32[]{:S(2)}, u32[]{:S(2)}) collective-permute-start(f32[384,128]{1,0:T(8,128)S(1)} %collective-permute-done.14.refs_14_), channel_id=1, source_target_pairs={{0,336},{48,0},{96,48},{144,96},{192,144},{240,192},{288,240},{336... | collective-permute-start | bytes 589832 | tf_op jit(solution)/shard_map/ppermute | solution.py:251
  58.9 0.0 collective-permute-done.5.refs_5_
  58.9 1.9 %collective-permute-start.7 = (f32[384,128]{1,0:T(8,128)S(1)}, f32[384,128]{1,0:T(8,128)S(1)}, u32[]{:S(2)}, u32[]{:S(2)}) collective-permute-start(f32[384,128]{1,0:T(8,128)S(1)} %collective-permute-done.5.refs_5_), channel_id=1, source_target_pairs={{0,48},{48,96},{96,144},{144,192},{192,240},{240,288},{288,336},{3... | collective-permute-start | bytes 589832 | tf_op jit(solution)/shard_map/ppermute | solution.py:251
  60.9 0.0 collective-permute-done.6.refs_6_
  60.9 1.6 collective-permute-done.15.refs_15_
  62.5 6.1 %collective-permute-done.7.refs_7_ = f32[384,128]{1,0:T(8,128)S(1)} collective-permute-done((f32[384,128]{1,0:T(8,128)S(1)}, f32[384,128]{1,0:T(8,128)S(1)}, u32[]{:S(2)}, u32[]{:S(2)}) %collective-permute-start.7) | collective-permute-done | bytes 196640 | tf_op jit(solution)/shard_map/ppermute | solution.py:251
  68.6 1.8 %shard_map.60 = (bf16[24,128,256]{2,1,0:T(8,128)(2,1)S(1)}, bf16[24,128,256]{2,1,0:T(8,128)(2,1)S(1)}, f32[12,128,256]{2,1,0:T(8,128)}) custom-call(f32[384,128]{1,0:T(8,128)S(1)} %collective-permute-done.refs_0_, f32[384,128]{1,0:T(8,128)S(1)} %collective-permute-done.1.refs_1_, f32[384,128]{1,0:T(8,128)S(1)} %collective-permute-done.2.refs_2_, ...), custom_call_target="tpu_custom_call" | custom-call | tf_op jit(solution)/shard_map/pallas_call | solution.py:93
  70.4 10.1 %collective-permute-start.16 = (f32[12,128,256]{2,1,0:T(8,128)}, f32[12,128,256]{2,1,0:T(8,128)}, u32[]{:S(2)}, u32[]{:S(2)}) collective-permute-start(f32[12,128,256]{2,1,0:T(8,128)} %get-tuple-element.20), channel_id=1, source_target_pairs={{0,1},{1,0},{2,3},{3,2},{4,5},{5,4},{6,7},{7,6},{8,9},{9,8},{10,11... | collective-permute-start | bytes 4718600 | tf_op jit(solution)/shard_map/ppermute | solution.py:251
  80.5 3.3 %all-gather.6.cloned.1.call-done = f32[9216,128]{1,0:T(8,128)} async-done(((f32[384,128]{1,0:T(8,128)}), f32[9216,128]{1,0:T(8,128)}) %all-gather.6.cloned.1.call-update) | async-done | bytes 4718608 | tf_op jit(solution)/shard_map/all_gather | solution.py:282
  83.8 4.4 %shard_map.61 = (f32[384,128]{1,0:T(8,128)S(1)}, f32[384,128]{1,0:T(8,128)S(1)}) custom-call(f32[24,384,128]{2,1,0:T(8,128)} %bitcast.11, bf16[24,128,256]{2,1,0:T(8,128)(2,1)S(1)} %get-tuple-element.16.hi, bf16[24,128,256]{2,1,0:T(8,128)(2,1)S(1)} %get-tuple-element.17.lo), custom_call_target="tpu_custom_call" | custom-call | flops 1811939328 | tf_op jit(solution)/shard_map/pallas_call | solution.py:147
  88.2 0.0 collective-permute-done.16.took
  88.2 7.3 %all-gather.1 = f32[768,128]{1,0:T(8,128)S(1)} all-gather(f32[384,128]{1,0:T(8,128)S(1)} %get-tuple-element.25), channel_id=3, replica_groups=mesh['xh'=2,'y'=8,'xl'=2,'z'=12,'c'=2] {'xl'}, dimensions={0}, use_global_device_ids=true | all-gather | bytes 589824 | tf_op jit(solution)/shard_map/all_gather | solution.py:237
  95.6 0.6 shard_map.63.refs_0_
  96.2 1.9 %collective-permute-start.21 = (f32[384,128]{1,0:T(8,128)S(1)}, f32[384,128]{1,0:T(8,128)S(1)}, u32[]{:S(2)}, u32[]{:S(2)}) collective-permute-start(f32[384,128]{1,0:T(8,128)S(1)} %shard_map.63.refs_0_), channel_id=1, source_target_pairs={{0,2},{2,4},{4,6},{6,8},{8,10},{10,12},{12,14},{14,16},{16,18},{18... | collective-permute-start | bytes 589832 | tf_op jit(solution)/shard_map/ppermute | solution.py:251
  98.1 7.8 %collective-permute-start.17 = (f32[384,128]{1,0:T(8,128)S(1)}, f32[384,128]{1,0:T(8,128)S(1)}, u32[]{:S(2)}, u32[]{:S(2)}) collective-permute-start(f32[384,128]{1,0:T(8,128)S(1)} %shard_map.63.refs_0_), channel_id=1, source_target_pairs={{0,22},{2,0},{4,2},{6,4},{8,6},{10,8},{12,10},{14,12},{16,14},{18,... | collective-permute-start | bytes 589832 | tf_op jit(solution)/shard_map/ppermute | solution.py:251
  105.9 2.8 %collective-permute-done.21.refs_1_ = f32[384,128]{1,0:T(8,128)S(1)} collective-permute-done((f32[384,128]{1,0:T(8,128)S(1)}, f32[384,128]{1,0:T(8,128)S(1)}, u32[]{:S(2)}, u32[]{:S(2)}) %collective-permute-start.21) | collective-permute-done | bytes 196640 | tf_op jit(solution)/shard_map/ppermute | solution.py:251
  108.7 1.9 %collective-permute-start.22 = (f32[384,128]{1,0:T(8,128)S(1)}, f32[384,128]{1,0:T(8,128)S(1)}, u32[]{:S(2)}, u32[]{:S(2)}) collective-permute-start(f32[384,128]{1,0:T(8,128)S(1)} %collective-permute-done.21.refs_1_), channel_id=1, source_target_pairs={{0,2},{2,4},{4,6},{6,8},{8,10},{10,12},{12,14},{14,16},{16,18},{18... | collective-permute-start | bytes 589832 | tf_op jit(solution)/shard_map/ppermute | solution.py:251
  110.6 0.0 collective-permute-done.17.refs_2_
  110.6 4.6 %collective-permute-start.18 = (f32[384,128]{1,0:T(8,128)S(1)}, f32[384,128]{1,0:T(8,128)S(1)}, u32[]{:S(2)}, u32[]{:S(2)}) collective-permute-start(f32[384,128]{1,0:T(8,128)S(1)} %collective-permute-done.17.refs_2_), channel_id=1, source_target_pairs={{0,22},{2,0},{4,2},{6,4},{8,6},{10,8},{12,10},{14,12},{16,14},{18,... | collective-permute-start | bytes 589832 | tf_op jit(solution)/shard_map/ppermute | solution.py:251
  115.2 1.8 %collective-permute-done.22.refs_3_ = f32[384,128]{1,0:T(8,128)S(1)} collective-permute-done((f32[384,128]{1,0:T(8,128)S(1)}, f32[384,128]{1,0:T(8,128)S(1)}, u32[]{:S(2)}, u32[]{:S(2)}) %collective-permute-start.22) | collective-permute-done | bytes 196640 | tf_op jit(solution)/shard_map/ppermute | solution.py:251
  117.1 1.9 %collective-permute-start.23 = (f32[384,128]{1,0:T(8,128)S(1)}, f32[384,128]{1,0:T(8,128)S(1)}, u32[]{:S(2)}, u32[]{:S(2)}) collective-permute-start(f32[384,128]{1,0:T(8,128)S(1)} %collective-permute-done.22.refs_3_), channel_id=1, source_target_pairs={{0,2},{2,4},{4,6},{6,8},{8,10},{10,12},{12,14},{14,16},{16,18},{18... | collective-permute-start | bytes 589832 | tf_op jit(solution)/shard_map/ppermute | solution.py:251
  119.0 4.6 %collective-permute-start.19 = (f32[384,128]{1,0:T(8,128)S(1)}, f32[384,128]{1,0:T(8,128)S(1)}, u32[]{:S(2)}, u32[]{:S(2)}) collective-permute-start(f32[384,128]{1,0:T(8,128)S(1)} %collective-permute-done.18.refs_0_), channel_id=1, source_target_pairs={{0,22},{2,0},{4,2},{6,4},{8,6},{10,8},{12,10},{14,12},{16,14},{18,... | collective-permute-start | bytes 589832 | tf_op jit(solution)/shard_map/ppermute | solution.py:251
  123.6 1.1 collective-permute-done.23.refs_1_
  124.7 1.9 %collective-permute-start.24 = (f32[384,128]{1,0:T(8,128)S(1)}, f32[384,128]{1,0:T(8,128)S(1)}, u32[]{:S(2)}, u32[]{:S(2)}) collective-permute-start(f32[384,128]{1,0:T(8,128)S(1)} %collective-permute-done.23.refs_1_), channel_id=1, source_target_pairs={{0,2},{2,4},{4,6},{6,8},{8,10},{10,12},{12,14},{14,16},{16,18},{18... | collective-permute-start | bytes 589832 | tf_op jit(solution)/shard_map/ppermute | solution.py:251
  126.6 0.0 collective-permute-done.19.refs_2_
  126.6 4.6 %collective-permute-start.20 = (f32[384,128]{1,0:T(8,128)S(1)}, f32[384,128]{1,0:T(8,128)S(1)}, u32[]{:S(2)}, u32[]{:S(2)}) collective-permute-start(f32[384,128]{1,0:T(8,128)S(1)} %collective-permute-done.19.refs_2_), channel_id=1, source_target_pairs={{0,22},{2,0},{4,2},{6,4},{8,6},{10,8},{12,10},{14,12},{16,14},{18,... | collective-permute-start | bytes 589832 | tf_op jit(solution)/shard_map/ppermute | solution.py:251
  131.2 1.1 collective-permute-done.24.refs_3_
  132.3 1.9 %collective-permute-start.25 = (f32[384,128]{1,0:T(8,128)S(1)}, f32[384,128]{1,0:T(8,128)S(1)}, u32[]{:S(2)}, u32[]{:S(2)}) collective-permute-start(f32[384,128]{1,0:T(8,128)S(1)} %collective-permute-done.24.refs_3_), channel_id=1, source_target_pairs={{0,2},{2,4},{4,6},{6,8},{8,10},{10,12},{12,14},{14,16},{16,18},{18... | collective-permute-start | bytes 589832 | tf_op jit(solution)/shard_map/ppermute | solution.py:251
  134.2 4.6 %collective-permute-start.26 = (f32[384,128]{1,0:T(8,128)S(1)}, f32[384,128]{1,0:T(8,128)S(1)}, u32[]{:S(2)}, u32[]{:S(2)}) collective-permute-start(f32[384,128]{1,0:T(8,128)S(1)} %collective-permute-done.20.refs_0_), channel_id=1, source_target_pairs={{0,22},{2,0},{4,2},{6,4},{8,6},{10,8},{12,10},{14,12},{16,14},{18,... | collective-permute-start | bytes 589832 | tf_op jit(solution)/shard_map/ppermute | solution.py:251
  138.8 1.1 collective-permute-done.25.refs_1_
  139.9 1.9 %collective-permute-start.27 = (f32[384,128]{1,0:T(8,128)S(1)}, f32[384,128]{1,0:T(8,128)S(1)}, u32[]{:S(2)}, u32[]{:S(2)}) collective-permute-start(f32[384,128]{1,0:T(8,128)S(1)} %collective-permute-done.25.refs_1_), channel_id=1, source_target_pairs={{0,2},{2,4},{4,6},{6,8},{8,10},{10,12},{12,14},{14,16},{16,18},{18... | collective-permute-start | bytes 589832 | tf_op jit(solution)/shard_map/ppermute | solution.py:251
  141.8 1.6 shard_map.62
  143.5 0.8 shard_map.64.refs_4_
  144.3 0.8 shard_map.65.refs_4_
  145.1 2.4 %collective-permute-done.27.refs_3_ = f32[384,128]{1,0:T(8,128)S(1)} collective-permute-done((f32[384,128]{1,0:T(8,128)S(1)}, f32[384,128]{1,0:T(8,128)S(1)}, u32[]{:S(2)}, u32[]{:S(2)}) %collective-permute-start.27) | collective-permute-done | bytes 196640 | tf_op jit(solution)/shard_map/ppermute | solution.py:251
  147.5 0.8 shard_map.66
  148.3 8.7 %all-gather.2 = f32[768,256]{1,0:T(8,128)S(1)} all-gather(f32[384,256]{1,0:T(8,128)S(1)} %get-tuple-element.27), channel_id=4, replica_groups=mesh['xh'=2,'y'=8,'xl'=2,'z'=12,'c'=2] {'c'}, dimensions={0}, use_global_device_ids=true | all-gather | bytes 1179648 | tf_op jit(solution)/shard_map/all_gather | solution.py:207
  157.0 0.1 shard_map.67
  157.0 6.8 %all-gather.3 = f32[768,128]{1,0:T(8,128)S(1)} all-gather(f32[384,128]{1,0:T(8,128)S(1)} %get-tuple-element.29), channel_id=5, replica_groups=mesh['xh'=2,'y'=8,'xl'=2,'z'=12,'c'=2] {'xl'}, dimensions={0}, use_global_device_ids=true | all-gather | bytes 589824 | tf_op jit(solution)/shard_map/all_gather | solution.py:237
  163.8 1.3 shard_map.68
  (10 shorter events, 0.0 us)
Async XLA Ops:
  7.2 76.7 %all-gather.6.cloned.1.call-start = ((), (), s32[]{:S(2)}) async-start(), calls=%async_computation | async-start | bytes 4915200 | tf_op jit(solution)/shard_map/all_gather | solution.py:282
  8.9 8.4 %collective-permute-start.8 = (f32[384,128]{1,0:T(8,128)}, f32[384,128]{1,0:T(8,128)S(1)}, u32[]{:S(2)}, u32[]{:S(2)}) collective-permute-start(f32[384,128]{1,0:T(8,128)} %shard_map.59), channel_id=1, source_target_pairs={{24,0},{384,408},{0,384},{408,24},{25,1},{385,409},{1,385},{409,25... | collective-permute-start | bytes 589832 | tf_op jit(solution)/shard_map/ppermute | solution.py:285
  14.4 9.0 %collective-permute-start = (f32[384,128]{1,0:T(8,128)}, f32[384,128]{1,0:T(8,128)S(1)}, u32[]{:S(2)}, u32[]{:S(2)}) collective-permute-start(f32[384,128]{1,0:T(8,128)} %shard_map.59), channel_id=1, source_target_pairs={{0,0},{24,384},{384,24},{408,408},{1,1},{25,385},{385,25},{409,409... | collective-permute-start | bytes 589832 | tf_op jit(solution)/shard_map/ppermute | solution.py:284
  17.3 14.5 %collective-permute-start.10 = (f32[384,128]{1,0:T(8,128)S(1)}, f32[384,128]{1,0:T(8,128)S(1)}, u32[]{:S(2)}, u32[]{:S(2)}) collective-permute-start(f32[384,128]{1,0:T(8,128)S(1)} %collective-permute-done.8.refs_8_), channel_id=1, source_target_pairs={{0,336},{48,0},{96,48},{144,96},{192,144},{240,192},{288,240},{336... | collective-permute-start | bytes 589832 | tf_op jit(solution)/shard_map/ppermute | solution.py:251
  23.4 11.8 %collective-permute-start.1 = (f32[384,128]{1,0:T(8,128)S(1)}, f32[384,128]{1,0:T(8,128)S(1)}, u32[]{:S(2)}, u32[]{:S(2)}) collective-permute-start(f32[384,128]{1,0:T(8,128)S(1)} %collective-permute-done.refs_0_), channel_id=1, source_target_pairs={{0,48},{48,96},{96,144},{144,192},{192,240},{240,288},{288,336},{3... | collective-permute-start | bytes 589832 | tf_op jit(solution)/shard_map/ppermute | solution.py:251
  25.3 11.8 %collective-permute-start.9 = (f32[384,128]{1,0:T(8,128)S(1)}, f32[384,128]{1,0:T(8,128)S(1)}, u32[]{:S(2)}, u32[]{:S(2)}) collective-permute-start(f32[384,128]{1,0:T(8,128)S(1)} %collective-permute-done.8.refs_8_), channel_id=1, source_target_pairs={{0,48},{48,96},{96,144},{144,192},{192,240},{240,288},{288,336},{3... | collective-permute-start | bytes 589832 | tf_op jit(solution)/shard_map/ppermute | solution.py:251
  27.3 11.8 %collective-permute-start.2 = (f32[384,128]{1,0:T(8,128)S(1)}, f32[384,128]{1,0:T(8,128)S(1)}, u32[]{:S(2)}, u32[]{:S(2)}) collective-permute-start(f32[384,128]{1,0:T(8,128)S(1)} %collective-permute-done.refs_0_), channel_id=1, source_target_pairs={{0,336},{48,0},{96,48},{144,96},{192,144},{240,192},{288,240},{336... | collective-permute-start | bytes 589832 | tf_op jit(solution)/shard_map/ppermute | solution.py:251
  31.8 11.8 %collective-permute-start.12 = (f32[384,128]{1,0:T(8,128)S(1)}, f32[384,128]{1,0:T(8,128)S(1)}, u32[]{:S(2)}, u32[]{:S(2)}) collective-permute-start(f32[384,128]{1,0:T(8,128)S(1)} %collective-permute-done.10.refs_10_), channel_id=1, source_target_pairs={{0,336},{48,0},{96,48},{144,96},{192,144},{240,192},{288,240},{336... | collective-permute-start | bytes 589832 | tf_op jit(solution)/shard_map/ppermute | solution.py:251
  35.2 11.8 %collective-permute-start.3 = (f32[384,128]{1,0:T(8,128)S(1)}, f32[384,128]{1,0:T(8,128)S(1)}, u32[]{:S(2)}, u32[]{:S(2)}) collective-permute-start(f32[384,128]{1,0:T(8,128)S(1)} %collective-permute-done.1.refs_1_), channel_id=1, source_target_pairs={{0,48},{48,96},{96,144},{144,192},{192,240},{240,288},{288,336},{3... | collective-permute-start | bytes 589832 | tf_op jit(solution)/shard_map/ppermute | solution.py:251
  37.2 11.8 %collective-permute-start.11 = (f32[384,128]{1,0:T(8,128)S(1)}, f32[384,128]{1,0:T(8,128)S(1)}, u32[]{:S(2)}, u32[]{:S(2)}) collective-permute-start(f32[384,128]{1,0:T(8,128)S(1)} %collective-permute-done.9.refs_9_), channel_id=1, source_target_pairs={{0,48},{48,96},{96,144},{144,192},{192,240},{240,288},{288,336},{3... | collective-permute-start | bytes 589832 | tf_op jit(solution)/shard_map/ppermute | solution.py:251
  39.1 11.8 %collective-permute-start.4 = (f32[384,128]{1,0:T(8,128)S(1)}, f32[384,128]{1,0:T(8,128)S(1)}, u32[]{:S(2)}, u32[]{:S(2)}) collective-permute-start(f32[384,128]{1,0:T(8,128)S(1)} %collective-permute-done.2.refs_2_), channel_id=1, source_target_pairs={{0,336},{48,0},{96,48},{144,96},{192,144},{240,192},{288,240},{336... | collective-permute-start | bytes 589832 | tf_op jit(solution)/shard_map/ppermute | solution.py:251
  43.7 11.8 %collective-permute-start.14 = (f32[384,128]{1,0:T(8,128)S(1)}, f32[384,128]{1,0:T(8,128)S(1)}, u32[]{:S(2)}, u32[]{:S(2)}) collective-permute-start(f32[384,128]{1,0:T(8,128)S(1)} %collective-permute-done.12.refs_12_), channel_id=1, source_target_pairs={{0,336},{48,0},{96,48},{144,96},{192,144},{240,192},{288,240},{336... | collective-permute-start | bytes 589832 | tf_op jit(solution)/shard_map/ppermute | solution.py:251
  47.1 11.8 %collective-permute-start.5 = (f32[384,128]{1,0:T(8,128)S(1)}, f32[384,128]{1,0:T(8,128)S(1)}, u32[]{:S(2)}, u32[]{:S(2)}) collective-permute-start(f32[384,128]{1,0:T(8,128)S(1)} %collective-permute-done.3.refs_3_), channel_id=1, source_target_pairs={{0,48},{48,96},{96,144},{144,192},{192,240},{240,288},{288,336},{3... | collective-permute-start | bytes 589832 | tf_op jit(solution)/shard_map/ppermute | solution.py:251
  49.0 11.8 %collective-permute-start.13 = (f32[384,128]{1,0:T(8,128)S(1)}, f32[384,128]{1,0:T(8,128)S(1)}, u32[]{:S(2)}, u32[]{:S(2)}) collective-permute-start(f32[384,128]{1,0:T(8,128)S(1)} %collective-permute-done.11.refs_11_), channel_id=1, source_target_pairs={{0,48},{48,96},{96,144},{144,192},{192,240},{240,288},{288,336},{3... | collective-permute-start | bytes 589832 | tf_op jit(solution)/shard_map/ppermute | solution.py:251
  51.0 9.9 %collective-permute-start.6 = (f32[384,128]{1,0:T(8,128)S(1)}, f32[384,128]{1,0:T(8,128)S(1)}, u32[]{:S(2)}, u32[]{:S(2)}) collective-permute-start(f32[384,128]{1,0:T(8,128)S(1)} %collective-permute-done.4.refs_4_), channel_id=1, source_target_pairs={{0,336},{48,0},{96,48},{144,96},{192,144},{240,192},{288,240},{336... | collective-permute-start | bytes 589832 | tf_op jit(solution)/shard_map/ppermute | solution.py:251
  55.5 6.9 %collective-permute-start.15 = (f32[384,128]{1,0:T(8,128)S(1)}, f32[384,128]{1,0:T(8,128)S(1)}, u32[]{:S(2)}, u32[]{:S(2)}) collective-permute-start(f32[384,128]{1,0:T(8,128)S(1)} %collective-permute-done.14.refs_14_), channel_id=1, source_target_pairs={{0,336},{48,0},{96,48},{144,96},{192,144},{240,192},{288,240},{336... | collective-permute-start | bytes 589832 | tf_op jit(solution)/shard_map/ppermute | solution.py:251
  58.9 9.7 %collective-permute-start.7 = (f32[384,128]{1,0:T(8,128)S(1)}, f32[384,128]{1,0:T(8,128)S(1)}, u32[]{:S(2)}, u32[]{:S(2)}) collective-permute-start(f32[384,128]{1,0:T(8,128)S(1)} %collective-permute-done.5.refs_5_), channel_id=1, source_target_pairs={{0,48},{48,96},{96,144},{144,192},{192,240},{240,288},{288,336},{3... | collective-permute-start | bytes 589832 | tf_op jit(solution)/shard_map/ppermute | solution.py:251
  70.4 17.8 %collective-permute-start.16 = (f32[12,128,256]{2,1,0:T(8,128)}, f32[12,128,256]{2,1,0:T(8,128)}, u32[]{:S(2)}, u32[]{:S(2)}) collective-permute-start(f32[12,128,256]{2,1,0:T(8,128)} %get-tuple-element.20), channel_id=1, source_target_pairs={{0,1},{1,0},{2,3},{3,2},{4,5},{5,4},{6,7},{7,6},{8,9},{9,8},{10,11... | collective-permute-start | bytes 4718600 | tf_op jit(solution)/shard_map/ppermute | solution.py:251
  83.8 11.7 %copy-start = (s32[6,2]{0,1:T(2,128)S(1)}, s32[6,2]{0,1:T(2,128)}, u32[]{:S(2)}) copy-start(s32[6,2]{0,1:T(2,128)} %param.7) | copy-start | bytes 148
  96.2 12.6 %collective-permute-start.21 = (f32[384,128]{1,0:T(8,128)S(1)}, f32[384,128]{1,0:T(8,128)S(1)}, u32[]{:S(2)}, u32[]{:S(2)}) collective-permute-start(f32[384,128]{1,0:T(8,128)S(1)} %shard_map.63.refs_0_), channel_id=1, source_target_pairs={{0,2},{2,4},{4,6},{6,8},{8,10},{10,12},{12,14},{14,16},{16,18},{18... | collective-permute-start | bytes 589832 | tf_op jit(solution)/shard_map/ppermute | solution.py:251
  98.1 12.6 %collective-permute-start.17 = (f32[384,128]{1,0:T(8,128)S(1)}, f32[384,128]{1,0:T(8,128)S(1)}, u32[]{:S(2)}, u32[]{:S(2)}) collective-permute-start(f32[384,128]{1,0:T(8,128)S(1)} %shard_map.63.refs_0_), channel_id=1, source_target_pairs={{0,22},{2,0},{4,2},{6,4},{8,6},{10,8},{12,10},{14,12},{16,14},{18,... | collective-permute-start | bytes 589832 | tf_op jit(solution)/shard_map/ppermute | solution.py:251
  108.7 8.4 %collective-permute-start.22 = (f32[384,128]{1,0:T(8,128)S(1)}, f32[384,128]{1,0:T(8,128)S(1)}, u32[]{:S(2)}, u32[]{:S(2)}) collective-permute-start(f32[384,128]{1,0:T(8,128)S(1)} %collective-permute-done.21.refs_1_), channel_id=1, source_target_pairs={{0,2},{2,4},{4,6},{6,8},{8,10},{10,12},{12,14},{14,16},{16,18},{18... | collective-permute-start | bytes 589832 | tf_op jit(solution)/shard_map/ppermute | solution.py:251
  110.6 8.3 %collective-permute-start.18 = (f32[384,128]{1,0:T(8,128)S(1)}, f32[384,128]{1,0:T(8,128)S(1)}, u32[]{:S(2)}, u32[]{:S(2)}) collective-permute-start(f32[384,128]{1,0:T(8,128)S(1)} %collective-permute-done.17.refs_2_), channel_id=1, source_target_pairs={{0,22},{2,0},{4,2},{6,4},{8,6},{10,8},{12,10},{14,12},{16,14},{18,... | collective-permute-start | bytes 589832 | tf_op jit(solution)/shard_map/ppermute | solution.py:251
  117.1 7.6 %collective-permute-start.23 = (f32[384,128]{1,0:T(8,128)S(1)}, f32[384,128]{1,0:T(8,128)S(1)}, u32[]{:S(2)}, u32[]{:S(2)}) collective-permute-start(f32[384,128]{1,0:T(8,128)S(1)} %collective-permute-done.22.refs_3_), channel_id=1, source_target_pairs={{0,2},{2,4},{4,6},{6,8},{8,10},{10,12},{12,14},{14,16},{16,18},{18... | collective-permute-start | bytes 589832 | tf_op jit(solution)/shard_map/ppermute | solution.py:251
  119.0 7.6 %collective-permute-start.19 = (f32[384,128]{1,0:T(8,128)S(1)}, f32[384,128]{1,0:T(8,128)S(1)}, u32[]{:S(2)}, u32[]{:S(2)}) collective-permute-start(f32[384,128]{1,0:T(8,128)S(1)} %collective-permute-done.18.refs_0_), channel_id=1, source_target_pairs={{0,22},{2,0},{4,2},{6,4},{8,6},{10,8},{12,10},{14,12},{16,14},{18,... | collective-permute-start | bytes 589832 | tf_op jit(solution)/shard_map/ppermute | solution.py:251
  124.7 7.6 %collective-permute-start.24 = (f32[384,128]{1,0:T(8,128)S(1)}, f32[384,128]{1,0:T(8,128)S(1)}, u32[]{:S(2)}, u32[]{:S(2)}) collective-permute-start(f32[384,128]{1,0:T(8,128)S(1)} %collective-permute-done.23.refs_1_), channel_id=1, source_target_pairs={{0,2},{2,4},{4,6},{6,8},{8,10},{10,12},{12,14},{14,16},{16,18},{18... | collective-permute-start | bytes 589832 | tf_op jit(solution)/shard_map/ppermute | solution.py:251
  126.6 7.6 %collective-permute-start.20 = (f32[384,128]{1,0:T(8,128)S(1)}, f32[384,128]{1,0:T(8,128)S(1)}, u32[]{:S(2)}, u32[]{:S(2)}) collective-permute-start(f32[384,128]{1,0:T(8,128)S(1)} %collective-permute-done.19.refs_2_), channel_id=1, source_target_pairs={{0,22},{2,0},{4,2},{6,4},{8,6},{10,8},{12,10},{14,12},{16,14},{18,... | collective-permute-start | bytes 589832 | tf_op jit(solution)/shard_map/ppermute | solution.py:251
  132.3 7.6 %collective-permute-start.25 = (f32[384,128]{1,0:T(8,128)S(1)}, f32[384,128]{1,0:T(8,128)S(1)}, u32[]{:S(2)}, u32[]{:S(2)}) collective-permute-start(f32[384,128]{1,0:T(8,128)S(1)} %collective-permute-done.24.refs_3_), channel_id=1, source_target_pairs={{0,2},{2,4},{4,6},{6,8},{8,10},{10,12},{12,14},{14,16},{16,18},{18... | collective-permute-start | bytes 589832 | tf_op jit(solution)/shard_map/ppermute | solution.py:251
  134.2 10.9 %collective-permute-start.26 = (f32[384,128]{1,0:T(8,128)S(1)}, f32[384,128]{1,0:T(8,128)S(1)}, u32[]{:S(2)}, u32[]{:S(2)}) collective-permute-start(f32[384,128]{1,0:T(8,128)S(1)} %collective-permute-done.20.refs_0_), channel_id=1, source_target_pairs={{0,22},{2,0},{4,2},{6,4},{8,6},{10,8},{12,10},{14,12},{16,14},{18,... | collective-permute-start | bytes 589832 | tf_op jit(solution)/shard_map/ppermute | solution.py:251
  139.9 7.6 %collective-permute-start.27 = (f32[384,128]{1,0:T(8,128)S(1)}, f32[384,128]{1,0:T(8,128)S(1)}, u32[]{:S(2)}, u32[]{:S(2)}) collective-permute-start(f32[384,128]{1,0:T(8,128)S(1)} %collective-permute-done.25.refs_1_), channel_id=1, source_target_pairs={{0,2},{2,4},{4,6},{6,8},{8,10},{10,12},{12,14},{14,16},{16,18},{18... | collective-permute-start | bytes 589832 | tf_op jit(solution)/shard_map/ppermute | solution.py:251
Sparse Core Ops, SparseCore 0:
  11.0 72.7 all-gather.5

commit v7 on v6

--- a/solution.py
+++ b/solution.py
@@ -160,38 +160,31 @@
     )(left, hi, lo)
 
 
-def second_kernel(offsets, has_acc, last, hi, lo, *refs):
-    n = len(offsets)
-    acc = refs[n][...] if has_acc else None
-    outs = refs[n + has_acc :]
+def second_kernel(offsets, hi, lo, *refs):
+    blocks, (own, give) = refs[:-2], refs[-2:]
     z = lax.axis_index("z")
     at = [lax.rem(z + (off + NZ), NZ) for off in offsets]
-    for k in range(0, n, 2):
-        a = jnp.concatenate([refs[k][...], refs[k + 1][...]], axis=1)
-        bh = jnp.concatenate([hi[at[k]], hi[at[k + 1]]], axis=0)
-        bl = jnp.concatenate([lo[at[k]], lo[at[k + 1]]], axis=0)
+    acc = None
+    for k in range(0, len(offsets), 2):
+        pair = range(k, min(k + 2, len(offsets)))
+        a = jnp.concatenate([blocks[i][...] for i in pair], axis=1)
+        bh = jnp.concatenate([hi[at[i]] for i in pair], axis=0)
+        bl = jnp.concatenate([lo[at[i]] for i in pair], axis=0)
         term = split_dot(a, bh, bl)
         acc = term if acc is None else acc + term
-    if last:
-        outs[0][...] = acc[:, :256]
-        outs[1][...] = acc[:, 256:]
-    else:
-        outs[0][...] = acc
-
-
-def second_product(operand, blocks, acc=None, last=False):
+    own[...] = acc[:, :256]
+    give[...] = acc[:, 256:]
+
+
+def second_product(operand, blocks):
     offsets = tuple(off for off, _ in blocks)
     rows, cols = blocks[0][1].shape
-    args = list(operand) + [x for _, x in blocks] + ([] if acc is None else [acc])
-    if last:
-        shapes = (jax.ShapeDtypeStruct((rows, 2 * cols), F32),) * 2
-    else:
-        shapes = jax.ShapeDtypeStruct((rows, 4 * cols), F32)
-    return pl.pallas_call(
-        functools.partial(second_kernel, offsets, acc is not None, last),
-        out_shape=shapes,
+    args = list(operand) + [x for _, x in blocks]
+    return pl.pallas_call(
+        functools.partial(second_kernel, offsets),
+        out_shape=(jax.ShapeDtypeStruct((rows, 2 * cols), F32),) * 2,
         in_specs=[VM] * len(args),
-        out_specs=(VM, VM) if last else VM,
+        out_specs=(VM, VM),
         compiler_params=PARAMS,
         cost_estimate=pl.CostEstimate(
             flops=len(offsets) * 3 * 2 * rows * cols * 4 * cols, bytes_accessed=0, transcendentals=0
@@ -199,21 +192,26 @@
     )(*args)
 
 
-def join_kernel(own, both, mine, other):
-    put_halves(own[...] + both[1 - lax.axis_index("c")], mine, other)
-
-
-def join(own, give):
+def join_kernel(hi, lo, own, both, near_block, far_block, mine, other):
+    c = lax.axis_index("c")
+    u = 2 * lax.rem(lax.axis_index("z") + NZ // 2, NZ)
+    a = jnp.concatenate([near_block[...], far_block[...]], axis=1)
+    bh = jnp.concatenate([hi[u + c], hi[u + 1 - c]], axis=0)
+    bl = jnp.concatenate([lo[u + c], lo[u + 1 - c]], axis=0)
+    put_halves(own[...] + both[1 - c] + split_dot(a, bh, bl), mine, other)
+
+
+def join(hi, lo, own, give, last, last_sib):
     both = lax.all_gather(give, "c", axis=0)
-    rows, cols = own.shape
-    block = jax.ShapeDtypeStruct((rows, cols // 2), F32)
+    args = (hi, lo, own, both, last, last_sib)
+    block = jax.ShapeDtypeStruct(last.shape, F32)
     return pl.pallas_call(
         join_kernel,
         out_shape=(block, block),
-        in_specs=[VM, VM],
+        in_specs=[VM] * len(args),
         out_specs=(VM, VM),
         compiler_params=PARAMS,
-    )(own, both)
+    )(*args)
 
 
 def filter_kernel(final, kept, mine, pair, *refs):
@@ -293,15 +291,16 @@
     mine, other, took = together(*first_product(left, hi, lo), took)
     square = filtered(kept.T, (mine, other))
 
-    operand = phase_rows(hi, lo, took)
-    up, down = chain(square, "z", 1, 6), chain(square, "z", -1, 5)
+    down = chain(square, "z", -1, 1)
+    down[0], operand = together(down[0], phase_rows(hi, lo, took))
+    down += chain(down[0], "z", -1, 4)
+    up = chain(square, "z", 1, 6)
+    crossed = [(2 * z + c, 2 * ((z - 1) % NZ) + 1 - c) for z in range(NZ) for c in range(2)]
+    last_sib = lax.ppermute(down[4], ("z", "c"), crossed)
     blocks = [(0, square)]
     for s in range(5):
         blocks += [(-s - 1, up[s]), (s + 1, down[s])]
-    blocks.append((-6, up[5]))
-    acc = second_product(operand, blocks[:4])
-    acc = second_product(operand, blocks[4:8], acc)
-    halves = join(*second_product(operand, blocks[8:], acc, last=True))
+    halves = join(hi, lo, *second_product(operand, blocks), up[5], last_sib)
     return filtered(kept.T, halves, square)
 
 

time: 173 us -> 175 us (1.012)
  starting transfers between devices: 98.1 us -> 111 us
  blocking collectives: 22.8 us -> 15.6 us
  waiting for transfers between devices: 22.8 us -> 18 us
    ppermute x0 -> x1, starting transfers between devices: none -> 10.7 us  [body(): last_sib = lax.ppermute(down[4], ('z', 'c'), crossed)]
    all_gather x1, blocking collectives: 8.65 us -> 2.39 us  [join(): both = lax.all_gather(give, 'c', axis=0)]
    ppermute x26, waiting for transfers between devices: 18.1 us -> 13.3 us  [shift(): return lax.ppermute(x, axis, [(i, (i + step) % n) for i in range(n)])]
    ppermute x26, starting transfers between devices: 91 us -> 93.5 us  [shift(): return lax.ppermute(x, axis, [(i, (i + step) % n) for i in range(n)])]
  transfers between devices with their start and end apart: 29 -> 30, of which waited for: 10 -> 10; matrix products, arithmetic and copies ran while one was open for 0% -> 0% of each run, Pallas kernels for 5% -> 6%
where the time goes in v7:
time: 175 us; the launch traced here: 173 us
  starting transfers between devices  111 us (63%)
  waiting for transfers between devices  18 us (10%)
  blocking collectives  15.6 us (9%)
  between operations  14.4 us (8%)
  Pallas kernels  13.8 us (8%)
    ppermute x26, starting transfers between devices, shift(): return lax.ppermute(x, axis, [(i, (i + step) % n) for i in range(n)])  93.5 us
    ppermute x26, waiting for transfers between devices, shift(): return lax.ppermute(x, axis, [(i, (i + step) % n) for i in range(n)])  13.3 us
    all_gather x2, blocking collectives, filtered(): pair = lax.all_gather(other, 'xl', axis=0)  13.2 us
    ppermute x1, starting transfers between devices, body(): last_sib = lax.ppermute(down[4], ('z', 'c'), crossed)  10.7 us
    ppermute x1, starting transfers between devices, body(): far = lax.ppermute(masked, ('xh', 'xl'), [(1, 0), (2, 3), (0, 2), (3, 1)])  5.48 us
    pallas_call x1, Pallas kernels, first_product(): pl.pallas_call(first_kernel, out_shape=(block, block), in_specs=[HB, VM,...  4.38 us
  transfers between devices with their start and end apart: 30, of which 10 were waited for; matrix products, arithmetic and copies ran while one was open for 0% of the time, Pallas kernels for 6%

profile of v7, /device:TPU:1, one launch (start us, length us, event | category | flops | bytes accessed | tf_op | source)
XLA Modules:
  0.0 173.1 jit_solution(7395901984974851067)
XLA Ops:
  7.2 0.0 all-gather.6.cloned.1.call-start
  7.2 1.7 shard_map.59
  8.9 0.0 all-gather.6.cloned.1.call-update
  8.9 5.5 %collective-permute-start.8 = (f32[384,128]{1,0:T(8,128)}, f32[384,128]{1,0:T(8,128)S(1)}, u32[]{:S(2)}, u32[]{:S(2)}) collective-permute-start(f32[384,128]{1,0:T(8,128)} %shard_map.59), channel_id=1, source_target_pairs={{24,0},{384,408},{0,384},{408,24},{25,1},{385,409},{1,385},{409,25... | collective-permute-start | bytes 589832 | tf_op jit(solution)/shard_map/ppermute | solution.py:283
  14.4 1.6 collective-permute-start
  16.0 1.3 collective-permute-done.8.refs_8_
  17.3 6.1 %collective-permute-start.10 = (f32[384,128]{1,0:T(8,128)S(1)}, f32[384,128]{1,0:T(8,128)S(1)}, u32[]{:S(2)}, u32[]{:S(2)}) collective-permute-start(f32[384,128]{1,0:T(8,128)S(1)} %collective-permute-done.8.refs_8_), channel_id=1, source_target_pairs={{0,336},{48,0},{96,48},{144,96},{192,144},{240,192},{288,240},{336... | collective-permute-start | bytes 589832 | tf_op jit(solution)/shard_map/ppermute | solution.py:249
  23.4 1.9 %collective-permute-start.1 = (f32[384,128]{1,0:T(8,128)S(1)}, f32[384,128]{1,0:T(8,128)S(1)}, u32[]{:S(2)}, u32[]{:S(2)}) collective-permute-start(f32[384,128]{1,0:T(8,128)S(1)} %collective-permute-done.refs_0_), channel_id=1, source_target_pairs={{0,48},{48,96},{96,144},{144,192},{192,240},{240,288},{288,336},{3... | collective-permute-start | bytes 589832 | tf_op jit(solution)/shard_map/ppermute | solution.py:249
  25.3 1.9 %collective-permute-start.9 = (f32[384,128]{1,0:T(8,128)S(1)}, f32[384,128]{1,0:T(8,128)S(1)}, u32[]{:S(2)}, u32[]{:S(2)}) collective-permute-start(f32[384,128]{1,0:T(8,128)S(1)} %collective-permute-done.8.refs_8_), channel_id=1, source_target_pairs={{0,48},{48,96},{96,144},{144,192},{192,240},{240,288},{288,336},{3... | collective-permute-start | bytes 589832 | tf_op jit(solution)/shard_map/ppermute | solution.py:249
  27.3 4.6 %collective-permute-start.2 = (f32[384,128]{1,0:T(8,128)S(1)}, f32[384,128]{1,0:T(8,128)S(1)}, u32[]{:S(2)}, u32[]{:S(2)}) collective-permute-start(f32[384,128]{1,0:T(8,128)S(1)} %collective-permute-done.refs_0_), channel_id=1, source_target_pairs={{0,336},{48,0},{96,48},{144,96},{192,144},{240,192},{288,240},{336... | collective-permute-start | bytes 589832 | tf_op jit(solution)/shard_map/ppermute | solution.py:249
  31.8 3.4 %collective-permute-start.12 = (f32[384,128]{1,0:T(8,128)S(1)}, f32[384,128]{1,0:T(8,128)S(1)}, u32[]{:S(2)}, u32[]{:S(2)}) collective-permute-start(f32[384,128]{1,0:T(8,128)S(1)} %collective-permute-done.10.refs_10_), channel_id=1, source_target_pairs={{0,336},{48,0},{96,48},{144,96},{192,144},{240,192},{288,240},{336... | collective-permute-start | bytes 589832 | tf_op jit(solution)/shard_map/ppermute | solution.py:249
  35.2 0.0 collective-permute-done.1.refs_1_
  35.2 1.9 %collective-permute-start.3 = (f32[384,128]{1,0:T(8,128)S(1)}, f32[384,128]{1,0:T(8,128)S(1)}, u32[]{:S(2)}, u32[]{:S(2)}) collective-permute-start(f32[384,128]{1,0:T(8,128)S(1)} %collective-permute-done.1.refs_1_), channel_id=1, source_target_pairs={{0,48},{48,96},{96,144},{144,192},{192,240},{240,288},{288,336},{3... | collective-permute-start | bytes 589832 | tf_op jit(solution)/shard_map/ppermute | solution.py:249
  37.2 0.0 collective-permute-done.9.refs_9_
  37.2 1.9 %collective-permute-start.11 = (f32[384,128]{1,0:T(8,128)S(1)}, f32[384,128]{1,0:T(8,128)S(1)}, u32[]{:S(2)}, u32[]{:S(2)}) collective-permute-start(f32[384,128]{1,0:T(8,128)S(1)} %collective-permute-done.9.refs_9_), channel_id=1, source_target_pairs={{0,48},{48,96},{96,144},{144,192},{192,240},{240,288},{288,336},{3... | collective-permute-start | bytes 589832 | tf_op jit(solution)/shard_map/ppermute | solution.py:249
  39.1 4.6 %collective-permute-start.4 = (f32[384,128]{1,0:T(8,128)S(1)}, f32[384,128]{1,0:T(8,128)S(1)}, u32[]{:S(2)}, u32[]{:S(2)}) collective-permute-start(f32[384,128]{1,0:T(8,128)S(1)} %collective-permute-done.2.refs_2_), channel_id=1, source_target_pairs={{0,336},{48,0},{96,48},{144,96},{192,144},{240,192},{288,240},{336... | collective-permute-start | bytes 589832 | tf_op jit(solution)/shard_map/ppermute | solution.py:249
  43.7 0.0 collective-permute-done.12.refs_12_
  43.7 3.4 %collective-permute-start.14 = (f32[384,128]{1,0:T(8,128)S(1)}, f32[384,128]{1,0:T(8,128)S(1)}, u32[]{:S(2)}, u32[]{:S(2)}) collective-permute-start(f32[384,128]{1,0:T(8,128)S(1)} %collective-permute-done.12.refs_12_), channel_id=1, source_target_pairs={{0,336},{48,0},{96,48},{144,96},{192,144},{240,192},{288,240},{336... | collective-permute-start | bytes 589832 | tf_op jit(solution)/shard_map/ppermute | solution.py:249
  47.1 1.9 %collective-permute-start.5 = (f32[384,128]{1,0:T(8,128)S(1)}, f32[384,128]{1,0:T(8,128)S(1)}, u32[]{:S(2)}, u32[]{:S(2)}) collective-permute-start(f32[384,128]{1,0:T(8,128)S(1)} %collective-permute-done.3.refs_3_), channel_id=1, source_target_pairs={{0,48},{48,96},{96,144},{144,192},{192,240},{240,288},{288,336},{3... | collective-permute-start | bytes 589832 | tf_op jit(solution)/shard_map/ppermute | solution.py:249
  49.0 0.0 collective-permute-done.11.refs_11_
  49.0 1.9 %collective-permute-start.13 = (f32[384,128]{1,0:T(8,128)S(1)}, f32[384,128]{1,0:T(8,128)S(1)}, u32[]{:S(2)}, u32[]{:S(2)}) collective-permute-start(f32[384,128]{1,0:T(8,128)S(1)} %collective-permute-done.11.refs_11_), channel_id=1, source_target_pairs={{0,48},{48,96},{96,144},{144,192},{192,240},{240,288},{288,336},{3... | collective-permute-start | bytes 589832 | tf_op jit(solution)/shard_map/ppermute | solution.py:249
  50.9 0.0 collective-permute-done.4.refs_4_
  51.0 4.6 %collective-permute-start.6 = (f32[384,128]{1,0:T(8,128)S(1)}, f32[384,128]{1,0:T(8,128)S(1)}, u32[]{:S(2)}, u32[]{:S(2)}) collective-permute-start(f32[384,128]{1,0:T(8,128)S(1)} %collective-permute-done.4.refs_4_), channel_id=1, source_target_pairs={{0,336},{48,0},{96,48},{144,96},{192,144},{240,192},{288,240},{336... | collective-permute-start | bytes 589832 | tf_op jit(solution)/shard_map/ppermute | solution.py:249
  55.5 0.0 collective-permute-done.14.refs_14_
  55.5 3.4 %collective-permute-start.15 = (f32[384,128]{1,0:T(8,128)S(1)}, f32[384,128]{1,0:T(8,128)S(1)}, u32[]{:S(2)}, u32[]{:S(2)}) collective-permute-start(f32[384,128]{1,0:T(8,128)S(1)} %collective-permute-done.14.refs_14_), channel_id=1, source_target_pairs={{0,336},{48,0},{96,48},{144,96},{192,144},{240,192},{288,240},{336... | collective-permute-start | bytes 589832 | tf_op jit(solution)/shard_map/ppermute | solution.py:249
  58.9 0.0 collective-permute-done.5.refs_5_
  58.9 1.9 %collective-permute-start.7 = (f32[384,128]{1,0:T(8,128)S(1)}, f32[384,128]{1,0:T(8,128)S(1)}, u32[]{:S(2)}, u32[]{:S(2)}) collective-permute-start(f32[384,128]{1,0:T(8,128)S(1)} %collective-permute-done.5.refs_5_), channel_id=1, source_target_pairs={{0,48},{48,96},{96,144},{144,192},{192,240},{240,288},{288,336},{3... | collective-permute-start | bytes 589832 | tf_op jit(solution)/shard_map/ppermute | solution.py:249
  60.9 0.0 collective-permute-done.6.refs_6_
  60.9 1.6 collective-permute-done.15.refs_15_
  62.5 6.1 %collective-permute-done.7.refs_7_ = f32[384,128]{1,0:T(8,128)S(1)} collective-permute-done((f32[384,128]{1,0:T(8,128)S(1)}, f32[384,128]{1,0:T(8,128)S(1)}, u32[]{:S(2)}, u32[]{:S(2)}) %collective-permute-start.7) | collective-permute-done | bytes 196640 | tf_op jit(solution)/shard_map/ppermute | solution.py:249
  68.6 1.8 %shard_map.60 = (bf16[24,128,256]{2,1,0:T(8,128)(2,1)S(1)}, bf16[24,128,256]{2,1,0:T(8,128)(2,1)S(1)}, f32[12,128,256]{2,1,0:T(8,128)}) custom-call(f32[384,128]{1,0:T(8,128)S(1)} %collective-permute-done.refs_0_, f32[384,128]{1,0:T(8,128)S(1)} %collective-permute-done.1.refs_1_, f32[384,128]{1,0:T(8,128)S(1)} %collective-permute-done.2.refs_2_, ...), custom_call_target="tpu_custom_call" | custom-call | tf_op jit(solution)/shard_map/pallas_call | solution.py:93
  70.4 10.1 %collective-permute-start.16 = (f32[12,128,256]{2,1,0:T(8,128)}, f32[12,128,256]{2,1,0:T(8,128)}, u32[]{:S(2)}, u32[]{:S(2)}) collective-permute-start(f32[12,128,256]{2,1,0:T(8,128)} %get-tuple-element.23), channel_id=1, source_target_pairs={{0,1},{1,0},{2,3},{3,2},{4,5},{5,4},{6,7},{7,6},{8,9},{9,8},{10,11... | collective-permute-start | bytes 4718600 | tf_op jit(solution)/shard_map/ppermute | solution.py:249
  80.5 3.3 %all-gather.6.cloned.1.call-done = f32[9216,128]{1,0:T(8,128)} async-done(((f32[384,128]{1,0:T(8,128)}), f32[9216,128]{1,0:T(8,128)}) %all-gather.6.cloned.1.call-update) | async-done | bytes 4718608 | tf_op jit(solution)/shard_map/all_gather | solution.py:280
  83.8 4.4 %shard_map.61 = (f32[384,128]{1,0:T(8,128)S(1)}, f32[384,128]{1,0:T(8,128)S(1)}) custom-call(f32[24,384,128]{2,1,0:T(8,128)} %bitcast.11, bf16[24,128,256]{2,1,0:T(8,128)(2,1)S(1)} %get-tuple-element.19.hi, bf16[24,128,256]{2,1,0:T(8,128)(2,1)S(1)} %get-tuple-element.20.lo), custom_call_target="tpu_custom_call" | custom-call | flops 1811939328 | tf_op jit(solution)/shard_map/pallas_call | solution.py:147
  88.2 0.0 collective-permute-done.16.took
  88.2 7.3 %all-gather.1 = f32[768,128]{1,0:T(8,128)S(1)} all-gather(f32[384,128]{1,0:T(8,128)S(1)} %get-tuple-element.25), channel_id=3, replica_groups=mesh['xh'=2,'y'=8,'xl'=2,'z'=12,'c'=2] {'xl'}, dimensions={0}, use_global_device_ids=true | all-gather | bytes 589824 | tf_op jit(solution)/shard_map/all_gather | solution.py:235
  95.6 0.6 shard_map.62.refs_0_
  96.2 7.8 %collective-permute-start.17 = (f32[384,128]{1,0:T(8,128)S(1)}, f32[384,128]{1,0:T(8,128)S(1)}, u32[]{:S(2)}, u32[]{:S(2)}) collective-permute-start(f32[384,128]{1,0:T(8,128)S(1)} %shard_map.62.refs_0_), channel_id=1, source_target_pairs={{0,22},{2,0},{4,2},{6,4},{8,6},{10,8},{12,10},{14,12},{16,14},{18,... | collective-permute-start | bytes 589832 | tf_op jit(solution)/shard_map/ppermute | solution.py:249
  104.0 1.9 %collective-permute-start.18 = (f32[384,128]{1,0:T(8,128)S(1)}, f32[384,128]{1,0:T(8,128)S(1)}, u32[]{:S(2)}, u32[]{:S(2)}) collective-permute-start(f32[384,128]{1,0:T(8,128)S(1)} %shard_map.62.refs_0_), channel_id=1, source_target_pairs={{0,2},{2,4},{4,6},{6,8},{8,10},{10,12},{12,14},{14,16},{16,18},{18... | collective-permute-start | bytes 589832 | tf_op jit(solution)/shard_map/ppermute | solution.py:249
  105.9 1.6 shard_map.63
  107.6 0.1 collective-permute-done.17.refs_2_
  107.6 5.3 %collective-permute-start.20 = (f32[384,128]{1,0:T(8,128)S(1)}, f32[384,128]{1,0:T(8,128)S(1)}, u32[]{:S(2)}, u32[]{:S(2)}) collective-permute-start(f32[384,128]{1,0:T(8,128)S(1)} %collective-permute-done.17.refs_2_), channel_id=1, source_target_pairs={{0,22},{2,0},{4,2},{6,4},{8,6},{10,8},{12,10},{14,12},{16,14},{18,... | collective-permute-start | bytes 589832 | tf_op jit(solution)/shard_map/ppermute | solution.py:249
  113.0 1.9 %collective-permute-start.19 = (f32[384,128]{1,0:T(8,128)S(1)}, f32[384,128]{1,0:T(8,128)S(1)}, u32[]{:S(2)}, u32[]{:S(2)}) collective-permute-start(f32[384,128]{1,0:T(8,128)S(1)} %collective-permute-done.18.refs_1_), channel_id=1, source_target_pairs={{0,2},{2,4},{4,6},{6,8},{8,10},{10,12},{12,14},{14,16},{16,18},{18... | collective-permute-start | bytes 589832 | tf_op jit(solution)/shard_map/ppermute | solution.py:249
  114.9 0.7 collective-permute-done.20.refs_4_
  115.6 5.4 %collective-permute-start.22 = (f32[384,128]{1,0:T(8,128)S(1)}, f32[384,128]{1,0:T(8,128)S(1)}, u32[]{:S(2)}, u32[]{:S(2)}) collective-permute-start(f32[384,128]{1,0:T(8,128)S(1)} %collective-permute-done.20.refs_4_), channel_id=1, source_target_pairs={{0,22},{2,0},{4,2},{6,4},{8,6},{10,8},{12,10},{14,12},{16,14},{18,... | collective-permute-start | bytes 589832 | tf_op jit(solution)/shard_map/ppermute | solution.py:249
  121.0 0.0 collective-permute-done.19.refs_3_
  121.0 1.9 %collective-permute-start.21 = (f32[384,128]{1,0:T(8,128)S(1)}, f32[384,128]{1,0:T(8,128)S(1)}, u32[]{:S(2)}, u32[]{:S(2)}) collective-permute-start(f32[384,128]{1,0:T(8,128)S(1)} %collective-permute-done.19.refs_3_), channel_id=1, source_target_pairs={{0,2},{2,4},{4,6},{6,8},{8,10},{10,12},{12,14},{14,16},{16,18},{18... | collective-permute-start | bytes 589832 | tf_op jit(solution)/shard_map/ppermute | solution.py:249
  122.9 0.7 collective-permute-done.22.refs_6_
  123.6 5.0 %collective-permute-start.24 = (f32[384,128]{1,0:T(8,128)S(1)}, f32[384,128]{1,0:T(8,128)S(1)}, u32[]{:S(2)}, u32[]{:S(2)}) collective-permute-start(f32[384,128]{1,0:T(8,128)S(1)} %collective-permute-done.22.refs_6_), channel_id=1, source_target_pairs={{0,22},{2,0},{4,2},{6,4},{8,6},{10,8},{12,10},{14,12},{16,14},{18,... | collective-permute-start | bytes 589832 | tf_op jit(solution)/shard_map/ppermute | solution.py:249
  128.6 0.0 collective-permute-done.21.refs_5_
  128.6 1.9 %collective-permute-start.23 = (f32[384,128]{1,0:T(8,128)S(1)}, f32[384,128]{1,0:T(8,128)S(1)}, u32[]{:S(2)}, u32[]{:S(2)}) collective-permute-start(f32[384,128]{1,0:T(8,128)S(1)} %collective-permute-done.21.refs_5_), channel_id=1, source_target_pairs={{0,2},{2,4},{4,6},{6,8},{8,10},{10,12},{12,14},{14,16},{16,18},{18... | collective-permute-start | bytes 589832 | tf_op jit(solution)/shard_map/ppermute | solution.py:249
  130.6 0.7 collective-permute-done.24.refs_8_
  131.2 5.0 %collective-permute-start.26 = (f32[384,128]{1,0:T(8,128)S(1)}, f32[384,128]{1,0:T(8,128)S(1)}, u32[]{:S(2)}, u32[]{:S(2)}) collective-permute-start(f32[384,128]{1,0:T(8,128)S(1)} %collective-permute-done.24.refs_8_), channel_id=1, source_target_pairs={{0,22},{2,0},{4,2},{6,4},{8,6},{10,8},{12,10},{14,12},{16,14},{18,... | collective-permute-start | bytes 589832 | tf_op jit(solution)/shard_map/ppermute | solution.py:249
  136.2 0.0 collective-permute-done.23.refs_7_
  136.2 1.9 %collective-permute-start.25 = (f32[384,128]{1,0:T(8,128)S(1)}, f32[384,128]{1,0:T(8,128)S(1)}, u32[]{:S(2)}, u32[]{:S(2)}) collective-permute-start(f32[384,128]{1,0:T(8,128)S(1)} %collective-permute-done.23.refs_7_), channel_id=1, source_target_pairs={{0,2},{2,4},{4,6},{6,8},{8,10},{10,12},{12,14},{14,16},{16,18},{18... | collective-permute-start | bytes 589832 | tf_op jit(solution)/shard_map/ppermute | solution.py:249
  138.2 0.7 collective-permute-done.26.refs_10_
  138.8 10.7 %collective-permute-start.28 = (f32[384,128]{1,0:T(8,128)S(1)}, f32[384,128]{1,0:T(8,128)S(1)}, u32[]{:S(2)}, u32[]{:S(2)}) collective-permute-start(f32[384,128]{1,0:T(8,128)S(1)} %collective-permute-done.26.refs_10_), channel_id=1, source_target_pairs={{0,23},{1,22},{2,1},{3,0},{4,3},{5,2},{6,5},{7,4},{8,7},{9,6},{10,... | collective-permute-start | bytes 589832 | tf_op jit(solution)/shard_map/ppermute | solution.py:299
  149.6 1.9 %collective-permute-start.27 = (f32[384,128]{1,0:T(8,128)S(1)}, f32[384,128]{1,0:T(8,128)S(1)}, u32[]{:S(2)}, u32[]{:S(2)}) collective-permute-start(f32[384,128]{1,0:T(8,128)S(1)} %collective-permute-done.25.refs_9_), channel_id=1, source_target_pairs={{0,2},{2,4},{4,6},{6,8},{8,10},{10,12},{12,14},{14,16},{16,18},{18... | collective-permute-start | bytes 589832 | tf_op jit(solution)/shard_map/ppermute | solution.py:249
  151.5 2.0 %shard_map.64 = (f32[384,256]{1,0:T(8,128)S(1)}, f32[384,256]{1,0:T(8,128)S(1)}) custom-call(bf16[12,128,512]{2,1,0:T(8,128)(2,1)S(1)} %get-tuple-element.29.hi, bf16[12,128,512]{2,1,0:T(8,128)(2,1)S(1)} %get-tuple-element.30.lo, f32[384,128]{1,0:T(8,128)S(1)} %shard_map.62.refs_0_, f32[384,128]{1,0:T(8,128)S(1)} %collective-permute-done.18.refs_1_, ...), custom_call_target="tpu_custom_call" | custom-call | flops 1660944384 | tf_op jit(solution)/shard_map/pallas_call | solution.py:183
  153.5 2.4 %all-gather.2 = f32[768,256]{1,0:T(8,128)S(1)} all-gather(f32[384,256]{1,0:T(8,128)S(1)} %get-tuple-element.33), channel_id=4, replica_groups=mesh['xh'=2,'y'=8,'xl'=2,'z'=12,'c'=2] {'c'}, dimensions={0}, use_global_device_ids=true | all-gather | bytes 1179648 | tf_op jit(solution)/shard_map/all_gather | solution.py:205
  155.9 2.8 %collective-permute-done.27.near_block = f32[384,128]{1,0:T(8,128)S(1)} collective-permute-done((f32[384,128]{1,0:T(8,128)S(1)}, f32[384,128]{1,0:T(8,128)S(1)}, u32[]{:S(2)}, u32[]{:S(2)}) %collective-permute-start.27) | collective-permute-done | bytes 196640 | tf_op jit(solution)/shard_map/ppermute | solution.py:249
  158.8 0.3 shard_map.65
  159.1 5.8 %all-gather.3 = f32[768,128]{1,0:T(8,128)S(1)} all-gather(f32[384,128]{1,0:T(8,128)S(1)} %get-tuple-element.35), channel_id=5, replica_groups=mesh['xh'=2,'y'=8,'xl'=2,'z'=12,'c'=2] {'xl'}, dimensions={0}, use_global_device_ids=true | all-gather | bytes 589824 | tf_op jit(solution)/shard_map/all_gather | solution.py:235
  164.9 1.3 shard_map.66
  (10 shorter events, 0.0 us)
Async XLA Ops:
  7.2 76.7 %all-gather.6.cloned.1.call-start = ((), (), s32[]{:S(2)}) async-start(), calls=%async_computation | async-start | bytes 4915200 | tf_op jit(solution)/shard_map/all_gather | solution.py:280
  8.9 8.4 %collective-permute-start.8 = (f32[384,128]{1,0:T(8,128)}, f32[384,128]{1,0:T(8,128)S(1)}, u32[]{:S(2)}, u32[]{:S(2)}) collective-permute-start(f32[384,128]{1,0:T(8,128)} %shard_map.59), channel_id=1, source_target_pairs={{24,0},{384,408},{0,384},{408,24},{25,1},{385,409},{1,385},{409,25... | collective-permute-start | bytes 589832 | tf_op jit(solution)/shard_map/ppermute | solution.py:283
  14.4 9.0 %collective-permute-start = (f32[384,128]{1,0:T(8,128)}, f32[384,128]{1,0:T(8,128)S(1)}, u32[]{:S(2)}, u32[]{:S(2)}) collective-permute-start(f32[384,128]{1,0:T(8,128)} %shard_map.59), channel_id=1, source_target_pairs={{0,0},{24,384},{384,24},{408,408},{1,1},{25,385},{385,25},{409,409... | collective-permute-start | bytes 589832 | tf_op jit(solution)/shard_map/ppermute | solution.py:282
  17.3 14.5 %collective-permute-start.10 = (f32[384,128]{1,0:T(8,128)S(1)}, f32[384,128]{1,0:T(8,128)S(1)}, u32[]{:S(2)}, u32[]{:S(2)}) collective-permute-start(f32[384,128]{1,0:T(8,128)S(1)} %collective-permute-done.8.refs_8_), channel_id=1, source_target_pairs={{0,336},{48,0},{96,48},{144,96},{192,144},{240,192},{288,240},{336... | collective-permute-start | bytes 589832 | tf_op jit(solution)/shard_map/ppermute | solution.py:249
  23.4 11.8 %collective-permute-start.1 = (f32[384,128]{1,0:T(8,128)S(1)}, f32[384,128]{1,0:T(8,128)S(1)}, u32[]{:S(2)}, u32[]{:S(2)}) collective-permute-start(f32[384,128]{1,0:T(8,128)S(1)} %collective-permute-done.refs_0_), channel_id=1, source_target_pairs={{0,48},{48,96},{96,144},{144,192},{192,240},{240,288},{288,336},{3... | collective-permute-start | bytes 589832 | tf_op jit(solution)/shard_map/ppermute | solution.py:249
  25.3 11.8 %collective-permute-start.9 = (f32[384,128]{1,0:T(8,128)S(1)}, f32[384,128]{1,0:T(8,128)S(1)}, u32[]{:S(2)}, u32[]{:S(2)}) collective-permute-start(f32[384,128]{1,0:T(8,128)S(1)} %collective-permute-done.8.refs_8_), channel_id=1, source_target_pairs={{0,48},{48,96},{96,144},{144,192},{192,240},{240,288},{288,336},{3... | collective-permute-start | bytes 589832 | tf_op jit(solution)/shard_map/ppermute | solution.py:249
  27.3 11.8 %collective-permute-start.2 = (f32[384,128]{1,0:T(8,128)S(1)}, f32[384,128]{1,0:T(8,128)S(1)}, u32[]{:S(2)}, u32[]{:S(2)}) collective-permute-start(f32[384,128]{1,0:T(8,128)S(1)} %collective-permute-done.refs_0_), channel_id=1, source_target_pairs={{0,336},{48,0},{96,48},{144,96},{192,144},{240,192},{288,240},{336... | collective-permute-start | bytes 589832 | tf_op jit(solution)/shard_map/ppermute | solution.py:249
  31.8 11.8 %collective-permute-start.12 = (f32[384,128]{1,0:T(8,128)S(1)}, f32[384,128]{1,0:T(8,128)S(1)}, u32[]{:S(2)}, u32[]{:S(2)}) collective-permute-start(f32[384,128]{1,0:T(8,128)S(1)} %collective-permute-done.10.refs_10_), channel_id=1, source_target_pairs={{0,336},{48,0},{96,48},{144,96},{192,144},{240,192},{288,240},{336... | collective-permute-start | bytes 589832 | tf_op jit(solution)/shard_map/ppermute | solution.py:249
  35.2 11.8 %collective-permute-start.3 = (f32[384,128]{1,0:T(8,128)S(1)}, f32[384,128]{1,0:T(8,128)S(1)}, u32[]{:S(2)}, u32[]{:S(2)}) collective-permute-start(f32[384,128]{1,0:T(8,128)S(1)} %collective-permute-done.1.refs_1_), channel_id=1, source_target_pairs={{0,48},{48,96},{96,144},{144,192},{192,240},{240,288},{288,336},{3... | collective-permute-start | bytes 589832 | tf_op jit(solution)/shard_map/ppermute | solution.py:249
  37.2 11.8 %collective-permute-start.11 = (f32[384,128]{1,0:T(8,128)S(1)}, f32[384,128]{1,0:T(8,128)S(1)}, u32[]{:S(2)}, u32[]{:S(2)}) collective-permute-start(f32[384,128]{1,0:T(8,128)S(1)} %collective-permute-done.9.refs_9_), channel_id=1, source_target_pairs={{0,48},{48,96},{96,144},{144,192},{192,240},{240,288},{288,336},{3... | collective-permute-start | bytes 589832 | tf_op jit(solution)/shard_map/ppermute | solution.py:249
  39.1 11.8 %collective-permute-start.4 = (f32[384,128]{1,0:T(8,128)S(1)}, f32[384,128]{1,0:T(8,128)S(1)}, u32[]{:S(2)}, u32[]{:S(2)}) collective-permute-start(f32[384,128]{1,0:T(8,128)S(1)} %collective-permute-done.2.refs_2_), channel_id=1, source_target_pairs={{0,336},{48,0},{96,48},{144,96},{192,144},{240,192},{288,240},{336... | collective-permute-start | bytes 589832 | tf_op jit(solution)/shard_map/ppermute | solution.py:249
  43.7 11.8 %collective-permute-start.14 = (f32[384,128]{1,0:T(8,128)S(1)}, f32[384,128]{1,0:T(8,128)S(1)}, u32[]{:S(2)}, u32[]{:S(2)}) collective-permute-start(f32[384,128]{1,0:T(8,128)S(1)} %collective-permute-done.12.refs_12_), channel_id=1, source_target_pairs={{0,336},{48,0},{96,48},{144,96},{192,144},{240,192},{288,240},{336... | collective-permute-start | bytes 589832 | tf_op jit(solution)/shard_map/ppermute | solution.py:249
  47.1 11.8 %collective-permute-start.5 = (f32[384,128]{1,0:T(8,128)S(1)}, f32[384,128]{1,0:T(8,128)S(1)}, u32[]{:S(2)}, u32[]{:S(2)}) collective-permute-start(f32[384,128]{1,0:T(8,128)S(1)} %collective-permute-done.3.refs_3_), channel_id=1, source_target_pairs={{0,48},{48,96},{96,144},{144,192},{192,240},{240,288},{288,336},{3... | collective-permute-start | bytes 589832 | tf_op jit(solution)/shard_map/ppermute | solution.py:249
  49.0 11.8 %collective-permute-start.13 = (f32[384,128]{1,0:T(8,128)S(1)}, f32[384,128]{1,0:T(8,128)S(1)}, u32[]{:S(2)}, u32[]{:S(2)}) collective-permute-start(f32[384,128]{1,0:T(8,128)S(1)} %collective-permute-done.11.refs_11_), channel_id=1, source_target_pairs={{0,48},{48,96},{96,144},{144,192},{192,240},{240,288},{288,336},{3... | collective-permute-start | bytes 589832 | tf_op jit(solution)/shard_map/ppermute | solution.py:249
  51.0 9.9 %collective-permute-start.6 = (f32[384,128]{1,0:T(8,128)S(1)}, f32[384,128]{1,0:T(8,128)S(1)}, u32[]{:S(2)}, u32[]{:S(2)}) collective-permute-start(f32[384,128]{1,0:T(8,128)S(1)} %collective-permute-done.4.refs_4_), channel_id=1, source_target_pairs={{0,336},{48,0},{96,48},{144,96},{192,144},{240,192},{288,240},{336... | collective-permute-start | bytes 589832 | tf_op jit(solution)/shard_map/ppermute | solution.py:249
  55.5 6.9 %collective-permute-start.15 = (f32[384,128]{1,0:T(8,128)S(1)}, f32[384,128]{1,0:T(8,128)S(1)}, u32[]{:S(2)}, u32[]{:S(2)}) collective-permute-start(f32[384,128]{1,0:T(8,128)S(1)} %collective-permute-done.14.refs_14_), channel_id=1, source_target_pairs={{0,336},{48,0},{96,48},{144,96},{192,144},{240,192},{288,240},{336... | collective-permute-start | bytes 589832 | tf_op jit(solution)/shard_map/ppermute | solution.py:249
  58.9 9.7 %collective-permute-start.7 = (f32[384,128]{1,0:T(8,128)S(1)}, f32[384,128]{1,0:T(8,128)S(1)}, u32[]{:S(2)}, u32[]{:S(2)}) collective-permute-start(f32[384,128]{1,0:T(8,128)S(1)} %collective-permute-done.5.refs_5_), channel_id=1, source_target_pairs={{0,48},{48,96},{96,144},{144,192},{192,240},{240,288},{288,336},{3... | collective-permute-start | bytes 589832 | tf_op jit(solution)/shard_map/ppermute | solution.py:249
  70.4 17.8 %collective-permute-start.16 = (f32[12,128,256]{2,1,0:T(8,128)}, f32[12,128,256]{2,1,0:T(8,128)}, u32[]{:S(2)}, u32[]{:S(2)}) collective-permute-start(f32[12,128,256]{2,1,0:T(8,128)} %get-tuple-element.23), channel_id=1, source_target_pairs={{0,1},{1,0},{2,3},{3,2},{4,5},{5,4},{6,7},{7,6},{8,9},{9,8},{10,11... | collective-permute-start | bytes 4718600 | tf_op jit(solution)/shard_map/ppermute | solution.py:249
  83.8 11.7 %copy-start = (s32[6,2]{0,1:T(2,128)S(1)}, s32[6,2]{0,1:T(2,128)}, u32[]{:S(2)}) copy-start(s32[6,2]{0,1:T(2,128)} %param.7) | copy-start | bytes 148
  96.2 11.5 %collective-permute-start.17 = (f32[384,128]{1,0:T(8,128)S(1)}, f32[384,128]{1,0:T(8,128)S(1)}, u32[]{:S(2)}, u32[]{:S(2)}) collective-permute-start(f32[384,128]{1,0:T(8,128)S(1)} %shard_map.62.refs_0_), channel_id=1, source_target_pairs={{0,22},{2,0},{4,2},{6,4},{8,6},{10,8},{12,10},{14,12},{16,14},{18,... | collective-permute-start | bytes 589832 | tf_op jit(solution)/shard_map/ppermute | solution.py:249
  104.0 9.0 %collective-permute-start.18 = (f32[384,128]{1,0:T(8,128)S(1)}, f32[384,128]{1,0:T(8,128)S(1)}, u32[]{:S(2)}, u32[]{:S(2)}) collective-permute-start(f32[384,128]{1,0:T(8,128)S(1)} %shard_map.62.refs_0_), channel_id=1, source_target_pairs={{0,2},{2,4},{4,6},{6,8},{8,10},{10,12},{12,14},{14,16},{16,18},{18... | collective-permute-start | bytes 589832 | tf_op jit(solution)/shard_map/ppermute | solution.py:249
  107.6 7.9 %collective-permute-start.20 = (f32[384,128]{1,0:T(8,128)S(1)}, f32[384,128]{1,0:T(8,128)S(1)}, u32[]{:S(2)}, u32[]{:S(2)}) collective-permute-start(f32[384,128]{1,0:T(8,128)S(1)} %collective-permute-done.17.refs_2_), channel_id=1, source_target_pairs={{0,22},{2,0},{4,2},{6,4},{8,6},{10,8},{12,10},{14,12},{16,14},{18,... | collective-permute-start | bytes 589832 | tf_op jit(solution)/shard_map/ppermute | solution.py:249
  113.0 8.0 %collective-permute-start.19 = (f32[384,128]{1,0:T(8,128)S(1)}, f32[384,128]{1,0:T(8,128)S(1)}, u32[]{:S(2)}, u32[]{:S(2)}) collective-permute-start(f32[384,128]{1,0:T(8,128)S(1)} %collective-permute-done.18.refs_1_), channel_id=1, source_target_pairs={{0,2},{2,4},{4,6},{6,8},{8,10},{10,12},{12,14},{14,16},{16,18},{18... | collective-permute-start | bytes 589832 | tf_op jit(solution)/shard_map/ppermute | solution.py:249
  115.6 8.0 %collective-permute-start.22 = (f32[384,128]{1,0:T(8,128)S(1)}, f32[384,128]{1,0:T(8,128)S(1)}, u32[]{:S(2)}, u32[]{:S(2)}) collective-permute-start(f32[384,128]{1,0:T(8,128)S(1)} %collective-permute-done.20.refs_4_), channel_id=1, source_target_pairs={{0,22},{2,0},{4,2},{6,4},{8,6},{10,8},{12,10},{14,12},{16,14},{18,... | collective-permute-start | bytes 589832 | tf_op jit(solution)/shard_map/ppermute | solution.py:249
  121.0 7.6 %collective-permute-start.21 = (f32[384,128]{1,0:T(8,128)S(1)}, f32[384,128]{1,0:T(8,128)S(1)}, u32[]{:S(2)}, u32[]{:S(2)}) collective-permute-start(f32[384,128]{1,0:T(8,128)S(1)} %collective-permute-done.19.refs_3_), channel_id=1, source_target_pairs={{0,2},{2,4},{4,6},{6,8},{8,10},{10,12},{12,14},{14,16},{16,18},{18... | collective-permute-start | bytes 589832 | tf_op jit(solution)/shard_map/ppermute | solution.py:249
  123.6 7.6 %collective-permute-start.24 = (f32[384,128]{1,0:T(8,128)S(1)}, f32[384,128]{1,0:T(8,128)S(1)}, u32[]{:S(2)}, u32[]{:S(2)}) collective-permute-start(f32[384,128]{1,0:T(8,128)S(1)} %collective-permute-done.22.refs_6_), channel_id=1, source_target_pairs={{0,22},{2,0},{4,2},{6,4},{8,6},{10,8},{12,10},{14,12},{16,14},{18,... | collective-permute-start | bytes 589832 | tf_op jit(solution)/shard_map/ppermute | solution.py:249
  128.6 7.6 %collective-permute-start.23 = (f32[384,128]{1,0:T(8,128)S(1)}, f32[384,128]{1,0:T(8,128)S(1)}, u32[]{:S(2)}, u32[]{:S(2)}) collective-permute-start(f32[384,128]{1,0:T(8,128)S(1)} %collective-permute-done.21.refs_5_), channel_id=1, source_target_pairs={{0,2},{2,4},{4,6},{6,8},{8,10},{10,12},{12,14},{14,16},{16,18},{18... | collective-permute-start | bytes 589832 | tf_op jit(solution)/shard_map/ppermute | solution.py:249
  131.2 7.6 %collective-permute-start.26 = (f32[384,128]{1,0:T(8,128)S(1)}, f32[384,128]{1,0:T(8,128)S(1)}, u32[]{:S(2)}, u32[]{:S(2)}) collective-permute-start(f32[384,128]{1,0:T(8,128)S(1)} %collective-permute-done.24.refs_8_), channel_id=1, source_target_pairs={{0,22},{2,0},{4,2},{6,4},{8,6},{10,8},{12,10},{14,12},{16,14},{18,... | collective-permute-start | bytes 589832 | tf_op jit(solution)/shard_map/ppermute | solution.py:249
  136.2 13.3 %collective-permute-start.25 = (f32[384,128]{1,0:T(8,128)S(1)}, f32[384,128]{1,0:T(8,128)S(1)}, u32[]{:S(2)}, u32[]{:S(2)}) collective-permute-start(f32[384,128]{1,0:T(8,128)S(1)} %collective-permute-done.23.refs_7_), channel_id=1, source_target_pairs={{0,2},{2,4},{4,6},{6,8},{8,10},{10,12},{12,14},{14,16},{16,18},{18... | collective-permute-start | bytes 589832 | tf_op jit(solution)/shard_map/ppermute | solution.py:249
  138.8 17.1 %collective-permute-start.28 = (f32[384,128]{1,0:T(8,128)S(1)}, f32[384,128]{1,0:T(8,128)S(1)}, u32[]{:S(2)}, u32[]{:S(2)}) collective-permute-start(f32[384,128]{1,0:T(8,128)S(1)} %collective-permute-done.26.refs_10_), channel_id=1, source_target_pairs={{0,23},{1,22},{2,1},{3,0},{4,3},{5,2},{6,5},{7,4},{8,7},{9,6},{10,... | collective-permute-start | bytes 589832 | tf_op jit(solution)/shard_map/ppermute | solution.py:299
  149.6 9.2 %collective-permute-start.27 = (f32[384,128]{1,0:T(8,128)S(1)}, f32[384,128]{1,0:T(8,128)S(1)}, u32[]{:S(2)}, u32[]{:S(2)}) collective-permute-start(f32[384,128]{1,0:T(8,128)S(1)} %collective-permute-done.25.refs_9_), channel_id=1, source_target_pairs={{0,2},{2,4},{4,6},{6,8},{8,10},{10,12},{12,14},{14,16},{16,18},{18... | collective-permute-start | bytes 589832 | tf_op jit(solution)/shard_map/ppermute | solution.py:249
Sparse Core Ops, SparseCore 0:
  11.0 72.7 all-gather.5

commit v8 on v6

--- a/solution.py
+++ b/solution.py
@@ -165,7 +165,8 @@
     acc = refs[n][...] if has_acc else None
     outs = refs[n + has_acc :]
     z = lax.axis_index("z")
-    at = [lax.rem(z + (off + NZ), NZ) for off in offsets]
+    sign = 1 - 2 * lax.rem(z + lax.axis_index("c"), 2)
+    at = [lax.rem(z + sign * off + NZ, NZ) for off in offsets]
     for k in range(0, n, 2):
         a = jnp.concatenate([refs[k][...], refs[k + 1][...]], axis=1)
         bh = jnp.concatenate([hi[at[k]], hi[at[k + 1]]], axis=0)
@@ -259,6 +260,19 @@
     out = []
     for _ in range(count):
         x = shift(x, axis, step)
+        out.append(x)
+    return out
+
+
+def swaps(x, first, count):
+    out = []
+    for s in range(count):
+        pairs = []
+        for z in range(NZ):
+            for c in range(2):
+                to = z + 1 if (z + first + s + c) % 2 == 0 else z - 1
+                pairs.append((2 * z + c, 2 * (to % NZ) + c))
+        x = lax.ppermute(x, ("z", "c"), pairs)
         out.append(x)
     return out
 
@@ -294,11 +308,12 @@
     square = filtered(kept.T, (mine, other))
 
     operand = phase_rows(hi, lo, took)
-    up, down = chain(square, "z", 1, 6), chain(square, "z", -1, 5)
+    ahead, back = swaps(square, 0, 6), swaps(square, 1, 5)
     blocks = [(0, square)]
     for s in range(5):
-        blocks += [(-s - 1, up[s]), (s + 1, down[s])]
-    blocks.append((-6, up[5]))
+        off = s + 1 if s % 2 == 0 else -s - 1
+        blocks += [(off, ahead[s]), (-off, back[s])]
+    blocks.append((-6, ahead[5]))
     acc = second_product(operand, blocks[:4])
     acc = second_product(operand, blocks[4:8], acc)
     halves = join(*second_product(operand, blocks[8:], acc, last=True))

time: 173 us -> 177 us (1.023)
  blocking collectives: 22.8 us -> 25.8 us
  waiting for transfers between devices: 22.8 us -> 25.6 us
  starting transfers between devices: 98.1 us -> 95.8 us
    ppermute x26 -> x15, starting transfers between devices: 91 us -> 53.4 us  [shift(): return lax.ppermute(x, axis, [(i, (i + step) % n) for i in range(n)])]
    ppermute x0 -> x11, starting transfers between devices: none -> 35.3 us  [swaps(): x = lax.ppermute(x, ('z', 'c'), pairs)]
    ppermute x0 -> x11, waiting for transfers between devices: none -> 13.2 us  [swaps(): x = lax.ppermute(x, ('z', 'c'), pairs)]
    ppermute x26 -> x15, waiting for transfers between devices: 18.1 us -> 7.76 us  [shift(): return lax.ppermute(x, axis, [(i, (i + step) % n) for i in range(n)])]
    all_gather x1, blocking collectives: 8.65 us -> 11.4 us  [join(): both = lax.all_gather(give, 'c', axis=0)]
  transfers between devices with their start and end apart: 29 -> 29, of which waited for: 10 -> 12; matrix products, arithmetic and copies ran while one was open for 0% -> 0% of each run, Pallas kernels for 5% -> 5%
where the time goes in v8:
time: 177 us; the launch traced here: 176 us
  starting transfers between devices  95.8 us (54%)
  blocking collectives  25.8 us (15%)
  waiting for transfers between devices  25.6 us (14%)
  between operations  14.4 us (8%)
  Pallas kernels  13.9 us (8%)
    ppermute x15, starting transfers between devices, shift(): return lax.ppermute(x, axis, [(i, (i + step) % n) for i in range(n)])  53.4 us
    ppermute x11, starting transfers between devices, swaps(): x = lax.ppermute(x, ('z', 'c'), pairs)  35.3 us
    all_gather x2, blocking collectives, filtered(): pair = lax.all_gather(other, 'xl', axis=0)  14.4 us
    ppermute x11, waiting for transfers between devices, swaps(): x = lax.ppermute(x, ('z', 'c'), pairs)  13.2 us
    all_gather x1, blocking collectives, join(): both = lax.all_gather(give, 'c', axis=0)  11.4 us
    ppermute x15, waiting for transfers between devices, shift(): return lax.ppermute(x, axis, [(i, (i + step) % n) for i in range(n)])  7.76 us
    ppermute x1, starting transfers between devices, body(): far = lax.ppermute(masked, ('xh', 'xl'), [(1, 0), (2, 3), (0, 2), (3, 1)])  5.48 us
    pallas_call x1, Pallas kernels, first_product(): pl.pallas_call(first_kernel, out_shape=(block, block), in_specs=[HB, VM,...  4.38 us
  transfers between devices with their start and end apart: 29, of which 12 were waited for; matrix products, arithmetic and copies ran while one was open for 0% of the time, Pallas kernels for 5%

profile of v8, /device:TPU:1, one launch (start us, length us, event | category | flops | bytes accessed | tf_op | source)
XLA Modules:
  0.0 175.6 jit_solution(8244614002275456156)
XLA Ops:
  7.2 0.0 all-gather.6.cloned.1.call-start
  7.2 1.7 shard_map.59
  8.9 0.0 all-gather.6.cloned.1.call-update
  8.9 5.5 %collective-permute-start.8 = (f32[384,128]{1,0:T(8,128)}, f32[384,128]{1,0:T(8,128)S(1)}, u32[]{:S(2)}, u32[]{:S(2)}) collective-permute-start(f32[384,128]{1,0:T(8,128)} %shard_map.59), channel_id=1, source_target_pairs={{24,0},{384,408},{0,384},{408,24},{25,1},{385,409},{1,385},{409,25... | collective-permute-start | bytes 589832 | tf_op jit(solution)/shard_map/ppermute | solution.py:299
  14.4 1.6 collective-permute-start
  16.0 1.3 collective-permute-done.8.refs_8_
  17.3 6.1 %collective-permute-start.10 = (f32[384,128]{1,0:T(8,128)S(1)}, f32[384,128]{1,0:T(8,128)S(1)}, u32[]{:S(2)}, u32[]{:S(2)}) collective-permute-start(f32[384,128]{1,0:T(8,128)S(1)} %collective-permute-done.8.refs_8_), channel_id=1, source_target_pairs={{0,336},{48,0},{96,48},{144,96},{192,144},{240,192},{288,240},{336... | collective-permute-start | bytes 589832 | tf_op jit(solution)/shard_map/ppermute | solution.py:252
  23.4 1.9 %collective-permute-start.1 = (f32[384,128]{1,0:T(8,128)S(1)}, f32[384,128]{1,0:T(8,128)S(1)}, u32[]{:S(2)}, u32[]{:S(2)}) collective-permute-start(f32[384,128]{1,0:T(8,128)S(1)} %collective-permute-done.refs_0_), channel_id=1, source_target_pairs={{0,48},{48,96},{96,144},{144,192},{192,240},{240,288},{288,336},{3... | collective-permute-start | bytes 589832 | tf_op jit(solution)/shard_map/ppermute | solution.py:252
  25.3 1.9 %collective-permute-start.9 = (f32[384,128]{1,0:T(8,128)S(1)}, f32[384,128]{1,0:T(8,128)S(1)}, u32[]{:S(2)}, u32[]{:S(2)}) collective-permute-start(f32[384,128]{1,0:T(8,128)S(1)} %collective-permute-done.8.refs_8_), channel_id=1, source_target_pairs={{0,48},{48,96},{96,144},{144,192},{192,240},{240,288},{288,336},{3... | collective-permute-start | bytes 589832 | tf_op jit(solution)/shard_map/ppermute | solution.py:252
  27.3 4.6 %collective-permute-start.2 = (f32[384,128]{1,0:T(8,128)S(1)}, f32[384,128]{1,0:T(8,128)S(1)}, u32[]{:S(2)}, u32[]{:S(2)}) collective-permute-start(f32[384,128]{1,0:T(8,128)S(1)} %collective-permute-done.refs_0_), channel_id=1, source_target_pairs={{0,336},{48,0},{96,48},{144,96},{192,144},{240,192},{288,240},{336... | collective-permute-start | bytes 589832 | tf_op jit(solution)/shard_map/ppermute | solution.py:252
  31.8 3.4 %collective-permute-start.12 = (f32[384,128]{1,0:T(8,128)S(1)}, f32[384,128]{1,0:T(8,128)S(1)}, u32[]{:S(2)}, u32[]{:S(2)}) collective-permute-start(f32[384,128]{1,0:T(8,128)S(1)} %collective-permute-done.10.refs_10_), channel_id=1, source_target_pairs={{0,336},{48,0},{96,48},{144,96},{192,144},{240,192},{288,240},{336... | collective-permute-start | bytes 589832 | tf_op jit(solution)/shard_map/ppermute | solution.py:252
  35.2 0.0 collective-permute-done.1.refs_1_
  35.2 1.9 %collective-permute-start.3 = (f32[384,128]{1,0:T(8,128)S(1)}, f32[384,128]{1,0:T(8,128)S(1)}, u32[]{:S(2)}, u32[]{:S(2)}) collective-permute-start(f32[384,128]{1,0:T(8,128)S(1)} %collective-permute-done.1.refs_1_), channel_id=1, source_target_pairs={{0,48},{48,96},{96,144},{144,192},{192,240},{240,288},{288,336},{3... | collective-permute-start | bytes 589832 | tf_op jit(solution)/shard_map/ppermute | solution.py:252
  37.2 0.0 collective-permute-done.9.refs_9_
  37.2 1.9 %collective-permute-start.11 = (f32[384,128]{1,0:T(8,128)S(1)}, f32[384,128]{1,0:T(8,128)S(1)}, u32[]{:S(2)}, u32[]{:S(2)}) collective-permute-start(f32[384,128]{1,0:T(8,128)S(1)} %collective-permute-done.9.refs_9_), channel_id=1, source_target_pairs={{0,48},{48,96},{96,144},{144,192},{192,240},{240,288},{288,336},{3... | collective-permute-start | bytes 589832 | tf_op jit(solution)/shard_map/ppermute | solution.py:252
  39.1 4.6 %collective-permute-start.4 = (f32[384,128]{1,0:T(8,128)S(1)}, f32[384,128]{1,0:T(8,128)S(1)}, u32[]{:S(2)}, u32[]{:S(2)}) collective-permute-start(f32[384,128]{1,0:T(8,128)S(1)} %collective-permute-done.2.refs_2_), channel_id=1, source_target_pairs={{0,336},{48,0},{96,48},{144,96},{192,144},{240,192},{288,240},{336... | collective-permute-start | bytes 589832 | tf_op jit(solution)/shard_map/ppermute | solution.py:252
  43.7 0.0 collective-permute-done.12.refs_12_
  43.7 3.4 %collective-permute-start.14 = (f32[384,128]{1,0:T(8,128)S(1)}, f32[384,128]{1,0:T(8,128)S(1)}, u32[]{:S(2)}, u32[]{:S(2)}) collective-permute-start(f32[384,128]{1,0:T(8,128)S(1)} %collective-permute-done.12.refs_12_), channel_id=1, source_target_pairs={{0,336},{48,0},{96,48},{144,96},{192,144},{240,192},{288,240},{336... | collective-permute-start | bytes 589832 | tf_op jit(solution)/shard_map/ppermute | solution.py:252
  47.1 1.9 %collective-permute-start.5 = (f32[384,128]{1,0:T(8,128)S(1)}, f32[384,128]{1,0:T(8,128)S(1)}, u32[]{:S(2)}, u32[]{:S(2)}) collective-permute-start(f32[384,128]{1,0:T(8,128)S(1)} %collective-permute-done.3.refs_3_), channel_id=1, source_target_pairs={{0,48},{48,96},{96,144},{144,192},{192,240},{240,288},{288,336},{3... | collective-permute-start | bytes 589832 | tf_op jit(solution)/shard_map/ppermute | solution.py:252
  49.0 0.0 collective-permute-done.11.refs_11_
  49.0 1.9 %collective-permute-start.13 = (f32[384,128]{1,0:T(8,128)S(1)}, f32[384,128]{1,0:T(8,128)S(1)}, u32[]{:S(2)}, u32[]{:S(2)}) collective-permute-start(f32[384,128]{1,0:T(8,128)S(1)} %collective-permute-done.11.refs_11_), channel_id=1, source_target_pairs={{0,48},{48,96},{96,144},{144,192},{192,240},{240,288},{288,336},{3... | collective-permute-start | bytes 589832 | tf_op jit(solution)/shard_map/ppermute | solution.py:252
  50.9 0.0 collective-permute-done.4.refs_4_
  51.0 4.6 %collective-permute-start.6 = (f32[384,128]{1,0:T(8,128)S(1)}, f32[384,128]{1,0:T(8,128)S(1)}, u32[]{:S(2)}, u32[]{:S(2)}) collective-permute-start(f32[384,128]{1,0:T(8,128)S(1)} %collective-permute-done.4.refs_4_), channel_id=1, source_target_pairs={{0,336},{48,0},{96,48},{144,96},{192,144},{240,192},{288,240},{336... | collective-permute-start | bytes 589832 | tf_op jit(solution)/shard_map/ppermute | solution.py:252
  55.5 0.0 collective-permute-done.14.refs_14_
  55.5 3.4 %collective-permute-start.15 = (f32[384,128]{1,0:T(8,128)S(1)}, f32[384,128]{1,0:T(8,128)S(1)}, u32[]{:S(2)}, u32[]{:S(2)}) collective-permute-start(f32[384,128]{1,0:T(8,128)S(1)} %collective-permute-done.14.refs_14_), channel_id=1, source_target_pairs={{0,336},{48,0},{96,48},{144,96},{192,144},{240,192},{288,240},{336... | collective-permute-start | bytes 589832 | tf_op jit(solution)/shard_map/ppermute | solution.py:252
  58.9 0.0 collective-permute-done.5.refs_5_
  58.9 1.9 %collective-permute-start.7 = (f32[384,128]{1,0:T(8,128)S(1)}, f32[384,128]{1,0:T(8,128)S(1)}, u32[]{:S(2)}, u32[]{:S(2)}) collective-permute-start(f32[384,128]{1,0:T(8,128)S(1)} %collective-permute-done.5.refs_5_), channel_id=1, source_target_pairs={{0,48},{48,96},{96,144},{144,192},{192,240},{240,288},{288,336},{3... | collective-permute-start | bytes 589832 | tf_op jit(solution)/shard_map/ppermute | solution.py:252
  60.9 0.0 collective-permute-done.6.refs_6_
  60.9 1.6 collective-permute-done.15.refs_15_
  62.5 6.1 %collective-permute-done.7.refs_7_ = f32[384,128]{1,0:T(8,128)S(1)} collective-permute-done((f32[384,128]{1,0:T(8,128)S(1)}, f32[384,128]{1,0:T(8,128)S(1)}, u32[]{:S(2)}, u32[]{:S(2)}) %collective-permute-start.7) | collective-permute-done | bytes 196640 | tf_op jit(solution)/shard_map/ppermute | solution.py:252
  68.6 1.8 %shard_map.60 = (bf16[24,128,256]{2,1,0:T(8,128)(2,1)S(1)}, bf16[24,128,256]{2,1,0:T(8,128)(2,1)S(1)}, f32[12,128,256]{2,1,0:T(8,128)}) custom-call(f32[384,128]{1,0:T(8,128)S(1)} %collective-permute-done.refs_0_, f32[384,128]{1,0:T(8,128)S(1)} %collective-permute-done.1.refs_1_, f32[384,128]{1,0:T(8,128)S(1)} %collective-permute-done.2.refs_2_, ...), custom_call_target="tpu_custom_call" | custom-call | tf_op jit(solution)/shard_map/pallas_call | solution.py:93
  70.4 10.1 %collective-permute-start.16 = (f32[12,128,256]{2,1,0:T(8,128)}, f32[12,128,256]{2,1,0:T(8,128)}, u32[]{:S(2)}, u32[]{:S(2)}) collective-permute-start(f32[12,128,256]{2,1,0:T(8,128)} %get-tuple-element.20), channel_id=1, source_target_pairs={{0,1},{1,0},{2,3},{3,2},{4,5},{5,4},{6,7},{7,6},{8,9},{9,8},{10,11... | collective-permute-start | bytes 4718600 | tf_op jit(solution)/shard_map/ppermute | solution.py:252
  80.5 3.3 %all-gather.6.cloned.1.call-done = f32[9216,128]{1,0:T(8,128)} async-done(((f32[384,128]{1,0:T(8,128)}), f32[9216,128]{1,0:T(8,128)}) %all-gather.6.cloned.1.call-update) | async-done | bytes 4718608 | tf_op jit(solution)/shard_map/all_gather | solution.py:296
  83.8 4.4 %shard_map.61 = (f32[384,128]{1,0:T(8,128)S(1)}, f32[384,128]{1,0:T(8,128)S(1)}) custom-call(f32[24,384,128]{2,1,0:T(8,128)} %bitcast.11, bf16[24,128,256]{2,1,0:T(8,128)(2,1)S(1)} %get-tuple-element.16.hi, bf16[24,128,256]{2,1,0:T(8,128)(2,1)S(1)} %get-tuple-element.17.lo), custom_call_target="tpu_custom_call" | custom-call | flops 1811939328 | tf_op jit(solution)/shard_map/pallas_call | solution.py:147
  88.2 0.0 collective-permute-done.16.took
  88.2 7.3 %all-gather.1 = f32[768,128]{1,0:T(8,128)S(1)} all-gather(f32[384,128]{1,0:T(8,128)S(1)} %get-tuple-element.25), channel_id=3, replica_groups=mesh['xh'=2,'y'=8,'xl'=2,'z'=12,'c'=2] {'xl'}, dimensions={0}, use_global_device_ids=true | all-gather | bytes 589824 | tf_op jit(solution)/shard_map/all_gather | solution.py:238
  95.6 0.6 shard_map.63.refs_0_
  96.2 7.8 %collective-permute-start.21 = (f32[384,128]{1,0:T(8,128)S(1)}, f32[384,128]{1,0:T(8,128)S(1)}, u32[]{:S(2)}, u32[]{:S(2)}) collective-permute-start(f32[384,128]{1,0:T(8,128)S(1)} %shard_map.63.refs_0_), channel_id=1, source_target_pairs={{0,2},{1,23},{2,0},{3,5},{4,6},{5,3},{6,4},{7,9},{8,10},{9,7},{10,... | collective-permute-start | bytes 589832 | tf_op jit(solution)/shard_map/ppermute | solution.py:275
  104.0 1.9 %collective-permute-start.17 = (f32[384,128]{1,0:T(8,128)S(1)}, f32[384,128]{1,0:T(8,128)S(1)}, u32[]{:S(2)}, u32[]{:S(2)}) collective-permute-start(f32[384,128]{1,0:T(8,128)S(1)} %shard_map.63.refs_0_), channel_id=1, source_target_pairs={{0,22},{1,3},{2,4},{3,1},{4,2},{5,7},{6,8},{7,5},{8,6},{9,11},{10,... | collective-permute-start | bytes 589832 | tf_op jit(solution)/shard_map/ppermute | solution.py:275
  105.9 1.1 collective-permute-done.21.refs_1_
  107.1 2.3 %collective-permute-start.22 = (f32[384,128]{1,0:T(8,128)S(1)}, f32[384,128]{1,0:T(8,128)S(1)}, u32[]{:S(2)}, u32[]{:S(2)}) collective-permute-start(f32[384,128]{1,0:T(8,128)S(1)} %collective-permute-done.21.refs_1_), channel_id=1, source_target_pairs={{0,22},{1,3},{2,4},{3,1},{4,2},{5,7},{6,8},{7,5},{8,6},{9,11},{10,... | collective-permute-start | bytes 589832 | tf_op jit(solution)/shard_map/ppermute | solution.py:275
  109.3 1.3 collective-permute-done.17.refs_2_
  110.6 3.3 %collective-permute-start.18 = (f32[384,128]{1,0:T(8,128)S(1)}, f32[384,128]{1,0:T(8,128)S(1)}, u32[]{:S(2)}, u32[]{:S(2)}) collective-permute-start(f32[384,128]{1,0:T(8,128)S(1)} %collective-permute-done.17.refs_2_), channel_id=1, source_target_pairs={{0,2},{1,23},{2,0},{3,5},{4,6},{5,3},{6,4},{7,9},{8,10},{9,7},{10,... | collective-permute-start | bytes 589832 | tf_op jit(solution)/shard_map/ppermute | solution.py:275
  113.9 4.1 %collective-permute-start.23 = (f32[384,128]{1,0:T(8,128)S(1)}, f32[384,128]{1,0:T(8,128)S(1)}, u32[]{:S(2)}, u32[]{:S(2)}) collective-permute-start(f32[384,128]{1,0:T(8,128)S(1)} %collective-permute-done.22.refs_3_), channel_id=1, source_target_pairs={{0,2},{1,23},{2,0},{3,5},{4,6},{5,3},{6,4},{7,9},{8,10},{9,7},{10,... | collective-permute-start | bytes 589832 | tf_op jit(solution)/shard_map/ppermute | solution.py:275
  118.0 0.7 collective-permute-done.18.refs_0_
  118.7 1.9 %collective-permute-start.19 = (f32[384,128]{1,0:T(8,128)S(1)}, f32[384,128]{1,0:T(8,128)S(1)}, u32[]{:S(2)}, u32[]{:S(2)}) collective-permute-start(f32[384,128]{1,0:T(8,128)S(1)} %collective-permute-done.18.refs_0_), channel_id=1, source_target_pairs={{0,22},{1,3},{2,4},{3,1},{4,2},{5,7},{6,8},{7,5},{8,6},{9,11},{10,... | collective-permute-start | bytes 589832 | tf_op jit(solution)/shard_map/ppermute | solution.py:275
  120.7 0.8 collective-permute-done.23.refs_1_
  121.5 2.5 %collective-permute-start.24 = (f32[384,128]{1,0:T(8,128)S(1)}, f32[384,128]{1,0:T(8,128)S(1)}, u32[]{:S(2)}, u32[]{:S(2)}) collective-permute-start(f32[384,128]{1,0:T(8,128)S(1)} %collective-permute-done.23.refs_1_), channel_id=1, source_target_pairs={{0,22},{1,3},{2,4},{3,1},{4,2},{5,7},{6,8},{7,5},{8,6},{9,11},{10,... | collective-permute-start | bytes 589832 | tf_op jit(solution)/shard_map/ppermute | solution.py:275
  124.0 2.9 %collective-permute-done.19.refs_2_ = f32[384,128]{1,0:T(8,128)S(1)} collective-permute-done((f32[384,128]{1,0:T(8,128)S(1)}, f32[384,128]{1,0:T(8,128)S(1)}, u32[]{:S(2)}, u32[]{:S(2)}) %collective-permute-start.19) | collective-permute-done | bytes 196640 | tf_op jit(solution)/shard_map/ppermute | solution.py:275
  126.9 4.9 %collective-permute-start.20 = (f32[384,128]{1,0:T(8,128)S(1)}, f32[384,128]{1,0:T(8,128)S(1)}, u32[]{:S(2)}, u32[]{:S(2)}) collective-permute-start(f32[384,128]{1,0:T(8,128)S(1)} %collective-permute-done.19.refs_2_), channel_id=1, source_target_pairs={{0,2},{1,23},{2,0},{3,5},{4,6},{5,3},{6,4},{7,9},{8,10},{9,7},{10,... | collective-permute-start | bytes 589832 | tf_op jit(solution)/shard_map/ppermute | solution.py:275
  131.9 2.7 %collective-permute-start.25 = (f32[384,128]{1,0:T(8,128)S(1)}, f32[384,128]{1,0:T(8,128)S(1)}, u32[]{:S(2)}, u32[]{:S(2)}) collective-permute-start(f32[384,128]{1,0:T(8,128)S(1)} %collective-permute-done.24.refs_3_), channel_id=1, source_target_pairs={{0,2},{1,23},{2,0},{3,5},{4,6},{5,3},{6,4},{7,9},{8,10},{9,7},{10,... | collective-permute-start | bytes 589832 | tf_op jit(solution)/shard_map/ppermute | solution.py:275
  134.6 0.3 collective-permute-done.20.refs_0_
  134.9 1.9 %collective-permute-start.26 = (f32[384,128]{1,0:T(8,128)S(1)}, f32[384,128]{1,0:T(8,128)S(1)}, u32[]{:S(2)}, u32[]{:S(2)}) collective-permute-start(f32[384,128]{1,0:T(8,128)S(1)} %collective-permute-done.20.refs_0_), channel_id=1, source_target_pairs={{0,22},{1,3},{2,4},{3,1},{4,2},{5,7},{6,8},{7,5},{8,6},{9,11},{10,... | collective-permute-start | bytes 589832 | tf_op jit(solution)/shard_map/ppermute | solution.py:275
  136.8 2.7 %collective-permute-done.25.refs_1_ = f32[384,128]{1,0:T(8,128)S(1)} collective-permute-done((f32[384,128]{1,0:T(8,128)S(1)}, f32[384,128]{1,0:T(8,128)S(1)}, u32[]{:S(2)}, u32[]{:S(2)}) %collective-permute-start.25) | collective-permute-done | bytes 196640 | tf_op jit(solution)/shard_map/ppermute | solution.py:275
  139.5 1.9 %collective-permute-start.27 = (f32[384,128]{1,0:T(8,128)S(1)}, f32[384,128]{1,0:T(8,128)S(1)}, u32[]{:S(2)}, u32[]{:S(2)}) collective-permute-start(f32[384,128]{1,0:T(8,128)S(1)} %collective-permute-done.25.refs_1_), channel_id=1, source_target_pairs={{0,22},{1,3},{2,4},{3,1},{4,2},{5,7},{6,8},{7,5},{8,6},{9,11},{10,... | collective-permute-start | bytes 589832 | tf_op jit(solution)/shard_map/ppermute | solution.py:275
  141.4 1.6 shard_map.62
  143.0 0.8 shard_map.64.refs_4_
  143.9 0.8 shard_map.65.refs_4_
  144.7 3.4 %collective-permute-done.27.refs_3_ = f32[384,128]{1,0:T(8,128)S(1)} collective-permute-done((f32[384,128]{1,0:T(8,128)S(1)}, f32[384,128]{1,0:T(8,128)S(1)}, u32[]{:S(2)}, u32[]{:S(2)}) %collective-permute-start.27) | collective-permute-done | bytes 196640 | tf_op jit(solution)/shard_map/ppermute | solution.py:275
  148.1 0.8 shard_map.66
  148.9 11.4 %all-gather.2 = f32[768,256]{1,0:T(8,128)S(1)} all-gather(f32[384,256]{1,0:T(8,128)S(1)} %get-tuple-element.27), channel_id=4, replica_groups=mesh['xh'=2,'y'=8,'xl'=2,'z'=12,'c'=2] {'c'}, dimensions={0}, use_global_device_ids=true | all-gather | bytes 1179648 | tf_op jit(solution)/shard_map/all_gather | solution.py:208
  160.2 0.1 shard_map.67
  160.3 7.1 %all-gather.3 = f32[768,128]{1,0:T(8,128)S(1)} all-gather(f32[384,128]{1,0:T(8,128)S(1)} %get-tuple-element.29), channel_id=5, replica_groups=mesh['xh'=2,'y'=8,'xl'=2,'z'=12,'c'=2] {'xl'}, dimensions={0}, use_global_device_ids=true | all-gather | bytes 589824 | tf_op jit(solution)/shard_map/all_gather | solution.py:238
  167.4 1.3 shard_map.68
  (10 shorter events, 0.0 us)
Async XLA Ops:
  7.2 76.7 %all-gather.6.cloned.1.call-start = ((), (), s32[]{:S(2)}) async-start(), calls=%async_computation | async-start | bytes 4915200 | tf_op jit(solution)/shard_map/all_gather | solution.py:296
  8.9 8.4 %collective-permute-start.8 = (f32[384,128]{1,0:T(8,128)}, f32[384,128]{1,0:T(8,128)S(1)}, u32[]{:S(2)}, u32[]{:S(2)}) collective-permute-start(f32[384,128]{1,0:T(8,128)} %shard_map.59), channel_id=1, source_target_pairs={{24,0},{384,408},{0,384},{408,24},{25,1},{385,409},{1,385},{409,25... | collective-permute-start | bytes 589832 | tf_op jit(solution)/shard_map/ppermute | solution.py:299
  14.4 9.0 %collective-permute-start = (f32[384,128]{1,0:T(8,128)}, f32[384,128]{1,0:T(8,128)S(1)}, u32[]{:S(2)}, u32[]{:S(2)}) collective-permute-start(f32[384,128]{1,0:T(8,128)} %shard_map.59), channel_id=1, source_target_pairs={{0,0},{24,384},{384,24},{408,408},{1,1},{25,385},{385,25},{409,409... | collective-permute-start | bytes 589832 | tf_op jit(solution)/shard_map/ppermute | solution.py:298
  17.3 14.5 %collective-permute-start.10 = (f32[384,128]{1,0:T(8,128)S(1)}, f32[384,128]{1,0:T(8,128)S(1)}, u32[]{:S(2)}, u32[]{:S(2)}) collective-permute-start(f32[384,128]{1,0:T(8,128)S(1)} %collective-permute-done.8.refs_8_), channel_id=1, source_target_pairs={{0,336},{48,0},{96,48},{144,96},{192,144},{240,192},{288,240},{336... | collective-permute-start | bytes 589832 | tf_op jit(solution)/shard_map/ppermute | solution.py:252
  23.4 11.8 %collective-permute-start.1 = (f32[384,128]{1,0:T(8,128)S(1)}, f32[384,128]{1,0:T(8,128)S(1)}, u32[]{:S(2)}, u32[]{:S(2)}) collective-permute-start(f32[384,128]{1,0:T(8,128)S(1)} %collective-permute-done.refs_0_), channel_id=1, source_target_pairs={{0,48},{48,96},{96,144},{144,192},{192,240},{240,288},{288,336},{3... | collective-permute-start | bytes 589832 | tf_op jit(solution)/shard_map/ppermute | solution.py:252
  25.3 11.8 %collective-permute-start.9 = (f32[384,128]{1,0:T(8,128)S(1)}, f32[384,128]{1,0:T(8,128)S(1)}, u32[]{:S(2)}, u32[]{:S(2)}) collective-permute-start(f32[384,128]{1,0:T(8,128)S(1)} %collective-permute-done.8.refs_8_), channel_id=1, source_target_pairs={{0,48},{48,96},{96,144},{144,192},{192,240},{240,288},{288,336},{3... | collective-permute-start | bytes 589832 | tf_op jit(solution)/shard_map/ppermute | solution.py:252
  27.3 11.8 %collective-permute-start.2 = (f32[384,128]{1,0:T(8,128)S(1)}, f32[384,128]{1,0:T(8,128)S(1)}, u32[]{:S(2)}, u32[]{:S(2)}) collective-permute-start(f32[384,128]{1,0:T(8,128)S(1)} %collective-permute-done.refs_0_), channel_id=1, source_target_pairs={{0,336},{48,0},{96,48},{144,96},{192,144},{240,192},{288,240},{336... | collective-permute-start | bytes 589832 | tf_op jit(solution)/shard_map/ppermute | solution.py:252
  31.8 11.8 %collective-permute-start.12 = (f32[384,128]{1,0:T(8,128)S(1)}, f32[384,128]{1,0:T(8,128)S(1)}, u32[]{:S(2)}, u32[]{:S(2)}) collective-permute-start(f32[384,128]{1,0:T(8,128)S(1)} %collective-permute-done.10.refs_10_), channel_id=1, source_target_pairs={{0,336},{48,0},{96,48},{144,96},{192,144},{240,192},{288,240},{336... | collective-permute-start | bytes 589832 | tf_op jit(solution)/shard_map/ppermute | solution.py:252
  35.2 11.8 %collective-permute-start.3 = (f32[384,128]{1,0:T(8,128)S(1)}, f32[384,128]{1,0:T(8,128)S(1)}, u32[]{:S(2)}, u32[]{:S(2)}) collective-permute-start(f32[384,128]{1,0:T(8,128)S(1)} %collective-permute-done.1.refs_1_), channel_id=1, source_target_pairs={{0,48},{48,96},{96,144},{144,192},{192,240},{240,288},{288,336},{3... | collective-permute-start | bytes 589832 | tf_op jit(solution)/shard_map/ppermute | solution.py:252
  37.2 11.8 %collective-permute-start.11 = (f32[384,128]{1,0:T(8,128)S(1)}, f32[384,128]{1,0:T(8,128)S(1)}, u32[]{:S(2)}, u32[]{:S(2)}) collective-permute-start(f32[384,128]{1,0:T(8,128)S(1)} %collective-permute-done.9.refs_9_), channel_id=1, source_target_pairs={{0,48},{48,96},{96,144},{144,192},{192,240},{240,288},{288,336},{3... | collective-permute-start | bytes 589832 | tf_op jit(solution)/shard_map/ppermute | solution.py:252
  39.1 11.8 %collective-permute-start.4 = (f32[384,128]{1,0:T(8,128)S(1)}, f32[384,128]{1,0:T(8,128)S(1)}, u32[]{:S(2)}, u32[]{:S(2)}) collective-permute-start(f32[384,128]{1,0:T(8,128)S(1)} %collective-permute-done.2.refs_2_), channel_id=1, source_target_pairs={{0,336},{48,0},{96,48},{144,96},{192,144},{240,192},{288,240},{336... | collective-permute-start | bytes 589832 | tf_op jit(solution)/shard_map/ppermute | solution.py:252
  43.7 11.8 %collective-permute-start.14 = (f32[384,128]{1,0:T(8,128)S(1)}, f32[384,128]{1,0:T(8,128)S(1)}, u32[]{:S(2)}, u32[]{:S(2)}) collective-permute-start(f32[384,128]{1,0:T(8,128)S(1)} %collective-permute-done.12.refs_12_), channel_id=1, source_target_pairs={{0,336},{48,0},{96,48},{144,96},{192,144},{240,192},{288,240},{336... | collective-permute-start | bytes 589832 | tf_op jit(solution)/shard_map/ppermute | solution.py:252
  47.1 11.8 %collective-permute-start.5 = (f32[384,128]{1,0:T(8,128)S(1)}, f32[384,128]{1,0:T(8,128)S(1)}, u32[]{:S(2)}, u32[]{:S(2)}) collective-permute-start(f32[384,128]{1,0:T(8,128)S(1)} %collective-permute-done.3.refs_3_), channel_id=1, source_target_pairs={{0,48},{48,96},{96,144},{144,192},{192,240},{240,288},{288,336},{3... | collective-permute-start | bytes 589832 | tf_op jit(solution)/shard_map/ppermute | solution.py:252
  49.0 11.8 %collective-permute-start.13 = (f32[384,128]{1,0:T(8,128)S(1)}, f32[384,128]{1,0:T(8,128)S(1)}, u32[]{:S(2)}, u32[]{:S(2)}) collective-permute-start(f32[384,128]{1,0:T(8,128)S(1)} %collective-permute-done.11.refs_11_), channel_id=1, source_target_pairs={{0,48},{48,96},{96,144},{144,192},{192,240},{240,288},{288,336},{3... | collective-permute-start | bytes 589832 | tf_op jit(solution)/shard_map/ppermute | solution.py:252
  51.0 9.9 %collective-permute-start.6 = (f32[384,128]{1,0:T(8,128)S(1)}, f32[384,128]{1,0:T(8,128)S(1)}, u32[]{:S(2)}, u32[]{:S(2)}) collective-permute-start(f32[384,128]{1,0:T(8,128)S(1)} %collective-permute-done.4.refs_4_), channel_id=1, source_target_pairs={{0,336},{48,0},{96,48},{144,96},{192,144},{240,192},{288,240},{336... | collective-permute-start | bytes 589832 | tf_op jit(solution)/shard_map/ppermute | solution.py:252
  55.5 6.9 %collective-permute-start.15 = (f32[384,128]{1,0:T(8,128)S(1)}, f32[384,128]{1,0:T(8,128)S(1)}, u32[]{:S(2)}, u32[]{:S(2)}) collective-permute-start(f32[384,128]{1,0:T(8,128)S(1)} %collective-permute-done.14.refs_14_), channel_id=1, source_target_pairs={{0,336},{48,0},{96,48},{144,96},{192,144},{240,192},{288,240},{336... | collective-permute-start | bytes 589832 | tf_op jit(solution)/shard_map/ppermute | solution.py:252
  58.9 9.7 %collective-permute-start.7 = (f32[384,128]{1,0:T(8,128)S(1)}, f32[384,128]{1,0:T(8,128)S(1)}, u32[]{:S(2)}, u32[]{:S(2)}) collective-permute-start(f32[384,128]{1,0:T(8,128)S(1)} %collective-permute-done.5.refs_5_), channel_id=1, source_target_pairs={{0,48},{48,96},{96,144},{144,192},{192,240},{240,288},{288,336},{3... | collective-permute-start | bytes 589832 | tf_op jit(solution)/shard_map/ppermute | solution.py:252
  70.4 17.8 %collective-permute-start.16 = (f32[12,128,256]{2,1,0:T(8,128)}, f32[12,128,256]{2,1,0:T(8,128)}, u32[]{:S(2)}, u32[]{:S(2)}) collective-permute-start(f32[12,128,256]{2,1,0:T(8,128)} %get-tuple-element.20), channel_id=1, source_target_pairs={{0,1},{1,0},{2,3},{3,2},{4,5},{5,4},{6,7},{7,6},{8,9},{9,8},{10,11... | collective-permute-start | bytes 4718600 | tf_op jit(solution)/shard_map/ppermute | solution.py:252
  83.8 11.7 %copy-start = (s32[6,2]{0,1:T(2,128)S(1)}, s32[6,2]{0,1:T(2,128)}, u32[]{:S(2)}) copy-start(s32[6,2]{0,1:T(2,128)} %param.7) | copy-start | bytes 148
  96.2 10.9 %collective-permute-start.21 = (f32[384,128]{1,0:T(8,128)S(1)}, f32[384,128]{1,0:T(8,128)S(1)}, u32[]{:S(2)}, u32[]{:S(2)}) collective-permute-start(f32[384,128]{1,0:T(8,128)S(1)} %shard_map.63.refs_0_), channel_id=1, source_target_pairs={{0,2},{1,23},{2,0},{3,5},{4,6},{5,3},{6,4},{7,9},{8,10},{9,7},{10,... | collective-permute-start | bytes 589832 | tf_op jit(solution)/shard_map/ppermute | solution.py:275
  104.0 6.6 %collective-permute-start.17 = (f32[384,128]{1,0:T(8,128)S(1)}, f32[384,128]{1,0:T(8,128)S(1)}, u32[]{:S(2)}, u32[]{:S(2)}) collective-permute-start(f32[384,128]{1,0:T(8,128)S(1)} %shard_map.63.refs_0_), channel_id=1, source_target_pairs={{0,22},{1,3},{2,4},{3,1},{4,2},{5,7},{6,8},{7,5},{8,6},{9,11},{10,... | collective-permute-start | bytes 589832 | tf_op jit(solution)/shard_map/ppermute | solution.py:275
  107.1 6.8 %collective-permute-start.22 = (f32[384,128]{1,0:T(8,128)S(1)}, f32[384,128]{1,0:T(8,128)S(1)}, u32[]{:S(2)}, u32[]{:S(2)}) collective-permute-start(f32[384,128]{1,0:T(8,128)S(1)} %collective-permute-done.21.refs_1_), channel_id=1, source_target_pairs={{0,22},{1,3},{2,4},{3,1},{4,2},{5,7},{6,8},{7,5},{8,6},{9,11},{10,... | collective-permute-start | bytes 589832 | tf_op jit(solution)/shard_map/ppermute | solution.py:275
  110.6 8.1 %collective-permute-start.18 = (f32[384,128]{1,0:T(8,128)S(1)}, f32[384,128]{1,0:T(8,128)S(1)}, u32[]{:S(2)}, u32[]{:S(2)}) collective-permute-start(f32[384,128]{1,0:T(8,128)S(1)} %collective-permute-done.17.refs_2_), channel_id=1, source_target_pairs={{0,2},{1,23},{2,0},{3,5},{4,6},{5,3},{6,4},{7,9},{8,10},{9,7},{10,... | collective-permute-start | bytes 589832 | tf_op jit(solution)/shard_map/ppermute | solution.py:275
  113.9 7.6 %collective-permute-start.23 = (f32[384,128]{1,0:T(8,128)S(1)}, f32[384,128]{1,0:T(8,128)S(1)}, u32[]{:S(2)}, u32[]{:S(2)}) collective-permute-start(f32[384,128]{1,0:T(8,128)S(1)} %collective-permute-done.22.refs_3_), channel_id=1, source_target_pairs={{0,2},{1,23},{2,0},{3,5},{4,6},{5,3},{6,4},{7,9},{8,10},{9,7},{10,... | collective-permute-start | bytes 589832 | tf_op jit(solution)/shard_map/ppermute | solution.py:275
  118.7 8.2 %collective-permute-start.19 = (f32[384,128]{1,0:T(8,128)S(1)}, f32[384,128]{1,0:T(8,128)S(1)}, u32[]{:S(2)}, u32[]{:S(2)}) collective-permute-start(f32[384,128]{1,0:T(8,128)S(1)} %collective-permute-done.18.refs_0_), channel_id=1, source_target_pairs={{0,22},{1,3},{2,4},{3,1},{4,2},{5,7},{6,8},{7,5},{8,6},{9,11},{10,... | collective-permute-start | bytes 589832 | tf_op jit(solution)/shard_map/ppermute | solution.py:275
  121.5 10.3 %collective-permute-start.24 = (f32[384,128]{1,0:T(8,128)S(1)}, f32[384,128]{1,0:T(8,128)S(1)}, u32[]{:S(2)}, u32[]{:S(2)}) collective-permute-start(f32[384,128]{1,0:T(8,128)S(1)} %collective-permute-done.23.refs_1_), channel_id=1, source_target_pairs={{0,22},{1,3},{2,4},{3,1},{4,2},{5,7},{6,8},{7,5},{8,6},{9,11},{10,... | collective-permute-start | bytes 589832 | tf_op jit(solution)/shard_map/ppermute | solution.py:275
  126.9 8.0 %collective-permute-start.20 = (f32[384,128]{1,0:T(8,128)S(1)}, f32[384,128]{1,0:T(8,128)S(1)}, u32[]{:S(2)}, u32[]{:S(2)}) collective-permute-start(f32[384,128]{1,0:T(8,128)S(1)} %collective-permute-done.19.refs_2_), channel_id=1, source_target_pairs={{0,2},{1,23},{2,0},{3,5},{4,6},{5,3},{6,4},{7,9},{8,10},{9,7},{10,... | collective-permute-start | bytes 589832 | tf_op jit(solution)/shard_map/ppermute | solution.py:275
  131.9 7.6 %collective-permute-start.25 = (f32[384,128]{1,0:T(8,128)S(1)}, f32[384,128]{1,0:T(8,128)S(1)}, u32[]{:S(2)}, u32[]{:S(2)}) collective-permute-start(f32[384,128]{1,0:T(8,128)S(1)} %collective-permute-done.24.refs_3_), channel_id=1, source_target_pairs={{0,2},{1,23},{2,0},{3,5},{4,6},{5,3},{6,4},{7,9},{8,10},{9,7},{10,... | collective-permute-start | bytes 589832 | tf_op jit(solution)/shard_map/ppermute | solution.py:275
  134.9 9.8 %collective-permute-start.26 = (f32[384,128]{1,0:T(8,128)S(1)}, f32[384,128]{1,0:T(8,128)S(1)}, u32[]{:S(2)}, u32[]{:S(2)}) collective-permute-start(f32[384,128]{1,0:T(8,128)S(1)} %collective-permute-done.20.refs_0_), channel_id=1, source_target_pairs={{0,22},{1,3},{2,4},{3,1},{4,2},{5,7},{6,8},{7,5},{8,6},{9,11},{10,... | collective-permute-start | bytes 589832 | tf_op jit(solution)/shard_map/ppermute | solution.py:275
  139.5 8.6 %collective-permute-start.27 = (f32[384,128]{1,0:T(8,128)S(1)}, f32[384,128]{1,0:T(8,128)S(1)}, u32[]{:S(2)}, u32[]{:S(2)}) collective-permute-start(f32[384,128]{1,0:T(8,128)S(1)} %collective-permute-done.25.refs_1_), channel_id=1, source_target_pairs={{0,22},{1,3},{2,4},{3,1},{4,2},{5,7},{6,8},{7,5},{8,6},{9,11},{10,... | collective-permute-start | bytes 589832 | tf_op jit(solution)/shard_map/ppermute | solution.py:275
Sparse Core Ops, SparseCore 0:
  11.0 72.7 all-gather.5

commit v9 on v6

--- a/solution.py
+++ b/solution.py
@@ -294,11 +294,12 @@
     square = filtered(kept.T, (mine, other))
 
     operand = phase_rows(hi, lo, took)
-    up, down = chain(square, "z", 1, 6), chain(square, "z", -1, 5)
+    away = shift(square, "z", 6)
+    up, down = chain(square, "z", 1, 4), chain(square, "z", -1, 4)
     blocks = [(0, square)]
-    for s in range(5):
+    for s in range(3):
         blocks += [(-s - 1, up[s]), (s + 1, down[s])]
-    blocks.append((-6, up[5]))
+    blocks += [(6, away), (-4, up[3]), (4, down[3]), (5, shift(away, "z", 1)), (-5, shift(away, "z", -1))]
     acc = second_product(operand, blocks[:4])
     acc = second_product(operand, blocks[4:8], acc)
     halves = join(*second_product(operand, blocks[8:], acc, last=True))

time: 173 us -> 174 us (level)
  waiting for transfers between devices: 22.8 us -> 27.4 us
  blocking collectives: 22.8 us -> 18.7 us
    ppermute x26, waiting for transfers between devices: 18.1 us -> 22.7 us  [shift(): return lax.ppermute(x, axis, [(i, (i + step) % n) for i in range(n)])]
    all_gather x1, blocking collectives: 8.65 us -> 4.57 us  [join(): both = lax.all_gather(give, 'c', axis=0)]
  transfers between devices with their start and end apart: 29 -> 29, of which waited for: 10 -> 6; matrix products, arithmetic and copies ran while one was open for 0% -> 0% of each run, Pallas kernels for 5% -> 5%
where the time goes in v9:
time: 174 us; the launch traced here: 173 us
  starting transfers between devices  99 us (57%)
  waiting for transfers between devices  27.4 us (16%)
  blocking collectives  18.7 us (11%)
  between operations  14.5 us (8%)
  Pallas kernels  13.9 us (8%)
    ppermute x26, starting transfers between devices, shift(): return lax.ppermute(x, axis, [(i, (i + step) % n) for i in range(n)])  91.9 us
    ppermute x26, waiting for transfers between devices, shift(): return lax.ppermute(x, axis, [(i, (i + step) % n) for i in range(n)])  22.7 us
    all_gather x2, blocking collectives, filtered(): pair = lax.all_gather(other, 'xl', axis=0)  14.1 us
    ppermute x1, starting transfers between devices, body(): far = lax.ppermute(masked, ('xh', 'xl'), [(1, 0), (2, 3), (0, 2), (3, 1)])  5.48 us
    all_gather x1, blocking collectives, join(): both = lax.all_gather(give, 'c', axis=0)  4.57 us
    pallas_call x1, Pallas kernels, first_product(): pl.pallas_call(first_kernel, out_shape=(block, block), in_specs=[HB, VM,...  4.38 us
  transfers between devices with their start and end apart: 29, of which 6 were waited for; matrix products, arithmetic and copies ran while one was open for 0% of the time, Pallas kernels for 5%

profile of v9, /device:TPU:1, one launch (start us, length us, event | category | flops | bytes accessed | tf_op | source)
XLA Modules:
  0.0 173.4 jit_solution(9682290768474059626)
XLA Ops:
  7.2 0.0 all-gather.6.cloned.1.call-start
  7.2 1.7 shard_map.59
  8.9 0.0 all-gather.6.cloned.1.call-update
  8.9 5.5 %collective-permute-start.8 = (f32[384,128]{1,0:T(8,128)}, f32[384,128]{1,0:T(8,128)S(1)}, u32[]{:S(2)}, u32[]{:S(2)}) collective-permute-start(f32[384,128]{1,0:T(8,128)} %shard_map.59), channel_id=1, source_target_pairs={{24,0},{384,408},{0,384},{408,24},{25,1},{385,409},{1,385},{409,25... | collective-permute-start | bytes 589832 | tf_op jit(solution)/shard_map/ppermute | solution.py:285
  14.4 1.6 collective-permute-start
  16.0 1.3 collective-permute-done.8.refs_8_
  17.3 6.1 %collective-permute-start.10 = (f32[384,128]{1,0:T(8,128)S(1)}, f32[384,128]{1,0:T(8,128)S(1)}, u32[]{:S(2)}, u32[]{:S(2)}) collective-permute-start(f32[384,128]{1,0:T(8,128)S(1)} %collective-permute-done.8.refs_8_), channel_id=1, source_target_pairs={{0,336},{48,0},{96,48},{144,96},{192,144},{240,192},{288,240},{336... | collective-permute-start | bytes 589832 | tf_op jit(solution)/shard_map/ppermute | solution.py:251
  23.4 1.9 %collective-permute-start.1 = (f32[384,128]{1,0:T(8,128)S(1)}, f32[384,128]{1,0:T(8,128)S(1)}, u32[]{:S(2)}, u32[]{:S(2)}) collective-permute-start(f32[384,128]{1,0:T(8,128)S(1)} %collective-permute-done.refs_0_), channel_id=1, source_target_pairs={{0,48},{48,96},{96,144},{144,192},{192,240},{240,288},{288,336},{3... | collective-permute-start | bytes 589832 | tf_op jit(solution)/shard_map/ppermute | solution.py:251
  25.3 1.9 %collective-permute-start.9 = (f32[384,128]{1,0:T(8,128)S(1)}, f32[384,128]{1,0:T(8,128)S(1)}, u32[]{:S(2)}, u32[]{:S(2)}) collective-permute-start(f32[384,128]{1,0:T(8,128)S(1)} %collective-permute-done.8.refs_8_), channel_id=1, source_target_pairs={{0,48},{48,96},{96,144},{144,192},{192,240},{240,288},{288,336},{3... | collective-permute-start | bytes 589832 | tf_op jit(solution)/shard_map/ppermute | solution.py:251
  27.3 4.6 %collective-permute-start.2 = (f32[384,128]{1,0:T(8,128)S(1)}, f32[384,128]{1,0:T(8,128)S(1)}, u32[]{:S(2)}, u32[]{:S(2)}) collective-permute-start(f32[384,128]{1,0:T(8,128)S(1)} %collective-permute-done.refs_0_), channel_id=1, source_target_pairs={{0,336},{48,0},{96,48},{144,96},{192,144},{240,192},{288,240},{336... | collective-permute-start | bytes 589832 | tf_op jit(solution)/shard_map/ppermute | solution.py:251
  31.8 3.4 %collective-permute-start.12 = (f32[384,128]{1,0:T(8,128)S(1)}, f32[384,128]{1,0:T(8,128)S(1)}, u32[]{:S(2)}, u32[]{:S(2)}) collective-permute-start(f32[384,128]{1,0:T(8,128)S(1)} %collective-permute-done.10.refs_10_), channel_id=1, source_target_pairs={{0,336},{48,0},{96,48},{144,96},{192,144},{240,192},{288,240},{336... | collective-permute-start | bytes 589832 | tf_op jit(solution)/shard_map/ppermute | solution.py:251
  35.2 0.0 collective-permute-done.1.refs_1_
  35.2 1.9 %collective-permute-start.3 = (f32[384,128]{1,0:T(8,128)S(1)}, f32[384,128]{1,0:T(8,128)S(1)}, u32[]{:S(2)}, u32[]{:S(2)}) collective-permute-start(f32[384,128]{1,0:T(8,128)S(1)} %collective-permute-done.1.refs_1_), channel_id=1, source_target_pairs={{0,48},{48,96},{96,144},{144,192},{192,240},{240,288},{288,336},{3... | collective-permute-start | bytes 589832 | tf_op jit(solution)/shard_map/ppermute | solution.py:251
  37.2 0.0 collective-permute-done.9.refs_9_
  37.2 1.9 %collective-permute-start.11 = (f32[384,128]{1,0:T(8,128)S(1)}, f32[384,128]{1,0:T(8,128)S(1)}, u32[]{:S(2)}, u32[]{:S(2)}) collective-permute-start(f32[384,128]{1,0:T(8,128)S(1)} %collective-permute-done.9.refs_9_), channel_id=1, source_target_pairs={{0,48},{48,96},{96,144},{144,192},{192,240},{240,288},{288,336},{3... | collective-permute-start | bytes 589832 | tf_op jit(solution)/shard_map/ppermute | solution.py:251
  39.1 4.6 %collective-permute-start.4 = (f32[384,128]{1,0:T(8,128)S(1)}, f32[384,128]{1,0:T(8,128)S(1)}, u32[]{:S(2)}, u32[]{:S(2)}) collective-permute-start(f32[384,128]{1,0:T(8,128)S(1)} %collective-permute-done.2.refs_2_), channel_id=1, source_target_pairs={{0,336},{48,0},{96,48},{144,96},{192,144},{240,192},{288,240},{336... | collective-permute-start | bytes 589832 | tf_op jit(solution)/shard_map/ppermute | solution.py:251
  43.7 0.0 collective-permute-done.12.refs_12_
  43.7 3.4 %collective-permute-start.14 = (f32[384,128]{1,0:T(8,128)S(1)}, f32[384,128]{1,0:T(8,128)S(1)}, u32[]{:S(2)}, u32[]{:S(2)}) collective-permute-start(f32[384,128]{1,0:T(8,128)S(1)} %collective-permute-done.12.refs_12_), channel_id=1, source_target_pairs={{0,336},{48,0},{96,48},{144,96},{192,144},{240,192},{288,240},{336... | collective-permute-start | bytes 589832 | tf_op jit(solution)/shard_map/ppermute | solution.py:251
  47.1 1.9 %collective-permute-start.5 = (f32[384,128]{1,0:T(8,128)S(1)}, f32[384,128]{1,0:T(8,128)S(1)}, u32[]{:S(2)}, u32[]{:S(2)}) collective-permute-start(f32[384,128]{1,0:T(8,128)S(1)} %collective-permute-done.3.refs_3_), channel_id=1, source_target_pairs={{0,48},{48,96},{96,144},{144,192},{192,240},{240,288},{288,336},{3... | collective-permute-start | bytes 589832 | tf_op jit(solution)/shard_map/ppermute | solution.py:251
  49.0 0.0 collective-permute-done.11.refs_11_
  49.0 1.9 %collective-permute-start.13 = (f32[384,128]{1,0:T(8,128)S(1)}, f32[384,128]{1,0:T(8,128)S(1)}, u32[]{:S(2)}, u32[]{:S(2)}) collective-permute-start(f32[384,128]{1,0:T(8,128)S(1)} %collective-permute-done.11.refs_11_), channel_id=1, source_target_pairs={{0,48},{48,96},{96,144},{144,192},{192,240},{240,288},{288,336},{3... | collective-permute-start | bytes 589832 | tf_op jit(solution)/shard_map/ppermute | solution.py:251
  50.9 0.0 collective-permute-done.4.refs_4_
  51.0 4.6 %collective-permute-start.6 = (f32[384,128]{1,0:T(8,128)S(1)}, f32[384,128]{1,0:T(8,128)S(1)}, u32[]{:S(2)}, u32[]{:S(2)}) collective-permute-start(f32[384,128]{1,0:T(8,128)S(1)} %collective-permute-done.4.refs_4_), channel_id=1, source_target_pairs={{0,336},{48,0},{96,48},{144,96},{192,144},{240,192},{288,240},{336... | collective-permute-start | bytes 589832 | tf_op jit(solution)/shard_map/ppermute | solution.py:251
  55.5 0.0 collective-permute-done.14.refs_14_
  55.5 3.4 %collective-permute-start.15 = (f32[384,128]{1,0:T(8,128)S(1)}, f32[384,128]{1,0:T(8,128)S(1)}, u32[]{:S(2)}, u32[]{:S(2)}) collective-permute-start(f32[384,128]{1,0:T(8,128)S(1)} %collective-permute-done.14.refs_14_), channel_id=1, source_target_pairs={{0,336},{48,0},{96,48},{144,96},{192,144},{240,192},{288,240},{336... | collective-permute-start | bytes 589832 | tf_op jit(solution)/shard_map/ppermute | solution.py:251
  58.9 0.0 collective-permute-done.5.refs_5_
  58.9 1.9 %collective-permute-start.7 = (f32[384,128]{1,0:T(8,128)S(1)}, f32[384,128]{1,0:T(8,128)S(1)}, u32[]{:S(2)}, u32[]{:S(2)}) collective-permute-start(f32[384,128]{1,0:T(8,128)S(1)} %collective-permute-done.5.refs_5_), channel_id=1, source_target_pairs={{0,48},{48,96},{96,144},{144,192},{192,240},{240,288},{288,336},{3... | collective-permute-start | bytes 589832 | tf_op jit(solution)/shard_map/ppermute | solution.py:251
  60.9 0.0 collective-permute-done.6.refs_6_
  60.9 1.6 collective-permute-done.15.refs_15_
  62.5 6.1 %collective-permute-done.7.refs_7_ = f32[384,128]{1,0:T(8,128)S(1)} collective-permute-done((f32[384,128]{1,0:T(8,128)S(1)}, f32[384,128]{1,0:T(8,128)S(1)}, u32[]{:S(2)}, u32[]{:S(2)}) %collective-permute-start.7) | collective-permute-done | bytes 196640 | tf_op jit(solution)/shard_map/ppermute | solution.py:251
  68.6 1.8 %shard_map.60 = (bf16[24,128,256]{2,1,0:T(8,128)(2,1)S(1)}, bf16[24,128,256]{2,1,0:T(8,128)(2,1)S(1)}, f32[12,128,256]{2,1,0:T(8,128)}) custom-call(f32[384,128]{1,0:T(8,128)S(1)} %collective-permute-done.refs_0_, f32[384,128]{1,0:T(8,128)S(1)} %collective-permute-done.1.refs_1_, f32[384,128]{1,0:T(8,128)S(1)} %collective-permute-done.2.refs_2_, ...), custom_call_target="tpu_custom_call" | custom-call | tf_op jit(solution)/shard_map/pallas_call | solution.py:93
  70.4 10.1 %collective-permute-start.16 = (f32[12,128,256]{2,1,0:T(8,128)}, f32[12,128,256]{2,1,0:T(8,128)}, u32[]{:S(2)}, u32[]{:S(2)}) collective-permute-start(f32[12,128,256]{2,1,0:T(8,128)} %get-tuple-element.20), channel_id=1, source_target_pairs={{0,1},{1,0},{2,3},{3,2},{4,5},{5,4},{6,7},{7,6},{8,9},{9,8},{10,11... | collective-permute-start | bytes 4718600 | tf_op jit(solution)/shard_map/ppermute | solution.py:251
  80.5 3.3 %all-gather.6.cloned.1.call-done = f32[9216,128]{1,0:T(8,128)} async-done(((f32[384,128]{1,0:T(8,128)}), f32[9216,128]{1,0:T(8,128)}) %all-gather.6.cloned.1.call-update) | async-done | bytes 4718608 | tf_op jit(solution)/shard_map/all_gather | solution.py:282
  83.8 4.4 %shard_map.61 = (f32[384,128]{1,0:T(8,128)S(1)}, f32[384,128]{1,0:T(8,128)S(1)}) custom-call(f32[24,384,128]{2,1,0:T(8,128)} %bitcast.11, bf16[24,128,256]{2,1,0:T(8,128)(2,1)S(1)} %get-tuple-element.16.hi, bf16[24,128,256]{2,1,0:T(8,128)(2,1)S(1)} %get-tuple-element.17.lo), custom_call_target="tpu_custom_call" | custom-call | flops 1811939328 | tf_op jit(solution)/shard_map/pallas_call | solution.py:147
  88.2 0.0 collective-permute-done.16.took
  88.2 7.3 %all-gather.1 = f32[768,128]{1,0:T(8,128)S(1)} all-gather(f32[384,128]{1,0:T(8,128)S(1)} %get-tuple-element.25), channel_id=3, replica_groups=mesh['xh'=2,'y'=8,'xl'=2,'z'=12,'c'=2] {'xl'}, dimensions={0}, use_global_device_ids=true | all-gather | bytes 589824 | tf_op jit(solution)/shard_map/all_gather | solution.py:237
  95.6 0.6 shard_map.63.refs_0_
  96.2 1.9 %collective-permute-start.17 = (f32[384,128]{1,0:T(8,128)S(1)}, f32[384,128]{1,0:T(8,128)S(1)}, u32[]{:S(2)}, u32[]{:S(2)}) collective-permute-start(f32[384,128]{1,0:T(8,128)S(1)} %shard_map.63.refs_0_), channel_id=1, source_target_pairs={{0,2},{2,4},{4,6},{6,8},{8,10},{10,12},{12,14},{14,16},{16,18},{18... | collective-permute-start | bytes 589832 | tf_op jit(solution)/shard_map/ppermute | solution.py:251
  98.1 7.8 %collective-permute-start.21 = (f32[384,128]{1,0:T(8,128)S(1)}, f32[384,128]{1,0:T(8,128)S(1)}, u32[]{:S(2)}, u32[]{:S(2)}) collective-permute-start(f32[384,128]{1,0:T(8,128)S(1)} %shard_map.63.refs_0_), channel_id=1, source_target_pairs={{0,22},{2,0},{4,2},{6,4},{8,6},{10,8},{12,10},{14,12},{16,14},{18,... | collective-permute-start | bytes 589832 | tf_op jit(solution)/shard_map/ppermute | solution.py:251
  105.9 2.8 %collective-permute-done.17.refs_1_ = f32[384,128]{1,0:T(8,128)S(1)} collective-permute-done((f32[384,128]{1,0:T(8,128)S(1)}, f32[384,128]{1,0:T(8,128)S(1)}, u32[]{:S(2)}, u32[]{:S(2)}) %collective-permute-start.17) | collective-permute-done | bytes 196640 | tf_op jit(solution)/shard_map/ppermute | solution.py:251
  108.7 1.9 %collective-permute-start.18 = (f32[384,128]{1,0:T(8,128)S(1)}, f32[384,128]{1,0:T(8,128)S(1)}, u32[]{:S(2)}, u32[]{:S(2)}) collective-permute-start(f32[384,128]{1,0:T(8,128)S(1)} %collective-permute-done.17.refs_1_), channel_id=1, source_target_pairs={{0,2},{2,4},{4,6},{6,8},{8,10},{10,12},{12,14},{14,16},{16,18},{18... | collective-permute-start | bytes 589832 | tf_op jit(solution)/shard_map/ppermute | solution.py:251
  110.6 0.0 collective-permute-done.21.refs_2_
  110.6 4.6 %collective-permute-start.22 = (f32[384,128]{1,0:T(8,128)S(1)}, f32[384,128]{1,0:T(8,128)S(1)}, u32[]{:S(2)}, u32[]{:S(2)}) collective-permute-start(f32[384,128]{1,0:T(8,128)S(1)} %collective-permute-done.21.refs_2_), channel_id=1, source_target_pairs={{0,22},{2,0},{4,2},{6,4},{8,6},{10,8},{12,10},{14,12},{16,14},{18,... | collective-permute-start | bytes 589832 | tf_op jit(solution)/shard_map/ppermute | solution.py:251
  115.2 2.7 %collective-permute-start.25 = (f32[384,128]{1,0:T(8,128)S(1)}, f32[384,128]{1,0:T(8,128)S(1)}, u32[]{:S(2)}, u32[]{:S(2)}) collective-permute-start(f32[384,128]{1,0:T(8,128)S(1)} %shard_map.63.refs_0_), channel_id=1, source_target_pairs={{0,12},{2,14},{4,16},{6,18},{8,20},{10,22},{12,0},{14,2},{16,4},{1... | collective-permute-start | bytes 589832 | tf_op jit(solution)/shard_map/ppermute | solution.py:251
  118.0 3.7 %collective-permute-start.19 = (f32[384,128]{1,0:T(8,128)S(1)}, f32[384,128]{1,0:T(8,128)S(1)}, u32[]{:S(2)}, u32[]{:S(2)}) collective-permute-start(f32[384,128]{1,0:T(8,128)S(1)} %collective-permute-done.18.refs_3_), channel_id=1, source_target_pairs={{0,2},{2,4},{4,6},{6,8},{8,10},{10,12},{12,14},{14,16},{16,18},{18... | collective-permute-start | bytes 589832 | tf_op jit(solution)/shard_map/ppermute | solution.py:251
  121.7 0.0 collective-permute-done.22.refs_0_
  121.7 2.8 %collective-permute-start.23 = (f32[384,128]{1,0:T(8,128)S(1)}, f32[384,128]{1,0:T(8,128)S(1)}, u32[]{:S(2)}, u32[]{:S(2)}) collective-permute-start(f32[384,128]{1,0:T(8,128)S(1)} %collective-permute-done.22.refs_0_), channel_id=1, source_target_pairs={{0,22},{2,0},{4,2},{6,4},{8,6},{10,8},{12,10},{14,12},{16,14},{18,... | collective-permute-start | bytes 589832 | tf_op jit(solution)/shard_map/ppermute | solution.py:251
  124.5 12.2 %collective-permute-done.25.refs_3_ = f32[384,128]{1,0:T(8,128)S(1)} collective-permute-done((f32[384,128]{1,0:T(8,128)S(1)}, f32[384,128]{1,0:T(8,128)S(1)}, u32[]{:S(2)}, u32[]{:S(2)}) %collective-permute-start.25) | collective-permute-done | bytes 196640 | tf_op jit(solution)/shard_map/ppermute | solution.py:251
  136.7 1.9 %collective-permute-start.26 = (f32[384,128]{1,0:T(8,128)S(1)}, f32[384,128]{1,0:T(8,128)S(1)}, u32[]{:S(2)}, u32[]{:S(2)}) collective-permute-start(f32[384,128]{1,0:T(8,128)S(1)} %collective-permute-done.25.refs_3_), channel_id=1, source_target_pairs={{0,2},{2,4},{4,6},{6,8},{8,10},{10,12},{12,14},{14,16},{16,18},{18... | collective-permute-start | bytes 589832 | tf_op jit(solution)/shard_map/ppermute | solution.py:251
  138.6 4.6 %collective-permute-start.27 = (f32[384,128]{1,0:T(8,128)S(1)}, f32[384,128]{1,0:T(8,128)S(1)}, u32[]{:S(2)}, u32[]{:S(2)}) collective-permute-start(f32[384,128]{1,0:T(8,128)S(1)} %collective-permute-done.25.refs_3_), channel_id=1, source_target_pairs={{0,22},{2,0},{4,2},{6,4},{8,6},{10,8},{12,10},{14,12},{16,14},{18,... | collective-permute-start | bytes 589832 | tf_op jit(solution)/shard_map/ppermute | solution.py:251
  143.2 0.0 collective-permute-done.19.refs_1_
  143.2 1.9 %collective-permute-start.20 = (f32[384,128]{1,0:T(8,128)S(1)}, f32[384,128]{1,0:T(8,128)S(1)}, u32[]{:S(2)}, u32[]{:S(2)}) collective-permute-start(f32[384,128]{1,0:T(8,128)S(1)} %collective-permute-done.19.refs_1_), channel_id=1, source_target_pairs={{0,2},{2,4},{4,6},{6,8},{8,10},{10,12},{12,14},{14,16},{16,18},{18... | collective-permute-start | bytes 589832 | tf_op jit(solution)/shard_map/ppermute | solution.py:251
  145.1 0.0 collective-permute-done.23.refs_2_
  145.1 4.6 %collective-permute-start.24 = (f32[384,128]{1,0:T(8,128)S(1)}, f32[384,128]{1,0:T(8,128)S(1)}, u32[]{:S(2)}, u32[]{:S(2)}) collective-permute-start(f32[384,128]{1,0:T(8,128)S(1)} %collective-permute-done.23.refs_2_), channel_id=1, source_target_pairs={{0,22},{2,0},{4,2},{6,4},{8,6},{10,8},{12,10},{14,12},{16,14},{18,... | collective-permute-start | bytes 589832 | tf_op jit(solution)/shard_map/ppermute | solution.py:251
  149.7 1.6 shard_map.62
  151.4 0.8 shard_map.64.refs_4_
  152.2 0.8 shard_map.65.refs_4_
  153.0 0.0 collective-permute-done.26.refs_2_
  153.0 0.0 collective-permute-done.27.refs_3_
  153.0 0.8 shard_map.66
  153.8 4.6 %all-gather.2 = f32[768,256]{1,0:T(8,128)S(1)} all-gather(f32[384,256]{1,0:T(8,128)S(1)} %get-tuple-element.27), channel_id=4, replica_groups=mesh['xh'=2,'y'=8,'xl'=2,'z'=12,'c'=2] {'c'}, dimensions={0}, use_global_device_ids=true | all-gather | bytes 1179648 | tf_op jit(solution)/shard_map/all_gather | solution.py:207
  158.4 0.1 shard_map.67
  158.5 6.8 %all-gather.3 = f32[768,128]{1,0:T(8,128)S(1)} all-gather(f32[384,128]{1,0:T(8,128)S(1)} %get-tuple-element.29), channel_id=5, replica_groups=mesh['xh'=2,'y'=8,'xl'=2,'z'=12,'c'=2] {'xl'}, dimensions={0}, use_global_device_ids=true | all-gather | bytes 589824 | tf_op jit(solution)/shard_map/all_gather | solution.py:237
  165.3 1.3 shard_map.68
  (10 shorter events, 0.0 us)
Async XLA Ops:
  7.2 76.7 %all-gather.6.cloned.1.call-start = ((), (), s32[]{:S(2)}) async-start(), calls=%async_computation | async-start | bytes 4915200 | tf_op jit(solution)/shard_map/all_gather | solution.py:282
  8.9 8.4 %collective-permute-start.8 = (f32[384,128]{1,0:T(8,128)}, f32[384,128]{1,0:T(8,128)S(1)}, u32[]{:S(2)}, u32[]{:S(2)}) collective-permute-start(f32[384,128]{1,0:T(8,128)} %shard_map.59), channel_id=1, source_target_pairs={{24,0},{384,408},{0,384},{408,24},{25,1},{385,409},{1,385},{409,25... | collective-permute-start | bytes 589832 | tf_op jit(solution)/shard_map/ppermute | solution.py:285
  14.4 9.0 %collective-permute-start = (f32[384,128]{1,0:T(8,128)}, f32[384,128]{1,0:T(8,128)S(1)}, u32[]{:S(2)}, u32[]{:S(2)}) collective-permute-start(f32[384,128]{1,0:T(8,128)} %shard_map.59), channel_id=1, source_target_pairs={{0,0},{24,384},{384,24},{408,408},{1,1},{25,385},{385,25},{409,409... | collective-permute-start | bytes 589832 | tf_op jit(solution)/shard_map/ppermute | solution.py:284
  17.3 14.5 %collective-permute-start.10 = (f32[384,128]{1,0:T(8,128)S(1)}, f32[384,128]{1,0:T(8,128)S(1)}, u32[]{:S(2)}, u32[]{:S(2)}) collective-permute-start(f32[384,128]{1,0:T(8,128)S(1)} %collective-permute-done.8.refs_8_), channel_id=1, source_target_pairs={{0,336},{48,0},{96,48},{144,96},{192,144},{240,192},{288,240},{336... | collective-permute-start | bytes 589832 | tf_op jit(solution)/shard_map/ppermute | solution.py:251
  23.4 11.8 %collective-permute-start.1 = (f32[384,128]{1,0:T(8,128)S(1)}, f32[384,128]{1,0:T(8,128)S(1)}, u32[]{:S(2)}, u32[]{:S(2)}) collective-permute-start(f32[384,128]{1,0:T(8,128)S(1)} %collective-permute-done.refs_0_), channel_id=1, source_target_pairs={{0,48},{48,96},{96,144},{144,192},{192,240},{240,288},{288,336},{3... | collective-permute-start | bytes 589832 | tf_op jit(solution)/shard_map/ppermute | solution.py:251
  25.3 11.8 %collective-permute-start.9 = (f32[384,128]{1,0:T(8,128)S(1)}, f32[384,128]{1,0:T(8,128)S(1)}, u32[]{:S(2)}, u32[]{:S(2)}) collective-permute-start(f32[384,128]{1,0:T(8,128)S(1)} %collective-permute-done.8.refs_8_), channel_id=1, source_target_pairs={{0,48},{48,96},{96,144},{144,192},{192,240},{240,288},{288,336},{3... | collective-permute-start | bytes 589832 | tf_op jit(solution)/shard_map/ppermute | solution.py:251
  27.3 11.8 %collective-permute-start.2 = (f32[384,128]{1,0:T(8,128)S(1)}, f32[384,128]{1,0:T(8,128)S(1)}, u32[]{:S(2)}, u32[]{:S(2)}) collective-permute-start(f32[384,128]{1,0:T(8,128)S(1)} %collective-permute-done.refs_0_), channel_id=1, source_target_pairs={{0,336},{48,0},{96,48},{144,96},{192,144},{240,192},{288,240},{336... | collective-permute-start | bytes 589832 | tf_op jit(solution)/shard_map/ppermute | solution.py:251
  31.8 11.8 %collective-permute-start.12 = (f32[384,128]{1,0:T(8,128)S(1)}, f32[384,128]{1,0:T(8,128)S(1)}, u32[]{:S(2)}, u32[]{:S(2)}) collective-permute-start(f32[384,128]{1,0:T(8,128)S(1)} %collective-permute-done.10.refs_10_), channel_id=1, source_target_pairs={{0,336},{48,0},{96,48},{144,96},{192,144},{240,192},{288,240},{336... | collective-permute-start | bytes 589832 | tf_op jit(solution)/shard_map/ppermute | solution.py:251
  35.2 11.8 %collective-permute-start.3 = (f32[384,128]{1,0:T(8,128)S(1)}, f32[384,128]{1,0:T(8,128)S(1)}, u32[]{:S(2)}, u32[]{:S(2)}) collective-permute-start(f32[384,128]{1,0:T(8,128)S(1)} %collective-permute-done.1.refs_1_), channel_id=1, source_target_pairs={{0,48},{48,96},{96,144},{144,192},{192,240},{240,288},{288,336},{3... | collective-permute-start | bytes 589832 | tf_op jit(solution)/shard_map/ppermute | solution.py:251
  37.2 11.8 %collective-permute-start.11 = (f32[384,128]{1,0:T(8,128)S(1)}, f32[384,128]{1,0:T(8,128)S(1)}, u32[]{:S(2)}, u32[]{:S(2)}) collective-permute-start(f32[384,128]{1,0:T(8,128)S(1)} %collective-permute-done.9.refs_9_), channel_id=1, source_target_pairs={{0,48},{48,96},{96,144},{144,192},{192,240},{240,288},{288,336},{3... | collective-permute-start | bytes 589832 | tf_op jit(solution)/shard_map/ppermute | solution.py:251
  39.1 11.8 %collective-permute-start.4 = (f32[384,128]{1,0:T(8,128)S(1)}, f32[384,128]{1,0:T(8,128)S(1)}, u32[]{:S(2)}, u32[]{:S(2)}) collective-permute-start(f32[384,128]{1,0:T(8,128)S(1)} %collective-permute-done.2.refs_2_), channel_id=1, source_target_pairs={{0,336},{48,0},{96,48},{144,96},{192,144},{240,192},{288,240},{336... | collective-permute-start | bytes 589832 | tf_op jit(solution)/shard_map/ppermute | solution.py:251
  43.7 11.8 %collective-permute-start.14 = (f32[384,128]{1,0:T(8,128)S(1)}, f32[384,128]{1,0:T(8,128)S(1)}, u32[]{:S(2)}, u32[]{:S(2)}) collective-permute-start(f32[384,128]{1,0:T(8,128)S(1)} %collective-permute-done.12.refs_12_), channel_id=1, source_target_pairs={{0,336},{48,0},{96,48},{144,96},{192,144},{240,192},{288,240},{336... | collective-permute-start | bytes 589832 | tf_op jit(solution)/shard_map/ppermute | solution.py:251
  47.1 11.8 %collective-permute-start.5 = (f32[384,128]{1,0:T(8,128)S(1)}, f32[384,128]{1,0:T(8,128)S(1)}, u32[]{:S(2)}, u32[]{:S(2)}) collective-permute-start(f32[384,128]{1,0:T(8,128)S(1)} %collective-permute-done.3.refs_3_), channel_id=1, source_target_pairs={{0,48},{48,96},{96,144},{144,192},{192,240},{240,288},{288,336},{3... | collective-permute-start | bytes 589832 | tf_op jit(solution)/shard_map/ppermute | solution.py:251
  49.0 11.8 %collective-permute-start.13 = (f32[384,128]{1,0:T(8,128)S(1)}, f32[384,128]{1,0:T(8,128)S(1)}, u32[]{:S(2)}, u32[]{:S(2)}) collective-permute-start(f32[384,128]{1,0:T(8,128)S(1)} %collective-permute-done.11.refs_11_), channel_id=1, source_target_pairs={{0,48},{48,96},{96,144},{144,192},{192,240},{240,288},{288,336},{3... | collective-permute-start | bytes 589832 | tf_op jit(solution)/shard_map/ppermute | solution.py:251
  51.0 9.9 %collective-permute-start.6 = (f32[384,128]{1,0:T(8,128)S(1)}, f32[384,128]{1,0:T(8,128)S(1)}, u32[]{:S(2)}, u32[]{:S(2)}) collective-permute-start(f32[384,128]{1,0:T(8,128)S(1)} %collective-permute-done.4.refs_4_), channel_id=1, source_target_pairs={{0,336},{48,0},{96,48},{144,96},{192,144},{240,192},{288,240},{336... | collective-permute-start | bytes 589832 | tf_op jit(solution)/shard_map/ppermute | solution.py:251
  55.5 6.9 %collective-permute-start.15 = (f32[384,128]{1,0:T(8,128)S(1)}, f32[384,128]{1,0:T(8,128)S(1)}, u32[]{:S(2)}, u32[]{:S(2)}) collective-permute-start(f32[384,128]{1,0:T(8,128)S(1)} %collective-permute-done.14.refs_14_), channel_id=1, source_target_pairs={{0,336},{48,0},{96,48},{144,96},{192,144},{240,192},{288,240},{336... | collective-permute-start | bytes 589832 | tf_op jit(solution)/shard_map/ppermute | solution.py:251
  58.9 9.7 %collective-permute-start.7 = (f32[384,128]{1,0:T(8,128)S(1)}, f32[384,128]{1,0:T(8,128)S(1)}, u32[]{:S(2)}, u32[]{:S(2)}) collective-permute-start(f32[384,128]{1,0:T(8,128)S(1)} %collective-permute-done.5.refs_5_), channel_id=1, source_target_pairs={{0,48},{48,96},{96,144},{144,192},{192,240},{240,288},{288,336},{3... | collective-permute-start | bytes 589832 | tf_op jit(solution)/shard_map/ppermute | solution.py:251
  70.4 17.8 %collective-permute-start.16 = (f32[12,128,256]{2,1,0:T(8,128)}, f32[12,128,256]{2,1,0:T(8,128)}, u32[]{:S(2)}, u32[]{:S(2)}) collective-permute-start(f32[12,128,256]{2,1,0:T(8,128)} %get-tuple-element.20), channel_id=1, source_target_pairs={{0,1},{1,0},{2,3},{3,2},{4,5},{5,4},{6,7},{7,6},{8,9},{9,8},{10,11... | collective-permute-start | bytes 4718600 | tf_op jit(solution)/shard_map/ppermute | solution.py:251
  83.8 11.7 %copy-start = (s32[6,2]{0,1:T(2,128)S(1)}, s32[6,2]{0,1:T(2,128)}, u32[]{:S(2)}) copy-start(s32[6,2]{0,1:T(2,128)} %param.7) | copy-start | bytes 148
  96.2 12.6 %collective-permute-start.17 = (f32[384,128]{1,0:T(8,128)S(1)}, f32[384,128]{1,0:T(8,128)S(1)}, u32[]{:S(2)}, u32[]{:S(2)}) collective-permute-start(f32[384,128]{1,0:T(8,128)S(1)} %shard_map.63.refs_0_), channel_id=1, source_target_pairs={{0,2},{2,4},{4,6},{6,8},{8,10},{10,12},{12,14},{14,16},{16,18},{18... | collective-permute-start | bytes 589832 | tf_op jit(solution)/shard_map/ppermute | solution.py:251
  98.1 12.6 %collective-permute-start.21 = (f32[384,128]{1,0:T(8,128)S(1)}, f32[384,128]{1,0:T(8,128)S(1)}, u32[]{:S(2)}, u32[]{:S(2)}) collective-permute-start(f32[384,128]{1,0:T(8,128)S(1)} %shard_map.63.refs_0_), channel_id=1, source_target_pairs={{0,22},{2,0},{4,2},{6,4},{8,6},{10,8},{12,10},{14,12},{16,14},{18,... | collective-permute-start | bytes 589832 | tf_op jit(solution)/shard_map/ppermute | solution.py:251
  108.7 9.3 %collective-permute-start.18 = (f32[384,128]{1,0:T(8,128)S(1)}, f32[384,128]{1,0:T(8,128)S(1)}, u32[]{:S(2)}, u32[]{:S(2)}) collective-permute-start(f32[384,128]{1,0:T(8,128)S(1)} %collective-permute-done.17.refs_1_), channel_id=1, source_target_pairs={{0,2},{2,4},{4,6},{6,8},{8,10},{10,12},{12,14},{14,16},{16,18},{18... | collective-permute-start | bytes 589832 | tf_op jit(solution)/shard_map/ppermute | solution.py:251
  110.6 11.0 %collective-permute-start.22 = (f32[384,128]{1,0:T(8,128)S(1)}, f32[384,128]{1,0:T(8,128)S(1)}, u32[]{:S(2)}, u32[]{:S(2)}) collective-permute-start(f32[384,128]{1,0:T(8,128)S(1)} %collective-permute-done.21.refs_2_), channel_id=1, source_target_pairs={{0,22},{2,0},{4,2},{6,4},{8,6},{10,8},{12,10},{14,12},{16,14},{18,... | collective-permute-start | bytes 589832 | tf_op jit(solution)/shard_map/ppermute | solution.py:251
  115.2 21.5 %collective-permute-start.25 = (f32[384,128]{1,0:T(8,128)S(1)}, f32[384,128]{1,0:T(8,128)S(1)}, u32[]{:S(2)}, u32[]{:S(2)}) collective-permute-start(f32[384,128]{1,0:T(8,128)S(1)} %shard_map.63.refs_0_), channel_id=1, source_target_pairs={{0,12},{2,14},{4,16},{6,18},{8,20},{10,22},{12,0},{14,2},{16,4},{1... | collective-permute-start | bytes 589832 | tf_op jit(solution)/shard_map/ppermute | solution.py:251
  118.0 25.2 %collective-permute-start.19 = (f32[384,128]{1,0:T(8,128)S(1)}, f32[384,128]{1,0:T(8,128)S(1)}, u32[]{:S(2)}, u32[]{:S(2)}) collective-permute-start(f32[384,128]{1,0:T(8,128)S(1)} %collective-permute-done.18.refs_3_), channel_id=1, source_target_pairs={{0,2},{2,4},{4,6},{6,8},{8,10},{10,12},{12,14},{14,16},{16,18},{18... | collective-permute-start | bytes 589832 | tf_op jit(solution)/shard_map/ppermute | solution.py:251
  121.7 23.4 %collective-permute-start.23 = (f32[384,128]{1,0:T(8,128)S(1)}, f32[384,128]{1,0:T(8,128)S(1)}, u32[]{:S(2)}, u32[]{:S(2)}) collective-permute-start(f32[384,128]{1,0:T(8,128)S(1)} %collective-permute-done.22.refs_0_), channel_id=1, source_target_pairs={{0,22},{2,0},{4,2},{6,4},{8,6},{10,8},{12,10},{14,12},{16,14},{18,... | collective-permute-start | bytes 589832 | tf_op jit(solution)/shard_map/ppermute | solution.py:251
  136.7 16.3 %collective-permute-start.26 = (f32[384,128]{1,0:T(8,128)S(1)}, f32[384,128]{1,0:T(8,128)S(1)}, u32[]{:S(2)}, u32[]{:S(2)}) collective-permute-start(f32[384,128]{1,0:T(8,128)S(1)} %collective-permute-done.25.refs_3_), channel_id=1, source_target_pairs={{0,2},{2,4},{4,6},{6,8},{8,10},{10,12},{12,14},{14,16},{16,18},{18... | collective-permute-start | bytes 589832 | tf_op jit(solution)/shard_map/ppermute | solution.py:251
  138.6 14.4 %collective-permute-start.27 = (f32[384,128]{1,0:T(8,128)S(1)}, f32[384,128]{1,0:T(8,128)S(1)}, u32[]{:S(2)}, u32[]{:S(2)}) collective-permute-start(f32[384,128]{1,0:T(8,128)S(1)} %collective-permute-done.25.refs_3_), channel_id=1, source_target_pairs={{0,22},{2,0},{4,2},{6,4},{8,6},{10,8},{12,10},{14,12},{16,14},{18,... | collective-permute-start | bytes 589832 | tf_op jit(solution)/shard_map/ppermute | solution.py:251
  143.2 9.8 %collective-permute-start.20 = (f32[384,128]{1,0:T(8,128)S(1)}, f32[384,128]{1,0:T(8,128)S(1)}, u32[]{:S(2)}, u32[]{:S(2)}) collective-permute-start(f32[384,128]{1,0:T(8,128)S(1)} %collective-permute-done.19.refs_1_), channel_id=1, source_target_pairs={{0,2},{2,4},{4,6},{6,8},{8,10},{10,12},{12,14},{14,16},{16,18},{18... | collective-permute-start | bytes 589832 | tf_op jit(solution)/shard_map/ppermute | solution.py:251
  145.1 7.9 %collective-permute-start.24 = (f32[384,128]{1,0:T(8,128)S(1)}, f32[384,128]{1,0:T(8,128)S(1)}, u32[]{:S(2)}, u32[]{:S(2)}) collective-permute-start(f32[384,128]{1,0:T(8,128)S(1)} %collective-permute-done.23.refs_2_), channel_id=1, source_target_pairs={{0,22},{2,0},{4,2},{6,4},{8,6},{10,8},{12,10},{14,12},{16,14},{18,... | collective-permute-start | bytes 589832 | tf_op jit(solution)/shard_map/ppermute | solution.py:251
Sparse Core Ops, SparseCore 0:
  11.0 72.7 all-gather.5

commit v10 on v9

--- a/solution.py
+++ b/solution.py
@@ -295,7 +295,10 @@
 
     operand = phase_rows(hi, lo, took)
     away = shift(square, "z", 6)
-    up, down = chain(square, "z", 1, 4), chain(square, "z", -1, 4)
+    up, down = chain(square, "z", 1, 2), chain(square, "z", -1, 2)
+    down[1], away = together(down[1], away)
+    up += chain(up[1], "z", 1, 2)
+    down += chain(down[1], "z", -1, 2)
     blocks = [(0, square)]
     for s in range(3):
         blocks += [(-s - 1, up[s]), (s + 1, down[s])]

time: 174 us -> 176 us (1.011)
  waiting for transfers between devices: 27.4 us -> 29.2 us
    ppermute x26, waiting for transfers between devices: 22.7 us -> 24.5 us  [shift(): return lax.ppermute(x, axis, [(i, (i + step) % n) for i in range(n)])]
  transfers between devices with their start and end apart: 29 -> 29, of which waited for: 6 -> 8; matrix products, arithmetic and copies ran while one was open for 0% -> 0% of each run, Pallas kernels for 5% -> 5%
where the time goes in v10:
time: 176 us; the launch traced here: 175 us
  starting transfers between devices  98.2 us (56%)
  waiting for transfers between devices  29.2 us (17%)
  blocking collectives  19.2 us (11%)
  between operations  14.5 us (8%)
  Pallas kernels  13.9 us (8%)
    ppermute x26, starting transfers between devices, shift(): return lax.ppermute(x, axis, [(i, (i + step) % n) for i in range(n)])  91.1 us
    ppermute x26, waiting for transfers between devices, shift(): return lax.ppermute(x, axis, [(i, (i + step) % n) for i in range(n)])  24.5 us
    all_gather x2, blocking collectives, filtered(): pair = lax.all_gather(other, 'xl', axis=0)  14.1 us
    ppermute x1, starting transfers between devices, body(): far = lax.ppermute(masked, ('xh', 'xl'), [(1, 0), (2, 3), (0, 2), (3, 1)])  5.48 us
    all_gather x1, blocking collectives, join(): both = lax.all_gather(give, 'c', axis=0)  5.03 us
    pallas_call x1, Pallas kernels, first_product(): pl.pallas_call(first_kernel, out_shape=(block, block), in_specs=[HB, VM,...  4.38 us
  transfers between devices with their start and end apart: 29, of which 8 were waited for; matrix products, arithmetic and copies ran while one was open for 0% of the time, Pallas kernels for 5%

profile of v10, /device:TPU:1, one launch (start us, length us, event | category | flops | bytes accessed | tf_op | source)
XLA Modules:
  0.0 174.9 jit_solution(13005587596687948367)
XLA Ops:
  7.2 0.0 all-gather.6.cloned.1.call-start
  7.2 1.7 shard_map.59
  8.9 0.0 all-gather.6.cloned.1.call-update
  8.9 5.5 %collective-permute-start.8 = (f32[384,128]{1,0:T(8,128)}, f32[384,128]{1,0:T(8,128)S(1)}, u32[]{:S(2)}, u32[]{:S(2)}) collective-permute-start(f32[384,128]{1,0:T(8,128)} %shard_map.59), channel_id=1, source_target_pairs={{24,0},{384,408},{0,384},{408,24},{25,1},{385,409},{1,385},{409,25... | collective-permute-start | bytes 589832 | tf_op jit(solution)/shard_map/ppermute | solution.py:285
  14.4 1.6 collective-permute-start
  16.0 1.3 collective-permute-done.8.refs_8_
  17.3 6.1 %collective-permute-start.10 = (f32[384,128]{1,0:T(8,128)S(1)}, f32[384,128]{1,0:T(8,128)S(1)}, u32[]{:S(2)}, u32[]{:S(2)}) collective-permute-start(f32[384,128]{1,0:T(8,128)S(1)} %collective-permute-done.8.refs_8_), channel_id=1, source_target_pairs={{0,336},{48,0},{96,48},{144,96},{192,144},{240,192},{288,240},{336... | collective-permute-start | bytes 589832 | tf_op jit(solution)/shard_map/ppermute | solution.py:251
  23.4 1.9 %collective-permute-start.1 = (f32[384,128]{1,0:T(8,128)S(1)}, f32[384,128]{1,0:T(8,128)S(1)}, u32[]{:S(2)}, u32[]{:S(2)}) collective-permute-start(f32[384,128]{1,0:T(8,128)S(1)} %collective-permute-done.refs_0_), channel_id=1, source_target_pairs={{0,48},{48,96},{96,144},{144,192},{192,240},{240,288},{288,336},{3... | collective-permute-start | bytes 589832 | tf_op jit(solution)/shard_map/ppermute | solution.py:251
  25.3 1.9 %collective-permute-start.9 = (f32[384,128]{1,0:T(8,128)S(1)}, f32[384,128]{1,0:T(8,128)S(1)}, u32[]{:S(2)}, u32[]{:S(2)}) collective-permute-start(f32[384,128]{1,0:T(8,128)S(1)} %collective-permute-done.8.refs_8_), channel_id=1, source_target_pairs={{0,48},{48,96},{96,144},{144,192},{192,240},{240,288},{288,336},{3... | collective-permute-start | bytes 589832 | tf_op jit(solution)/shard_map/ppermute | solution.py:251
  27.3 4.6 %collective-permute-start.2 = (f32[384,128]{1,0:T(8,128)S(1)}, f32[384,128]{1,0:T(8,128)S(1)}, u32[]{:S(2)}, u32[]{:S(2)}) collective-permute-start(f32[384,128]{1,0:T(8,128)S(1)} %collective-permute-done.refs_0_), channel_id=1, source_target_pairs={{0,336},{48,0},{96,48},{144,96},{192,144},{240,192},{288,240},{336... | collective-permute-start | bytes 589832 | tf_op jit(solution)/shard_map/ppermute | solution.py:251
  31.8 3.4 %collective-permute-start.12 = (f32[384,128]{1,0:T(8,128)S(1)}, f32[384,128]{1,0:T(8,128)S(1)}, u32[]{:S(2)}, u32[]{:S(2)}) collective-permute-start(f32[384,128]{1,0:T(8,128)S(1)} %collective-permute-done.10.refs_10_), channel_id=1, source_target_pairs={{0,336},{48,0},{96,48},{144,96},{192,144},{240,192},{288,240},{336... | collective-permute-start | bytes 589832 | tf_op jit(solution)/shard_map/ppermute | solution.py:251
  35.2 0.0 collective-permute-done.1.refs_1_
  35.2 1.9 %collective-permute-start.3 = (f32[384,128]{1,0:T(8,128)S(1)}, f32[384,128]{1,0:T(8,128)S(1)}, u32[]{:S(2)}, u32[]{:S(2)}) collective-permute-start(f32[384,128]{1,0:T(8,128)S(1)} %collective-permute-done.1.refs_1_), channel_id=1, source_target_pairs={{0,48},{48,96},{96,144},{144,192},{192,240},{240,288},{288,336},{3... | collective-permute-start | bytes 589832 | tf_op jit(solution)/shard_map/ppermute | solution.py:251
  37.2 0.0 collective-permute-done.9.refs_9_
  37.2 1.9 %collective-permute-start.11 = (f32[384,128]{1,0:T(8,128)S(1)}, f32[384,128]{1,0:T(8,128)S(1)}, u32[]{:S(2)}, u32[]{:S(2)}) collective-permute-start(f32[384,128]{1,0:T(8,128)S(1)} %collective-permute-done.9.refs_9_), channel_id=1, source_target_pairs={{0,48},{48,96},{96,144},{144,192},{192,240},{240,288},{288,336},{3... | collective-permute-start | bytes 589832 | tf_op jit(solution)/shard_map/ppermute | solution.py:251
  39.1 4.6 %collective-permute-start.4 = (f32[384,128]{1,0:T(8,128)S(1)}, f32[384,128]{1,0:T(8,128)S(1)}, u32[]{:S(2)}, u32[]{:S(2)}) collective-permute-start(f32[384,128]{1,0:T(8,128)S(1)} %collective-permute-done.2.refs_2_), channel_id=1, source_target_pairs={{0,336},{48,0},{96,48},{144,96},{192,144},{240,192},{288,240},{336... | collective-permute-start | bytes 589832 | tf_op jit(solution)/shard_map/ppermute | solution.py:251
  43.7 0.0 collective-permute-done.12.refs_12_
  43.7 3.4 %collective-permute-start.14 = (f32[384,128]{1,0:T(8,128)S(1)}, f32[384,128]{1,0:T(8,128)S(1)}, u32[]{:S(2)}, u32[]{:S(2)}) collective-permute-start(f32[384,128]{1,0:T(8,128)S(1)} %collective-permute-done.12.refs_12_), channel_id=1, source_target_pairs={{0,336},{48,0},{96,48},{144,96},{192,144},{240,192},{288,240},{336... | collective-permute-start | bytes 589832 | tf_op jit(solution)/shard_map/ppermute | solution.py:251
  47.1 1.9 %collective-permute-start.5 = (f32[384,128]{1,0:T(8,128)S(1)}, f32[384,128]{1,0:T(8,128)S(1)}, u32[]{:S(2)}, u32[]{:S(2)}) collective-permute-start(f32[384,128]{1,0:T(8,128)S(1)} %collective-permute-done.3.refs_3_), channel_id=1, source_target_pairs={{0,48},{48,96},{96,144},{144,192},{192,240},{240,288},{288,336},{3... | collective-permute-start | bytes 589832 | tf_op jit(solution)/shard_map/ppermute | solution.py:251
  49.0 0.0 collective-permute-done.11.refs_11_
  49.0 1.9 %collective-permute-start.13 = (f32[384,128]{1,0:T(8,128)S(1)}, f32[384,128]{1,0:T(8,128)S(1)}, u32[]{:S(2)}, u32[]{:S(2)}) collective-permute-start(f32[384,128]{1,0:T(8,128)S(1)} %collective-permute-done.11.refs_11_), channel_id=1, source_target_pairs={{0,48},{48,96},{96,144},{144,192},{192,240},{240,288},{288,336},{3... | collective-permute-start | bytes 589832 | tf_op jit(solution)/shard_map/ppermute | solution.py:251
  50.9 0.0 collective-permute-done.4.refs_4_
  51.0 4.6 %collective-permute-start.6 = (f32[384,128]{1,0:T(8,128)S(1)}, f32[384,128]{1,0:T(8,128)S(1)}, u32[]{:S(2)}, u32[]{:S(2)}) collective-permute-start(f32[384,128]{1,0:T(8,128)S(1)} %collective-permute-done.4.refs_4_), channel_id=1, source_target_pairs={{0,336},{48,0},{96,48},{144,96},{192,144},{240,192},{288,240},{336... | collective-permute-start | bytes 589832 | tf_op jit(solution)/shard_map/ppermute | solution.py:251
  55.5 0.0 collective-permute-done.14.refs_14_
  55.5 3.4 %collective-permute-start.15 = (f32[384,128]{1,0:T(8,128)S(1)}, f32[384,128]{1,0:T(8,128)S(1)}, u32[]{:S(2)}, u32[]{:S(2)}) collective-permute-start(f32[384,128]{1,0:T(8,128)S(1)} %collective-permute-done.14.refs_14_), channel_id=1, source_target_pairs={{0,336},{48,0},{96,48},{144,96},{192,144},{240,192},{288,240},{336... | collective-permute-start | bytes 589832 | tf_op jit(solution)/shard_map/ppermute | solution.py:251
  58.9 0.0 collective-permute-done.5.refs_5_
  58.9 1.9 %collective-permute-start.7 = (f32[384,128]{1,0:T(8,128)S(1)}, f32[384,128]{1,0:T(8,128)S(1)}, u32[]{:S(2)}, u32[]{:S(2)}) collective-permute-start(f32[384,128]{1,0:T(8,128)S(1)} %collective-permute-done.5.refs_5_), channel_id=1, source_target_pairs={{0,48},{48,96},{96,144},{144,192},{192,240},{240,288},{288,336},{3... | collective-permute-start | bytes 589832 | tf_op jit(solution)/shard_map/ppermute | solution.py:251
  60.9 0.0 collective-permute-done.6.refs_6_
  60.9 1.6 collective-permute-done.15.refs_15_
  62.5 6.1 %collective-permute-done.7.refs_7_ = f32[384,128]{1,0:T(8,128)S(1)} collective-permute-done((f32[384,128]{1,0:T(8,128)S(1)}, f32[384,128]{1,0:T(8,128)S(1)}, u32[]{:S(2)}, u32[]{:S(2)}) %collective-permute-start.7) | collective-permute-done | bytes 196640 | tf_op jit(solution)/shard_map/ppermute | solution.py:251
  68.6 1.8 %shard_map.60 = (bf16[24,128,256]{2,1,0:T(8,128)(2,1)S(1)}, bf16[24,128,256]{2,1,0:T(8,128)(2,1)S(1)}, f32[12,128,256]{2,1,0:T(8,128)}) custom-call(f32[384,128]{1,0:T(8,128)S(1)} %collective-permute-done.refs_0_, f32[384,128]{1,0:T(8,128)S(1)} %collective-permute-done.1.refs_1_, f32[384,128]{1,0:T(8,128)S(1)} %collective-permute-done.2.refs_2_, ...), custom_call_target="tpu_custom_call" | custom-call | tf_op jit(solution)/shard_map/pallas_call | solution.py:93
  70.4 10.1 %collective-permute-start.16 = (f32[12,128,256]{2,1,0:T(8,128)}, f32[12,128,256]{2,1,0:T(8,128)}, u32[]{:S(2)}, u32[]{:S(2)}) collective-permute-start(f32[12,128,256]{2,1,0:T(8,128)} %get-tuple-element.22), channel_id=1, source_target_pairs={{0,1},{1,0},{2,3},{3,2},{4,5},{5,4},{6,7},{7,6},{8,9},{9,8},{10,11... | collective-permute-start | bytes 4718600 | tf_op jit(solution)/shard_map/ppermute | solution.py:251
  80.5 3.3 %all-gather.6.cloned.1.call-done = f32[9216,128]{1,0:T(8,128)} async-done(((f32[384,128]{1,0:T(8,128)}), f32[9216,128]{1,0:T(8,128)}) %all-gather.6.cloned.1.call-update) | async-done | bytes 4718608 | tf_op jit(solution)/shard_map/all_gather | solution.py:282
  83.8 4.4 %shard_map.61 = (f32[384,128]{1,0:T(8,128)S(1)}, f32[384,128]{1,0:T(8,128)S(1)}) custom-call(f32[24,384,128]{2,1,0:T(8,128)} %bitcast.11, bf16[24,128,256]{2,1,0:T(8,128)(2,1)S(1)} %get-tuple-element.18.hi, bf16[24,128,256]{2,1,0:T(8,128)(2,1)S(1)} %get-tuple-element.19.lo), custom_call_target="tpu_custom_call" | custom-call | flops 1811939328 | tf_op jit(solution)/shard_map/pallas_call | solution.py:147
  88.2 0.0 collective-permute-done.16.took
  88.2 7.3 %all-gather.1 = f32[768,128]{1,0:T(8,128)S(1)} all-gather(f32[384,128]{1,0:T(8,128)S(1)} %get-tuple-element.27), channel_id=3, replica_groups=mesh['xh'=2,'y'=8,'xl'=2,'z'=12,'c'=2] {'xl'}, dimensions={0}, use_global_device_ids=true | all-gather | bytes 589824 | tf_op jit(solution)/shard_map/all_gather | solution.py:237
  95.6 0.6 shard_map.63.refs_0_
  96.2 7.8 %collective-permute-start.21 = (f32[384,128]{1,0:T(8,128)S(1)}, f32[384,128]{1,0:T(8,128)S(1)}, u32[]{:S(2)}, u32[]{:S(2)}) collective-permute-start(f32[384,128]{1,0:T(8,128)S(1)} %shard_map.63.refs_0_), channel_id=1, source_target_pairs={{0,22},{2,0},{4,2},{6,4},{8,6},{10,8},{12,10},{14,12},{16,14},{18,... | collective-permute-start | bytes 589832 | tf_op jit(solution)/shard_map/ppermute | solution.py:251
  104.0 1.9 %collective-permute-start.17 = (f32[384,128]{1,0:T(8,128)S(1)}, f32[384,128]{1,0:T(8,128)S(1)}, u32[]{:S(2)}, u32[]{:S(2)}) collective-permute-start(f32[384,128]{1,0:T(8,128)S(1)} %shard_map.63.refs_0_), channel_id=1, source_target_pairs={{0,2},{2,4},{4,6},{6,8},{8,10},{10,12},{12,14},{14,16},{16,18},{18... | collective-permute-start | bytes 589832 | tf_op jit(solution)/shard_map/ppermute | solution.py:251
  105.9 4.3 %collective-permute-start.23 = (f32[384,128]{1,0:T(8,128)S(1)}, f32[384,128]{1,0:T(8,128)S(1)}, u32[]{:S(2)}, u32[]{:S(2)}) collective-permute-start(f32[384,128]{1,0:T(8,128)S(1)} %shard_map.63.refs_0_), channel_id=1, source_target_pairs={{0,12},{2,14},{4,16},{6,18},{8,20},{10,22},{12,0},{14,2},{16,4},{1... | collective-permute-start | bytes 589832 | tf_op jit(solution)/shard_map/ppermute | solution.py:251
  110.2 0.0 collective-permute-done.21.refs_2_
  110.2 2.7 %collective-permute-start.22 = (f32[384,128]{1,0:T(8,128)S(1)}, f32[384,128]{1,0:T(8,128)S(1)}, u32[]{:S(2)}, u32[]{:S(2)}) collective-permute-start(f32[384,128]{1,0:T(8,128)S(1)} %collective-permute-done.21.refs_2_), channel_id=1, source_target_pairs={{0,22},{2,0},{4,2},{6,4},{8,6},{10,8},{12,10},{14,12},{16,14},{18,... | collective-permute-start | bytes 589832 | tf_op jit(solution)/shard_map/ppermute | solution.py:251
  113.0 6.4 %collective-permute-done.17.refs_1_ = f32[384,128]{1,0:T(8,128)S(1)} collective-permute-done((f32[384,128]{1,0:T(8,128)S(1)}, f32[384,128]{1,0:T(8,128)S(1)}, u32[]{:S(2)}, u32[]{:S(2)}) %collective-permute-start.17) | collective-permute-done | bytes 196640 | tf_op jit(solution)/shard_map/ppermute | solution.py:251
  119.3 1.9 %collective-permute-start.18 = (f32[384,128]{1,0:T(8,128)S(1)}, f32[384,128]{1,0:T(8,128)S(1)}, u32[]{:S(2)}, u32[]{:S(2)}) collective-permute-start(f32[384,128]{1,0:T(8,128)S(1)} %collective-permute-done.17.refs_1_), channel_id=1, source_target_pairs={{0,2},{2,4},{4,6},{6,8},{8,10},{10,12},{12,14},{14,16},{16,18},{18... | collective-permute-start | bytes 589832 | tf_op jit(solution)/shard_map/ppermute | solution.py:251
  121.3 4.4 %collective-permute-done.23.refs_3_ = f32[384,128]{1,0:T(8,128)S(1)} collective-permute-done((f32[384,128]{1,0:T(8,128)S(1)}, f32[384,128]{1,0:T(8,128)S(1)}, u32[]{:S(2)}, u32[]{:S(2)}) %collective-permute-start.23) | collective-permute-done | bytes 196640 | tf_op jit(solution)/shard_map/ppermute | solution.py:251
  125.6 3.6 %collective-permute-done.22.refs_0_ = f32[384,128]{1,0:T(8,128)S(1)} collective-permute-done((f32[384,128]{1,0:T(8,128)S(1)}, f32[384,128]{1,0:T(8,128)S(1)}, u32[]{:S(2)}, u32[]{:S(2)}) %collective-permute-start.22) | collective-permute-done | bytes 196640 | tf_op jit(solution)/shard_map/ppermute | solution.py:251
  129.2 5.3 %collective-permute-start.24 = (f32[384,128]{1,0:T(8,128)S(1)}, f32[384,128]{1,0:T(8,128)S(1)}, u32[]{:S(2)}, u32[]{:S(2)}) collective-permute-start(f32[384,128]{1,0:T(8,128)S(1)} %collective-permute-done.22.refs_0_), channel_id=1, source_target_pairs={{0,22},{2,0},{4,2},{6,4},{8,6},{10,8},{12,10},{14,12},{16,14},{18,... | collective-permute-start | bytes 589832 | tf_op jit(solution)/shard_map/ppermute | solution.py:251
  134.6 1.9 %collective-permute-start.19 = (f32[384,128]{1,0:T(8,128)S(1)}, f32[384,128]{1,0:T(8,128)S(1)}, u32[]{:S(2)}, u32[]{:S(2)}) collective-permute-start(f32[384,128]{1,0:T(8,128)S(1)} %collective-permute-done.18.refs_3_), channel_id=1, source_target_pairs={{0,2},{2,4},{4,6},{6,8},{8,10},{10,12},{12,14},{14,16},{16,18},{18... | collective-permute-start | bytes 589832 | tf_op jit(solution)/shard_map/ppermute | solution.py:251
  136.5 1.9 %collective-permute-start.26 = (f32[384,128]{1,0:T(8,128)S(1)}, f32[384,128]{1,0:T(8,128)S(1)}, u32[]{:S(2)}, u32[]{:S(2)}) collective-permute-start(f32[384,128]{1,0:T(8,128)S(1)} %collective-permute-done.23.refs_3_), channel_id=1, source_target_pairs={{0,2},{2,4},{4,6},{6,8},{8,10},{10,12},{12,14},{14,16},{16,18},{18... | collective-permute-start | bytes 589832 | tf_op jit(solution)/shard_map/ppermute | solution.py:251
  138.4 4.6 %collective-permute-start.27 = (f32[384,128]{1,0:T(8,128)S(1)}, f32[384,128]{1,0:T(8,128)S(1)}, u32[]{:S(2)}, u32[]{:S(2)}) collective-permute-start(f32[384,128]{1,0:T(8,128)S(1)} %collective-permute-done.23.refs_3_), channel_id=1, source_target_pairs={{0,22},{2,0},{4,2},{6,4},{8,6},{10,8},{12,10},{14,12},{16,14},{18,... | collective-permute-start | bytes 589832 | tf_op jit(solution)/shard_map/ppermute | solution.py:251
  143.0 3.4 %collective-permute-start.25 = (f32[384,128]{1,0:T(8,128)S(1)}, f32[384,128]{1,0:T(8,128)S(1)}, u32[]{:S(2)}, u32[]{:S(2)}) collective-permute-start(f32[384,128]{1,0:T(8,128)S(1)} %collective-permute-done.24.refs_2_), channel_id=1, source_target_pairs={{0,22},{2,0},{4,2},{6,4},{8,6},{10,8},{12,10},{14,12},{16,14},{18,... | collective-permute-start | bytes 589832 | tf_op jit(solution)/shard_map/ppermute | solution.py:251
  146.4 0.0 collective-permute-done.19.refs_1_
  146.4 1.9 %collective-permute-start.20 = (f32[384,128]{1,0:T(8,128)S(1)}, f32[384,128]{1,0:T(8,128)S(1)}, u32[]{:S(2)}, u32[]{:S(2)}) collective-permute-start(f32[384,128]{1,0:T(8,128)S(1)} %collective-permute-done.19.refs_1_), channel_id=1, source_target_pairs={{0,2},{2,4},{4,6},{6,8},{8,10},{10,12},{12,14},{14,16},{16,18},{18... | collective-permute-start | bytes 589832 | tf_op jit(solution)/shard_map/ppermute | solution.py:251
  148.3 1.6 shard_map.62
  150.0 0.8 shard_map.64.refs_4_
  150.8 0.8 shard_map.65.refs_4_
  151.6 0.0 collective-permute-done.26.refs_2_
  151.6 0.0 collective-permute-done.25.refs_1_
  151.6 2.4 %collective-permute-done.20.refs_0_ = f32[384,128]{1,0:T(8,128)S(1)} collective-permute-done((f32[384,128]{1,0:T(8,128)S(1)}, f32[384,128]{1,0:T(8,128)S(1)}, u32[]{:S(2)}, u32[]{:S(2)}) %collective-permute-start.20) | collective-permute-done | bytes 196640 | tf_op jit(solution)/shard_map/ppermute | solution.py:251
  154.0 0.8 shard_map.66
  154.8 5.0 %all-gather.2 = f32[768,256]{1,0:T(8,128)S(1)} all-gather(f32[384,256]{1,0:T(8,128)S(1)} %get-tuple-element.31), channel_id=4, replica_groups=mesh['xh'=2,'y'=8,'xl'=2,'z'=12,'c'=2] {'c'}, dimensions={0}, use_global_device_ids=true | all-gather | bytes 1179648 | tf_op jit(solution)/shard_map/all_gather | solution.py:207
  159.8 0.1 shard_map.67
  159.9 6.8 %all-gather.3 = f32[768,128]{1,0:T(8,128)S(1)} all-gather(f32[384,128]{1,0:T(8,128)S(1)} %get-tuple-element.33), channel_id=5, replica_groups=mesh['xh'=2,'y'=8,'xl'=2,'z'=12,'c'=2] {'xl'}, dimensions={0}, use_global_device_ids=true | all-gather | bytes 589824 | tf_op jit(solution)/shard_map/all_gather | solution.py:237
  166.7 1.3 shard_map.68
  (10 shorter events, 0.0 us)
Async XLA Ops:
  7.2 76.7 %all-gather.6.cloned.1.call-start = ((), (), s32[]{:S(2)}) async-start(), calls=%async_computation | async-start | bytes 4915200 | tf_op jit(solution)/shard_map/all_gather | solution.py:282
  8.9 8.4 %collective-permute-start.8 = (f32[384,128]{1,0:T(8,128)}, f32[384,128]{1,0:T(8,128)S(1)}, u32[]{:S(2)}, u32[]{:S(2)}) collective-permute-start(f32[384,128]{1,0:T(8,128)} %shard_map.59), channel_id=1, source_target_pairs={{24,0},{384,408},{0,384},{408,24},{25,1},{385,409},{1,385},{409,25... | collective-permute-start | bytes 589832 | tf_op jit(solution)/shard_map/ppermute | solution.py:285
  14.4 9.0 %collective-permute-start = (f32[384,128]{1,0:T(8,128)}, f32[384,128]{1,0:T(8,128)S(1)}, u32[]{:S(2)}, u32[]{:S(2)}) collective-permute-start(f32[384,128]{1,0:T(8,128)} %shard_map.59), channel_id=1, source_target_pairs={{0,0},{24,384},{384,24},{408,408},{1,1},{25,385},{385,25},{409,409... | collective-permute-start | bytes 589832 | tf_op jit(solution)/shard_map/ppermute | solution.py:284
  17.3 14.5 %collective-permute-start.10 = (f32[384,128]{1,0:T(8,128)S(1)}, f32[384,128]{1,0:T(8,128)S(1)}, u32[]{:S(2)}, u32[]{:S(2)}) collective-permute-start(f32[384,128]{1,0:T(8,128)S(1)} %collective-permute-done.8.refs_8_), channel_id=1, source_target_pairs={{0,336},{48,0},{96,48},{144,96},{192,144},{240,192},{288,240},{336... | collective-permute-start | bytes 589832 | tf_op jit(solution)/shard_map/ppermute | solution.py:251
  23.4 11.8 %collective-permute-start.1 = (f32[384,128]{1,0:T(8,128)S(1)}, f32[384,128]{1,0:T(8,128)S(1)}, u32[]{:S(2)}, u32[]{:S(2)}) collective-permute-start(f32[384,128]{1,0:T(8,128)S(1)} %collective-permute-done.refs_0_), channel_id=1, source_target_pairs={{0,48},{48,96},{96,144},{144,192},{192,240},{240,288},{288,336},{3... | collective-permute-start | bytes 589832 | tf_op jit(solution)/shard_map/ppermute | solution.py:251
  25.3 11.8 %collective-permute-start.9 = (f32[384,128]{1,0:T(8,128)S(1)}, f32[384,128]{1,0:T(8,128)S(1)}, u32[]{:S(2)}, u32[]{:S(2)}) collective-permute-start(f32[384,128]{1,0:T(8,128)S(1)} %collective-permute-done.8.refs_8_), channel_id=1, source_target_pairs={{0,48},{48,96},{96,144},{144,192},{192,240},{240,288},{288,336},{3... | collective-permute-start | bytes 589832 | tf_op jit(solution)/shard_map/ppermute | solution.py:251
  27.3 11.8 %collective-permute-start.2 = (f32[384,128]{1,0:T(8,128)S(1)}, f32[384,128]{1,0:T(8,128)S(1)}, u32[]{:S(2)}, u32[]{:S(2)}) collective-permute-start(f32[384,128]{1,0:T(8,128)S(1)} %collective-permute-done.refs_0_), channel_id=1, source_target_pairs={{0,336},{48,0},{96,48},{144,96},{192,144},{240,192},{288,240},{336... | collective-permute-start | bytes 589832 | tf_op jit(solution)/shard_map/ppermute | solution.py:251
  31.8 11.8 %collective-permute-start.12 = (f32[384,128]{1,0:T(8,128)S(1)}, f32[384,128]{1,0:T(8,128)S(1)}, u32[]{:S(2)}, u32[]{:S(2)}) collective-permute-start(f32[384,128]{1,0:T(8,128)S(1)} %collective-permute-done.10.refs_10_), channel_id=1, source_target_pairs={{0,336},{48,0},{96,48},{144,96},{192,144},{240,192},{288,240},{336... | collective-permute-start | bytes 589832 | tf_op jit(solution)/shard_map/ppermute | solution.py:251
  35.2 11.8 %collective-permute-start.3 = (f32[384,128]{1,0:T(8,128)S(1)}, f32[384,128]{1,0:T(8,128)S(1)}, u32[]{:S(2)}, u32[]{:S(2)}) collective-permute-start(f32[384,128]{1,0:T(8,128)S(1)} %collective-permute-done.1.refs_1_), channel_id=1, source_target_pairs={{0,48},{48,96},{96,144},{144,192},{192,240},{240,288},{288,336},{3... | collective-permute-start | bytes 589832 | tf_op jit(solution)/shard_map/ppermute | solution.py:251
  37.2 11.8 %collective-permute-start.11 = (f32[384,128]{1,0:T(8,128)S(1)}, f32[384,128]{1,0:T(8,128)S(1)}, u32[]{:S(2)}, u32[]{:S(2)}) collective-permute-start(f32[384,128]{1,0:T(8,128)S(1)} %collective-permute-done.9.refs_9_), channel_id=1, source_target_pairs={{0,48},{48,96},{96,144},{144,192},{192,240},{240,288},{288,336},{3... | collective-permute-start | bytes 589832 | tf_op jit(solution)/shard_map/ppermute | solution.py:251
  39.1 11.8 %collective-permute-start.4 = (f32[384,128]{1,0:T(8,128)S(1)}, f32[384,128]{1,0:T(8,128)S(1)}, u32[]{:S(2)}, u32[]{:S(2)}) collective-permute-start(f32[384,128]{1,0:T(8,128)S(1)} %collective-permute-done.2.refs_2_), channel_id=1, source_target_pairs={{0,336},{48,0},{96,48},{144,96},{192,144},{240,192},{288,240},{336... | collective-permute-start | bytes 589832 | tf_op jit(solution)/shard_map/ppermute | solution.py:251
  43.7 11.8 %collective-permute-start.14 = (f32[384,128]{1,0:T(8,128)S(1)}, f32[384,128]{1,0:T(8,128)S(1)}, u32[]{:S(2)}, u32[]{:S(2)}) collective-permute-start(f32[384,128]{1,0:T(8,128)S(1)} %collective-permute-done.12.refs_12_), channel_id=1, source_target_pairs={{0,336},{48,0},{96,48},{144,96},{192,144},{240,192},{288,240},{336... | collective-permute-start | bytes 589832 | tf_op jit(solution)/shard_map/ppermute | solution.py:251
  47.1 11.8 %collective-permute-start.5 = (f32[384,128]{1,0:T(8,128)S(1)}, f32[384,128]{1,0:T(8,128)S(1)}, u32[]{:S(2)}, u32[]{:S(2)}) collective-permute-start(f32[384,128]{1,0:T(8,128)S(1)} %collective-permute-done.3.refs_3_), channel_id=1, source_target_pairs={{0,48},{48,96},{96,144},{144,192},{192,240},{240,288},{288,336},{3... | collective-permute-start | bytes 589832 | tf_op jit(solution)/shard_map/ppermute | solution.py:251
  49.0 11.8 %collective-permute-start.13 = (f32[384,128]{1,0:T(8,128)S(1)}, f32[384,128]{1,0:T(8,128)S(1)}, u32[]{:S(2)}, u32[]{:S(2)}) collective-permute-start(f32[384,128]{1,0:T(8,128)S(1)} %collective-permute-done.11.refs_11_), channel_id=1, source_target_pairs={{0,48},{48,96},{96,144},{144,192},{192,240},{240,288},{288,336},{3... | collective-permute-start | bytes 589832 | tf_op jit(solution)/shard_map/ppermute | solution.py:251
  51.0 9.9 %collective-permute-start.6 = (f32[384,128]{1,0:T(8,128)S(1)}, f32[384,128]{1,0:T(8,128)S(1)}, u32[]{:S(2)}, u32[]{:S(2)}) collective-permute-start(f32[384,128]{1,0:T(8,128)S(1)} %collective-permute-done.4.refs_4_), channel_id=1, source_target_pairs={{0,336},{48,0},{96,48},{144,96},{192,144},{240,192},{288,240},{336... | collective-permute-start | bytes 589832 | tf_op jit(solution)/shard_map/ppermute | solution.py:251
  55.5 6.9 %collective-permute-start.15 = (f32[384,128]{1,0:T(8,128)S(1)}, f32[384,128]{1,0:T(8,128)S(1)}, u32[]{:S(2)}, u32[]{:S(2)}) collective-permute-start(f32[384,128]{1,0:T(8,128)S(1)} %collective-permute-done.14.refs_14_), channel_id=1, source_target_pairs={{0,336},{48,0},{96,48},{144,96},{192,144},{240,192},{288,240},{336... | collective-permute-start | bytes 589832 | tf_op jit(solution)/shard_map/ppermute | solution.py:251
  58.9 9.7 %collective-permute-start.7 = (f32[384,128]{1,0:T(8,128)S(1)}, f32[384,128]{1,0:T(8,128)S(1)}, u32[]{:S(2)}, u32[]{:S(2)}) collective-permute-start(f32[384,128]{1,0:T(8,128)S(1)} %collective-permute-done.5.refs_5_), channel_id=1, source_target_pairs={{0,48},{48,96},{96,144},{144,192},{192,240},{240,288},{288,336},{3... | collective-permute-start | bytes 589832 | tf_op jit(solution)/shard_map/ppermute | solution.py:251
  70.4 17.8 %collective-permute-start.16 = (f32[12,128,256]{2,1,0:T(8,128)}, f32[12,128,256]{2,1,0:T(8,128)}, u32[]{:S(2)}, u32[]{:S(2)}) collective-permute-start(f32[12,128,256]{2,1,0:T(8,128)} %get-tuple-element.22), channel_id=1, source_target_pairs={{0,1},{1,0},{2,3},{3,2},{4,5},{5,4},{6,7},{7,6},{8,9},{9,8},{10,11... | collective-permute-start | bytes 4718600 | tf_op jit(solution)/shard_map/ppermute | solution.py:251
  83.8 11.7 %copy-start = (s32[6,2]{0,1:T(2,128)S(1)}, s32[6,2]{0,1:T(2,128)}, u32[]{:S(2)}) copy-start(s32[6,2]{0,1:T(2,128)} %param.7) | copy-start | bytes 148
  96.2 14.1 %collective-permute-start.21 = (f32[384,128]{1,0:T(8,128)S(1)}, f32[384,128]{1,0:T(8,128)S(1)}, u32[]{:S(2)}, u32[]{:S(2)}) collective-permute-start(f32[384,128]{1,0:T(8,128)S(1)} %shard_map.63.refs_0_), channel_id=1, source_target_pairs={{0,22},{2,0},{4,2},{6,4},{8,6},{10,8},{12,10},{14,12},{16,14},{18,... | collective-permute-start | bytes 589832 | tf_op jit(solution)/shard_map/ppermute | solution.py:251
  104.0 15.3 %collective-permute-start.17 = (f32[384,128]{1,0:T(8,128)S(1)}, f32[384,128]{1,0:T(8,128)S(1)}, u32[]{:S(2)}, u32[]{:S(2)}) collective-permute-start(f32[384,128]{1,0:T(8,128)S(1)} %shard_map.63.refs_0_), channel_id=1, source_target_pairs={{0,2},{2,4},{4,6},{6,8},{8,10},{10,12},{12,14},{14,16},{16,18},{18... | collective-permute-start | bytes 589832 | tf_op jit(solution)/shard_map/ppermute | solution.py:251
  105.9 19.7 %collective-permute-start.23 = (f32[384,128]{1,0:T(8,128)S(1)}, f32[384,128]{1,0:T(8,128)S(1)}, u32[]{:S(2)}, u32[]{:S(2)}) collective-permute-start(f32[384,128]{1,0:T(8,128)S(1)} %shard_map.63.refs_0_), channel_id=1, source_target_pairs={{0,12},{2,14},{4,16},{6,18},{8,20},{10,22},{12,0},{14,2},{16,4},{1... | collective-permute-start | bytes 589832 | tf_op jit(solution)/shard_map/ppermute | solution.py:251
  110.2 19.0 %collective-permute-start.22 = (f32[384,128]{1,0:T(8,128)S(1)}, f32[384,128]{1,0:T(8,128)S(1)}, u32[]{:S(2)}, u32[]{:S(2)}) collective-permute-start(f32[384,128]{1,0:T(8,128)S(1)} %collective-permute-done.21.refs_2_), channel_id=1, source_target_pairs={{0,22},{2,0},{4,2},{6,4},{8,6},{10,8},{12,10},{14,12},{16,14},{18,... | collective-permute-start | bytes 589832 | tf_op jit(solution)/shard_map/ppermute | solution.py:251
  119.3 15.2 %collective-permute-start.18 = (f32[384,128]{1,0:T(8,128)S(1)}, f32[384,128]{1,0:T(8,128)S(1)}, u32[]{:S(2)}, u32[]{:S(2)}) collective-permute-start(f32[384,128]{1,0:T(8,128)S(1)} %collective-permute-done.17.refs_1_), channel_id=1, source_target_pairs={{0,2},{2,4},{4,6},{6,8},{8,10},{10,12},{12,14},{14,16},{16,18},{18... | collective-permute-start | bytes 589832 | tf_op jit(solution)/shard_map/ppermute | solution.py:251
  129.2 13.8 %collective-permute-start.24 = (f32[384,128]{1,0:T(8,128)S(1)}, f32[384,128]{1,0:T(8,128)S(1)}, u32[]{:S(2)}, u32[]{:S(2)}) collective-permute-start(f32[384,128]{1,0:T(8,128)S(1)} %collective-permute-done.22.refs_0_), channel_id=1, source_target_pairs={{0,22},{2,0},{4,2},{6,4},{8,6},{10,8},{12,10},{14,12},{16,14},{18,... | collective-permute-start | bytes 589832 | tf_op jit(solution)/shard_map/ppermute | solution.py:251
  134.6 11.8 %collective-permute-start.19 = (f32[384,128]{1,0:T(8,128)S(1)}, f32[384,128]{1,0:T(8,128)S(1)}, u32[]{:S(2)}, u32[]{:S(2)}) collective-permute-start(f32[384,128]{1,0:T(8,128)S(1)} %collective-permute-done.18.refs_3_), channel_id=1, source_target_pairs={{0,2},{2,4},{4,6},{6,8},{8,10},{10,12},{12,14},{14,16},{16,18},{18... | collective-permute-start | bytes 589832 | tf_op jit(solution)/shard_map/ppermute | solution.py:251
  136.5 15.1 %collective-permute-start.26 = (f32[384,128]{1,0:T(8,128)S(1)}, f32[384,128]{1,0:T(8,128)S(1)}, u32[]{:S(2)}, u32[]{:S(2)}) collective-permute-start(f32[384,128]{1,0:T(8,128)S(1)} %collective-permute-done.23.refs_3_), channel_id=1, source_target_pairs={{0,2},{2,4},{4,6},{6,8},{8,10},{10,12},{12,14},{14,16},{16,18},{18... | collective-permute-start | bytes 589832 | tf_op jit(solution)/shard_map/ppermute | solution.py:251
  138.4 13.2 %collective-permute-start.27 = (f32[384,128]{1,0:T(8,128)S(1)}, f32[384,128]{1,0:T(8,128)S(1)}, u32[]{:S(2)}, u32[]{:S(2)}) collective-permute-start(f32[384,128]{1,0:T(8,128)S(1)} %collective-permute-done.23.refs_3_), channel_id=1, source_target_pairs={{0,22},{2,0},{4,2},{6,4},{8,6},{10,8},{12,10},{14,12},{16,14},{18,... | collective-permute-start | bytes 589832 | tf_op jit(solution)/shard_map/ppermute | solution.py:251
  143.0 8.6 %collective-permute-start.25 = (f32[384,128]{1,0:T(8,128)S(1)}, f32[384,128]{1,0:T(8,128)S(1)}, u32[]{:S(2)}, u32[]{:S(2)}) collective-permute-start(f32[384,128]{1,0:T(8,128)S(1)} %collective-permute-done.24.refs_2_), channel_id=1, source_target_pairs={{0,22},{2,0},{4,2},{6,4},{8,6},{10,8},{12,10},{14,12},{16,14},{18,... | collective-permute-start | bytes 589832 | tf_op jit(solution)/shard_map/ppermute | solution.py:251
  146.4 7.6 %collective-permute-start.20 = (f32[384,128]{1,0:T(8,128)S(1)}, f32[384,128]{1,0:T(8,128)S(1)}, u32[]{:S(2)}, u32[]{:S(2)}) collective-permute-start(f32[384,128]{1,0:T(8,128)S(1)} %collective-permute-done.19.refs_1_), channel_id=1, source_target_pairs={{0,2},{2,4},{4,6},{6,8},{8,10},{10,12},{12,14},{14,16},{16,18},{18... | collective-permute-start | bytes 589832 | tf_op jit(solution)/shard_map/ppermute | solution.py:251
Sparse Core Ops, SparseCore 0:
  11.0 72.7 all-gather.5

commit v11 on v6

--- a/solution.py
+++ b/solution.py
@@ -124,12 +124,18 @@
     copies = [
         pltpu.make_async_copy(left.at[pl.ds(per * p, per)], held.at[p], sems.at[p]) for p in range(parts)
     ]
-    for copy in copies:
+    half = parts // 2
+    for copy in copies[:half]:
         copy.start()
-    for copy in copies:
-        copy.wait()
     acc = None
     for z in range(NZ):
+        if z == 0:
+            for first, second in zip(copies[:half], copies[half:]):
+                first.wait()
+                second.start()
+        if z == NZ // 2:
+            for copy in copies[half:]:
+                copy.wait()
         u = 2 * z
         p, k = divmod(u, per)
         a = jnp.concatenate([held[p, k], held[p, k + 1]], axis=1)
@@ -167,9 +173,10 @@
     z = lax.axis_index("z")
     at = [lax.rem(z + (off + NZ), NZ) for off in offsets]
     for k in range(0, n, 2):
-        a = jnp.concatenate([refs[k][...], refs[k + 1][...]], axis=1)
-        bh = jnp.concatenate([hi[at[k]], hi[at[k + 1]]], axis=0)
-        bl = jnp.concatenate([lo[at[k]], lo[at[k + 1]]], axis=0)
+        pair = range(k, min(k + 2, n))
+        a = jnp.concatenate([refs[i][...] for i in pair], axis=1)
+        bh = jnp.concatenate([hi[at[i]] for i in pair], axis=0)
+        bl = jnp.concatenate([lo[at[i]] for i in pair], axis=0)
         term = split_dot(a, bh, bl)
         acc = term if acc is None else acc + term
     if last:
@@ -301,7 +308,8 @@
     blocks.append((-6, up[5]))
     acc = second_product(operand, blocks[:4])
     acc = second_product(operand, blocks[4:8], acc)
-    halves = join(*second_product(operand, blocks[8:], acc, last=True))
+    acc = second_product(operand, blocks[8:11], acc)
+    halves = join(*second_product(operand, blocks[11:], acc, last=True))
     return filtered(kept.T, halves, square)
 
 

time: 173 us -> 174 us (level)
  transfers between devices with their start and end apart: 29 -> 29, of which waited for: 10 -> 10; matrix products, arithmetic and copies ran while one was open for 0% -> 0% of each run, Pallas kernels for 5% -> 7%
where the time goes in v11:
time: 174 us; the launch traced here: 173 us
  starting transfers between devices  98.1 us (56%)
  blocking collectives  22.8 us (13%)
  waiting for transfers between devices  22 us (13%)
  Pallas kernels  15.6 us (9%)
  between operations  14.5 us (8%)
    ppermute x26, starting transfers between devices, shift(): return lax.ppermute(x, axis, [(i, (i + step) % n) for i in range(n)])  91 us
    ppermute x26, waiting for transfers between devices, shift(): return lax.ppermute(x, axis, [(i, (i + step) % n) for i in range(n)])  17.3 us
    all_gather x2, blocking collectives, filtered(): pair = lax.all_gather(other, 'xl', axis=0)  14.1 us
    all_gather x1, blocking collectives, join(): both = lax.all_gather(give, 'c', axis=0)  8.65 us
    pallas_call x1, Pallas kernels, first_product(): pl.pallas_call(first_kernel, out_shape=(block, block), in_specs=[HB, VM,...  5.61 us
    ppermute x1, starting transfers between devices, body(): far = lax.ppermute(masked, ('xh', 'xl'), [(1, 0), (2, 3), (0, 2), (3, 1)])  5.48 us
  transfers between devices with their start and end apart: 29, of which 10 were waited for; matrix products, arithmetic and copies ran while one was open for 0% of the time, Pallas kernels for 7%

profile of v11, /device:TPU:1, one launch (start us, length us, event | category | flops | bytes accessed | tf_op | source)
XLA Modules:
  0.0 172.9 jit_solution(10068729394643690817)
XLA Ops:
  7.2 0.0 all-gather.6.cloned.1.call-start
  7.2 1.7 shard_map.59
  8.9 0.0 all-gather.6.cloned.1.call-update
  8.9 5.5 %collective-permute-start.8 = (f32[384,128]{1,0:T(8,128)}, f32[384,128]{1,0:T(8,128)S(1)}, u32[]{:S(2)}, u32[]{:S(2)}) collective-permute-start(f32[384,128]{1,0:T(8,128)} %shard_map.59), channel_id=1, source_target_pairs={{24,0},{384,408},{0,384},{408,24},{25,1},{385,409},{1,385},{409,25... | collective-permute-start | bytes 589832 | tf_op jit(solution)/shard_map/ppermute | solution.py:292
  14.4 1.6 collective-permute-start
  16.0 1.3 collective-permute-done.8.refs_8_
  17.3 6.1 %collective-permute-start.10 = (f32[384,128]{1,0:T(8,128)S(1)}, f32[384,128]{1,0:T(8,128)S(1)}, u32[]{:S(2)}, u32[]{:S(2)}) collective-permute-start(f32[384,128]{1,0:T(8,128)S(1)} %collective-permute-done.8.refs_8_), channel_id=1, source_target_pairs={{0,336},{48,0},{96,48},{144,96},{192,144},{240,192},{288,240},{336... | collective-permute-start | bytes 589832 | tf_op jit(solution)/shard_map/ppermute | solution.py:258
  23.4 1.9 %collective-permute-start.1 = (f32[384,128]{1,0:T(8,128)S(1)}, f32[384,128]{1,0:T(8,128)S(1)}, u32[]{:S(2)}, u32[]{:S(2)}) collective-permute-start(f32[384,128]{1,0:T(8,128)S(1)} %collective-permute-done.refs_0_), channel_id=1, source_target_pairs={{0,48},{48,96},{96,144},{144,192},{192,240},{240,288},{288,336},{3... | collective-permute-start | bytes 589832 | tf_op jit(solution)/shard_map/ppermute | solution.py:258
  25.3 1.9 %collective-permute-start.9 = (f32[384,128]{1,0:T(8,128)S(1)}, f32[384,128]{1,0:T(8,128)S(1)}, u32[]{:S(2)}, u32[]{:S(2)}) collective-permute-start(f32[384,128]{1,0:T(8,128)S(1)} %collective-permute-done.8.refs_8_), channel_id=1, source_target_pairs={{0,48},{48,96},{96,144},{144,192},{192,240},{240,288},{288,336},{3... | collective-permute-start | bytes 589832 | tf_op jit(solution)/shard_map/ppermute | solution.py:258
  27.3 4.6 %collective-permute-start.2 = (f32[384,128]{1,0:T(8,128)S(1)}, f32[384,128]{1,0:T(8,128)S(1)}, u32[]{:S(2)}, u32[]{:S(2)}) collective-permute-start(f32[384,128]{1,0:T(8,128)S(1)} %collective-permute-done.refs_0_), channel_id=1, source_target_pairs={{0,336},{48,0},{96,48},{144,96},{192,144},{240,192},{288,240},{336... | collective-permute-start | bytes 589832 | tf_op jit(solution)/shard_map/ppermute | solution.py:258
  31.8 3.4 %collective-permute-start.12 = (f32[384,128]{1,0:T(8,128)S(1)}, f32[384,128]{1,0:T(8,128)S(1)}, u32[]{:S(2)}, u32[]{:S(2)}) collective-permute-start(f32[384,128]{1,0:T(8,128)S(1)} %collective-permute-done.10.refs_10_), channel_id=1, source_target_pairs={{0,336},{48,0},{96,48},{144,96},{192,144},{240,192},{288,240},{336... | collective-permute-start | bytes 589832 | tf_op jit(solution)/shard_map/ppermute | solution.py:258
  35.2 0.0 collective-permute-done.1.refs_1_
  35.2 1.9 %collective-permute-start.3 = (f32[384,128]{1,0:T(8,128)S(1)}, f32[384,128]{1,0:T(8,128)S(1)}, u32[]{:S(2)}, u32[]{:S(2)}) collective-permute-start(f32[384,128]{1,0:T(8,128)S(1)} %collective-permute-done.1.refs_1_), channel_id=1, source_target_pairs={{0,48},{48,96},{96,144},{144,192},{192,240},{240,288},{288,336},{3... | collective-permute-start | bytes 589832 | tf_op jit(solution)/shard_map/ppermute | solution.py:258
  37.2 0.0 collective-permute-done.9.refs_9_
  37.2 1.9 %collective-permute-start.11 = (f32[384,128]{1,0:T(8,128)S(1)}, f32[384,128]{1,0:T(8,128)S(1)}, u32[]{:S(2)}, u32[]{:S(2)}) collective-permute-start(f32[384,128]{1,0:T(8,128)S(1)} %collective-permute-done.9.refs_9_), channel_id=1, source_target_pairs={{0,48},{48,96},{96,144},{144,192},{192,240},{240,288},{288,336},{3... | collective-permute-start | bytes 589832 | tf_op jit(solution)/shard_map/ppermute | solution.py:258
  39.1 4.6 %collective-permute-start.4 = (f32[384,128]{1,0:T(8,128)S(1)}, f32[384,128]{1,0:T(8,128)S(1)}, u32[]{:S(2)}, u32[]{:S(2)}) collective-permute-start(f32[384,128]{1,0:T(8,128)S(1)} %collective-permute-done.2.refs_2_), channel_id=1, source_target_pairs={{0,336},{48,0},{96,48},{144,96},{192,144},{240,192},{288,240},{336... | collective-permute-start | bytes 589832 | tf_op jit(solution)/shard_map/ppermute | solution.py:258
  43.7 0.0 collective-permute-done.12.refs_12_
  43.7 3.4 %collective-permute-start.14 = (f32[384,128]{1,0:T(8,128)S(1)}, f32[384,128]{1,0:T(8,128)S(1)}, u32[]{:S(2)}, u32[]{:S(2)}) collective-permute-start(f32[384,128]{1,0:T(8,128)S(1)} %collective-permute-done.12.refs_12_), channel_id=1, source_target_pairs={{0,336},{48,0},{96,48},{144,96},{192,144},{240,192},{288,240},{336... | collective-permute-start | bytes 589832 | tf_op jit(solution)/shard_map/ppermute | solution.py:258
  47.1 1.9 %collective-permute-start.5 = (f32[384,128]{1,0:T(8,128)S(1)}, f32[384,128]{1,0:T(8,128)S(1)}, u32[]{:S(2)}, u32[]{:S(2)}) collective-permute-start(f32[384,128]{1,0:T(8,128)S(1)} %collective-permute-done.3.refs_3_), channel_id=1, source_target_pairs={{0,48},{48,96},{96,144},{144,192},{192,240},{240,288},{288,336},{3... | collective-permute-start | bytes 589832 | tf_op jit(solution)/shard_map/ppermute | solution.py:258
  49.0 0.0 collective-permute-done.11.refs_11_
  49.0 1.9 %collective-permute-start.13 = (f32[384,128]{1,0:T(8,128)S(1)}, f32[384,128]{1,0:T(8,128)S(1)}, u32[]{:S(2)}, u32[]{:S(2)}) collective-permute-start(f32[384,128]{1,0:T(8,128)S(1)} %collective-permute-done.11.refs_11_), channel_id=1, source_target_pairs={{0,48},{48,96},{96,144},{144,192},{192,240},{240,288},{288,336},{3... | collective-permute-start | bytes 589832 | tf_op jit(solution)/shard_map/ppermute | solution.py:258
  50.9 0.0 collective-permute-done.4.refs_4_
  51.0 4.6 %collective-permute-start.6 = (f32[384,128]{1,0:T(8,128)S(1)}, f32[384,128]{1,0:T(8,128)S(1)}, u32[]{:S(2)}, u32[]{:S(2)}) collective-permute-start(f32[384,128]{1,0:T(8,128)S(1)} %collective-permute-done.4.refs_4_), channel_id=1, source_target_pairs={{0,336},{48,0},{96,48},{144,96},{192,144},{240,192},{288,240},{336... | collective-permute-start | bytes 589832 | tf_op jit(solution)/shard_map/ppermute | solution.py:258
  55.5 0.0 collective-permute-done.14.refs_14_
  55.5 3.4 %collective-permute-start.15 = (f32[384,128]{1,0:T(8,128)S(1)}, f32[384,128]{1,0:T(8,128)S(1)}, u32[]{:S(2)}, u32[]{:S(2)}) collective-permute-start(f32[384,128]{1,0:T(8,128)S(1)} %collective-permute-done.14.refs_14_), channel_id=1, source_target_pairs={{0,336},{48,0},{96,48},{144,96},{192,144},{240,192},{288,240},{336... | collective-permute-start | bytes 589832 | tf_op jit(solution)/shard_map/ppermute | solution.py:258
  58.9 0.0 collective-permute-done.5.refs_5_
  58.9 1.9 %collective-permute-start.7 = (f32[384,128]{1,0:T(8,128)S(1)}, f32[384,128]{1,0:T(8,128)S(1)}, u32[]{:S(2)}, u32[]{:S(2)}) collective-permute-start(f32[384,128]{1,0:T(8,128)S(1)} %collective-permute-done.5.refs_5_), channel_id=1, source_target_pairs={{0,48},{48,96},{96,144},{144,192},{192,240},{240,288},{288,336},{3... | collective-permute-start | bytes 589832 | tf_op jit(solution)/shard_map/ppermute | solution.py:258
  60.9 0.0 collective-permute-done.6.refs_6_
  60.9 1.6 collective-permute-done.15.refs_15_
  62.5 6.1 %collective-permute-done.7.refs_7_ = f32[384,128]{1,0:T(8,128)S(1)} collective-permute-done((f32[384,128]{1,0:T(8,128)S(1)}, f32[384,128]{1,0:T(8,128)S(1)}, u32[]{:S(2)}, u32[]{:S(2)}) %collective-permute-start.7) | collective-permute-done | bytes 196640 | tf_op jit(solution)/shard_map/ppermute | solution.py:258
  68.6 1.8 %shard_map.60 = (bf16[24,128,256]{2,1,0:T(8,128)(2,1)S(1)}, bf16[24,128,256]{2,1,0:T(8,128)(2,1)S(1)}, f32[12,128,256]{2,1,0:T(8,128)}) custom-call(f32[384,128]{1,0:T(8,128)S(1)} %collective-permute-done.refs_0_, f32[384,128]{1,0:T(8,128)S(1)} %collective-permute-done.1.refs_1_, f32[384,128]{1,0:T(8,128)S(1)} %collective-permute-done.2.refs_2_, ...), custom_call_target="tpu_custom_call" | custom-call | tf_op jit(solution)/shard_map/pallas_call | solution.py:93
  70.4 10.1 %collective-permute-start.16 = (f32[12,128,256]{2,1,0:T(8,128)}, f32[12,128,256]{2,1,0:T(8,128)}, u32[]{:S(2)}, u32[]{:S(2)}) collective-permute-start(f32[12,128,256]{2,1,0:T(8,128)} %get-tuple-element.20), channel_id=1, source_target_pairs={{0,1},{1,0},{2,3},{3,2},{4,5},{5,4},{6,7},{7,6},{8,9},{9,8},{10,11... | collective-permute-start | bytes 4718600 | tf_op jit(solution)/shard_map/ppermute | solution.py:258
  80.5 3.3 %all-gather.6.cloned.1.call-done = f32[9216,128]{1,0:T(8,128)} async-done(((f32[384,128]{1,0:T(8,128)}), f32[9216,128]{1,0:T(8,128)}) %all-gather.6.cloned.1.call-update) | async-done | bytes 4718608 | tf_op jit(solution)/shard_map/all_gather | solution.py:289
  83.8 5.6 %shard_map.61 = (f32[384,128]{1,0:T(8,128)S(1)}, f32[384,128]{1,0:T(8,128)S(1)}) custom-call(f32[24,384,128]{2,1,0:T(8,128)} %bitcast.11, bf16[24,128,256]{2,1,0:T(8,128)(2,1)S(1)} %get-tuple-element.16.hi, bf16[24,128,256]{2,1,0:T(8,128)(2,1)S(1)} %get-tuple-element.17.lo), custom_call_target="tpu_custom_call" | custom-call | flops 1811939328 | tf_op jit(solution)/shard_map/pallas_call | solution.py:153
  89.5 0.0 collective-permute-done.16.took
  89.5 7.3 %all-gather.1 = f32[768,128]{1,0:T(8,128)S(1)} all-gather(f32[384,128]{1,0:T(8,128)S(1)} %get-tuple-element.25), channel_id=3, replica_groups=mesh['xh'=2,'y'=8,'xl'=2,'z'=12,'c'=2] {'xl'}, dimensions={0}, use_global_device_ids=true | all-gather | bytes 589824 | tf_op jit(solution)/shard_map/all_gather | solution.py:244
  96.8 0.6 shard_map.63.refs_0_
  97.4 1.9 %collective-permute-start.17 = (f32[384,128]{1,0:T(8,128)S(1)}, f32[384,128]{1,0:T(8,128)S(1)}, u32[]{:S(2)}, u32[]{:S(2)}) collective-permute-start(f32[384,128]{1,0:T(8,128)S(1)} %shard_map.63.refs_0_), channel_id=1, source_target_pairs={{0,2},{2,4},{4,6},{6,8},{8,10},{10,12},{12,14},{14,16},{16,18},{18... | collective-permute-start | bytes 589832 | tf_op jit(solution)/shard_map/ppermute | solution.py:258
  99.3 7.8 %collective-permute-start.23 = (f32[384,128]{1,0:T(8,128)S(1)}, f32[384,128]{1,0:T(8,128)S(1)}, u32[]{:S(2)}, u32[]{:S(2)}) collective-permute-start(f32[384,128]{1,0:T(8,128)S(1)} %shard_map.63.refs_0_), channel_id=1, source_target_pairs={{0,22},{2,0},{4,2},{6,4},{8,6},{10,8},{12,10},{14,12},{16,14},{18,... | collective-permute-start | bytes 589832 | tf_op jit(solution)/shard_map/ppermute | solution.py:258
  107.2 2.8 %collective-permute-done.17.refs_1_ = f32[384,128]{1,0:T(8,128)S(1)} collective-permute-done((f32[384,128]{1,0:T(8,128)S(1)}, f32[384,128]{1,0:T(8,128)S(1)}, u32[]{:S(2)}, u32[]{:S(2)}) %collective-permute-start.17) | collective-permute-done | bytes 196640 | tf_op jit(solution)/shard_map/ppermute | solution.py:258
  110.0 1.9 %collective-permute-start.18 = (f32[384,128]{1,0:T(8,128)S(1)}, f32[384,128]{1,0:T(8,128)S(1)}, u32[]{:S(2)}, u32[]{:S(2)}) collective-permute-start(f32[384,128]{1,0:T(8,128)S(1)} %collective-permute-done.17.refs_1_), channel_id=1, source_target_pairs={{0,2},{2,4},{4,6},{6,8},{8,10},{10,12},{12,14},{14,16},{16,18},{18... | collective-permute-start | bytes 589832 | tf_op jit(solution)/shard_map/ppermute | solution.py:258
  111.9 0.0 collective-permute-done.23.refs_2_
  111.9 4.6 %collective-permute-start.24 = (f32[384,128]{1,0:T(8,128)S(1)}, f32[384,128]{1,0:T(8,128)S(1)}, u32[]{:S(2)}, u32[]{:S(2)}) collective-permute-start(f32[384,128]{1,0:T(8,128)S(1)} %collective-permute-done.23.refs_2_), channel_id=1, source_target_pairs={{0,22},{2,0},{4,2},{6,4},{8,6},{10,8},{12,10},{14,12},{16,14},{18,... | collective-permute-start | bytes 589832 | tf_op jit(solution)/shard_map/ppermute | solution.py:258
  116.5 1.8 %collective-permute-done.18.refs_3_ = f32[384,128]{1,0:T(8,128)S(1)} collective-permute-done((f32[384,128]{1,0:T(8,128)S(1)}, f32[384,128]{1,0:T(8,128)S(1)}, u32[]{:S(2)}, u32[]{:S(2)}) %collective-permute-start.18) | collective-permute-done | bytes 196640 | tf_op jit(solution)/shard_map/ppermute | solution.py:258
  118.3 1.9 %collective-permute-start.19 = (f32[384,128]{1,0:T(8,128)S(1)}, f32[384,128]{1,0:T(8,128)S(1)}, u32[]{:S(2)}, u32[]{:S(2)}) collective-permute-start(f32[384,128]{1,0:T(8,128)S(1)} %collective-permute-done.18.refs_3_), channel_id=1, source_target_pairs={{0,2},{2,4},{4,6},{6,8},{8,10},{10,12},{12,14},{14,16},{16,18},{18... | collective-permute-start | bytes 589832 | tf_op jit(solution)/shard_map/ppermute | solution.py:258
  120.2 4.6 %collective-permute-start.25 = (f32[384,128]{1,0:T(8,128)S(1)}, f32[384,128]{1,0:T(8,128)S(1)}, u32[]{:S(2)}, u32[]{:S(2)}) collective-permute-start(f32[384,128]{1,0:T(8,128)S(1)} %collective-permute-done.24.refs_0_), channel_id=1, source_target_pairs={{0,22},{2,0},{4,2},{6,4},{8,6},{10,8},{12,10},{14,12},{16,14},{18,... | collective-permute-start | bytes 589832 | tf_op jit(solution)/shard_map/ppermute | solution.py:258
  124.8 1.1 collective-permute-done.19.refs_1_
  125.9 1.9 %collective-permute-start.20 = (f32[384,128]{1,0:T(8,128)S(1)}, f32[384,128]{1,0:T(8,128)S(1)}, u32[]{:S(2)}, u32[]{:S(2)}) collective-permute-start(f32[384,128]{1,0:T(8,128)S(1)} %collective-permute-done.19.refs_1_), channel_id=1, source_target_pairs={{0,2},{2,4},{4,6},{6,8},{8,10},{10,12},{12,14},{14,16},{16,18},{18... | collective-permute-start | bytes 589832 | tf_op jit(solution)/shard_map/ppermute | solution.py:258
  127.8 4.6 %collective-permute-start.26 = (f32[384,128]{1,0:T(8,128)S(1)}, f32[384,128]{1,0:T(8,128)S(1)}, u32[]{:S(2)}, u32[]{:S(2)}) collective-permute-start(f32[384,128]{1,0:T(8,128)S(1)} %collective-permute-done.25.refs_2_), channel_id=1, source_target_pairs={{0,22},{2,0},{4,2},{6,4},{8,6},{10,8},{12,10},{14,12},{16,14},{18,... | collective-permute-start | bytes 589832 | tf_op jit(solution)/shard_map/ppermute | solution.py:258
  132.4 1.1 collective-permute-done.20.refs_3_
  133.5 1.9 %collective-permute-start.21 = (f32[384,128]{1,0:T(8,128)S(1)}, f32[384,128]{1,0:T(8,128)S(1)}, u32[]{:S(2)}, u32[]{:S(2)}) collective-permute-start(f32[384,128]{1,0:T(8,128)S(1)} %collective-permute-done.20.refs_3_), channel_id=1, source_target_pairs={{0,2},{2,4},{4,6},{6,8},{8,10},{10,12},{12,14},{14,16},{16,18},{18... | collective-permute-start | bytes 589832 | tf_op jit(solution)/shard_map/ppermute | solution.py:258
  135.5 4.6 %collective-permute-start.27 = (f32[384,128]{1,0:T(8,128)S(1)}, f32[384,128]{1,0:T(8,128)S(1)}, u32[]{:S(2)}, u32[]{:S(2)}) collective-permute-start(f32[384,128]{1,0:T(8,128)S(1)} %collective-permute-done.26.refs_0_), channel_id=1, source_target_pairs={{0,22},{2,0},{4,2},{6,4},{8,6},{10,8},{12,10},{14,12},{16,14},{18,... | collective-permute-start | bytes 589832 | tf_op jit(solution)/shard_map/ppermute | solution.py:258
  140.0 1.1 collective-permute-done.21.refs_1_
  141.1 1.9 %collective-permute-start.22 = (f32[384,128]{1,0:T(8,128)S(1)}, f32[384,128]{1,0:T(8,128)S(1)}, u32[]{:S(2)}, u32[]{:S(2)}) collective-permute-start(f32[384,128]{1,0:T(8,128)S(1)} %collective-permute-done.21.refs_1_), channel_id=1, source_target_pairs={{0,2},{2,4},{4,6},{6,8},{8,10},{10,12},{12,14},{14,16},{16,18},{18... | collective-permute-start | bytes 589832 | tf_op jit(solution)/shard_map/ppermute | solution.py:258
  143.1 1.6 shard_map.62
  144.7 0.8 shard_map.64.refs_4_
  145.5 0.8 shard_map.65.refs_3_
  146.4 0.8 shard_map.66.refs_1_
  147.2 1.6 collective-permute-done.22.refs_0_
  148.8 0.5 shard_map.67
  149.2 8.6 %all-gather.2 = f32[768,256]{1,0:T(8,128)S(1)} all-gather(f32[384,256]{1,0:T(8,128)S(1)} %get-tuple-element.27), channel_id=4, replica_groups=mesh['xh'=2,'y'=8,'xl'=2,'z'=12,'c'=2] {'c'}, dimensions={0}, use_global_device_ids=true | all-gather | bytes 1179648 | tf_op jit(solution)/shard_map/all_gather | solution.py:214
  157.9 0.1 shard_map.68
  157.9 6.8 %all-gather.3 = f32[768,128]{1,0:T(8,128)S(1)} all-gather(f32[384,128]{1,0:T(8,128)S(1)} %get-tuple-element.29), channel_id=5, replica_groups=mesh['xh'=2,'y'=8,'xl'=2,'z'=12,'c'=2] {'xl'}, dimensions={0}, use_global_device_ids=true | all-gather | bytes 589824 | tf_op jit(solution)/shard_map/all_gather | solution.py:244
  164.7 1.3 shard_map.69
  (11 shorter events, 0.0 us)
Async XLA Ops:
  7.2 76.7 %all-gather.6.cloned.1.call-start = ((), (), s32[]{:S(2)}) async-start(), calls=%async_computation | async-start | bytes 4915200 | tf_op jit(solution)/shard_map/all_gather | solution.py:289
  8.9 8.4 %collective-permute-start.8 = (f32[384,128]{1,0:T(8,128)}, f32[384,128]{1,0:T(8,128)S(1)}, u32[]{:S(2)}, u32[]{:S(2)}) collective-permute-start(f32[384,128]{1,0:T(8,128)} %shard_map.59), channel_id=1, source_target_pairs={{24,0},{384,408},{0,384},{408,24},{25,1},{385,409},{1,385},{409,25... | collective-permute-start | bytes 589832 | tf_op jit(solution)/shard_map/ppermute | solution.py:292
  14.4 9.0 %collective-permute-start = (f32[384,128]{1,0:T(8,128)}, f32[384,128]{1,0:T(8,128)S(1)}, u32[]{:S(2)}, u32[]{:S(2)}) collective-permute-start(f32[384,128]{1,0:T(8,128)} %shard_map.59), channel_id=1, source_target_pairs={{0,0},{24,384},{384,24},{408,408},{1,1},{25,385},{385,25},{409,409... | collective-permute-start | bytes 589832 | tf_op jit(solution)/shard_map/ppermute | solution.py:291
  17.3 14.5 %collective-permute-start.10 = (f32[384,128]{1,0:T(8,128)S(1)}, f32[384,128]{1,0:T(8,128)S(1)}, u32[]{:S(2)}, u32[]{:S(2)}) collective-permute-start(f32[384,128]{1,0:T(8,128)S(1)} %collective-permute-done.8.refs_8_), channel_id=1, source_target_pairs={{0,336},{48,0},{96,48},{144,96},{192,144},{240,192},{288,240},{336... | collective-permute-start | bytes 589832 | tf_op jit(solution)/shard_map/ppermute | solution.py:258
  23.4 11.8 %collective-permute-start.1 = (f32[384,128]{1,0:T(8,128)S(1)}, f32[384,128]{1,0:T(8,128)S(1)}, u32[]{:S(2)}, u32[]{:S(2)}) collective-permute-start(f32[384,128]{1,0:T(8,128)S(1)} %collective-permute-done.refs_0_), channel_id=1, source_target_pairs={{0,48},{48,96},{96,144},{144,192},{192,240},{240,288},{288,336},{3... | collective-permute-start | bytes 589832 | tf_op jit(solution)/shard_map/ppermute | solution.py:258
  25.3 11.8 %collective-permute-start.9 = (f32[384,128]{1,0:T(8,128)S(1)}, f32[384,128]{1,0:T(8,128)S(1)}, u32[]{:S(2)}, u32[]{:S(2)}) collective-permute-start(f32[384,128]{1,0:T(8,128)S(1)} %collective-permute-done.8.refs_8_), channel_id=1, source_target_pairs={{0,48},{48,96},{96,144},{144,192},{192,240},{240,288},{288,336},{3... | collective-permute-start | bytes 589832 | tf_op jit(solution)/shard_map/ppermute | solution.py:258
  27.3 11.8 %collective-permute-start.2 = (f32[384,128]{1,0:T(8,128)S(1)}, f32[384,128]{1,0:T(8,128)S(1)}, u32[]{:S(2)}, u32[]{:S(2)}) collective-permute-start(f32[384,128]{1,0:T(8,128)S(1)} %collective-permute-done.refs_0_), channel_id=1, source_target_pairs={{0,336},{48,0},{96,48},{144,96},{192,144},{240,192},{288,240},{336... | collective-permute-start | bytes 589832 | tf_op jit(solution)/shard_map/ppermute | solution.py:258
  31.8 11.8 %collective-permute-start.12 = (f32[384,128]{1,0:T(8,128)S(1)}, f32[384,128]{1,0:T(8,128)S(1)}, u32[]{:S(2)}, u32[]{:S(2)}) collective-permute-start(f32[384,128]{1,0:T(8,128)S(1)} %collective-permute-done.10.refs_10_), channel_id=1, source_target_pairs={{0,336},{48,0},{96,48},{144,96},{192,144},{240,192},{288,240},{336... | collective-permute-start | bytes 589832 | tf_op jit(solution)/shard_map/ppermute | solution.py:258
  35.2 11.8 %collective-permute-start.3 = (f32[384,128]{1,0:T(8,128)S(1)}, f32[384,128]{1,0:T(8,128)S(1)}, u32[]{:S(2)}, u32[]{:S(2)}) collective-permute-start(f32[384,128]{1,0:T(8,128)S(1)} %collective-permute-done.1.refs_1_), channel_id=1, source_target_pairs={{0,48},{48,96},{96,144},{144,192},{192,240},{240,288},{288,336},{3... | collective-permute-start | bytes 589832 | tf_op jit(solution)/shard_map/ppermute | solution.py:258
  37.2 11.8 %collective-permute-start.11 = (f32[384,128]{1,0:T(8,128)S(1)}, f32[384,128]{1,0:T(8,128)S(1)}, u32[]{:S(2)}, u32[]{:S(2)}) collective-permute-start(f32[384,128]{1,0:T(8,128)S(1)} %collective-permute-done.9.refs_9_), channel_id=1, source_target_pairs={{0,48},{48,96},{96,144},{144,192},{192,240},{240,288},{288,336},{3... | collective-permute-start | bytes 589832 | tf_op jit(solution)/shard_map/ppermute | solution.py:258
  39.1 11.8 %collective-permute-start.4 = (f32[384,128]{1,0:T(8,128)S(1)}, f32[384,128]{1,0:T(8,128)S(1)}, u32[]{:S(2)}, u32[]{:S(2)}) collective-permute-start(f32[384,128]{1,0:T(8,128)S(1)} %collective-permute-done.2.refs_2_), channel_id=1, source_target_pairs={{0,336},{48,0},{96,48},{144,96},{192,144},{240,192},{288,240},{336... | collective-permute-start | bytes 589832 | tf_op jit(solution)/shard_map/ppermute | solution.py:258
  43.7 11.8 %collective-permute-start.14 = (f32[384,128]{1,0:T(8,128)S(1)}, f32[384,128]{1,0:T(8,128)S(1)}, u32[]{:S(2)}, u32[]{:S(2)}) collective-permute-start(f32[384,128]{1,0:T(8,128)S(1)} %collective-permute-done.12.refs_12_), channel_id=1, source_target_pairs={{0,336},{48,0},{96,48},{144,96},{192,144},{240,192},{288,240},{336... | collective-permute-start | bytes 589832 | tf_op jit(solution)/shard_map/ppermute | solution.py:258
  47.1 11.8 %collective-permute-start.5 = (f32[384,128]{1,0:T(8,128)S(1)}, f32[384,128]{1,0:T(8,128)S(1)}, u32[]{:S(2)}, u32[]{:S(2)}) collective-permute-start(f32[384,128]{1,0:T(8,128)S(1)} %collective-permute-done.3.refs_3_), channel_id=1, source_target_pairs={{0,48},{48,96},{96,144},{144,192},{192,240},{240,288},{288,336},{3... | collective-permute-start | bytes 589832 | tf_op jit(solution)/shard_map/ppermute | solution.py:258
  49.0 11.8 %collective-permute-start.13 = (f32[384,128]{1,0:T(8,128)S(1)}, f32[384,128]{1,0:T(8,128)S(1)}, u32[]{:S(2)}, u32[]{:S(2)}) collective-permute-start(f32[384,128]{1,0:T(8,128)S(1)} %collective-permute-done.11.refs_11_), channel_id=1, source_target_pairs={{0,48},{48,96},{96,144},{144,192},{192,240},{240,288},{288,336},{3... | collective-permute-start | bytes 589832 | tf_op jit(solution)/shard_map/ppermute | solution.py:258
  51.0 9.9 %collective-permute-start.6 = (f32[384,128]{1,0:T(8,128)S(1)}, f32[384,128]{1,0:T(8,128)S(1)}, u32[]{:S(2)}, u32[]{:S(2)}) collective-permute-start(f32[384,128]{1,0:T(8,128)S(1)} %collective-permute-done.4.refs_4_), channel_id=1, source_target_pairs={{0,336},{48,0},{96,48},{144,96},{192,144},{240,192},{288,240},{336... | collective-permute-start | bytes 589832 | tf_op jit(solution)/shard_map/ppermute | solution.py:258
  55.5 6.9 %collective-permute-start.15 = (f32[384,128]{1,0:T(8,128)S(1)}, f32[384,128]{1,0:T(8,128)S(1)}, u32[]{:S(2)}, u32[]{:S(2)}) collective-permute-start(f32[384,128]{1,0:T(8,128)S(1)} %collective-permute-done.14.refs_14_), channel_id=1, source_target_pairs={{0,336},{48,0},{96,48},{144,96},{192,144},{240,192},{288,240},{336... | collective-permute-start | bytes 589832 | tf_op jit(solution)/shard_map/ppermute | solution.py:258
  58.9 9.7 %collective-permute-start.7 = (f32[384,128]{1,0:T(8,128)S(1)}, f32[384,128]{1,0:T(8,128)S(1)}, u32[]{:S(2)}, u32[]{:S(2)}) collective-permute-start(f32[384,128]{1,0:T(8,128)S(1)} %collective-permute-done.5.refs_5_), channel_id=1, source_target_pairs={{0,48},{48,96},{96,144},{144,192},{192,240},{240,288},{288,336},{3... | collective-permute-start | bytes 589832 | tf_op jit(solution)/shard_map/ppermute | solution.py:258
  70.4 19.0 %collective-permute-start.16 = (f32[12,128,256]{2,1,0:T(8,128)}, f32[12,128,256]{2,1,0:T(8,128)}, u32[]{:S(2)}, u32[]{:S(2)}) collective-permute-start(f32[12,128,256]{2,1,0:T(8,128)} %get-tuple-element.20), channel_id=1, source_target_pairs={{0,1},{1,0},{2,3},{3,2},{4,5},{5,4},{6,7},{7,6},{8,9},{9,8},{10,11... | collective-permute-start | bytes 4718600 | tf_op jit(solution)/shard_map/ppermute | solution.py:258
  83.8 13.0 %copy-start = (s32[6,2]{0,1:T(2,128)S(1)}, s32[6,2]{0,1:T(2,128)}, u32[]{:S(2)}) copy-start(s32[6,2]{0,1:T(2,128)} %param.7) | copy-start | bytes 148
  97.4 12.6 %collective-permute-start.17 = (f32[384,128]{1,0:T(8,128)S(1)}, f32[384,128]{1,0:T(8,128)S(1)}, u32[]{:S(2)}, u32[]{:S(2)}) collective-permute-start(f32[384,128]{1,0:T(8,128)S(1)} %shard_map.63.refs_0_), channel_id=1, source_target_pairs={{0,2},{2,4},{4,6},{6,8},{8,10},{10,12},{12,14},{14,16},{16,18},{18... | collective-permute-start | bytes 589832 | tf_op jit(solution)/shard_map/ppermute | solution.py:258
  99.3 12.6 %collective-permute-start.23 = (f32[384,128]{1,0:T(8,128)S(1)}, f32[384,128]{1,0:T(8,128)S(1)}, u32[]{:S(2)}, u32[]{:S(2)}) collective-permute-start(f32[384,128]{1,0:T(8,128)S(1)} %shard_map.63.refs_0_), channel_id=1, source_target_pairs={{0,22},{2,0},{4,2},{6,4},{8,6},{10,8},{12,10},{14,12},{16,14},{18,... | collective-permute-start | bytes 589832 | tf_op jit(solution)/shard_map/ppermute | solution.py:258
  110.0 8.4 %collective-permute-start.18 = (f32[384,128]{1,0:T(8,128)S(1)}, f32[384,128]{1,0:T(8,128)S(1)}, u32[]{:S(2)}, u32[]{:S(2)}) collective-permute-start(f32[384,128]{1,0:T(8,128)S(1)} %collective-permute-done.17.refs_1_), channel_id=1, source_target_pairs={{0,2},{2,4},{4,6},{6,8},{8,10},{10,12},{12,14},{14,16},{16,18},{18... | collective-permute-start | bytes 589832 | tf_op jit(solution)/shard_map/ppermute | solution.py:258
  111.9 8.3 %collective-permute-start.24 = (f32[384,128]{1,0:T(8,128)S(1)}, f32[384,128]{1,0:T(8,128)S(1)}, u32[]{:S(2)}, u32[]{:S(2)}) collective-permute-start(f32[384,128]{1,0:T(8,128)S(1)} %collective-permute-done.23.refs_2_), channel_id=1, source_target_pairs={{0,22},{2,0},{4,2},{6,4},{8,6},{10,8},{12,10},{14,12},{16,14},{18,... | collective-permute-start | bytes 589832 | tf_op jit(solution)/shard_map/ppermute | solution.py:258
  118.3 7.6 %collective-permute-start.19 = (f32[384,128]{1,0:T(8,128)S(1)}, f32[384,128]{1,0:T(8,128)S(1)}, u32[]{:S(2)}, u32[]{:S(2)}) collective-permute-start(f32[384,128]{1,0:T(8,128)S(1)} %collective-permute-done.18.refs_3_), channel_id=1, source_target_pairs={{0,2},{2,4},{4,6},{6,8},{8,10},{10,12},{12,14},{14,16},{16,18},{18... | collective-permute-start | bytes 589832 | tf_op jit(solution)/shard_map/ppermute | solution.py:258
  120.2 7.6 %collective-permute-start.25 = (f32[384,128]{1,0:T(8,128)S(1)}, f32[384,128]{1,0:T(8,128)S(1)}, u32[]{:S(2)}, u32[]{:S(2)}) collective-permute-start(f32[384,128]{1,0:T(8,128)S(1)} %collective-permute-done.24.refs_0_), channel_id=1, source_target_pairs={{0,22},{2,0},{4,2},{6,4},{8,6},{10,8},{12,10},{14,12},{16,14},{18,... | collective-permute-start | bytes 589832 | tf_op jit(solution)/shard_map/ppermute | solution.py:258
  125.9 7.6 %collective-permute-start.20 = (f32[384,128]{1,0:T(8,128)S(1)}, f32[384,128]{1,0:T(8,128)S(1)}, u32[]{:S(2)}, u32[]{:S(2)}) collective-permute-start(f32[384,128]{1,0:T(8,128)S(1)} %collective-permute-done.19.refs_1_), channel_id=1, source_target_pairs={{0,2},{2,4},{4,6},{6,8},{8,10},{10,12},{12,14},{14,16},{16,18},{18... | collective-permute-start | bytes 589832 | tf_op jit(solution)/shard_map/ppermute | solution.py:258
  127.8 7.6 %collective-permute-start.26 = (f32[384,128]{1,0:T(8,128)S(1)}, f32[384,128]{1,0:T(8,128)S(1)}, u32[]{:S(2)}, u32[]{:S(2)}) collective-permute-start(f32[384,128]{1,0:T(8,128)S(1)} %collective-permute-done.25.refs_2_), channel_id=1, source_target_pairs={{0,22},{2,0},{4,2},{6,4},{8,6},{10,8},{12,10},{14,12},{16,14},{18,... | collective-permute-start | bytes 589832 | tf_op jit(solution)/shard_map/ppermute | solution.py:258
  133.5 7.6 %collective-permute-start.21 = (f32[384,128]{1,0:T(8,128)S(1)}, f32[384,128]{1,0:T(8,128)S(1)}, u32[]{:S(2)}, u32[]{:S(2)}) collective-permute-start(f32[384,128]{1,0:T(8,128)S(1)} %collective-permute-done.20.refs_3_), channel_id=1, source_target_pairs={{0,2},{2,4},{4,6},{6,8},{8,10},{10,12},{12,14},{14,16},{16,18},{18... | collective-permute-start | bytes 589832 | tf_op jit(solution)/shard_map/ppermute | solution.py:258
  135.5 10.9 %collective-permute-start.27 = (f32[384,128]{1,0:T(8,128)S(1)}, f32[384,128]{1,0:T(8,128)S(1)}, u32[]{:S(2)}, u32[]{:S(2)}) collective-permute-start(f32[384,128]{1,0:T(8,128)S(1)} %collective-permute-done.26.refs_0_), channel_id=1, source_target_pairs={{0,22},{2,0},{4,2},{6,4},{8,6},{10,8},{12,10},{14,12},{16,14},{18,... | collective-permute-start | bytes 589832 | tf_op jit(solution)/shard_map/ppermute | solution.py:258
  141.1 7.6 %collective-permute-start.22 = (f32[384,128]{1,0:T(8,128)S(1)}, f32[384,128]{1,0:T(8,128)S(1)}, u32[]{:S(2)}, u32[]{:S(2)}) collective-permute-start(f32[384,128]{1,0:T(8,128)S(1)} %collective-permute-done.21.refs_1_), channel_id=1, source_target_pairs={{0,2},{2,4},{4,6},{6,8},{8,10},{10,12},{12,14},{14,16},{16,18},{18... | collective-permute-start | bytes 589832 | tf_op jit(solution)/shard_map/ppermute | solution.py:258
Sparse Core Ops, SparseCore 0:
  11.0 72.7 all-gather.5

commit v12 on v6

--- a/solution.py
+++ b/solution.py
@@ -167,9 +167,10 @@
     z = lax.axis_index("z")
     at = [lax.rem(z + (off + NZ), NZ) for off in offsets]
     for k in range(0, n, 2):
-        a = jnp.concatenate([refs[k][...], refs[k + 1][...]], axis=1)
-        bh = jnp.concatenate([hi[at[k]], hi[at[k + 1]]], axis=0)
-        bl = jnp.concatenate([lo[at[k]], lo[at[k + 1]]], axis=0)
+        pair = range(k, min(k + 2, n))
+        a = jnp.concatenate([refs[i][...] for i in pair], axis=1)
+        bh = jnp.concatenate([hi[at[i]] for i in pair], axis=0)
+        bl = jnp.concatenate([lo[at[i]] for i in pair], axis=0)
         term = split_dot(a, bh, bl)
         acc = term if acc is None else acc + term
     if last:
@@ -301,7 +302,8 @@
     blocks.append((-6, up[5]))
     acc = second_product(operand, blocks[:4])
     acc = second_product(operand, blocks[4:8], acc)
-    halves = join(*second_product(operand, blocks[8:], acc, last=True))
+    acc = second_product(operand, blocks[8:11], acc)
+    halves = join(*second_product(operand, blocks[11:], acc, last=True))
     return filtered(kept.T, halves, square)
 
 

time: 173 us -> 173 us (level)
  transfers between devices with their start and end apart: 29 -> 29, of which waited for: 10 -> 10; matrix products, arithmetic and copies ran while one was open for 0% -> 0% of each run, Pallas kernels for 5% -> 6%
where the time goes in v12:
time: 173 us; the launch traced here: 172 us
  starting transfers between devices  98.1 us (57%)
  blocking collectives  22.8 us (13%)
  waiting for transfers between devices  22 us (13%)
  between operations  14.5 us (8%)
  Pallas kernels  14.3 us (8%)
    ppermute x26, starting transfers between devices, shift(): return lax.ppermute(x, axis, [(i, (i + step) % n) for i in range(n)])  91 us
    ppermute x26, waiting for transfers between devices, shift(): return lax.ppermute(x, axis, [(i, (i + step) % n) for i in range(n)])  17.3 us
    all_gather x2, blocking collectives, filtered(): pair = lax.all_gather(other, 'xl', axis=0)  14.1 us
    all_gather x1, blocking collectives, join(): both = lax.all_gather(give, 'c', axis=0)  8.65 us
    ppermute x1, starting transfers between devices, body(): far = lax.ppermute(masked, ('xh', 'xl'), [(1, 0), (2, 3), (0, 2), (3, 1)])  5.48 us
    pallas_call x1, Pallas kernels, first_product(): pl.pallas_call(first_kernel, out_shape=(block, block), in_specs=[HB, VM,...  4.38 us
  transfers between devices with their start and end apart: 29, of which 10 were waited for; matrix products, arithmetic and copies ran while one was open for 0% of the time, Pallas kernels for 6%

profile of v12, /device:TPU:1, one launch (start us, length us, event | category | flops | bytes accessed | tf_op | source)
XLA Modules:
  0.0 171.7 jit_solution(9791142610561821874)
XLA Ops:
  7.2 0.0 all-gather.6.cloned.1.call-start
  7.2 1.7 shard_map.59
  8.9 0.0 all-gather.6.cloned.1.call-update
  8.9 5.5 %collective-permute-start.8 = (f32[384,128]{1,0:T(8,128)}, f32[384,128]{1,0:T(8,128)S(1)}, u32[]{:S(2)}, u32[]{:S(2)}) collective-permute-start(f32[384,128]{1,0:T(8,128)} %shard_map.59), channel_id=1, source_target_pairs={{24,0},{384,408},{0,384},{408,24},{25,1},{385,409},{1,385},{409,25... | collective-permute-start | bytes 589832 | tf_op jit(solution)/shard_map/ppermute | solution.py:286
  14.4 1.6 collective-permute-start
  16.0 1.3 collective-permute-done.8.refs_8_
  17.3 6.1 %collective-permute-start.10 = (f32[384,128]{1,0:T(8,128)S(1)}, f32[384,128]{1,0:T(8,128)S(1)}, u32[]{:S(2)}, u32[]{:S(2)}) collective-permute-start(f32[384,128]{1,0:T(8,128)S(1)} %collective-permute-done.8.refs_8_), channel_id=1, source_target_pairs={{0,336},{48,0},{96,48},{144,96},{192,144},{240,192},{288,240},{336... | collective-permute-start | bytes 589832 | tf_op jit(solution)/shard_map/ppermute | solution.py:252
  23.4 0.0 collective-permute-done.refs_0_
  23.4 1.9 %collective-permute-start.1 = (f32[384,128]{1,0:T(8,128)S(1)}, f32[384,128]{1,0:T(8,128)S(1)}, u32[]{:S(2)}, u32[]{:S(2)}) collective-permute-start(f32[384,128]{1,0:T(8,128)S(1)} %collective-permute-done.refs_0_), channel_id=1, source_target_pairs={{0,48},{48,96},{96,144},{144,192},{192,240},{240,288},{288,336},{3... | collective-permute-start | bytes 589832 | tf_op jit(solution)/shard_map/ppermute | solution.py:252
  25.3 1.9 %collective-permute-start.9 = (f32[384,128]{1,0:T(8,128)S(1)}, f32[384,128]{1,0:T(8,128)S(1)}, u32[]{:S(2)}, u32[]{:S(2)}) collective-permute-start(f32[384,128]{1,0:T(8,128)S(1)} %collective-permute-done.8.refs_8_), channel_id=1, source_target_pairs={{0,48},{48,96},{96,144},{144,192},{192,240},{240,288},{288,336},{3... | collective-permute-start | bytes 589832 | tf_op jit(solution)/shard_map/ppermute | solution.py:252
  27.3 4.6 %collective-permute-start.2 = (f32[384,128]{1,0:T(8,128)S(1)}, f32[384,128]{1,0:T(8,128)S(1)}, u32[]{:S(2)}, u32[]{:S(2)}) collective-permute-start(f32[384,128]{1,0:T(8,128)S(1)} %collective-permute-done.refs_0_), channel_id=1, source_target_pairs={{0,336},{48,0},{96,48},{144,96},{192,144},{240,192},{288,240},{336... | collective-permute-start | bytes 589832 | tf_op jit(solution)/shard_map/ppermute | solution.py:252
  31.8 0.0 collective-permute-done.10.refs_10_
  31.8 3.4 %collective-permute-start.12 = (f32[384,128]{1,0:T(8,128)S(1)}, f32[384,128]{1,0:T(8,128)S(1)}, u32[]{:S(2)}, u32[]{:S(2)}) collective-permute-start(f32[384,128]{1,0:T(8,128)S(1)} %collective-permute-done.10.refs_10_), channel_id=1, source_target_pairs={{0,336},{48,0},{96,48},{144,96},{192,144},{240,192},{288,240},{336... | collective-permute-start | bytes 589832 | tf_op jit(solution)/shard_map/ppermute | solution.py:252
  35.2 0.0 collective-permute-done.1.refs_1_
  35.2 1.9 %collective-permute-start.3 = (f32[384,128]{1,0:T(8,128)S(1)}, f32[384,128]{1,0:T(8,128)S(1)}, u32[]{:S(2)}, u32[]{:S(2)}) collective-permute-start(f32[384,128]{1,0:T(8,128)S(1)} %collective-permute-done.1.refs_1_), channel_id=1, source_target_pairs={{0,48},{48,96},{96,144},{144,192},{192,240},{240,288},{288,336},{3... | collective-permute-start | bytes 589832 | tf_op jit(solution)/shard_map/ppermute | solution.py:252
  37.2 1.9 %collective-permute-start.11 = (f32[384,128]{1,0:T(8,128)S(1)}, f32[384,128]{1,0:T(8,128)S(1)}, u32[]{:S(2)}, u32[]{:S(2)}) collective-permute-start(f32[384,128]{1,0:T(8,128)S(1)} %collective-permute-done.9.refs_9_), channel_id=1, source_target_pairs={{0,48},{48,96},{96,144},{144,192},{192,240},{240,288},{288,336},{3... | collective-permute-start | bytes 589832 | tf_op jit(solution)/shard_map/ppermute | solution.py:252
  39.1 4.6 %collective-permute-start.4 = (f32[384,128]{1,0:T(8,128)S(1)}, f32[384,128]{1,0:T(8,128)S(1)}, u32[]{:S(2)}, u32[]{:S(2)}) collective-permute-start(f32[384,128]{1,0:T(8,128)S(1)} %collective-permute-done.2.refs_2_), channel_id=1, source_target_pairs={{0,336},{48,0},{96,48},{144,96},{192,144},{240,192},{288,240},{336... | collective-permute-start | bytes 589832 | tf_op jit(solution)/shard_map/ppermute | solution.py:252
  43.7 3.4 %collective-permute-start.14 = (f32[384,128]{1,0:T(8,128)S(1)}, f32[384,128]{1,0:T(8,128)S(1)}, u32[]{:S(2)}, u32[]{:S(2)}) collective-permute-start(f32[384,128]{1,0:T(8,128)S(1)} %collective-permute-done.12.refs_12_), channel_id=1, source_target_pairs={{0,336},{48,0},{96,48},{144,96},{192,144},{240,192},{288,240},{336... | collective-permute-start | bytes 589832 | tf_op jit(solution)/shard_map/ppermute | solution.py:252
  47.1 1.9 %collective-permute-start.5 = (f32[384,128]{1,0:T(8,128)S(1)}, f32[384,128]{1,0:T(8,128)S(1)}, u32[]{:S(2)}, u32[]{:S(2)}) collective-permute-start(f32[384,128]{1,0:T(8,128)S(1)} %collective-permute-done.3.refs_3_), channel_id=1, source_target_pairs={{0,48},{48,96},{96,144},{144,192},{192,240},{240,288},{288,336},{3... | collective-permute-start | bytes 589832 | tf_op jit(solution)/shard_map/ppermute | solution.py:252
  49.0 0.0 collective-permute-done.11.refs_11_
  49.0 1.9 %collective-permute-start.13 = (f32[384,128]{1,0:T(8,128)S(1)}, f32[384,128]{1,0:T(8,128)S(1)}, u32[]{:S(2)}, u32[]{:S(2)}) collective-permute-start(f32[384,128]{1,0:T(8,128)S(1)} %collective-permute-done.11.refs_11_), channel_id=1, source_target_pairs={{0,48},{48,96},{96,144},{144,192},{192,240},{240,288},{288,336},{3... | collective-permute-start | bytes 589832 | tf_op jit(solution)/shard_map/ppermute | solution.py:252
  51.0 4.6 %collective-permute-start.6 = (f32[384,128]{1,0:T(8,128)S(1)}, f32[384,128]{1,0:T(8,128)S(1)}, u32[]{:S(2)}, u32[]{:S(2)}) collective-permute-start(f32[384,128]{1,0:T(8,128)S(1)} %collective-permute-done.4.refs_4_), channel_id=1, source_target_pairs={{0,336},{48,0},{96,48},{144,96},{192,144},{240,192},{288,240},{336... | collective-permute-start | bytes 589832 | tf_op jit(solution)/shard_map/ppermute | solution.py:252
  55.5 0.0 collective-permute-done.14.refs_14_
  55.5 3.4 %collective-permute-start.15 = (f32[384,128]{1,0:T(8,128)S(1)}, f32[384,128]{1,0:T(8,128)S(1)}, u32[]{:S(2)}, u32[]{:S(2)}) collective-permute-start(f32[384,128]{1,0:T(8,128)S(1)} %collective-permute-done.14.refs_14_), channel_id=1, source_target_pairs={{0,336},{48,0},{96,48},{144,96},{192,144},{240,192},{288,240},{336... | collective-permute-start | bytes 589832 | tf_op jit(solution)/shard_map/ppermute | solution.py:252
  58.9 1.9 %collective-permute-start.7 = (f32[384,128]{1,0:T(8,128)S(1)}, f32[384,128]{1,0:T(8,128)S(1)}, u32[]{:S(2)}, u32[]{:S(2)}) collective-permute-start(f32[384,128]{1,0:T(8,128)S(1)} %collective-permute-done.5.refs_5_), channel_id=1, source_target_pairs={{0,48},{48,96},{96,144},{144,192},{192,240},{240,288},{288,336},{3... | collective-permute-start | bytes 589832 | tf_op jit(solution)/shard_map/ppermute | solution.py:252
  60.9 0.0 collective-permute-done.6.refs_6_
  60.9 1.6 collective-permute-done.15.refs_15_
  62.5 6.1 %collective-permute-done.7.refs_7_ = f32[384,128]{1,0:T(8,128)S(1)} collective-permute-done((f32[384,128]{1,0:T(8,128)S(1)}, f32[384,128]{1,0:T(8,128)S(1)}, u32[]{:S(2)}, u32[]{:S(2)}) %collective-permute-start.7) | collective-permute-done | bytes 196640 | tf_op jit(solution)/shard_map/ppermute | solution.py:252
  68.6 1.8 %shard_map.60 = (bf16[24,128,256]{2,1,0:T(8,128)(2,1)S(1)}, bf16[24,128,256]{2,1,0:T(8,128)(2,1)S(1)}, f32[12,128,256]{2,1,0:T(8,128)}) custom-call(f32[384,128]{1,0:T(8,128)S(1)} %collective-permute-done.refs_0_, f32[384,128]{1,0:T(8,128)S(1)} %collective-permute-done.1.refs_1_, f32[384,128]{1,0:T(8,128)S(1)} %collective-permute-done.2.refs_2_, ...), custom_call_target="tpu_custom_call" | custom-call | tf_op jit(solution)/shard_map/pallas_call | solution.py:93
  70.4 10.1 %collective-permute-start.16 = (f32[12,128,256]{2,1,0:T(8,128)}, f32[12,128,256]{2,1,0:T(8,128)}, u32[]{:S(2)}, u32[]{:S(2)}) collective-permute-start(f32[12,128,256]{2,1,0:T(8,128)} %get-tuple-element.20), channel_id=1, source_target_pairs={{0,1},{1,0},{2,3},{3,2},{4,5},{5,4},{6,7},{7,6},{8,9},{9,8},{10,11... | collective-permute-start | bytes 4718600 | tf_op jit(solution)/shard_map/ppermute | solution.py:252
  80.5 3.3 %all-gather.6.cloned.1.call-done = f32[9216,128]{1,0:T(8,128)} async-done(((f32[384,128]{1,0:T(8,128)}), f32[9216,128]{1,0:T(8,128)}) %all-gather.6.cloned.1.call-update) | async-done | bytes 4718608 | tf_op jit(solution)/shard_map/all_gather | solution.py:283
  83.8 4.4 %shard_map.61 = (f32[384,128]{1,0:T(8,128)S(1)}, f32[384,128]{1,0:T(8,128)S(1)}) custom-call(f32[24,384,128]{2,1,0:T(8,128)} %bitcast.11, bf16[24,128,256]{2,1,0:T(8,128)(2,1)S(1)} %get-tuple-element.16.hi, bf16[24,128,256]{2,1,0:T(8,128)(2,1)S(1)} %get-tuple-element.17.lo), custom_call_target="tpu_custom_call" | custom-call | flops 1811939328 | tf_op jit(solution)/shard_map/pallas_call | solution.py:147
  88.2 0.0 collective-permute-done.16.took
  88.2 7.3 %all-gather.1 = f32[768,128]{1,0:T(8,128)S(1)} all-gather(f32[384,128]{1,0:T(8,128)S(1)} %get-tuple-element.25), channel_id=3, replica_groups=mesh['xh'=2,'y'=8,'xl'=2,'z'=12,'c'=2] {'xl'}, dimensions={0}, use_global_device_ids=true | all-gather | bytes 589824 | tf_op jit(solution)/shard_map/all_gather | solution.py:238
  95.6 0.6 shard_map.63.refs_0_
  96.2 1.9 %collective-permute-start.17 = (f32[384,128]{1,0:T(8,128)S(1)}, f32[384,128]{1,0:T(8,128)S(1)}, u32[]{:S(2)}, u32[]{:S(2)}) collective-permute-start(f32[384,128]{1,0:T(8,128)S(1)} %shard_map.63.refs_0_), channel_id=1, source_target_pairs={{0,2},{2,4},{4,6},{6,8},{8,10},{10,12},{12,14},{14,16},{16,18},{18... | collective-permute-start | bytes 589832 | tf_op jit(solution)/shard_map/ppermute | solution.py:252
  98.1 7.8 %collective-permute-start.23 = (f32[384,128]{1,0:T(8,128)S(1)}, f32[384,128]{1,0:T(8,128)S(1)}, u32[]{:S(2)}, u32[]{:S(2)}) collective-permute-start(f32[384,128]{1,0:T(8,128)S(1)} %shard_map.63.refs_0_), channel_id=1, source_target_pairs={{0,22},{2,0},{4,2},{6,4},{8,6},{10,8},{12,10},{14,12},{16,14},{18,... | collective-permute-start | bytes 589832 | tf_op jit(solution)/shard_map/ppermute | solution.py:252
  105.9 2.8 %collective-permute-done.17.refs_1_ = f32[384,128]{1,0:T(8,128)S(1)} collective-permute-done((f32[384,128]{1,0:T(8,128)S(1)}, f32[384,128]{1,0:T(8,128)S(1)}, u32[]{:S(2)}, u32[]{:S(2)}) %collective-permute-start.17) | collective-permute-done | bytes 196640 | tf_op jit(solution)/shard_map/ppermute | solution.py:252
  108.7 1.9 %collective-permute-start.18 = (f32[384,128]{1,0:T(8,128)S(1)}, f32[384,128]{1,0:T(8,128)S(1)}, u32[]{:S(2)}, u32[]{:S(2)}) collective-permute-start(f32[384,128]{1,0:T(8,128)S(1)} %collective-permute-done.17.refs_1_), channel_id=1, source_target_pairs={{0,2},{2,4},{4,6},{6,8},{8,10},{10,12},{12,14},{14,16},{16,18},{18... | collective-permute-start | bytes 589832 | tf_op jit(solution)/shard_map/ppermute | solution.py:252
  110.6 4.6 %collective-permute-start.24 = (f32[384,128]{1,0:T(8,128)S(1)}, f32[384,128]{1,0:T(8,128)S(1)}, u32[]{:S(2)}, u32[]{:S(2)}) collective-permute-start(f32[384,128]{1,0:T(8,128)S(1)} %collective-permute-done.23.refs_2_), channel_id=1, source_target_pairs={{0,22},{2,0},{4,2},{6,4},{8,6},{10,8},{12,10},{14,12},{16,14},{18,... | collective-permute-start | bytes 589832 | tf_op jit(solution)/shard_map/ppermute | solution.py:252
  115.2 1.8 %collective-permute-done.18.refs_3_ = f32[384,128]{1,0:T(8,128)S(1)} collective-permute-done((f32[384,128]{1,0:T(8,128)S(1)}, f32[384,128]{1,0:T(8,128)S(1)}, u32[]{:S(2)}, u32[]{:S(2)}) %collective-permute-start.18) | collective-permute-done | bytes 196640 | tf_op jit(solution)/shard_map/ppermute | solution.py:252
  117.1 1.9 %collective-permute-start.19 = (f32[384,128]{1,0:T(8,128)S(1)}, f32[384,128]{1,0:T(8,128)S(1)}, u32[]{:S(2)}, u32[]{:S(2)}) collective-permute-start(f32[384,128]{1,0:T(8,128)S(1)} %collective-permute-done.18.refs_3_), channel_id=1, source_target_pairs={{0,2},{2,4},{4,6},{6,8},{8,10},{10,12},{12,14},{14,16},{16,18},{18... | collective-permute-start | bytes 589832 | tf_op jit(solution)/shard_map/ppermute | solution.py:252
  119.0 0.0 collective-permute-done.24.refs_0_
  119.0 4.6 %collective-permute-start.25 = (f32[384,128]{1,0:T(8,128)S(1)}, f32[384,128]{1,0:T(8,128)S(1)}, u32[]{:S(2)}, u32[]{:S(2)}) collective-permute-start(f32[384,128]{1,0:T(8,128)S(1)} %collective-permute-done.24.refs_0_), channel_id=1, source_target_pairs={{0,22},{2,0},{4,2},{6,4},{8,6},{10,8},{12,10},{14,12},{16,14},{18,... | collective-permute-start | bytes 589832 | tf_op jit(solution)/shard_map/ppermute | solution.py:252
  123.6 1.1 collective-permute-done.19.refs_1_
  124.7 1.9 %collective-permute-start.20 = (f32[384,128]{1,0:T(8,128)S(1)}, f32[384,128]{1,0:T(8,128)S(1)}, u32[]{:S(2)}, u32[]{:S(2)}) collective-permute-start(f32[384,128]{1,0:T(8,128)S(1)} %collective-permute-done.19.refs_1_), channel_id=1, source_target_pairs={{0,2},{2,4},{4,6},{6,8},{8,10},{10,12},{12,14},{14,16},{16,18},{18... | collective-permute-start | bytes 589832 | tf_op jit(solution)/shard_map/ppermute | solution.py:252
  126.6 0.0 collective-permute-done.25.refs_2_
  126.6 4.6 %collective-permute-start.26 = (f32[384,128]{1,0:T(8,128)S(1)}, f32[384,128]{1,0:T(8,128)S(1)}, u32[]{:S(2)}, u32[]{:S(2)}) collective-permute-start(f32[384,128]{1,0:T(8,128)S(1)} %collective-permute-done.25.refs_2_), channel_id=1, source_target_pairs={{0,22},{2,0},{4,2},{6,4},{8,6},{10,8},{12,10},{14,12},{16,14},{18,... | collective-permute-start | bytes 589832 | tf_op jit(solution)/shard_map/ppermute | solution.py:252
  131.2 1.1 collective-permute-done.20.refs_3_
  132.3 1.9 %collective-permute-start.21 = (f32[384,128]{1,0:T(8,128)S(1)}, f32[384,128]{1,0:T(8,128)S(1)}, u32[]{:S(2)}, u32[]{:S(2)}) collective-permute-start(f32[384,128]{1,0:T(8,128)S(1)} %collective-permute-done.20.refs_3_), channel_id=1, source_target_pairs={{0,2},{2,4},{4,6},{6,8},{8,10},{10,12},{12,14},{14,16},{16,18},{18... | collective-permute-start | bytes 589832 | tf_op jit(solution)/shard_map/ppermute | solution.py:252
  134.2 4.6 %collective-permute-start.27 = (f32[384,128]{1,0:T(8,128)S(1)}, f32[384,128]{1,0:T(8,128)S(1)}, u32[]{:S(2)}, u32[]{:S(2)}) collective-permute-start(f32[384,128]{1,0:T(8,128)S(1)} %collective-permute-done.26.refs_0_), channel_id=1, source_target_pairs={{0,22},{2,0},{4,2},{6,4},{8,6},{10,8},{12,10},{14,12},{16,14},{18,... | collective-permute-start | bytes 589832 | tf_op jit(solution)/shard_map/ppermute | solution.py:252
  138.8 1.1 collective-permute-done.21.refs_1_
  139.9 1.9 %collective-permute-start.22 = (f32[384,128]{1,0:T(8,128)S(1)}, f32[384,128]{1,0:T(8,128)S(1)}, u32[]{:S(2)}, u32[]{:S(2)}) collective-permute-start(f32[384,128]{1,0:T(8,128)S(1)} %collective-permute-done.21.refs_1_), channel_id=1, source_target_pairs={{0,2},{2,4},{4,6},{6,8},{8,10},{10,12},{12,14},{14,16},{16,18},{18... | collective-permute-start | bytes 589832 | tf_op jit(solution)/shard_map/ppermute | solution.py:252
  141.8 1.6 shard_map.62
  143.5 0.8 shard_map.64.refs_4_
  144.3 0.8 shard_map.65.refs_3_
  145.1 0.0 collective-permute-done.27.refs_2_
  145.1 0.8 shard_map.66.refs_1_
  145.9 1.6 collective-permute-done.22.refs_0_
  147.5 0.5 shard_map.67
  148.0 8.6 %all-gather.2 = f32[768,256]{1,0:T(8,128)S(1)} all-gather(f32[384,256]{1,0:T(8,128)S(1)} %get-tuple-element.27), channel_id=4, replica_groups=mesh['xh'=2,'y'=8,'xl'=2,'z'=12,'c'=2] {'c'}, dimensions={0}, use_global_device_ids=true | all-gather | bytes 1179648 | tf_op jit(solution)/shard_map/all_gather | solution.py:208
  156.6 0.1 shard_map.68
  156.7 6.8 %all-gather.3 = f32[768,128]{1,0:T(8,128)S(1)} all-gather(f32[384,128]{1,0:T(8,128)S(1)} %get-tuple-element.29), channel_id=5, replica_groups=mesh['xh'=2,'y'=8,'xl'=2,'z'=12,'c'=2] {'xl'}, dimensions={0}, use_global_device_ids=true | all-gather | bytes 589824 | tf_op jit(solution)/shard_map/all_gather | solution.py:238
  163.5 1.3 shard_map.69
  (11 shorter events, 0.0 us)
Async XLA Ops:
  7.2 76.7 %all-gather.6.cloned.1.call-start = ((), (), s32[]{:S(2)}) async-start(), calls=%async_computation | async-start | bytes 4915200 | tf_op jit(solution)/shard_map/all_gather | solution.py:283
  8.9 8.4 %collective-permute-start.8 = (f32[384,128]{1,0:T(8,128)}, f32[384,128]{1,0:T(8,128)S(1)}, u32[]{:S(2)}, u32[]{:S(2)}) collective-permute-start(f32[384,128]{1,0:T(8,128)} %shard_map.59), channel_id=1, source_target_pairs={{24,0},{384,408},{0,384},{408,24},{25,1},{385,409},{1,385},{409,25... | collective-permute-start | bytes 589832 | tf_op jit(solution)/shard_map/ppermute | solution.py:286
  14.4 9.0 %collective-permute-start = (f32[384,128]{1,0:T(8,128)}, f32[384,128]{1,0:T(8,128)S(1)}, u32[]{:S(2)}, u32[]{:S(2)}) collective-permute-start(f32[384,128]{1,0:T(8,128)} %shard_map.59), channel_id=1, source_target_pairs={{0,0},{24,384},{384,24},{408,408},{1,1},{25,385},{385,25},{409,409... | collective-permute-start | bytes 589832 | tf_op jit(solution)/shard_map/ppermute | solution.py:285
  17.3 14.5 %collective-permute-start.10 = (f32[384,128]{1,0:T(8,128)S(1)}, f32[384,128]{1,0:T(8,128)S(1)}, u32[]{:S(2)}, u32[]{:S(2)}) collective-permute-start(f32[384,128]{1,0:T(8,128)S(1)} %collective-permute-done.8.refs_8_), channel_id=1, source_target_pairs={{0,336},{48,0},{96,48},{144,96},{192,144},{240,192},{288,240},{336... | collective-permute-start | bytes 589832 | tf_op jit(solution)/shard_map/ppermute | solution.py:252
  23.4 11.8 %collective-permute-start.1 = (f32[384,128]{1,0:T(8,128)S(1)}, f32[384,128]{1,0:T(8,128)S(1)}, u32[]{:S(2)}, u32[]{:S(2)}) collective-permute-start(f32[384,128]{1,0:T(8,128)S(1)} %collective-permute-done.refs_0_), channel_id=1, source_target_pairs={{0,48},{48,96},{96,144},{144,192},{192,240},{240,288},{288,336},{3... | collective-permute-start | bytes 589832 | tf_op jit(solution)/shard_map/ppermute | solution.py:252
  25.3 11.8 %collective-permute-start.9 = (f32[384,128]{1,0:T(8,128)S(1)}, f32[384,128]{1,0:T(8,128)S(1)}, u32[]{:S(2)}, u32[]{:S(2)}) collective-permute-start(f32[384,128]{1,0:T(8,128)S(1)} %collective-permute-done.8.refs_8_), channel_id=1, source_target_pairs={{0,48},{48,96},{96,144},{144,192},{192,240},{240,288},{288,336},{3... | collective-permute-start | bytes 589832 | tf_op jit(solution)/shard_map/ppermute | solution.py:252
  27.3 11.8 %collective-permute-start.2 = (f32[384,128]{1,0:T(8,128)S(1)}, f32[384,128]{1,0:T(8,128)S(1)}, u32[]{:S(2)}, u32[]{:S(2)}) collective-permute-start(f32[384,128]{1,0:T(8,128)S(1)} %collective-permute-done.refs_0_), channel_id=1, source_target_pairs={{0,336},{48,0},{96,48},{144,96},{192,144},{240,192},{288,240},{336... | collective-permute-start | bytes 589832 | tf_op jit(solution)/shard_map/ppermute | solution.py:252
  31.8 11.8 %collective-permute-start.12 = (f32[384,128]{1,0:T(8,128)S(1)}, f32[384,128]{1,0:T(8,128)S(1)}, u32[]{:S(2)}, u32[]{:S(2)}) collective-permute-start(f32[384,128]{1,0:T(8,128)S(1)} %collective-permute-done.10.refs_10_), channel_id=1, source_target_pairs={{0,336},{48,0},{96,48},{144,96},{192,144},{240,192},{288,240},{336... | collective-permute-start | bytes 589832 | tf_op jit(solution)/shard_map/ppermute | solution.py:252
  35.2 11.8 %collective-permute-start.3 = (f32[384,128]{1,0:T(8,128)S(1)}, f32[384,128]{1,0:T(8,128)S(1)}, u32[]{:S(2)}, u32[]{:S(2)}) collective-permute-start(f32[384,128]{1,0:T(8,128)S(1)} %collective-permute-done.1.refs_1_), channel_id=1, source_target_pairs={{0,48},{48,96},{96,144},{144,192},{192,240},{240,288},{288,336},{3... | collective-permute-start | bytes 589832 | tf_op jit(solution)/shard_map/ppermute | solution.py:252
  37.2 11.8 %collective-permute-start.11 = (f32[384,128]{1,0:T(8,128)S(1)}, f32[384,128]{1,0:T(8,128)S(1)}, u32[]{:S(2)}, u32[]{:S(2)}) collective-permute-start(f32[384,128]{1,0:T(8,128)S(1)} %collective-permute-done.9.refs_9_), channel_id=1, source_target_pairs={{0,48},{48,96},{96,144},{144,192},{192,240},{240,288},{288,336},{3... | collective-permute-start | bytes 589832 | tf_op jit(solution)/shard_map/ppermute | solution.py:252
  39.1 11.8 %collective-permute-start.4 = (f32[384,128]{1,0:T(8,128)S(1)}, f32[384,128]{1,0:T(8,128)S(1)}, u32[]{:S(2)}, u32[]{:S(2)}) collective-permute-start(f32[384,128]{1,0:T(8,128)S(1)} %collective-permute-done.2.refs_2_), channel_id=1, source_target_pairs={{0,336},{48,0},{96,48},{144,96},{192,144},{240,192},{288,240},{336... | collective-permute-start | bytes 589832 | tf_op jit(solution)/shard_map/ppermute | solution.py:252
  43.7 11.8 %collective-permute-start.14 = (f32[384,128]{1,0:T(8,128)S(1)}, f32[384,128]{1,0:T(8,128)S(1)}, u32[]{:S(2)}, u32[]{:S(2)}) collective-permute-start(f32[384,128]{1,0:T(8,128)S(1)} %collective-permute-done.12.refs_12_), channel_id=1, source_target_pairs={{0,336},{48,0},{96,48},{144,96},{192,144},{240,192},{288,240},{336... | collective-permute-start | bytes 589832 | tf_op jit(solution)/shard_map/ppermute | solution.py:252
  47.1 11.8 %collective-permute-start.5 = (f32[384,128]{1,0:T(8,128)S(1)}, f32[384,128]{1,0:T(8,128)S(1)}, u32[]{:S(2)}, u32[]{:S(2)}) collective-permute-start(f32[384,128]{1,0:T(8,128)S(1)} %collective-permute-done.3.refs_3_), channel_id=1, source_target_pairs={{0,48},{48,96},{96,144},{144,192},{192,240},{240,288},{288,336},{3... | collective-permute-start | bytes 589832 | tf_op jit(solution)/shard_map/ppermute | solution.py:252
  49.0 11.8 %collective-permute-start.13 = (f32[384,128]{1,0:T(8,128)S(1)}, f32[384,128]{1,0:T(8,128)S(1)}, u32[]{:S(2)}, u32[]{:S(2)}) collective-permute-start(f32[384,128]{1,0:T(8,128)S(1)} %collective-permute-done.11.refs_11_), channel_id=1, source_target_pairs={{0,48},{48,96},{96,144},{144,192},{192,240},{240,288},{288,336},{3... | collective-permute-start | bytes 589832 | tf_op jit(solution)/shard_map/ppermute | solution.py:252
  51.0 9.9 %collective-permute-start.6 = (f32[384,128]{1,0:T(8,128)S(1)}, f32[384,128]{1,0:T(8,128)S(1)}, u32[]{:S(2)}, u32[]{:S(2)}) collective-permute-start(f32[384,128]{1,0:T(8,128)S(1)} %collective-permute-done.4.refs_4_), channel_id=1, source_target_pairs={{0,336},{48,0},{96,48},{144,96},{192,144},{240,192},{288,240},{336... | collective-permute-start | bytes 589832 | tf_op jit(solution)/shard_map/ppermute | solution.py:252
  55.5 6.9 %collective-permute-start.15 = (f32[384,128]{1,0:T(8,128)S(1)}, f32[384,128]{1,0:T(8,128)S(1)}, u32[]{:S(2)}, u32[]{:S(2)}) collective-permute-start(f32[384,128]{1,0:T(8,128)S(1)} %collective-permute-done.14.refs_14_), channel_id=1, source_target_pairs={{0,336},{48,0},{96,48},{144,96},{192,144},{240,192},{288,240},{336... | collective-permute-start | bytes 589832 | tf_op jit(solution)/shard_map/ppermute | solution.py:252
  58.9 9.7 %collective-permute-start.7 = (f32[384,128]{1,0:T(8,128)S(1)}, f32[384,128]{1,0:T(8,128)S(1)}, u32[]{:S(2)}, u32[]{:S(2)}) collective-permute-start(f32[384,128]{1,0:T(8,128)S(1)} %collective-permute-done.5.refs_5_), channel_id=1, source_target_pairs={{0,48},{48,96},{96,144},{144,192},{192,240},{240,288},{288,336},{3... | collective-permute-start | bytes 589832 | tf_op jit(solution)/shard_map/ppermute | solution.py:252
  70.4 17.8 %collective-permute-start.16 = (f32[12,128,256]{2,1,0:T(8,128)}, f32[12,128,256]{2,1,0:T(8,128)}, u32[]{:S(2)}, u32[]{:S(2)}) collective-permute-start(f32[12,128,256]{2,1,0:T(8,128)} %get-tuple-element.20), channel_id=1, source_target_pairs={{0,1},{1,0},{2,3},{3,2},{4,5},{5,4},{6,7},{7,6},{8,9},{9,8},{10,11... | collective-permute-start | bytes 4718600 | tf_op jit(solution)/shard_map/ppermute | solution.py:252
  83.8 11.7 %copy-start = (s32[6,2]{0,1:T(2,128)S(1)}, s32[6,2]{0,1:T(2,128)}, u32[]{:S(2)}) copy-start(s32[6,2]{0,1:T(2,128)} %param.7) | copy-start | bytes 148
  96.2 12.6 %collective-permute-start.17 = (f32[384,128]{1,0:T(8,128)S(1)}, f32[384,128]{1,0:T(8,128)S(1)}, u32[]{:S(2)}, u32[]{:S(2)}) collective-permute-start(f32[384,128]{1,0:T(8,128)S(1)} %shard_map.63.refs_0_), channel_id=1, source_target_pairs={{0,2},{2,4},{4,6},{6,8},{8,10},{10,12},{12,14},{14,16},{16,18},{18... | collective-permute-start | bytes 589832 | tf_op jit(solution)/shard_map/ppermute | solution.py:252
  98.1 12.6 %collective-permute-start.23 = (f32[384,128]{1,0:T(8,128)S(1)}, f32[384,128]{1,0:T(8,128)S(1)}, u32[]{:S(2)}, u32[]{:S(2)}) collective-permute-start(f32[384,128]{1,0:T(8,128)S(1)} %shard_map.63.refs_0_), channel_id=1, source_target_pairs={{0,22},{2,0},{4,2},{6,4},{8,6},{10,8},{12,10},{14,12},{16,14},{18,... | collective-permute-start | bytes 589832 | tf_op jit(solution)/shard_map/ppermute | solution.py:252
  108.7 8.4 %collective-permute-start.18 = (f32[384,128]{1,0:T(8,128)S(1)}, f32[384,128]{1,0:T(8,128)S(1)}, u32[]{:S(2)}, u32[]{:S(2)}) collective-permute-start(f32[384,128]{1,0:T(8,128)S(1)} %collective-permute-done.17.refs_1_), channel_id=1, source_target_pairs={{0,2},{2,4},{4,6},{6,8},{8,10},{10,12},{12,14},{14,16},{16,18},{18... | collective-permute-start | bytes 589832 | tf_op jit(solution)/shard_map/ppermute | solution.py:252
  110.6 8.3 %collective-permute-start.24 = (f32[384,128]{1,0:T(8,128)S(1)}, f32[384,128]{1,0:T(8,128)S(1)}, u32[]{:S(2)}, u32[]{:S(2)}) collective-permute-start(f32[384,128]{1,0:T(8,128)S(1)} %collective-permute-done.23.refs_2_), channel_id=1, source_target_pairs={{0,22},{2,0},{4,2},{6,4},{8,6},{10,8},{12,10},{14,12},{16,14},{18,... | collective-permute-start | bytes 589832 | tf_op jit(solution)/shard_map/ppermute | solution.py:252
  117.1 7.6 %collective-permute-start.19 = (f32[384,128]{1,0:T(8,128)S(1)}, f32[384,128]{1,0:T(8,128)S(1)}, u32[]{:S(2)}, u32[]{:S(2)}) collective-permute-start(f32[384,128]{1,0:T(8,128)S(1)} %collective-permute-done.18.refs_3_), channel_id=1, source_target_pairs={{0,2},{2,4},{4,6},{6,8},{8,10},{10,12},{12,14},{14,16},{16,18},{18... | collective-permute-start | bytes 589832 | tf_op jit(solution)/shard_map/ppermute | solution.py:252
  119.0 7.6 %collective-permute-start.25 = (f32[384,128]{1,0:T(8,128)S(1)}, f32[384,128]{1,0:T(8,128)S(1)}, u32[]{:S(2)}, u32[]{:S(2)}) collective-permute-start(f32[384,128]{1,0:T(8,128)S(1)} %collective-permute-done.24.refs_0_), channel_id=1, source_target_pairs={{0,22},{2,0},{4,2},{6,4},{8,6},{10,8},{12,10},{14,12},{16,14},{18,... | collective-permute-start | bytes 589832 | tf_op jit(solution)/shard_map/ppermute | solution.py:252
  124.7 7.6 %collective-permute-start.20 = (f32[384,128]{1,0:T(8,128)S(1)}, f32[384,128]{1,0:T(8,128)S(1)}, u32[]{:S(2)}, u32[]{:S(2)}) collective-permute-start(f32[384,128]{1,0:T(8,128)S(1)} %collective-permute-done.19.refs_1_), channel_id=1, source_target_pairs={{0,2},{2,4},{4,6},{6,8},{8,10},{10,12},{12,14},{14,16},{16,18},{18... | collective-permute-start | bytes 589832 | tf_op jit(solution)/shard_map/ppermute | solution.py:252
  126.6 7.6 %collective-permute-start.26 = (f32[384,128]{1,0:T(8,128)S(1)}, f32[384,128]{1,0:T(8,128)S(1)}, u32[]{:S(2)}, u32[]{:S(2)}) collective-permute-start(f32[384,128]{1,0:T(8,128)S(1)} %collective-permute-done.25.refs_2_), channel_id=1, source_target_pairs={{0,22},{2,0},{4,2},{6,4},{8,6},{10,8},{12,10},{14,12},{16,14},{18,... | collective-permute-start | bytes 589832 | tf_op jit(solution)/shard_map/ppermute | solution.py:252
  132.3 7.6 %collective-permute-start.21 = (f32[384,128]{1,0:T(8,128)S(1)}, f32[384,128]{1,0:T(8,128)S(1)}, u32[]{:S(2)}, u32[]{:S(2)}) collective-permute-start(f32[384,128]{1,0:T(8,128)S(1)} %collective-permute-done.20.refs_3_), channel_id=1, source_target_pairs={{0,2},{2,4},{4,6},{6,8},{8,10},{10,12},{12,14},{14,16},{16,18},{18... | collective-permute-start | bytes 589832 | tf_op jit(solution)/shard_map/ppermute | solution.py:252
  134.2 10.9 %collective-permute-start.27 = (f32[384,128]{1,0:T(8,128)S(1)}, f32[384,128]{1,0:T(8,128)S(1)}, u32[]{:S(2)}, u32[]{:S(2)}) collective-permute-start(f32[384,128]{1,0:T(8,128)S(1)} %collective-permute-done.26.refs_0_), channel_id=1, source_target_pairs={{0,22},{2,0},{4,2},{6,4},{8,6},{10,8},{12,10},{14,12},{16,14},{18,... | collective-permute-start | bytes 589832 | tf_op jit(solution)/shard_map/ppermute | solution.py:252
  139.9 7.6 %collective-permute-start.22 = (f32[384,128]{1,0:T(8,128)S(1)}, f32[384,128]{1,0:T(8,128)S(1)}, u32[]{:S(2)}, u32[]{:S(2)}) collective-permute-start(f32[384,128]{1,0:T(8,128)S(1)} %collective-permute-done.21.refs_1_), channel_id=1, source_target_pairs={{0,2},{2,4},{4,6},{6,8},{8,10},{10,12},{12,14},{14,16},{16,18},{18... | collective-permute-start | bytes 589832 | tf_op jit(solution)/shard_map/ppermute | solution.py:252
Sparse Core Ops, SparseCore 0:
  11.0 72.7 all-gather.5

commit v13 on v12

--- a/solution.py
+++ b/solution.py
@@ -200,21 +200,26 @@
     )(*args)
 
 
-def join_kernel(own, both, mine, other):
-    put_halves(own[...] + both[1 - lax.axis_index("c")], mine, other)
-
-
-def join(own, give):
+def join_kernel(hi, lo, own, both, last, mine, other):
+    u = 2 * lax.rem(lax.axis_index("z") + NZ // 2, NZ)
+    a = jnp.concatenate([last[0], last[1]], axis=1)
+    bh = jnp.concatenate([hi[u], hi[u + 1]], axis=0)
+    bl = jnp.concatenate([lo[u], lo[u + 1]], axis=0)
+    total = own[...] + both[1 - lax.axis_index("c")] + split_dot(a, bh, bl)
+    put_halves(total, mine, other)
+
+
+def join(hi, lo, own, give, last):
     both = lax.all_gather(give, "c", axis=0)
-    rows, cols = own.shape
-    block = jax.ShapeDtypeStruct((rows, cols // 2), F32)
+    block = jax.ShapeDtypeStruct(last.shape, F32)
+    args = (hi, lo, own, both, lax.all_gather(last, "c", axis=0))
     return pl.pallas_call(
         join_kernel,
         out_shape=(block, block),
-        in_specs=[VM, VM],
+        in_specs=[VM] * len(args),
         out_specs=(VM, VM),
         compiler_params=PARAMS,
-    )(own, both)
+    )(*args)
 
 
 def filter_kernel(final, kept, mine, pair, *refs):
@@ -299,11 +304,9 @@
     blocks = [(0, square)]
     for s in range(5):
         blocks += [(-s - 1, up[s]), (s + 1, down[s])]
-    blocks.append((-6, up[5]))
     acc = second_product(operand, blocks[:4])
     acc = second_product(operand, blocks[4:8], acc)
-    acc = second_product(operand, blocks[8:11], acc)
-    halves = join(*second_product(operand, blocks[11:], acc, last=True))
+    halves = join(hi, lo, *second_product(operand, blocks[8:11], acc, last=True), up[5])
     return filtered(kept.T, halves, square)
 
 

time: 173 us -> 174 us (level)
  blocking collectives: 22.8 us -> 26.8 us
  waiting for transfers between devices: 22 us -> 19.3 us
    all_gather x0 -> x1, blocking collectives: none -> 5.72 us  [join(): args = (hi, lo, own, both, lax.all_gather(last, 'c', axis=0))]
    ppermute x26, waiting for transfers between devices: 17.3 us -> 14.6 us  [shift(): return lax.ppermute(x, axis, [(i, (i + step) % n) for i in range(n)])]
  transfers between devices with their start and end apart: 29 -> 29, of which waited for: 10 -> 8; matrix products, arithmetic and copies ran while one was open for 0% -> 0% of each run, Pallas kernels for 6% -> 6%
where the time goes in v13:
time: 174 us; the launch traced here: 173 us
  starting transfers between devices  98.1 us (56%)
  blocking collectives  26.8 us (15%)
  waiting for transfers between devices  19.3 us (11%)
  between operations  14.5 us (8%)
  Pallas kernels  14.2 us (8%)
    ppermute x26, starting transfers between devices, shift(): return lax.ppermute(x, axis, [(i, (i + step) % n) for i in range(n)])  91 us
    ppermute x26, waiting for transfers between devices, shift(): return lax.ppermute(x, axis, [(i, (i + step) % n) for i in range(n)])  14.6 us
    all_gather x2, blocking collectives, filtered(): pair = lax.all_gather(other, 'xl', axis=0)  14.1 us
    all_gather x1, blocking collectives, join(): both = lax.all_gather(give, 'c', axis=0)  6.92 us
    all_gather x1, blocking collectives, join(): args = (hi, lo, own, both, lax.all_gather(last, 'c', axis=0))  5.72 us
    ppermute x1, starting transfers between devices, body(): far = lax.ppermute(masked, ('xh', 'xl'), [(1, 0), (2, 3), (0, 2), (3, 1)])  5.48 us
    pallas_call x1, Pallas kernels, first_product(): pl.pallas_call(first_kernel, out_shape=(block, block), in_specs=[HB, VM,...  4.38 us
  transfers between devices with their start and end apart: 29, of which 8 were waited for; matrix products, arithmetic and copies ran while one was open for 0% of the time, Pallas kernels for 6%

profile of v13, /device:TPU:1, one launch (start us, length us, event | category | flops | bytes accessed | tf_op | source)
XLA Modules:
  0.0 172.8 jit_solution(11617154147138474741)
XLA Ops:
  7.2 0.0 all-gather.7.cloned.1.call-start
  7.2 1.7 shard_map.59
  8.9 0.0 all-gather.7.cloned.1.call-update
  8.9 5.5 %collective-permute-start.8 = (f32[384,128]{1,0:T(8,128)}, f32[384,128]{1,0:T(8,128)S(1)}, u32[]{:S(2)}, u32[]{:S(2)}) collective-permute-start(f32[384,128]{1,0:T(8,128)} %shard_map.59), channel_id=1, source_target_pairs={{24,0},{384,408},{0,384},{408,24},{25,1},{385,409},{1,385},{409,25... | collective-permute-start | bytes 589832 | tf_op jit(solution)/shard_map/ppermute | solution.py:291
  14.4 1.6 collective-permute-start
  16.0 1.3 collective-permute-done.8.refs_8_
  17.3 6.1 %collective-permute-start.10 = (f32[384,128]{1,0:T(8,128)S(1)}, f32[384,128]{1,0:T(8,128)S(1)}, u32[]{:S(2)}, u32[]{:S(2)}) collective-permute-start(f32[384,128]{1,0:T(8,128)S(1)} %collective-permute-done.8.refs_8_), channel_id=1, source_target_pairs={{0,336},{48,0},{96,48},{144,96},{192,144},{240,192},{288,240},{336... | collective-permute-start | bytes 589832 | tf_op jit(solution)/shard_map/ppermute | solution.py:257
  23.4 0.0 collective-permute-done.refs_0_
  23.4 1.9 %collective-permute-start.1 = (f32[384,128]{1,0:T(8,128)S(1)}, f32[384,128]{1,0:T(8,128)S(1)}, u32[]{:S(2)}, u32[]{:S(2)}) collective-permute-start(f32[384,128]{1,0:T(8,128)S(1)} %collective-permute-done.refs_0_), channel_id=1, source_target_pairs={{0,48},{48,96},{96,144},{144,192},{192,240},{240,288},{288,336},{3... | collective-permute-start | bytes 589832 | tf_op jit(solution)/shard_map/ppermute | solution.py:257
  25.3 1.9 %collective-permute-start.9 = (f32[384,128]{1,0:T(8,128)S(1)}, f32[384,128]{1,0:T(8,128)S(1)}, u32[]{:S(2)}, u32[]{:S(2)}) collective-permute-start(f32[384,128]{1,0:T(8,128)S(1)} %collective-permute-done.8.refs_8_), channel_id=1, source_target_pairs={{0,48},{48,96},{96,144},{144,192},{192,240},{240,288},{288,336},{3... | collective-permute-start | bytes 589832 | tf_op jit(solution)/shard_map/ppermute | solution.py:257
  27.3 4.6 %collective-permute-start.2 = (f32[384,128]{1,0:T(8,128)S(1)}, f32[384,128]{1,0:T(8,128)S(1)}, u32[]{:S(2)}, u32[]{:S(2)}) collective-permute-start(f32[384,128]{1,0:T(8,128)S(1)} %collective-permute-done.refs_0_), channel_id=1, source_target_pairs={{0,336},{48,0},{96,48},{144,96},{192,144},{240,192},{288,240},{336... | collective-permute-start | bytes 589832 | tf_op jit(solution)/shard_map/ppermute | solution.py:257
  31.8 0.0 collective-permute-done.10.refs_10_
  31.8 3.4 %collective-permute-start.12 = (f32[384,128]{1,0:T(8,128)S(1)}, f32[384,128]{1,0:T(8,128)S(1)}, u32[]{:S(2)}, u32[]{:S(2)}) collective-permute-start(f32[384,128]{1,0:T(8,128)S(1)} %collective-permute-done.10.refs_10_), channel_id=1, source_target_pairs={{0,336},{48,0},{96,48},{144,96},{192,144},{240,192},{288,240},{336... | collective-permute-start | bytes 589832 | tf_op jit(solution)/shard_map/ppermute | solution.py:257
  35.2 0.0 collective-permute-done.1.refs_1_
  35.2 1.9 %collective-permute-start.3 = (f32[384,128]{1,0:T(8,128)S(1)}, f32[384,128]{1,0:T(8,128)S(1)}, u32[]{:S(2)}, u32[]{:S(2)}) collective-permute-start(f32[384,128]{1,0:T(8,128)S(1)} %collective-permute-done.1.refs_1_), channel_id=1, source_target_pairs={{0,48},{48,96},{96,144},{144,192},{192,240},{240,288},{288,336},{3... | collective-permute-start | bytes 589832 | tf_op jit(solution)/shard_map/ppermute | solution.py:257
  37.2 0.0 collective-permute-done.9.refs_9_
  37.2 1.9 %collective-permute-start.11 = (f32[384,128]{1,0:T(8,128)S(1)}, f32[384,128]{1,0:T(8,128)S(1)}, u32[]{:S(2)}, u32[]{:S(2)}) collective-permute-start(f32[384,128]{1,0:T(8,128)S(1)} %collective-permute-done.9.refs_9_), channel_id=1, source_target_pairs={{0,48},{48,96},{96,144},{144,192},{192,240},{240,288},{288,336},{3... | collective-permute-start | bytes 589832 | tf_op jit(solution)/shard_map/ppermute | solution.py:257
  39.1 0.0 collective-permute-done.2.refs_2_
  39.1 4.6 %collective-permute-start.4 = (f32[384,128]{1,0:T(8,128)S(1)}, f32[384,128]{1,0:T(8,128)S(1)}, u32[]{:S(2)}, u32[]{:S(2)}) collective-permute-start(f32[384,128]{1,0:T(8,128)S(1)} %collective-permute-done.2.refs_2_), channel_id=1, source_target_pairs={{0,336},{48,0},{96,48},{144,96},{192,144},{240,192},{288,240},{336... | collective-permute-start | bytes 589832 | tf_op jit(solution)/shard_map/ppermute | solution.py:257
  43.7 3.4 %collective-permute-start.14 = (f32[384,128]{1,0:T(8,128)S(1)}, f32[384,128]{1,0:T(8,128)S(1)}, u32[]{:S(2)}, u32[]{:S(2)}) collective-permute-start(f32[384,128]{1,0:T(8,128)S(1)} %collective-permute-done.12.refs_12_), channel_id=1, source_target_pairs={{0,336},{48,0},{96,48},{144,96},{192,144},{240,192},{288,240},{336... | collective-permute-start | bytes 589832 | tf_op jit(solution)/shard_map/ppermute | solution.py:257
  47.1 1.9 %collective-permute-start.5 = (f32[384,128]{1,0:T(8,128)S(1)}, f32[384,128]{1,0:T(8,128)S(1)}, u32[]{:S(2)}, u32[]{:S(2)}) collective-permute-start(f32[384,128]{1,0:T(8,128)S(1)} %collective-permute-done.3.refs_3_), channel_id=1, source_target_pairs={{0,48},{48,96},{96,144},{144,192},{192,240},{240,288},{288,336},{3... | collective-permute-start | bytes 589832 | tf_op jit(solution)/shard_map/ppermute | solution.py:257
  49.0 0.0 collective-permute-done.11.refs_11_
  49.0 1.9 %collective-permute-start.13 = (f32[384,128]{1,0:T(8,128)S(1)}, f32[384,128]{1,0:T(8,128)S(1)}, u32[]{:S(2)}, u32[]{:S(2)}) collective-permute-start(f32[384,128]{1,0:T(8,128)S(1)} %collective-permute-done.11.refs_11_), channel_id=1, source_target_pairs={{0,48},{48,96},{96,144},{144,192},{192,240},{240,288},{288,336},{3... | collective-permute-start | bytes 589832 | tf_op jit(solution)/shard_map/ppermute | solution.py:257
  51.0 4.6 %collective-permute-start.6 = (f32[384,128]{1,0:T(8,128)S(1)}, f32[384,128]{1,0:T(8,128)S(1)}, u32[]{:S(2)}, u32[]{:S(2)}) collective-permute-start(f32[384,128]{1,0:T(8,128)S(1)} %collective-permute-done.4.refs_4_), channel_id=1, source_target_pairs={{0,336},{48,0},{96,48},{144,96},{192,144},{240,192},{288,240},{336... | collective-permute-start | bytes 589832 | tf_op jit(solution)/shard_map/ppermute | solution.py:257
  55.5 0.0 collective-permute-done.14.refs_14_
  55.5 3.4 %collective-permute-start.15 = (f32[384,128]{1,0:T(8,128)S(1)}, f32[384,128]{1,0:T(8,128)S(1)}, u32[]{:S(2)}, u32[]{:S(2)}) collective-permute-start(f32[384,128]{1,0:T(8,128)S(1)} %collective-permute-done.14.refs_14_), channel_id=1, source_target_pairs={{0,336},{48,0},{96,48},{144,96},{192,144},{240,192},{288,240},{336... | collective-permute-start | bytes 589832 | tf_op jit(solution)/shard_map/ppermute | solution.py:257
  58.9 1.9 %collective-permute-start.7 = (f32[384,128]{1,0:T(8,128)S(1)}, f32[384,128]{1,0:T(8,128)S(1)}, u32[]{:S(2)}, u32[]{:S(2)}) collective-permute-start(f32[384,128]{1,0:T(8,128)S(1)} %collective-permute-done.5.refs_5_), channel_id=1, source_target_pairs={{0,48},{48,96},{96,144},{144,192},{192,240},{240,288},{288,336},{3... | collective-permute-start | bytes 589832 | tf_op jit(solution)/shard_map/ppermute | solution.py:257
  60.9 0.0 collective-permute-done.13.refs_13_
  60.9 0.0 collective-permute-done.6.refs_6_
  60.9 1.6 collective-permute-done.15.refs_15_
  62.5 6.1 %collective-permute-done.7.refs_7_ = f32[384,128]{1,0:T(8,128)S(1)} collective-permute-done((f32[384,128]{1,0:T(8,128)S(1)}, f32[384,128]{1,0:T(8,128)S(1)}, u32[]{:S(2)}, u32[]{:S(2)}) %collective-permute-start.7) | collective-permute-done | bytes 196640 | tf_op jit(solution)/shard_map/ppermute | solution.py:257
  68.6 1.8 %shard_map.60 = (bf16[24,128,256]{2,1,0:T(8,128)(2,1)S(1)}, bf16[24,128,256]{2,1,0:T(8,128)(2,1)S(1)}, f32[12,128,256]{2,1,0:T(8,128)}) custom-call(f32[384,128]{1,0:T(8,128)S(1)} %collective-permute-done.refs_0_, f32[384,128]{1,0:T(8,128)S(1)} %collective-permute-done.1.refs_1_, f32[384,128]{1,0:T(8,128)S(1)} %collective-permute-done.2.refs_2_, ...), custom_call_target="tpu_custom_call" | custom-call | tf_op jit(solution)/shard_map/pallas_call | solution.py:93
  70.4 10.1 %collective-permute-start.16 = (f32[12,128,256]{2,1,0:T(8,128)}, f32[12,128,256]{2,1,0:T(8,128)}, u32[]{:S(2)}, u32[]{:S(2)}) collective-permute-start(f32[12,128,256]{2,1,0:T(8,128)} %get-tuple-element.20), channel_id=1, source_target_pairs={{0,1},{1,0},{2,3},{3,2},{4,5},{5,4},{6,7},{7,6},{8,9},{9,8},{10,11... | collective-permute-start | bytes 4718600 | tf_op jit(solution)/shard_map/ppermute | solution.py:257
  80.5 3.3 %all-gather.7.cloned.1.call-done = f32[9216,128]{1,0:T(8,128)} async-done(((f32[384,128]{1,0:T(8,128)}), f32[9216,128]{1,0:T(8,128)}) %all-gather.7.cloned.1.call-update) | async-done | bytes 4718608 | tf_op jit(solution)/shard_map/all_gather | solution.py:288
  83.8 4.4 %shard_map.61 = (f32[384,128]{1,0:T(8,128)S(1)}, f32[384,128]{1,0:T(8,128)S(1)}) custom-call(f32[24,384,128]{2,1,0:T(8,128)} %bitcast.13, bf16[24,128,256]{2,1,0:T(8,128)(2,1)S(1)} %get-tuple-element.16.hi, bf16[24,128,256]{2,1,0:T(8,128)(2,1)S(1)} %get-tuple-element.17.lo), custom_call_target="tpu_custom_call" | custom-call | flops 1811939328 | tf_op jit(solution)/shard_map/pallas_call | solution.py:147
  88.2 7.3 %all-gather.1 = f32[768,128]{1,0:T(8,128)S(1)} all-gather(f32[384,128]{1,0:T(8,128)S(1)} %get-tuple-element.25), channel_id=3, replica_groups=mesh['xh'=2,'y'=8,'xl'=2,'z'=12,'c'=2] {'xl'}, dimensions={0}, use_global_device_ids=true | all-gather | bytes 589824 | tf_op jit(solution)/shard_map/all_gather | solution.py:243
  95.6 0.6 shard_map.63.refs_0_
  96.2 1.9 %collective-permute-start.21 = (f32[384,128]{1,0:T(8,128)S(1)}, f32[384,128]{1,0:T(8,128)S(1)}, u32[]{:S(2)}, u32[]{:S(2)}) collective-permute-start(f32[384,128]{1,0:T(8,128)S(1)} %shard_map.63.refs_0_), channel_id=1, source_target_pairs={{0,2},{2,4},{4,6},{6,8},{8,10},{10,12},{12,14},{14,16},{16,18},{18... | collective-permute-start | bytes 589832 | tf_op jit(solution)/shard_map/ppermute | solution.py:257
  98.1 7.8 %collective-permute-start.17 = (f32[384,128]{1,0:T(8,128)S(1)}, f32[384,128]{1,0:T(8,128)S(1)}, u32[]{:S(2)}, u32[]{:S(2)}) collective-permute-start(f32[384,128]{1,0:T(8,128)S(1)} %shard_map.63.refs_0_), channel_id=1, source_target_pairs={{0,22},{2,0},{4,2},{6,4},{8,6},{10,8},{12,10},{14,12},{16,14},{18,... | collective-permute-start | bytes 589832 | tf_op jit(solution)/shard_map/ppermute | solution.py:257
  105.9 2.8 %collective-permute-done.21.refs_1_ = f32[384,128]{1,0:T(8,128)S(1)} collective-permute-done((f32[384,128]{1,0:T(8,128)S(1)}, f32[384,128]{1,0:T(8,128)S(1)}, u32[]{:S(2)}, u32[]{:S(2)}) %collective-permute-start.21) | collective-permute-done | bytes 196640 | tf_op jit(solution)/shard_map/ppermute | solution.py:257
  108.7 1.9 %collective-permute-start.22 = (f32[384,128]{1,0:T(8,128)S(1)}, f32[384,128]{1,0:T(8,128)S(1)}, u32[]{:S(2)}, u32[]{:S(2)}) collective-permute-start(f32[384,128]{1,0:T(8,128)S(1)} %collective-permute-done.21.refs_1_), channel_id=1, source_target_pairs={{0,2},{2,4},{4,6},{6,8},{8,10},{10,12},{12,14},{14,16},{16,18},{18... | collective-permute-start | bytes 589832 | tf_op jit(solution)/shard_map/ppermute | solution.py:257
  110.6 4.6 %collective-permute-start.18 = (f32[384,128]{1,0:T(8,128)S(1)}, f32[384,128]{1,0:T(8,128)S(1)}, u32[]{:S(2)}, u32[]{:S(2)}) collective-permute-start(f32[384,128]{1,0:T(8,128)S(1)} %collective-permute-done.17.refs_2_), channel_id=1, source_target_pairs={{0,22},{2,0},{4,2},{6,4},{8,6},{10,8},{12,10},{14,12},{16,14},{18,... | collective-permute-start | bytes 589832 | tf_op jit(solution)/shard_map/ppermute | solution.py:257
  115.2 1.8 %collective-permute-done.22.refs_3_ = f32[384,128]{1,0:T(8,128)S(1)} collective-permute-done((f32[384,128]{1,0:T(8,128)S(1)}, f32[384,128]{1,0:T(8,128)S(1)}, u32[]{:S(2)}, u32[]{:S(2)}) %collective-permute-start.22) | collective-permute-done | bytes 196640 | tf_op jit(solution)/shard_map/ppermute | solution.py:257
  117.1 1.9 %collective-permute-start.23 = (f32[384,128]{1,0:T(8,128)S(1)}, f32[384,128]{1,0:T(8,128)S(1)}, u32[]{:S(2)}, u32[]{:S(2)}) collective-permute-start(f32[384,128]{1,0:T(8,128)S(1)} %collective-permute-done.22.refs_3_), channel_id=1, source_target_pairs={{0,2},{2,4},{4,6},{6,8},{8,10},{10,12},{12,14},{14,16},{16,18},{18... | collective-permute-start | bytes 589832 | tf_op jit(solution)/shard_map/ppermute | solution.py:257
  119.0 0.0 collective-permute-done.18.refs_0_
  119.0 4.6 %collective-permute-start.19 = (f32[384,128]{1,0:T(8,128)S(1)}, f32[384,128]{1,0:T(8,128)S(1)}, u32[]{:S(2)}, u32[]{:S(2)}) collective-permute-start(f32[384,128]{1,0:T(8,128)S(1)} %collective-permute-done.18.refs_0_), channel_id=1, source_target_pairs={{0,22},{2,0},{4,2},{6,4},{8,6},{10,8},{12,10},{14,12},{16,14},{18,... | collective-permute-start | bytes 589832 | tf_op jit(solution)/shard_map/ppermute | solution.py:257
  123.6 1.1 collective-permute-done.23.refs_1_
  124.7 1.9 %collective-permute-start.24 = (f32[384,128]{1,0:T(8,128)S(1)}, f32[384,128]{1,0:T(8,128)S(1)}, u32[]{:S(2)}, u32[]{:S(2)}) collective-permute-start(f32[384,128]{1,0:T(8,128)S(1)} %collective-permute-done.23.refs_1_), channel_id=1, source_target_pairs={{0,2},{2,4},{4,6},{6,8},{8,10},{10,12},{12,14},{14,16},{16,18},{18... | collective-permute-start | bytes 589832 | tf_op jit(solution)/shard_map/ppermute | solution.py:257
  126.6 0.0 collective-permute-done.19.refs_2_
  126.6 4.6 %collective-permute-start.20 = (f32[384,128]{1,0:T(8,128)S(1)}, f32[384,128]{1,0:T(8,128)S(1)}, u32[]{:S(2)}, u32[]{:S(2)}) collective-permute-start(f32[384,128]{1,0:T(8,128)S(1)} %collective-permute-done.19.refs_2_), channel_id=1, source_target_pairs={{0,22},{2,0},{4,2},{6,4},{8,6},{10,8},{12,10},{14,12},{16,14},{18,... | collective-permute-start | bytes 589832 | tf_op jit(solution)/shard_map/ppermute | solution.py:257
  131.2 1.1 collective-permute-done.24.refs_3_
  132.3 1.9 %collective-permute-start.25 = (f32[384,128]{1,0:T(8,128)S(1)}, f32[384,128]{1,0:T(8,128)S(1)}, u32[]{:S(2)}, u32[]{:S(2)}) collective-permute-start(f32[384,128]{1,0:T(8,128)S(1)} %collective-permute-done.24.refs_3_), channel_id=1, source_target_pairs={{0,2},{2,4},{4,6},{6,8},{8,10},{10,12},{12,14},{14,16},{16,18},{18... | collective-permute-start | bytes 589832 | tf_op jit(solution)/shard_map/ppermute | solution.py:257
  134.2 4.6 %collective-permute-start.26 = (f32[384,128]{1,0:T(8,128)S(1)}, f32[384,128]{1,0:T(8,128)S(1)}, u32[]{:S(2)}, u32[]{:S(2)}) collective-permute-start(f32[384,128]{1,0:T(8,128)S(1)} %collective-permute-done.20.refs_0_), channel_id=1, source_target_pairs={{0,22},{2,0},{4,2},{6,4},{8,6},{10,8},{12,10},{14,12},{16,14},{18,... | collective-permute-start | bytes 589832 | tf_op jit(solution)/shard_map/ppermute | solution.py:257
  138.8 1.6 shard_map.62
  140.5 0.8 shard_map.64.refs_4_
  141.3 0.8 shard_map.65.refs_3_
  142.1 0.0 collective-permute-done.25.refs_1_
  142.1 1.9 %collective-permute-start.27 = (f32[384,128]{1,0:T(8,128)S(1)}, f32[384,128]{1,0:T(8,128)S(1)}, u32[]{:S(2)}, u32[]{:S(2)}) collective-permute-start(f32[384,128]{1,0:T(8,128)S(1)} %collective-permute-done.25.refs_1_), channel_id=1, source_target_pairs={{0,2},{2,4},{4,6},{6,8},{8,10},{10,12},{12,14},{14,16},{16,18},{18... | collective-permute-start | bytes 589832 | tf_op jit(solution)/shard_map/ppermute | solution.py:257
  144.0 0.8 shard_map.66
  144.8 6.9 %all-gather.2 = f32[768,256]{1,0:T(8,128)S(1)} all-gather(f32[384,256]{1,0:T(8,128)S(1)} %get-tuple-element.27), channel_id=4, replica_groups=mesh['xh'=2,'y'=8,'xl'=2,'z'=12,'c'=2] {'c'}, dimensions={0}, use_global_device_ids=true | all-gather | bytes 1179648 | tf_op jit(solution)/shard_map/all_gather | solution.py:213
  151.8 5.7 %all-gather.3 = f32[768,128]{1,0:T(8,128)S(1)} all-gather(f32[384,128]{1,0:T(8,128)S(1)} %collective-permute-done.27), channel_id=5, replica_groups=mesh['xh'=2,'y'=8,'xl'=2,'z'=12,'c'=2] {'c'}, dimensions={0}, use_global_device_ids=true | all-gather | bytes 589824 | tf_op jit(solution)/shard_map/all_gather | solution.py:215
  157.5 0.3 shard_map.67
  157.8 6.8 %all-gather.4 = f32[768,128]{1,0:T(8,128)S(1)} all-gather(f32[384,128]{1,0:T(8,128)S(1)} %get-tuple-element.29), channel_id=6, replica_groups=mesh['xh'=2,'y'=8,'xl'=2,'z'=12,'c'=2] {'xl'}, dimensions={0}, use_global_device_ids=true | all-gather | bytes 589824 | tf_op jit(solution)/shard_map/all_gather | solution.py:243
  164.6 1.3 shard_map.68
  (11 shorter events, 0.0 us)
Async XLA Ops:
  7.2 76.7 %all-gather.7.cloned.1.call-start = ((), (), s32[]{:S(2)}) async-start(), calls=%async_computation | async-start | bytes 4915200 | tf_op jit(solution)/shard_map/all_gather | solution.py:288
  8.9 8.4 %collective-permute-start.8 = (f32[384,128]{1,0:T(8,128)}, f32[384,128]{1,0:T(8,128)S(1)}, u32[]{:S(2)}, u32[]{:S(2)}) collective-permute-start(f32[384,128]{1,0:T(8,128)} %shard_map.59), channel_id=1, source_target_pairs={{24,0},{384,408},{0,384},{408,24},{25,1},{385,409},{1,385},{409,25... | collective-permute-start | bytes 589832 | tf_op jit(solution)/shard_map/ppermute | solution.py:291
  14.4 9.0 %collective-permute-start = (f32[384,128]{1,0:T(8,128)}, f32[384,128]{1,0:T(8,128)S(1)}, u32[]{:S(2)}, u32[]{:S(2)}) collective-permute-start(f32[384,128]{1,0:T(8,128)} %shard_map.59), channel_id=1, source_target_pairs={{0,0},{24,384},{384,24},{408,408},{1,1},{25,385},{385,25},{409,409... | collective-permute-start | bytes 589832 | tf_op jit(solution)/shard_map/ppermute | solution.py:290
  17.3 14.5 %collective-permute-start.10 = (f32[384,128]{1,0:T(8,128)S(1)}, f32[384,128]{1,0:T(8,128)S(1)}, u32[]{:S(2)}, u32[]{:S(2)}) collective-permute-start(f32[384,128]{1,0:T(8,128)S(1)} %collective-permute-done.8.refs_8_), channel_id=1, source_target_pairs={{0,336},{48,0},{96,48},{144,96},{192,144},{240,192},{288,240},{336... | collective-permute-start | bytes 589832 | tf_op jit(solution)/shard_map/ppermute | solution.py:257
  23.4 11.8 %collective-permute-start.1 = (f32[384,128]{1,0:T(8,128)S(1)}, f32[384,128]{1,0:T(8,128)S(1)}, u32[]{:S(2)}, u32[]{:S(2)}) collective-permute-start(f32[384,128]{1,0:T(8,128)S(1)} %collective-permute-done.refs_0_), channel_id=1, source_target_pairs={{0,48},{48,96},{96,144},{144,192},{192,240},{240,288},{288,336},{3... | collective-permute-start | bytes 589832 | tf_op jit(solution)/shard_map/ppermute | solution.py:257
  25.3 11.8 %collective-permute-start.9 = (f32[384,128]{1,0:T(8,128)S(1)}, f32[384,128]{1,0:T(8,128)S(1)}, u32[]{:S(2)}, u32[]{:S(2)}) collective-permute-start(f32[384,128]{1,0:T(8,128)S(1)} %collective-permute-done.8.refs_8_), channel_id=1, source_target_pairs={{0,48},{48,96},{96,144},{144,192},{192,240},{240,288},{288,336},{3... | collective-permute-start | bytes 589832 | tf_op jit(solution)/shard_map/ppermute | solution.py:257
  27.3 11.8 %collective-permute-start.2 = (f32[384,128]{1,0:T(8,128)S(1)}, f32[384,128]{1,0:T(8,128)S(1)}, u32[]{:S(2)}, u32[]{:S(2)}) collective-permute-start(f32[384,128]{1,0:T(8,128)S(1)} %collective-permute-done.refs_0_), channel_id=1, source_target_pairs={{0,336},{48,0},{96,48},{144,96},{192,144},{240,192},{288,240},{336... | collective-permute-start | bytes 589832 | tf_op jit(solution)/shard_map/ppermute | solution.py:257
  31.8 11.8 %collective-permute-start.12 = (f32[384,128]{1,0:T(8,128)S(1)}, f32[384,128]{1,0:T(8,128)S(1)}, u32[]{:S(2)}, u32[]{:S(2)}) collective-permute-start(f32[384,128]{1,0:T(8,128)S(1)} %collective-permute-done.10.refs_10_), channel_id=1, source_target_pairs={{0,336},{48,0},{96,48},{144,96},{192,144},{240,192},{288,240},{336... | collective-permute-start | bytes 589832 | tf_op jit(solution)/shard_map/ppermute | solution.py:257
  35.2 11.8 %collective-permute-start.3 = (f32[384,128]{1,0:T(8,128)S(1)}, f32[384,128]{1,0:T(8,128)S(1)}, u32[]{:S(2)}, u32[]{:S(2)}) collective-permute-start(f32[384,128]{1,0:T(8,128)S(1)} %collective-permute-done.1.refs_1_), channel_id=1, source_target_pairs={{0,48},{48,96},{96,144},{144,192},{192,240},{240,288},{288,336},{3... | collective-permute-start | bytes 589832 | tf_op jit(solution)/shard_map/ppermute | solution.py:257
  37.2 11.8 %collective-permute-start.11 = (f32[384,128]{1,0:T(8,128)S(1)}, f32[384,128]{1,0:T(8,128)S(1)}, u32[]{:S(2)}, u32[]{:S(2)}) collective-permute-start(f32[384,128]{1,0:T(8,128)S(1)} %collective-permute-done.9.refs_9_), channel_id=1, source_target_pairs={{0,48},{48,96},{96,144},{144,192},{192,240},{240,288},{288,336},{3... | collective-permute-start | bytes 589832 | tf_op jit(solution)/shard_map/ppermute | solution.py:257
  39.1 11.8 %collective-permute-start.4 = (f32[384,128]{1,0:T(8,128)S(1)}, f32[384,128]{1,0:T(8,128)S(1)}, u32[]{:S(2)}, u32[]{:S(2)}) collective-permute-start(f32[384,128]{1,0:T(8,128)S(1)} %collective-permute-done.2.refs_2_), channel_id=1, source_target_pairs={{0,336},{48,0},{96,48},{144,96},{192,144},{240,192},{288,240},{336... | collective-permute-start | bytes 589832 | tf_op jit(solution)/shard_map/ppermute | solution.py:257
  43.7 11.8 %collective-permute-start.14 = (f32[384,128]{1,0:T(8,128)S(1)}, f32[384,128]{1,0:T(8,128)S(1)}, u32[]{:S(2)}, u32[]{:S(2)}) collective-permute-start(f32[384,128]{1,0:T(8,128)S(1)} %collective-permute-done.12.refs_12_), channel_id=1, source_target_pairs={{0,336},{48,0},{96,48},{144,96},{192,144},{240,192},{288,240},{336... | collective-permute-start | bytes 589832 | tf_op jit(solution)/shard_map/ppermute | solution.py:257
  47.1 11.8 %collective-permute-start.5 = (f32[384,128]{1,0:T(8,128)S(1)}, f32[384,128]{1,0:T(8,128)S(1)}, u32[]{:S(2)}, u32[]{:S(2)}) collective-permute-start(f32[384,128]{1,0:T(8,128)S(1)} %collective-permute-done.3.refs_3_), channel_id=1, source_target_pairs={{0,48},{48,96},{96,144},{144,192},{192,240},{240,288},{288,336},{3... | collective-permute-start | bytes 589832 | tf_op jit(solution)/shard_map/ppermute | solution.py:257
  49.0 11.8 %collective-permute-start.13 = (f32[384,128]{1,0:T(8,128)S(1)}, f32[384,128]{1,0:T(8,128)S(1)}, u32[]{:S(2)}, u32[]{:S(2)}) collective-permute-start(f32[384,128]{1,0:T(8,128)S(1)} %collective-permute-done.11.refs_11_), channel_id=1, source_target_pairs={{0,48},{48,96},{96,144},{144,192},{192,240},{240,288},{288,336},{3... | collective-permute-start | bytes 589832 | tf_op jit(solution)/shard_map/ppermute | solution.py:257
  51.0 9.9 %collective-permute-start.6 = (f32[384,128]{1,0:T(8,128)S(1)}, f32[384,128]{1,0:T(8,128)S(1)}, u32[]{:S(2)}, u32[]{:S(2)}) collective-permute-start(f32[384,128]{1,0:T(8,128)S(1)} %collective-permute-done.4.refs_4_), channel_id=1, source_target_pairs={{0,336},{48,0},{96,48},{144,96},{192,144},{240,192},{288,240},{336... | collective-permute-start | bytes 589832 | tf_op jit(solution)/shard_map/ppermute | solution.py:257
  55.5 6.9 %collective-permute-start.15 = (f32[384,128]{1,0:T(8,128)S(1)}, f32[384,128]{1,0:T(8,128)S(1)}, u32[]{:S(2)}, u32[]{:S(2)}) collective-permute-start(f32[384,128]{1,0:T(8,128)S(1)} %collective-permute-done.14.refs_14_), channel_id=1, source_target_pairs={{0,336},{48,0},{96,48},{144,96},{192,144},{240,192},{288,240},{336... | collective-permute-start | bytes 589832 | tf_op jit(solution)/shard_map/ppermute | solution.py:257
  58.9 9.7 %collective-permute-start.7 = (f32[384,128]{1,0:T(8,128)S(1)}, f32[384,128]{1,0:T(8,128)S(1)}, u32[]{:S(2)}, u32[]{:S(2)}) collective-permute-start(f32[384,128]{1,0:T(8,128)S(1)} %collective-permute-done.5.refs_5_), channel_id=1, source_target_pairs={{0,48},{48,96},{96,144},{144,192},{192,240},{240,288},{288,336},{3... | collective-permute-start | bytes 589832 | tf_op jit(solution)/shard_map/ppermute | solution.py:257
  70.4 17.8 %collective-permute-start.16 = (f32[12,128,256]{2,1,0:T(8,128)}, f32[12,128,256]{2,1,0:T(8,128)}, u32[]{:S(2)}, u32[]{:S(2)}) collective-permute-start(f32[12,128,256]{2,1,0:T(8,128)} %get-tuple-element.20), channel_id=1, source_target_pairs={{0,1},{1,0},{2,3},{3,2},{4,5},{5,4},{6,7},{7,6},{8,9},{9,8},{10,11... | collective-permute-start | bytes 4718600 | tf_op jit(solution)/shard_map/ppermute | solution.py:257
  83.8 11.7 %copy-start = (s32[6,2]{0,1:T(2,128)S(1)}, s32[6,2]{0,1:T(2,128)}, u32[]{:S(2)}) copy-start(s32[6,2]{0,1:T(2,128)} %param.7) | copy-start | bytes 148
  96.2 12.6 %collective-permute-start.21 = (f32[384,128]{1,0:T(8,128)S(1)}, f32[384,128]{1,0:T(8,128)S(1)}, u32[]{:S(2)}, u32[]{:S(2)}) collective-permute-start(f32[384,128]{1,0:T(8,128)S(1)} %shard_map.63.refs_0_), channel_id=1, source_target_pairs={{0,2},{2,4},{4,6},{6,8},{8,10},{10,12},{12,14},{14,16},{16,18},{18... | collective-permute-start | bytes 589832 | tf_op jit(solution)/shard_map/ppermute | solution.py:257
  98.1 12.6 %collective-permute-start.17 = (f32[384,128]{1,0:T(8,128)S(1)}, f32[384,128]{1,0:T(8,128)S(1)}, u32[]{:S(2)}, u32[]{:S(2)}) collective-permute-start(f32[384,128]{1,0:T(8,128)S(1)} %shard_map.63.refs_0_), channel_id=1, source_target_pairs={{0,22},{2,0},{4,2},{6,4},{8,6},{10,8},{12,10},{14,12},{16,14},{18,... | collective-permute-start | bytes 589832 | tf_op jit(solution)/shard_map/ppermute | solution.py:257
  108.7 8.4 %collective-permute-start.22 = (f32[384,128]{1,0:T(8,128)S(1)}, f32[384,128]{1,0:T(8,128)S(1)}, u32[]{:S(2)}, u32[]{:S(2)}) collective-permute-start(f32[384,128]{1,0:T(8,128)S(1)} %collective-permute-done.21.refs_1_), channel_id=1, source_target_pairs={{0,2},{2,4},{4,6},{6,8},{8,10},{10,12},{12,14},{14,16},{16,18},{18... | collective-permute-start | bytes 589832 | tf_op jit(solution)/shard_map/ppermute | solution.py:257
  110.6 8.3 %collective-permute-start.18 = (f32[384,128]{1,0:T(8,128)S(1)}, f32[384,128]{1,0:T(8,128)S(1)}, u32[]{:S(2)}, u32[]{:S(2)}) collective-permute-start(f32[384,128]{1,0:T(8,128)S(1)} %collective-permute-done.17.refs_2_), channel_id=1, source_target_pairs={{0,22},{2,0},{4,2},{6,4},{8,6},{10,8},{12,10},{14,12},{16,14},{18,... | collective-permute-start | bytes 589832 | tf_op jit(solution)/shard_map/ppermute | solution.py:257
  117.1 7.6 %collective-permute-start.23 = (f32[384,128]{1,0:T(8,128)S(1)}, f32[384,128]{1,0:T(8,128)S(1)}, u32[]{:S(2)}, u32[]{:S(2)}) collective-permute-start(f32[384,128]{1,0:T(8,128)S(1)} %collective-permute-done.22.refs_3_), channel_id=1, source_target_pairs={{0,2},{2,4},{4,6},{6,8},{8,10},{10,12},{12,14},{14,16},{16,18},{18... | collective-permute-start | bytes 589832 | tf_op jit(solution)/shard_map/ppermute | solution.py:257
  119.0 7.6 %collective-permute-start.19 = (f32[384,128]{1,0:T(8,128)S(1)}, f32[384,128]{1,0:T(8,128)S(1)}, u32[]{:S(2)}, u32[]{:S(2)}) collective-permute-start(f32[384,128]{1,0:T(8,128)S(1)} %collective-permute-done.18.refs_0_), channel_id=1, source_target_pairs={{0,22},{2,0},{4,2},{6,4},{8,6},{10,8},{12,10},{14,12},{16,14},{18,... | collective-permute-start | bytes 589832 | tf_op jit(solution)/shard_map/ppermute | solution.py:257
  124.7 7.6 %collective-permute-start.24 = (f32[384,128]{1,0:T(8,128)S(1)}, f32[384,128]{1,0:T(8,128)S(1)}, u32[]{:S(2)}, u32[]{:S(2)}) collective-permute-start(f32[384,128]{1,0:T(8,128)S(1)} %collective-permute-done.23.refs_1_), channel_id=1, source_target_pairs={{0,2},{2,4},{4,6},{6,8},{8,10},{10,12},{12,14},{14,16},{16,18},{18... | collective-permute-start | bytes 589832 | tf_op jit(solution)/shard_map/ppermute | solution.py:257
  126.6 7.6 %collective-permute-start.20 = (f32[384,128]{1,0:T(8,128)S(1)}, f32[384,128]{1,0:T(8,128)S(1)}, u32[]{:S(2)}, u32[]{:S(2)}) collective-permute-start(f32[384,128]{1,0:T(8,128)S(1)} %collective-permute-done.19.refs_2_), channel_id=1, source_target_pairs={{0,22},{2,0},{4,2},{6,4},{8,6},{10,8},{12,10},{14,12},{16,14},{18,... | collective-permute-start | bytes 589832 | tf_op jit(solution)/shard_map/ppermute | solution.py:257
  132.3 9.8 %collective-permute-start.25 = (f32[384,128]{1,0:T(8,128)S(1)}, f32[384,128]{1,0:T(8,128)S(1)}, u32[]{:S(2)}, u32[]{:S(2)}) collective-permute-start(f32[384,128]{1,0:T(8,128)S(1)} %collective-permute-done.24.refs_3_), channel_id=1, source_target_pairs={{0,2},{2,4},{4,6},{6,8},{8,10},{10,12},{12,14},{14,16},{16,18},{18... | collective-permute-start | bytes 589832 | tf_op jit(solution)/shard_map/ppermute | solution.py:257
  134.2 9.8 %collective-permute-start.26 = (f32[384,128]{1,0:T(8,128)S(1)}, f32[384,128]{1,0:T(8,128)S(1)}, u32[]{:S(2)}, u32[]{:S(2)}) collective-permute-start(f32[384,128]{1,0:T(8,128)S(1)} %collective-permute-done.20.refs_0_), channel_id=1, source_target_pairs={{0,22},{2,0},{4,2},{6,4},{8,6},{10,8},{12,10},{14,12},{16,14},{18,... | collective-permute-start | bytes 589832 | tf_op jit(solution)/shard_map/ppermute | solution.py:257
  142.1 9.7 %collective-permute-start.27 = (f32[384,128]{1,0:T(8,128)S(1)}, f32[384,128]{1,0:T(8,128)S(1)}, u32[]{:S(2)}, u32[]{:S(2)}) collective-permute-start(f32[384,128]{1,0:T(8,128)S(1)} %collective-permute-done.25.refs_1_), channel_id=1, source_target_pairs={{0,2},{2,4},{4,6},{6,8},{8,10},{10,12},{12,14},{14,16},{16,18},{18... | collective-permute-start | bytes 589832 | tf_op jit(solution)/shard_map/ppermute | solution.py:257
Sparse Core Ops, SparseCore 0:
  11.0 72.7 all-gather.6
